TPU v7x, 32 devices: a whole 2x2x4 slice. The times are simulated.
32 devices in a mesh: dp: 16 (over z, x, core), tensor: 2 (over y).
Axes of the slice: x: 2, y: 2, z: 4, core: 2. Of those that a mesh axis runs over, the one named last changes fastest.
Arguments:
- layer_input: bfloat16 [4096, 2048], P(('dp', 'tensor')), may hold values from -17 to 17
- query_weight: bfloat16 [2048, 4096], P('dp', 'tensor'), may hold values from -0.125 to 0.125
- key_projection: bfloat16 [2048, 512], P('dp', 'tensor'), may hold values from -0.125 to 0.125
- value_projection: bfloat16 [2048, 512], P('dp', 'tensor'), may hold values from -0.125 to 0.125
- context_weight: bfloat16 [4096, 2048], P('tensor', 'dp'), may hold values from -0.75 to 0.75
- router_weight: bfloat16 [2048, 32], P('dp'), may hold values from -0.0625 to 0.0625
- expert_gate: bfloat16 [32, 2048, 768], P('dp', None, 'tensor'), may hold values from -0.125 to 0.125
- expert_up: bfloat16 [32, 2048, 768], P('dp', None, 'tensor'), may hold values from -0.125 to 0.125
- expert_down: bfloat16 [32, 768, 2048], P('dp', 'tensor'), may hold values from -0.875 to 0.875
- prenorm_gain: bfloat16 [2048], P('dp'), may hold values from 0.099609375 to 1.8984375
- midnorm_gain: bfloat16 [2048], P('dp'), may hold values from 0.099609375 to 1.8984375
- querynorm_gain: bfloat16 [128], P('dp'), may hold values from 0.099609375 to 1.8984375
- keynorm_gain: bfloat16 [128], P('dp'), may hold values from 0.099609375 to 1.8984375
- routes: int32 [4096, 8], P('dp'), may hold values from 0 to 31, all different within a row; in each aligned block of 256 rows (0 to 255, 256 to 511, ...) at most 80 rows name the same one
- lengths: int32 [16], replicated, may hold values from 1 to 256, 3072 in all
- sequence_order: int32 [16], replicated, may hold values from 0 to 15, each once
- output_cotangent: bfloat16 [4096, 2048], P(('dp', 'tensor')), may hold values from -6 to 6
Outputs:
- layer_output: bfloat16 [4096, 2048], P(('dp', 'tensor'))
- input_gradient: bfloat16 [4096, 2048], P(('dp', 'tensor'))
- query_gradient: float32 [2048, 4096], P('dp', 'tensor')
- key_gradient: float32 [2048, 512], P('dp', 'tensor')
- value_gradient: float32 [2048, 512], P('dp', 'tensor')
- context_gradient: float32 [4096, 2048], P('tensor', 'dp')
- router_gradient: float32 [2048, 32], P('dp')
- gate_gradient: float32 [32, 2048, 768], P('dp', None, 'tensor')
- up_gradient: float32 [32, 2048, 768], P('dp', None, 'tensor')
- down_gradient: float32 [32, 768, 2048], P('dp', 'tensor')
- prenorm_gradient: float32 [2048], P('dp')
- midnorm_gradient: float32 [2048], P('dp')
- querynorm_gradient: float32 [128], P('dp')
- keynorm_gradient: float32 [128], P('dp')
Inputs may be any that keep to these rules, and one draw needn't show every extreme that they name: `routes`: each row names 8 different experts; in the rows of one index of dp (aligned blocks of 256 rows) no expert is named by more than 80 rows, and in every draw some expert is named by exactly 80 rows of a block. The lengths sum to 3072; the largest is exactly 256. `sequence_order`: each sequence appears once.
All inputs are finite; a program needn't handle non-finite values.
Results may differ from a plain program's by a relative error of at most 0.019.
Values may be sent and summed in bfloat16 or wider, within the bound.
A program may use at most 256 MiB of HBM per device.

v0:
```python
import math

import jax
import jax.numpy as jnp
from jax import lax
from jax.sharding import PartitionSpec as P

HEAD_SIZE = 128
TOP = 8
EXP_DEV = 2


epsilon = 1e-06
rope_base = 1000000.0
masked_score = -1e30


def carried_in(value, axis, combine, identity):
    count, place = (lax.axis_size(axis), lax.axis_index(axis))
    everything = lax.all_gather(value, axis)
    start = jnp.broadcast_to(jnp.asarray(identity, value.dtype), value.shape)

    def hop(k, before):
        reached = k < place
        new = combine(before, everything[k])
        return jnp.where(reached, new, before)

    return lax.fori_loop(0, count, hop, start)


def rms_normalize(value_rows):
    scaling = lax.rsqrt(jnp.mean(value_rows * value_rows, axis=-1, keepdims=True) + epsilon)
    return (value_rows * scaling, scaling)


def norm_back(cotangent, unit_rows, scaling):
    return scaling * (
        cotangent - unit_rows * jnp.mean(cotangent * unit_rows, axis=-1, keepdims=True)
    )


def rotary_apply(value_rows, cosine_table, sine_values):
    middle = value_rows.shape[-1] // 2
    former = value_rows[..., :middle]
    latter = value_rows[..., middle:]
    return jnp.concatenate(
        [
            former * cosine_table - latter * sine_values,
            latter * cosine_table + former * sine_values,
        ],
        axis=-1,
    )


def matrix_product(former, latter):
    return jnp.dot(former, latter, preferred_element_type=jnp.float32)


def contract(former, latter):
    return lax.dot_general(
        former, latter, (((0,), (0,)), ((), ())), preferred_element_type=jnp.float32
    )


def transposed(former, latter):
    return lax.dot_general(
        former, latter, (((1,), (1,)), ((), ())), preferred_element_type=jnp.float32
    )


def to_owners(buffer):
    return lax.all_to_all(buffer, "dp", split_axis=1, concat_axis=1, tiled=True)


def owner_reduce(partial_rows):
    shares = lax.psum_scatter(
        partial_rows.astype(jnp.bfloat16), "tensor", scatter_dimension=2, tiled=True
    )
    return lax.all_gather(shares, "tensor", axis=2, tiled=True)


def body(
    layer_input,
    query_weight,
    key_projection,
    value_projection,
    context_weight,
    router_weight,
    expert_gate,
    expert_up,
    expert_down,
    prenorm_gain,
    midnorm_gain,
    querynorm_gain,
    keynorm_gain,
    routes,
    lengths,
    sequence_order,
    output_cotangent,
):
    tensor_count = lax.axis_size("tensor")
    tensor_index = lax.axis_index("tensor")
    dp_count = lax.axis_size("dp")
    own_rows = layer_input.shape[0]
    block_rows = own_rows * tensor_count
    features = layer_input.shape[1]
    expert_count = EXP_DEV * dp_count
    capacity = 3 * block_rows * TOP // (4 * EXP_DEV)
    most_rows = (5 * block_rows * TOP + 4 * expert_count - 1) // (4 * expert_count)
    slot_total = EXP_DEV * dp_count * most_rows
    (
        query_all,
        key_all,
        value_all,
        context_all,
        router_all,
        gain_first,
        gain_second,
        query_gain,
        gain_key,
    ) = (
        lax.all_gather(query_weight, "dp", axis=0, tiled=True),
        lax.all_gather(key_projection, "dp", axis=0, tiled=True),
        lax.all_gather(value_projection, "dp", axis=0, tiled=True),
        lax.all_gather(context_weight, "dp", axis=1, tiled=True),
        lax.all_gather(router_weight, "dp", axis=0, tiled=True),
        lax.all_gather(prenorm_gain, "dp", axis=0, tiled=True),
        lax.all_gather(midnorm_gain, "dp", axis=0, tiled=True),
        lax.all_gather(querynorm_gain, "dp", axis=0, tiled=True),
        lax.all_gather(keynorm_gain, "dp", axis=0, tiled=True),
    )
    input_rows, cot_rows = (
        lax.all_gather(layer_input, "tensor", axis=0, tiled=True),
        lax.all_gather(output_cotangent, "tensor", axis=0, tiled=True),
    )
    position = jnp.arange(block_rows, dtype=jnp.int32)
    seq_length = lengths[sequence_order[lax.axis_index("dp")]]
    token_live = position < seq_length
    frequency = jnp.exp(
        -math.log(rope_base) * jnp.arange(HEAD_SIZE // 2, dtype=jnp.float32) * (2.0 / HEAD_SIZE)
    )
    angles = position.astype(jnp.float32)[:, None] * frequency[None, :]
    cosine_table = jnp.cos(angles)[:, None, :]
    sine_values = jnp.sin(angles)[:, None, :]
    heads_query = query_all.shape[1] // HEAD_SIZE
    heads_key = key_all.shape[1] // HEAD_SIZE
    group_width = heads_query // heads_key
    gain_one = gain_first.astype(jnp.float32)
    gain_two = gain_second.astype(jnp.float32)
    query_factor = query_gain.astype(jnp.float32)
    key_factor = gain_key.astype(jnp.float32)
    stream = input_rows.astype(jnp.float32)
    unit_first, scale_first = rms_normalize(stream)
    first_layer_normed = (unit_first * gain_one).astype(jnp.bfloat16)
    query_unnormed = matrix_product(first_layer_normed, query_all).reshape(
        block_rows, heads_query, HEAD_SIZE
    )
    key_unnormed = matrix_product(first_layer_normed, key_all).reshape(
        block_rows, heads_key, HEAD_SIZE
    )
    value_rows = (
        matrix_product(first_layer_normed, value_all)
        .astype(jnp.bfloat16)
        .reshape(block_rows, heads_key, HEAD_SIZE)
    )
    query_unit, query_scale = rms_normalize(query_unnormed)
    key_unit, key_scale = rms_normalize(key_unnormed)
    query_rows = (
        rotary_apply(query_unit * query_factor, cosine_table, sine_values)
        .astype(jnp.bfloat16)
        .reshape(block_rows, heads_key, group_width, HEAD_SIZE)
    )
    keys_rot = rotary_apply(key_unit * key_factor, cosine_table, sine_values).astype(jnp.bfloat16)
    score_scale = HEAD_SIZE ** (-0.5)
    allowed = (position[None, :] <= position[:, None]) & token_live[None, :]

    def score_block():
        raw_scores = (
            jnp.einsum("ikrd,jkd->krij", query_rows, keys_rot, preferred_element_type=jnp.float32)
            * score_scale
        )
        return jnp.where(allowed, raw_scores, masked_score)

    scores = score_block()
    row_peak = jnp.max(scores, axis=-1, keepdims=True)
    log_total = row_peak + jnp.log(jnp.sum(jnp.exp(scores - row_peak), axis=-1, keepdims=True))
    soft_probs = jnp.exp(scores - log_total)
    context = jnp.einsum(
        "krij,jkd->ikrd",
        soft_probs.astype(jnp.bfloat16),
        value_rows,
        preferred_element_type=jnp.float32,
    )
    context = context.reshape(block_rows, heads_query * HEAD_SIZE).astype(jnp.bfloat16)
    attention = lax.psum(matrix_product(context, context_all), "tensor")
    residual = stream + attention
    unit_second, scale_second = rms_normalize(residual)
    normed_second = (unit_second * gain_two).astype(jnp.bfloat16)
    logits = matrix_product(normed_second, router_all)
    expert_ids = jnp.arange(expert_count, dtype=jnp.int32)
    route_hot = routes[:, :, None] == expert_ids[None, None, :]
    chosen = jnp.sum(jnp.where(route_hot, logits[:, None, :], 0.0), axis=-1)
    gate_weights = jax.nn.softmax(chosen, axis=-1)
    pair_expert = routes.reshape(-1)
    pair_live = jnp.repeat(token_live, TOP)
    pair_hot = ((pair_expert[:, None] == expert_ids[None, :]) & pair_live[:, None]).astype(
        jnp.int32
    )
    running = jnp.cumsum(pair_hot, axis=0)
    pair_rank = jnp.sum((running - pair_hot) * pair_hot, axis=1)
    counts = running[-1]
    earlier = carried_in(
        counts, "dp", lambda former, latter: former + latter, jnp.zeros_like(counts)
    )
    pair_slot = jnp.sum(earlier[None, :] * pair_hot, axis=1) + pair_rank
    pair_kept = pair_live & (pair_slot < capacity)
    local_expert = pair_expert % EXP_DEV
    owner_index = pair_expert // EXP_DEV
    buffer_index = (local_expert * dp_count + owner_index) * most_rows + pair_rank
    target = jnp.where(pair_kept, buffer_index, slot_total)
    pair_ids = jnp.arange(block_rows * TOP, dtype=jnp.int32)
    slot_pair = jnp.full((slot_total,), -1, dtype=jnp.int32).at[target].set(pair_ids, mode="drop")
    slot_used = slot_pair >= 0
    slot_safe = jnp.maximum(slot_pair, 0)
    slot_token = slot_safe // TOP
    bf_zero = jnp.zeros((), jnp.bfloat16)
    send_rows = jnp.where(slot_used[:, None], normed_second[slot_token], bf_zero)
    layout = (EXP_DEV, dp_count, most_rows, features)
    received = to_owners(send_rows.reshape(layout)).reshape(EXP_DEV, dp_count * most_rows, features)
    gate_pre = jnp.einsum("end,edf->enf", received, expert_gate, preferred_element_type=jnp.float32)
    up_pre = jnp.einsum("end,edf->enf", received, expert_up, preferred_element_type=jnp.float32)
    sigmoid_gate = jax.nn.sigmoid(gate_pre)
    gate_act = gate_pre * sigmoid_gate
    hidden = (gate_act * up_pre).astype(jnp.bfloat16)
    out_partial = jnp.einsum(
        "enf,efd->end", hidden, expert_down, preferred_element_type=jnp.float32
    )
    expert_out = owner_reduce(out_partial)
    width = expert_out.shape[2]
    returned = lax.all_to_all(
        expert_out.reshape(EXP_DEV, dp_count, most_rows, width),
        "dp",
        split_axis=1,
        concat_axis=1,
        tiled=True,
    ).reshape(slot_total, width)
    pair_place = jnp.where(pair_kept, buffer_index, 0)
    pair_out = jnp.where(pair_kept[:, None], returned[pair_place], bf_zero).reshape(
        block_rows, TOP, width
    )
    expert_part = jnp.sum(gate_weights[:, :, None] * pair_out, axis=1)
    cot_full = cot_rows.astype(jnp.float32)
    own_start = tensor_index * own_rows
    gate_part = jnp.sum(cot_full[:, None, :] * pair_out, axis=-1)
    expert_own = lax.dynamic_slice_in_dim(expert_part, own_start, own_rows, 0)
    residual_own = lax.dynamic_slice_in_dim(residual, own_start, own_rows, 0)
    layer_output = (residual_own + expert_own).astype(jnp.bfloat16)
    slot_gate = jnp.where(slot_used, gate_weights.reshape(-1)[slot_safe], 0.0)
    send_cot = (slot_gate[:, None] * cot_full[slot_token]).astype(jnp.bfloat16)
    expert_cot = to_owners(send_cot.reshape(layout)).reshape(
        EXP_DEV, dp_count * most_rows, features
    )
    hidden_cot = jnp.einsum(
        "end,efd->enf", expert_cot, expert_down, preferred_element_type=jnp.float32
    )
    gating_cot = (
        hidden_cot * up_pre * sigmoid_gate * (1.0 + gate_pre * (1.0 - sigmoid_gate))
    ).astype(jnp.bfloat16)
    upward_cot = (hidden_cot * gate_act).astype(jnp.bfloat16)
    down_gradient = jnp.einsum(
        "enf,end->efd", hidden, expert_cot, preferred_element_type=jnp.float32
    )
    gate_gradient = jnp.einsum(
        "end,enf->edf", received, gating_cot, preferred_element_type=jnp.float32
    )
    up_gradient = jnp.einsum(
        "end,enf->edf", received, upward_cot, preferred_element_type=jnp.float32
    )
    row_partial = jnp.einsum(
        "enf,edf->end", gating_cot, expert_gate, preferred_element_type=jnp.float32
    )
    row_partial = row_partial + jnp.einsum(
        "enf,edf->end", upward_cot, expert_up, preferred_element_type=jnp.float32
    )
    row_cot = owner_reduce(row_partial)
    row_back = lax.all_to_all(
        row_cot.reshape(EXP_DEV, dp_count, most_rows, width),
        "dp",
        split_axis=1,
        concat_axis=1,
        tiled=True,
    ).reshape(slot_total, width)
    pair_cot = jnp.where(pair_kept[:, None], row_back[pair_place], bf_zero).reshape(
        block_rows, TOP, width
    )
    normed_part = jnp.sum(pair_cot.astype(jnp.float32), axis=1)
    normed_cot = normed_part
    route_cot = gate_weights * (
        gate_part - jnp.sum(gate_weights * gate_part, axis=-1, keepdims=True)
    )
    logit_cot = jnp.sum(jnp.where(route_hot, route_cot[:, :, None], 0.0), axis=1).astype(
        jnp.bfloat16
    )
    router_gradient = contract(normed_second, logit_cot)
    normed_cot = normed_cot + transposed(logit_cot, router_all)
    midnorm_gradient = jnp.sum(normed_cot * unit_second, axis=0)
    residual_cot = cot_full + norm_back(normed_cot * gain_two, unit_second, scale_second)
    attention_cot = residual_cot.astype(jnp.bfloat16)
    context_gradient = contract(context, attention_cot)
    context_cot = (
        transposed(attention_cot, context_all)
        .astype(jnp.bfloat16)
        .reshape(block_rows, heads_key, group_width, HEAD_SIZE)
    )
    scores = score_block()
    soft_probs = jnp.exp(scores - log_total)
    prob_cot = jnp.einsum(
        "ikrd,jkd->krij", context_cot, value_rows, preferred_element_type=jnp.float32
    )
    score_cot = (
        soft_probs * (prob_cot - jnp.sum(soft_probs * prob_cot, axis=-1, keepdims=True))
    ).astype(jnp.bfloat16)
    value_cot = jnp.einsum(
        "krij,ikrd->jkd",
        soft_probs.astype(jnp.bfloat16),
        context_cot,
        preferred_element_type=jnp.float32,
    )
    value_cot = value_cot.astype(jnp.bfloat16).reshape(block_rows, heads_key * HEAD_SIZE)
    query_turned = (
        jnp.einsum(
            "krij,jkd->ikrd", score_cot, keys_rot, preferred_element_type=jnp.float32
        ).reshape(block_rows, heads_query, HEAD_SIZE)
        * score_scale
    )
    key_turned = (
        jnp.einsum("krij,ikrd->jkd", score_cot, query_rows, preferred_element_type=jnp.float32)
        * score_scale
    )
    query_back = rotary_apply(query_turned, cosine_table, -sine_values)
    key_back = rotary_apply(key_turned, cosine_table, -sine_values)
    querynorm_part = jnp.sum(query_back * query_unit, axis=(0, 1))
    keynorm_part = jnp.sum(key_back * key_unit, axis=(0, 1))
    query_raw_cot = (
        norm_back(query_back * query_factor, query_unit, query_scale)
        .astype(jnp.bfloat16)
        .reshape(block_rows, heads_query * HEAD_SIZE)
    )
    key_raw_cot = (
        norm_back(key_back * key_factor, key_unit, key_scale)
        .astype(jnp.bfloat16)
        .reshape(block_rows, heads_key * HEAD_SIZE)
    )
    query_gradient = contract(first_layer_normed, query_raw_cot)
    key_gradient = contract(first_layer_normed, key_raw_cot)
    value_gradient = contract(first_layer_normed, value_cot)
    first_part = (
        transposed(query_raw_cot, query_all)
        + transposed(key_raw_cot, key_all)
        + transposed(value_cot, value_all)
    )
    first_cot, querynorm_gradient, keynorm_gradient = (
        lax.psum(first_part.astype(jnp.bfloat16), "tensor").astype(jnp.float32),
        lax.psum(querynorm_part.astype(jnp.bfloat16), "tensor").astype(jnp.float32),
        lax.psum(keynorm_part.astype(jnp.bfloat16), "tensor").astype(jnp.float32),
    )
    prenorm_gradient = jnp.sum(first_cot * unit_first, axis=0)
    input_cot = residual_cot + norm_back(first_cot * gain_one, unit_first, scale_first)
    input_gradient = lax.dynamic_slice_in_dim(input_cot, own_start, own_rows, 0).astype(
        jnp.bfloat16
    )
    summed = (
        lax.psum_scatter(query_gradient, "dp", scatter_dimension=0, tiled=True),
        lax.psum_scatter(key_gradient, "dp", scatter_dimension=0, tiled=True),
        lax.psum_scatter(value_gradient, "dp", scatter_dimension=0, tiled=True),
        lax.psum_scatter(context_gradient, "dp", scatter_dimension=1, tiled=True),
        lax.psum_scatter(router_gradient, "dp", scatter_dimension=0, tiled=True),
        lax.psum_scatter(prenorm_gradient, "dp", scatter_dimension=0, tiled=True),
        lax.psum_scatter(midnorm_gradient, "dp", scatter_dimension=0, tiled=True),
        lax.psum_scatter(querynorm_gradient, "dp", scatter_dimension=0, tiled=True),
        lax.psum_scatter(keynorm_gradient, "dp", scatter_dimension=0, tiled=True),
    )
    return (
        layer_output,
        input_gradient,
        summed[0],
        summed[1],
        summed[2],
        summed[3],
        summed[4],
        gate_gradient,
        up_gradient,
        down_gradient,
        summed[5],
        summed[6],
        summed[7],
        summed[8],
    )


def solution(mesh):
    return jax.shard_map(
        body,
        mesh=mesh,
        in_specs=(
            P(("dp", "tensor"), None),
            P("dp", "tensor"),
            P("dp", "tensor"),
            P("dp", "tensor"),
            P("tensor", "dp"),
            P("dp", None),
            P("dp", None, "tensor"),
            P("dp", None, "tensor"),
            P("dp", "tensor", None),
            P("dp"),
            P("dp"),
            P("dp"),
            P("dp"),
            P("dp", None),
            P(),
            P(),
            P(("dp", "tensor"), None),
        ),
        out_specs=(
            P(("dp", "tensor"), None),
            P(("dp", "tensor"), None),
            P("dp", "tensor"),
            P("dp", "tensor"),
            P("dp", "tensor"),
            P("tensor", "dp"),
            P("dp", None),
            P("dp", None, "tensor"),
            P("dp", None, "tensor"),
            P("dp", "tensor", None),
            P("dp"),
            P("dp"),
            P("dp"),
            P("dp"),
        ),
        check_vma=False,
    )
```

profile of v0, /device:TPU:0, one launch (start us, length us, event | category | flops | bytes accessed | tf_op | source)
XLA Modules:
  0.0 2696.4 jit_solution(10694595598558692033)
XLA Ops:
  16.9 34.9 %all-reduce.7 = (bf16[128]{0:T(256)(128)(2,1)S(1)}, bf16[128]{0:T(256)(128)(2,1)S(1)}) all-reduce(bf16[128]{0:T(256)(128)(2,1)S(1)} %dynamic-update-slice.1, bf16[128]{0:T(256)(128)(2,1)S(1)} %dynamic-update-slice), channel_id=1, replica_groups=mesh['dp'=16,'tensor'=2] {'dp'}, use_global_device_ids=true, to_apply=%add.1 | all-reduce | flops 256 | bytes 1024
  52.3 17.2 all-gather
  73.9 15.9 reduce-window.6
  98.5 18.9 all-gather.2
  131.6 57.2 %all-gather.18.cloned.1.call-done = bf16[2048,2048]{1,0:T(8,128)(2,1)} async-done(((bf16[128,2048]{1,0:T(8,128)(2,1)}), bf16[2048,2048]{1,0:T(8,128)(2,1)}) %all-gather.18.cloned.1.call-update) | async-done | bytes 8388624 | tf_op jit(solution)/shard_map/all_gather | solution.py:122
  208.5 58.8 %all-gather.20.cloned.1.call-done = bf16[2048,2048]{1,0:T(8,128)(2,1)} async-done(((bf16[2048,128]{1,0:T(8,128)(2,1)}), bf16[2048,2048]{1,0:T(8,128)(2,1)}) %all-gather.20.cloned.1.call-update) | async-done | bytes 8388624 | tf_op jit(solution)/shard_map/all_gather | solution.py:125
  275.9 18.7 all-gather.1
  305.4 30.5 %all-reduce.12.cloned.1.call-done = f32[256,2048]{1,0:T(8,128)} async-done(((f32[256,2048]{1,0:T(8,128)}), f32[256,2048]{1,0:T(8,128)}) %all-reduce.12.cloned.1.call-update) | async-done | bytes 2097168 | tf_op jit(solution)/shard_map/psum | solution.py:195
  340.6 21.5 gather_fusion
  367.8 232.8 %all_to_all.20 = bf16[2,16,80,2048]{3,2,0,1:T(8,128)(2,1)} all-to-all(bf16[2,16,80,2048]{3,2,0,1:T(8,128)(2,1)S(1)} %copy_select_fusion), channel_id=1, replica_groups=mesh['dp'=16,'tensor'=2] {'dp'}, dimensions={1} | all-to-all | bytes 20971520 | tf_op jit(solution)/shard_map/all_to_all | solution.py:72
  637.7 122.2 %reduce-scatter.8.cloned.1.call-done = bf16[2,1280,1024]{2,1,0:T(8,128)(2,1)} async-done(((bf16[2,1280,2048]{2,1,0:T(8,128)(2,1)}), bf16[2,1280,1024]{2,1,0:T(8,128)(2,1)}) %reduce-scatter.8.cloned.1.call-update) | async-done | bytes 5242896 | tf_op jit(solution)/shard_map/reduce_scatter | solution.py:76
  759.9 131.2 %all-gather.22.cloned.1.call-done = bf16[2,1280,2048]{2,1,0:T(8,128)(2,1)} async-done(((bf16[2,1280,1024]{2,1,0:T(8,128)(2,1)}), bf16[2,1280,2048]{2,1,0:T(8,128)(2,1)}) %all-gather.22.cloned.1.call-update) | async-done | bytes 10485776 | tf_op jit(solution)/shard_map/all_gather | solution.py:79
  908.2 204.3 %all_gather.51 = bf16[2048,32]{0,1:T(8,128)(2,1)S(1)} all-gather(bf16[128,32]{0,1:T(8,128)(2,1)S(1)} %copy-done.70), channel_id=1, replica_groups=mesh['dp'=16,'tensor'=2] {'dp'}, dimensions={0}, use_global_device_ids=true | all-gather | bytes 139264 | tf_op jit(solution)/shard_map/all_gather | solution.py:126
  1115.4 21.5 gather_fusion.3
  1148.8 21.7 gather_fusion.1
  1176.9 13.6 gather_fusion.2
  1198.6 263.9 %all_to_all.21 = bf16[2,16,80,2048]{3,2,0,1:T(8,128)(2,1)} all-to-all(bf16[2,16,80,2048]{3,2,0,1:T(8,128)(2,1)S(1)} %fusion), channel_id=1, replica_groups=mesh['dp'=16,'tensor'=2] {'dp'}, dimensions={1} | all-to-all | bytes 20971520 | tf_op jit(solution)/shard_map/all_to_all | solution.py:72
  1472.6 11.7 multiply_convert_fusion
  1494.2 12.8 add_convert_fusion
  1507.1 122.2 %reduce-scatter.10.cloned.1.call-done = bf16[2,1280,1024]{2,1,0:T(8,128)(2,1)} async-done(((bf16[2,1280,2048]{2,1,0:T(8,128)(2,1)}), bf16[2,1280,1024]{2,1,0:T(8,128)(2,1)}) %reduce-scatter.10.cloned.1.call-update) | async-done | bytes 5242896 | tf_op jit(solution)/shard_map/reduce_scatter | solution.py:76
  1629.4 131.2 %all-gather.26.cloned.1.call-done = bf16[2,1280,2048]{2,1,0:T(8,128)(2,1)} async-done(((bf16[2,1280,1024]{2,1,0:T(8,128)(2,1)}), bf16[2,1280,2048]{2,1,0:T(8,128)(2,1)}) %all-gather.26.cloned.1.call-update) | async-done | bytes 10485776 | tf_op jit(solution)/shard_map/all_gather | solution.py:79
  1780.9 182.7 %all-to-all-done.3 = bf16[2,16,80,2048]{3,2,0,1:T(8,128)(2,1)} async-done(((bf16[2,16,80,2048]{3,2,0,1:T(8,128)(2,1)}), bf16[2,16,80,2048]{3,2,0,1:T(8,128)(2,1)}, u32[]{:S(2)}, u32[]{:S(2)}) %all-to-all-start.3) | async-done | bytes 10485792 | tf_op jit(solution)/shard_map/all_to_all | solution.py:286
  1973.6 21.7 gather_fusion.4
  1995.3 18.4 convert_reduce_fusion
  2084.2 11.7 fusion.63
  2095.9 10.4 fusion.62
  2121.0 15.0 all-reduce.14.cloned.1.call-done
  2140.5 84.9 %all-reduce.6 = (f32[2048]{0:T(1024)S(1)}, f32[2048]{0:T(1024)S(1)}, f32[128]{0:T(128)S(1)}, f32[128]{0:T(128)S(1)}) all-reduce(f32[2048]{0:T(1024)S(1)} %get-tuple-element.111, f32[2048]{0:T(1024)S(1)} %copy-done.65, bf16[128]{0:T(256)(128)(2,1)S(1)} %get-tuple-element.131, ...), channel_id=9, replica_groups=mesh['dp'=16,'tensor'=2] {'dp'}, use_global_device_ids=true, to_apply=%region_36.37.clone | all-reduce | flops 4352 | bytes 34304
  2230.8 29.4 %reduce-scatter.16.cloned.1.call-done = f32[128,256]{1,0:T(8,128)} async-done(((f32[2048,256]{1,0:T(8,128)}), f32[128,256]{1,0:T(8,128)}) %reduce-scatter.16.cloned.1.call-update) | async-done | bytes 131088 | tf_op jit(solution)/shard_map/reduce_scatter | solution.py:375
  2260.2 65.2 %reduce-scatter.14.cloned.1.call-done = f32[128,256]{1,0:T(8,128)} async-done(((f32[2048,256]{1,0:T(8,128)}), f32[128,256]{1,0:T(8,128)}) %reduce-scatter.14.cloned.1.call-update) | async-done | bytes 131088 | tf_op jit(solution)/shard_map/reduce_scatter | solution.py:374
  2325.4 182.1 %reduce-scatter.18.cloned.1.call-done = f32[2048,128]{1,0:T(8,128)} async-done(((f32[2048,2048]{1,0:T(8,128)}), f32[2048,128]{1,0:T(8,128)}) %reduce-scatter.18.cloned.1.call-update) | async-done | bytes 1048592 | tf_op jit(solution)/shard_map/reduce_scatter | solution.py:376
  2507.5 182.1 %reduce-scatter.12.cloned.1.call-done = f32[128,2048]{1,0:T(8,128)} async-done(((f32[2048,2048]{1,0:T(8,128)}), f32[128,2048]{1,0:T(8,128)}) %reduce-scatter.12.cloned.1.call-update) | async-done | bytes 1048592 | tf_op jit(solution)/shard_map/reduce_scatter | solution.py:373
  (385 shorter events, 310.8 us)
Async XLA Ops:
  7.2 622.2 %copy-start = (bf16[2,384,2048]{2,1,0:T(8,128)(2,1)S(1)}, bf16[2,384,2048]{2,1,0:T(8,128)(2,1)}, u32[]{:S(2)}) copy-start(bf16[2,384,2048]{2,1,0:T(8,128)(2,1)} %param.27) | copy-start | bytes 9437188
  7.2 112.2 %all-gather.12.cloned.1.call-start = ((), (), s32[]{:S(2)}) async-start(), calls=%async_computation.11 | async-start | bytes 1572864 | tf_op jit(solution)/shard_map/all_gather | solution.py:133
  7.9 113.1 %all-gather.16.cloned.1.call-start = ((), (), s32[]{:S(2)}) async-start(), calls=%async_computation.13 | async-start | bytes 1114112 | tf_op jit(solution)/shard_map/all_gather | solution.py:123
  8.7 120.1 %all-gather.14.cloned.1.call-start = ((), (), s32[]{:S(2)}) async-start(), calls=%async_computation.12 | async-start | bytes 1114112 | tf_op jit(solution)/shard_map/all_gather | solution.py:124
  9.4 179.4 %all-gather.18.cloned.1.call-start = ((), (), s32[]{:S(2)}) async-start(), calls=%async_computation.14 | async-start | bytes 8912896 | tf_op jit(solution)/shard_map/all_gather | solution.py:122
  10.0 257.2 %all-gather.20.cloned.1.call-start = ((), (), s32[]{:S(2)}) async-start(), calls=%async_computation.15 | async-start | bytes 8912896 | tf_op jit(solution)/shard_map/all_gather | solution.py:125
  10.6 325.3 %all-reduce.12.cloned.1.call-start = ((), (), s32[]{:S(2)}) async-start(), calls=%async_computation.16 | async-start | bytes 4194304 | tf_op jit(solution)/shard_map/psum | solution.py:195
  51.8 145.1 %copy-start.71 = (f32[128]{0:T(128)}, f32[128]{0:T(128)S(1)}, u32[]{:S(2)}) copy-start(f32[128]{0:T(128)S(1)} %convert_element_type.174) | copy-start | bytes 1540
  69.6 119.3 %copy-start.53 = (f32[16,1,128]{2,1,0:T(1,128)}, f32[16,1,128]{2,1,0:T(1,128)S(1)}, u32[]{:S(2)}) copy-start(f32[16,1,128]{2,1,0:T(1,128)S(1)} %convert_element_type.209) | copy-start | bytes 24580
  118.2 85.5 %copy-start.24 = (pred[256,256]{0,1:T(8,128)(4,1)}, pred[256,256]{0,1:T(8,128)(4,1)S(1)}, u32[]{:S(2)}) copy-start(pred[256,256]{0,1:T(8,128)(4,1)S(1)} %fusion.30) | copy-start | bytes 196612
  119.4 80.2 %copy-start.28 = (f32[256,64]{1,0:T(8,128)}, f32[256,64]{1,0:T(8,128)S(1)}, u32[]{:S(2)}) copy-start(f32[256,64]{1,0:T(8,128)S(1)} %get-tuple-element.165) | copy-start | bytes 196612
  121.0 67.9 %copy-start.60 = (f32[256]{0:T(256)}, f32[256]{0:T(256)S(1)}, u32[]{:S(2)}) copy-start(f32[256]{0:T(256)S(1)} %add_rsqrt_fusion.3) | copy-start | bytes 3076
  274.6 485.3 %reduce-scatter.8.cloned.1.call-start = ((), (), s32[]{:S(2)}) async-start(), calls=%async_computation.17 | async-start | bytes 15728640 | tf_op jit(solution)/shard_map/reduce_scatter | solution.py:76
  294.7 43.4 %copy-start.57 = (f32[16,1,128]{2,1,0:T(1,128)}, f32[16,1,128]{2,1,0:T(1,128)S(1)}, u32[]{:S(2)}) copy-start(f32[16,1,128]{2,1,0:T(1,128)S(1)} %convert_element_type.210) | copy-start | bytes 24580
  305.3 32.8 %copy-start.55 = (s32[2560]{0:T(1024)}, s32[2560]{0:T(1024)S(1)}, u32[]{:S(2)}) copy-start(s32[2560]{0:T(1024)S(1)} %scatter_custom_fusion) | copy-start | bytes 30724
  338.1 24.0 copy-start.67
  637.6 253.5 %all-gather.22.cloned.1.call-start = ((), (), s32[]{:S(2)}) async-start(), calls=%async_computation.18 | async-start | bytes 15728640 | tf_op jit(solution)/shard_map/all_gather | solution.py:79
  901.2 237.4 %all-to-all-start.1 = ((bf16[2,16,80,2048]{3,2,0,1:T(8,128)(2,1)}), bf16[2,16,80,2048]{3,2,0,1:T(8,128)(2,1)}, u32[]{:S(2)}, u32[]{:S(2)}) async-start(bf16[2,16,80,2048]{3,2,0,1:T(8,128)(2,1)} %copy.172), calls=%async_computation.2 | async-start | bytes 20971520 | tf_op jit(solution)/shard_map/all_to_all | solution.py:240
  907.0 205.6 %all-gather.24.cloned.1.call-start = ((), (), s32[]{:S(2)}) async-start(), calls=%async_computation.19 | async-start | bytes 1572864 | tf_op jit(solution)/shard_map/all_gather | solution.py:134
  907.8 721.6 %reduce-scatter.10.cloned.1.call-start = ((), (), s32[]{:S(2)}) async-start(), calls=%async_computation.20 | async-start | bytes 15728640 | tf_op jit(solution)/shard_map/reduce_scatter | solution.py:76
  908.0 228.8 %copy-start.49 = (pred[256,8]{1,0:T(8,128)(4,1)}, pred[256,8]{1,0:T(8,128)(4,1)S(1)}, u32[]{:S(2)}) copy-start(pred[256,8]{1,0:T(8,128)(4,1)S(1)} %broadcast_and_fusion) | copy-start | bytes 6148
  1115.4 23.1 copy-start.59
  1507.1 253.5 %all-gather.26.cloned.1.call-start = ((), (), s32[]{:S(2)}) async-start(), calls=%async_computation.21 | async-start | bytes 15728640 | tf_op jit(solution)/shard_map/all_gather | solution.py:79
  1770.6 193.0 %all-to-all-start.3 = ((bf16[2,16,80,2048]{3,2,0,1:T(8,128)(2,1)}), bf16[2,16,80,2048]{3,2,0,1:T(8,128)(2,1)}, u32[]{:S(2)}, u32[]{:S(2)}) async-start(bf16[2,16,80,2048]{3,2,0,1:T(8,128)(2,1)} %copy.178), calls=%async_computation.5 | async-start | bytes 20971520 | tf_op jit(solution)/shard_map/all_to_all | solution.py:286
  1776.4 359.6 %all-reduce.14.cloned.1.call-start = ((), (), s32[]{:S(2)}) async-start(), calls=%async_computation.22 | async-start | bytes 2097152 | tf_op jit(solution)/shard_map/psum | solution.py:363
  2056.4 174.3 %reduce-scatter.20.cloned.1.call-start = ((), (), s32[]{:S(2)}) async-start(), calls=%async_computation.27 | async-start | bytes 278528 | tf_op jit(solution)/shard_map/reduce_scatter | solution.py:377
  2057.6 202.7 %reduce-scatter.16.cloned.1.call-start = ((), (), s32[]{:S(2)}) async-start(), calls=%async_computation.25 | async-start | bytes 2228224 | tf_op jit(solution)/shard_map/reduce_scatter | solution.py:375
  2060.9 264.5 %reduce-scatter.14.cloned.1.call-start = ((), (), s32[]{:S(2)}) async-start(), calls=%async_computation.24 | async-start | bytes 2228224 | tf_op jit(solution)/shard_map/reduce_scatter | solution.py:374
  2063.0 444.6 %reduce-scatter.18.cloned.1.call-start = ((), (), s32[]{:S(2)}) async-start(), calls=%async_computation.26 | async-start | bytes 17825792 | tf_op jit(solution)/shard_map/reduce_scatter | solution.py:376
  2073.1 616.6 %reduce-scatter.12.cloned.1.call-start = ((), (), s32[]{:S(2)}) async-start(), calls=%async_computation.23 | async-start | bytes 17825792 | tf_op jit(solution)/shard_map/reduce_scatter | solution.py:373
  2084.2 22.1 slice-start.1
  2136.0 553.7 %copy-start.1 = (bf16[2,384,2048]{2,1,0:T(8,128)(2,1)S(1)}, bf16[2,384,2048]{2,1,0:T(8,128)(2,1)}, u32[]{:S(2)}) copy-start(bf16[2,384,2048]{2,1,0:T(8,128)(2,1)} %param.27) | copy-start | bytes 9437188
  (73 other events, 370.5 us)
Sparse Core Ops, SparseCore 0:
  9.6 23.9 all-gather.11
  35.8 37.9 all-gather.15
  75.9 36.9 all-gather.13
  115.0 73.8 all-gather.17
  190.8 76.3 all-gather.19
  274.8 61.0 all-reduce.11
  637.7 122.1 reduce-scatter.7
  761.5 129.5 all-gather.21
  909.5 21.6 all-gather.23
  1507.2 122.1 reduce-scatter.9
  1631.0 129.5 all-gather.25
  2056.6 79.3 all-reduce.13
  2140.1 55.2 reduce-scatter.19
  2199.6 60.6 reduce-scatter.15
  2264.9 60.5 reduce-scatter.13
  2330.0 177.5 reduce-scatter.17
  2512.1 177.5 reduce-scatter.11
where the time goes:
time: 2710 us; the launch traced here: 2700 us
  waiting for transfers between devices  1310 us (48%)
  blocking collectives  881 us (33%)
  local copies, waits for them, and re-layouts  213 us (8%)
  matrix products  155 us (6%)
  other arithmetic  101 us (4%)
    all_to_all x2, blocking collectives, to_owners(): return lax.all_to_all(buffer, 'dp', split_axis=1, concat_axis=1, tiled=True)  497 us
    all_gather x2, waiting for transfers between devices, owner_reduce(): return lax.all_gather(shares, 'tensor', axis=2, tiled=True)  262 us
    reduce_scatter x2, waiting for transfers between devices, owner_reduce(): lax.psum_scatter(partial_rows.astype(jnp.bfloat16), 'tensor', scatter_dim...  244 us
    all_gather x1, blocking collectives, body(): lax.all_gather(router_weight, 'dp', axis=0, tiled=True)  204 us
    all_to_all x1, waiting for transfers between devices, body(): lax.all_to_all(row_cot.reshape(EXP_DEV, dp_count, most_rows, width), 'dp'...  183 us
    reduce_scatter x1, waiting for transfers between devices, body(): lax.psum_scatter(query_gradient, 'dp', scatter_dimension=0, tiled=True)  182 us
    reduce_scatter x1, waiting for transfers between devices, body(): lax.psum_scatter(context_gradient, 'dp', scatter_dimension=1, tiled=True)  182 us
    unnamed x2, blocking collectives  120 us
  transfers between devices with their start and end apart: 19, of which 13 were waited for; matrix products, arithmetic and copies ran while one was open for 6% of the time, Pallas kernels for 0%

commit v1 on v0

--- a/solution.py
+++ b/solution.py
@@ -398,9 +398,330 @@
     )
 
 
+AUX = 128
+
+
+def gather_dp(value):
+    return lax.all_gather(value, "dp", axis=0, tiled=True)
+
+
+def gather_all(value):
+    return lax.all_gather(value, ("dp", "tensor"), axis=0, tiled=True)
+
+
+def scatter_all(value):
+    return lax.psum_scatter(value, ("dp", "tensor"), scatter_dimension=0, tiled=True)
+
+
+def scatter_dp(value):
+    return lax.psum_scatter(value, "dp", scatter_dimension=0, tiled=True)
+
+
+def split_high_low(value):
+    high = value.astype(jnp.bfloat16)
+    return high, (value - high.astype(jnp.float32)).astype(jnp.bfloat16)
+
+
+def gathered_body(
+    layer_input,
+    query_weight,
+    key_projection,
+    value_projection,
+    context_weight,
+    router_weight,
+    expert_gate,
+    expert_up,
+    expert_down,
+    prenorm_gain,
+    midnorm_gain,
+    querynorm_gain,
+    keynorm_gain,
+    routes,
+    lengths,
+    sequence_order,
+    output_cotangent,
+):
+    bf16, f32 = jnp.bfloat16, jnp.float32
+    tensor_count = lax.axis_size("tensor")
+    tensor_index = lax.axis_index("tensor")
+    dp_count = lax.axis_size("dp")
+    dp_index = lax.axis_index("dp")
+    own_rows, features = layer_input.shape
+    block_rows = own_rows * tensor_count
+    tokens = block_rows * dp_count
+    expert_count = EXP_DEV * dp_count
+    capacity = 3 * block_rows * TOP // (4 * EXP_DEV)
+    most_rows = (5 * block_rows * TOP + 4 * expert_count - 1) // (4 * expert_count)
+    shard = features // dp_count
+    query_width = query_weight.shape[1]
+    key_width = key_projection.shape[1]
+    norm_part = HEAD_SIZE // dp_count
+
+    gains = jnp.zeros((shard, AUX - expert_count), bf16)
+    gains = gains.at[:, 0].set(prenorm_gain).at[:, 1].set(midnorm_gain)
+    gains = gains.at[:norm_part, 2].set(querynorm_gain).at[:norm_part, 3].set(keynorm_gain)
+    packed = jnp.concatenate(
+        [query_weight, key_projection, value_projection, context_weight.T, router_weight, gains],
+        axis=1,
+    )
+    packed = gather_dp(packed)
+    edges = [0]
+    for width in (query_width, key_width, key_width, query_width, expert_count, AUX - expert_count):
+        edges.append(edges[-1] + width)
+    qkv_all = packed[:, : edges[3]]
+    context_all = packed[:, edges[3] : edges[4]]
+    router_all = packed[:, edges[4] : edges[5]]
+    gains_all = packed[:, edges[5] :].astype(f32)
+    gain_one, gain_two = gains_all[:, 0], gains_all[:, 1]
+    head_gains = gains_all.reshape(dp_count, shard, -1)[:, :norm_part, :]
+    query_factor = head_gains[:, :, 2].reshape(-1)
+    key_factor = head_gains[:, :, 3].reshape(-1)
+
+    cot_all = gather_all(output_cotangent)
+    routes_all = gather_dp(routes)
+    input_rows = lax.all_gather(layer_input, "tensor", axis=0, tiled=True)
+    position = jnp.arange(block_rows, dtype=jnp.int32)
+    block_lengths = lengths[sequence_order]
+    seq_length = block_lengths[dp_index]
+
+    frequency = jnp.exp(
+        -math.log(rope_base) * jnp.arange(HEAD_SIZE // 2, dtype=f32) * (2.0 / HEAD_SIZE)
+    )
+    angles = position.astype(f32)[:, None] * frequency[None, :]
+    cosine_table = jnp.cos(angles)[:, None, :]
+    sine_values = jnp.sin(angles)[:, None, :]
+    heads_query = query_width // HEAD_SIZE
+    heads_key = key_width // HEAD_SIZE
+    group_width = heads_query // heads_key
+    stream = input_rows.astype(f32)
+    unit_first, scale_first = rms_normalize(stream)
+    first_normed = (unit_first * gain_one).astype(bf16)
+    raw = matrix_product(first_normed, qkv_all)
+    query_unnormed = raw[:, : edges[1]].reshape(block_rows, heads_query, HEAD_SIZE)
+    key_unnormed = raw[:, edges[1] : edges[2]].reshape(block_rows, heads_key, HEAD_SIZE)
+    value_rows = raw[:, edges[2] :].astype(bf16).reshape(block_rows, heads_key, HEAD_SIZE)
+    query_unit, query_scale = rms_normalize(query_unnormed)
+    key_unit, key_scale = rms_normalize(key_unnormed)
+    query_rows = (
+        rotary_apply(query_unit * query_factor, cosine_table, sine_values)
+        .astype(bf16)
+        .reshape(block_rows, heads_key, group_width, HEAD_SIZE)
+    )
+    keys_rot = rotary_apply(key_unit * key_factor, cosine_table, sine_values).astype(bf16)
+    score_scale = HEAD_SIZE ** (-0.5)
+    allowed = (position[None, :] <= position[:, None]) & (position < seq_length)[None, :]
+    scores = (
+        jnp.einsum("ikrd,jkd->krij", query_rows, keys_rot, preferred_element_type=f32)
+        * score_scale
+    )
+    scores = jnp.where(allowed, scores, masked_score)
+    weights = jnp.exp(scores - jnp.max(scores, axis=-1, keepdims=True))
+    soft_probs = weights / jnp.sum(weights, axis=-1, keepdims=True)
+    probs_low = soft_probs.astype(bf16)
+    context = jnp.einsum("krij,jkd->ikrd", probs_low, value_rows, preferred_element_type=f32)
+    context = context.reshape(block_rows, query_width).astype(bf16)
+    attention = lax.psum_scatter(
+        transposed(context, context_all).astype(bf16),
+        "tensor",
+        scatter_dimension=0,
+        tiled=True,
+    )
+    residual = layer_input.astype(f32) + attention.astype(f32)
+    unit_second, scale_second = rms_normalize(residual)
+    normed_second = (unit_second * gain_two).astype(bf16)
+
+    normed_all = gather_all(normed_second)
+    logits = matrix_product(normed_all, router_all)
+    expert_ids = jnp.arange(expert_count, dtype=jnp.int32)
+    chosen = jnp.zeros((tokens, expert_count), jnp.bool_)
+    for j in range(TOP):
+        chosen = chosen | (routes_all[:, j : j + 1] == expert_ids[None, :])
+    peak = jnp.max(jnp.where(chosen, logits, masked_score), axis=-1, keepdims=True)
+    spread = jnp.where(chosen, jnp.exp(jnp.minimum(logits - peak, 0.0)), 0.0)
+    gates = spread / jnp.sum(spread, axis=-1, keepdims=True)
+    live = position[None, :] < block_lengths[:, None]
+    hot = chosen.reshape(dp_count, block_rows, expert_count) & live[:, :, None]
+    hot_low = hot.astype(bf16)
+    below = (position[None, :] < position[:, None]).astype(bf16)
+    rank = jnp.einsum("ts,bse->bte", below, hot_low, preferred_element_type=f32)
+    counts = jnp.sum(hot.astype(f32), axis=1)
+    earlier = jnp.cumsum(counts, axis=0) - counts
+    kept = hot & (earlier[:, None, :] + rank < capacity)
+
+    first_expert = dp_index * EXP_DEV
+    rank_own = lax.dynamic_slice_in_dim(rank, first_expert, EXP_DEV, 2)
+    kept_own = lax.dynamic_slice_in_dim(kept, first_expert, EXP_DEV, 2)
+    gates_own = lax.dynamic_slice_in_dim(
+        gates.reshape(dp_count, block_rows, expert_count), first_expert, EXP_DEV, 2
+    )
+    slots = jnp.arange(most_rows, dtype=f32)
+    place = kept_own.transpose(0, 2, 1)[:, :, None, :] & (
+        rank_own.transpose(0, 2, 1)[:, :, None, :] == slots[None, None, :, None]
+    )
+    place_low = place.astype(bf16).reshape(dp_count, EXP_DEV * most_rows, block_rows)
+    slot_gate = jnp.sum(
+        jnp.where(place, gates_own.transpose(0, 2, 1)[:, :, None, :], 0.0), axis=-1
+    )
+    slot_gate = slot_gate.transpose(1, 0, 2).reshape(EXP_DEV, dp_count * most_rows, 1)
+
+    def take(rows):
+        taken = jnp.einsum(
+            "bst,btd->bsd",
+            place_low,
+            rows.reshape(dp_count, block_rows, features),
+            preferred_element_type=f32,
+        ).astype(bf16)
+        return (
+            taken.reshape(dp_count, EXP_DEV, most_rows, features)
+            .transpose(1, 0, 2, 3)
+            .reshape(EXP_DEV, dp_count * most_rows, features)
+        )
+
+    def put(slot_rows):
+        ordered = (
+            slot_rows.astype(bf16)
+            .reshape(EXP_DEV, dp_count, most_rows, features)
+            .transpose(1, 0, 2, 3)
+            .reshape(dp_count, EXP_DEV * most_rows, features)
+        )
+        return (
+            jnp.einsum("bst,bsd->btd", place_low, ordered, preferred_element_type=f32)
+            .astype(bf16)
+            .reshape(tokens, features)
+        )
+
+    rows_in = take(normed_all)
+    cot_in = take(cot_all)
+    gate_pre = jnp.einsum("end,edf->enf", rows_in, expert_gate, preferred_element_type=f32)
+    up_pre = jnp.einsum("end,edf->enf", rows_in, expert_up, preferred_element_type=f32)
+    sigmoid_gate = jax.nn.sigmoid(gate_pre)
+    gate_act = gate_pre * sigmoid_gate
+    hidden = (gate_act * up_pre).astype(bf16)
+    out_partial = jnp.einsum("enf,efd->end", hidden, expert_down, preferred_element_type=f32)
+    expert_sum = scatter_all(put(out_partial * slot_gate))
+    layer_output = (residual + expert_sum.astype(f32)).astype(bf16)
+
+    down_cot = jnp.einsum("end,efd->enf", cot_in, expert_down, preferred_element_type=f32)
+    slot_cot = jnp.sum(hidden.astype(f32) * down_cot, axis=-1)
+    hidden_cot = down_cot * slot_gate
+    gating_cot = (
+        hidden_cot * up_pre * sigmoid_gate * (1.0 + gate_pre * (1.0 - sigmoid_gate))
+    ).astype(bf16)
+    upward_cot = (hidden_cot * gate_act).astype(bf16)
+    hidden_gated = (hidden.astype(f32) * slot_gate).astype(bf16)
+    down_gradient = jnp.einsum("enf,end->efd", hidden_gated, cot_in, preferred_element_type=f32)
+    gate_gradient = jnp.einsum("end,enf->edf", rows_in, gating_cot, preferred_element_type=f32)
+    up_gradient = jnp.einsum("end,enf->edf", rows_in, upward_cot, preferred_element_type=f32)
+    row_partial = jnp.einsum("enf,edf->end", gating_cot, expert_gate, preferred_element_type=f32)
+    row_partial = row_partial + jnp.einsum(
+        "enf,edf->end", upward_cot, expert_up, preferred_element_type=f32
+    )
+    slot_cot = slot_cot.reshape(EXP_DEV, dp_count, most_rows).transpose(1, 0, 2)
+    token_cot = jnp.sum(jnp.where(place, slot_cot[:, :, :, None], 0.0), axis=2)
+    token_cot = token_cot.transpose(0, 2, 1).reshape(tokens, EXP_DEV)
+    high, low = split_high_low(token_cot)
+    quad = jnp.stack([high, low], axis=-1).reshape(tokens, 2 * EXP_DEV)
+    aux = lax.dynamic_update_slice(
+        jnp.zeros((tokens, 2 * tensor_count * expert_count), bf16),
+        quad,
+        (0, tensor_index * 2 * expert_count + dp_index * 2 * EXP_DEV),
+    )
+    returned = scatter_all(jnp.concatenate([put(row_partial), aux], axis=1)).astype(f32)
+    gate_cot = jnp.sum(
+        returned[:, features:].reshape(own_rows, tensor_count, expert_count, 2), axis=(1, 3)
+    )
+    own_start = (dp_index * tensor_count + tensor_index) * own_rows
+    gates_mine = lax.dynamic_slice_in_dim(gates, own_start, own_rows, 0)
+    logit_cot = (
+        gates_mine * (gate_cot - jnp.sum(gates_mine * gate_cot, axis=-1, keepdims=True))
+    ).astype(bf16)
+    router_part = contract(normed_second, logit_cot)
+    normed_cot = returned[:, :features] + transposed(logit_cot, router_all)
+    midnorm_part = jnp.sum(normed_cot * unit_second, axis=0)
+    residual_cot = output_cotangent.astype(f32) + norm_back(
+        normed_cot * gain_two, unit_second, scale_second
+    )
+    attention_cot = lax.all_gather(residual_cot.astype(bf16), "tensor", axis=0, tiled=True)
+
+    context_part = contract(attention_cot, context)
+    context_cot = (
+        matrix_product(attention_cot, context_all)
+        .astype(bf16)
+        .reshape(block_rows, heads_key, group_width, HEAD_SIZE)
+    )
+    prob_cot = jnp.einsum("ikrd,jkd->krij", context_cot, value_rows, preferred_element_type=f32)
+    score_cot = (
+        soft_probs * (prob_cot - jnp.sum(soft_probs * prob_cot, axis=-1, keepdims=True))
+    ).astype(bf16)
+    value_cot = jnp.einsum("krij,ikrd->jkd", probs_low, context_cot, preferred_element_type=f32)
+    value_cot = value_cot.astype(bf16).reshape(block_rows, key_width)
+    query_turned = (
+        jnp.einsum("krij,jkd->ikrd", score_cot, keys_rot, preferred_element_type=f32).reshape(
+            block_rows, heads_query, HEAD_SIZE
+        )
+        * score_scale
+    )
+    key_turned = (
+        jnp.einsum("krij,ikrd->jkd", score_cot, query_rows, preferred_element_type=f32)
+        * score_scale
+    )
+    query_back = rotary_apply(query_turned, cosine_table, -sine_values)
+    key_back = rotary_apply(key_turned, cosine_table, -sine_values)
+    querynorm_part = jnp.sum(query_back * query_unit, axis=(0, 1))
+    keynorm_part = jnp.sum(key_back * key_unit, axis=(0, 1))
+    query_raw_cot = norm_back(query_back * query_factor, query_unit, query_scale).astype(bf16)
+    key_raw_cot = norm_back(key_back * key_factor, key_unit, key_scale).astype(bf16)
+    raw_cot = jnp.concatenate(
+        [
+            query_raw_cot.reshape(block_rows, query_width),
+            key_raw_cot.reshape(block_rows, key_width),
+            value_cot,
+        ],
+        axis=1,
+    )
+    qkv_part = contract(first_normed, raw_cot)
+    first_cot = lax.psum_scatter(
+        transposed(raw_cot, qkv_all).astype(bf16), "tensor", scatter_dimension=0, tiled=True
+    ).astype(f32)
+    row_start = tensor_index * own_rows
+    unit_own = lax.dynamic_slice_in_dim(unit_first, row_start, own_rows, 0)
+    scale_own = lax.dynamic_slice_in_dim(scale_first, row_start, own_rows, 0)
+    prenorm_part = jnp.sum(first_cot * unit_own, axis=0)
+    input_gradient = (
+        residual_cot + norm_back(first_cot * gain_one, unit_own, scale_own)
+    ).astype(bf16)
+
+    small = jnp.zeros((dp_count, shard, AUX), f32)
+    small = small.at[:, :, :expert_count].set(router_part.reshape(dp_count, shard, expert_count))
+    small = small.at[:, :, expert_count].set(prenorm_part.reshape(dp_count, shard))
+    small = small.at[:, :, expert_count + 1].set(midnorm_part.reshape(dp_count, shard))
+    small = small.at[:, :norm_part, expert_count + 2].set(querynorm_part.reshape(dp_count, -1))
+    small = small.at[:, :norm_part, expert_count + 3].set(keynorm_part.reshape(dp_count, -1))
+    small = scatter_dp(small.reshape(features, AUX))
+    small = lax.psum(small, "tensor")
+    summed = scatter_dp(jnp.concatenate([qkv_part.astype(bf16), context_part.astype(bf16)], axis=1))
+    summed = summed.astype(f32)
+    return (
+        layer_output,
+        input_gradient,
+        summed[:, : edges[1]],
+        summed[:, edges[1] : edges[2]],
+        summed[:, edges[2] : edges[3]],
+        summed[:, edges[3] :].T,
+        small[:, :expert_count],
+        gate_gradient,
+        up_gradient,
+        down_gradient,
+        small[:, expert_count],
+        small[:, expert_count + 1],
+        small[:norm_part, expert_count + 2],
+        small[:norm_part, expert_count + 3],
+    )
+
+
 def solution(mesh):
     return jax.shard_map(
-        body,
+        gathered_body if mesh.shape["dp"] <= 16 else body,
         mesh=mesh,
         in_specs=(
             P(("dp", "tensor"), None),

time: 2710 us -> 1750 us (0.65)
  blocking collectives: 881 us -> 22.2 us
  waiting for transfers between devices: 1310 us -> 1230 us
  local copies, waits for them, and re-layouts: 213 us -> 141 us
  matrix products: 155 us -> 220 us
    all_to_all x2 -> x0, blocking collectives: 497 us -> none  [to_owners(): return lax.all_to_all(buffer, 'dp', split_axis=1, concat_axis=1, tiled=True)]
    all_gather x4 -> x1, blocking collectives: 259 us -> 22.2 us  [gather_dp(): return lax.all_gather(value, 'dp', axis=0, tiled=True)]
    reduce_scatter x7 -> x6, waiting for transfers between devices: 703 us -> 929 us  [the longest x2 690 us: scatter_all(): lax.psum_scatter(value, ('dp', 'tensor'), scatter_dimension=0, tiled=True)]
    all_to_all x2 -> x0, waiting for transfers between devices: 183 us -> none  [the longest x1 183 us: body(): lax.all_to_all(row_cot.reshape(EXP_DEV, dp_count, most_rows, width), 'dp'...]
    unnamed x2 -> x0, blocking collectives: 120 us -> none
    gather x5 -> x1, local copies, waits for them, and re-layouts: 100 us -> 0.66 us  [gathered_body(): block_lengths = lengths[sequence_order]]
    all_gather x8 -> x5, waiting for transfers between devices: 378 us -> 280 us  [the longest x2 157 us: gather_all(): return lax.all_gather(value, ('dp', 'tensor'), axis=0, tiled=True)]
    dot_general x15 -> x19, matrix products: 95.9 us -> 159 us  [the longest x2 25.9 us: take(): jnp.einsum('bst,btd->bsd', place_low, rows.reshape(dp_count, block_rows,...]
  transfers between devices with their start and end apart: 19 -> 12, of which waited for: 13 -> 11; matrix products, arithmetic and copies ran while one was open for 6% -> 11% of each run, Pallas kernels for 0% -> 0%
where the time goes in v1:
time: 1750 us; the launch traced here: 1730 us
  waiting for transfers between devices  1230 us (70%)
  matrix products  220 us (13%)
  local copies, waits for them, and re-layouts  141 us (8%)
  other arithmetic  103 us (6%)
  blocking collectives  22.2 us (1%)
    reduce_scatter x2, waiting for transfers between devices, scatter_all(): lax.psum_scatter(value, ('dp', 'tensor'), scatter_dimension=0, tiled=True)  690 us
    reduce_scatter x2, waiting for transfers between devices, scatter_dp(): return lax.psum_scatter(value, 'dp', scatter_dimension=0, tiled=True)  207 us
    all_gather x2, waiting for transfers between devices, gather_all(): return lax.all_gather(value, ('dp', 'tensor'), axis=0, tiled=True)  157 us
    all_gather x1, waiting for transfers between devices, gather_dp(): return lax.all_gather(value, 'dp', axis=0, tiled=True)  107 us
  transfers between devices with their start and end apart: 12, of which 11 were waited for; matrix products, arithmetic and copies ran while one was open for 11% of the time, Pallas kernels for 0%

profile of v1, /device:TPU:0, one launch (start us, length us, event | category | flops | bytes accessed | tf_op | source)
XLA Modules:
  0.0 1734.0 jit_solution(4866840741283187243)
XLA Ops:
  38.7 107.2 %all-gather.8.cloned.1.call-done = bf16[2048,4736]{0,1:T(8,128)(2,1)} async-done(((bf16[128,4736]{0,1:T(8,128)(2,1)}), bf16[2048,4736]{0,1:T(8,128)(2,1)}) %all-gather.8.cloned.1.call-update) | async-done | bytes 19398672 | tf_op jit(solution)/shard_map/all_gather | solution.py:405
  190.8 19.0 %reduce-scatter.7.cloned.1.call-done = bf16[128,2048]{1,0:T(8,128)(2,1)} async-done(((bf16[256,2048]{1,0:T(8,128)(2,1)}), bf16[128,2048]{1,0:T(8,128)(2,1)}) %reduce-scatter.7.cloned.1.call-update) | async-done | bytes 524304 | tf_op jit(solution)/shard_map/reduce_scatter | solution.py:523
  214.2 22.2 %all_gather.20 = s32[4096,8]{0,1:T(8,128)S(1)} all-gather(s32[256,8]{0,1:T(8,128)S(1)} %copy-done.66), channel_id=1, replica_groups=mesh['dp'=16,'tensor'=2] {'dp'}, dimensions={0}, use_global_device_ids=true | all-gather | bytes 139264 | tf_op jit(solution)/shard_map/all_gather | solution.py:405
  248.4 62.9 %all-gather.12.cloned.1.call-done = bf16[4096,2048]{1,0:T(8,128)(2,1)} async-done(((bf16[128,2048]{1,0:T(8,128)(2,1)}), bf16[4096,2048]{1,0:T(8,128)(2,1)}) %all-gather.12.cloned.1.call-update) | async-done | bytes 16777232 | tf_op jit(solution)/shard_map/all_gather | solution.py:409
  311.3 12.9 convolution_convert_fusion.4
  324.2 10.1 copy.304
  334.3 93.9 %all-gather.10.cloned.1.call-done = bf16[4096,2048]{1,0:T(8,128)(2,1)} async-done(((bf16[128,2048]{1,0:T(8,128)(2,1)}), bf16[4096,2048]{1,0:T(8,128)(2,1)}) %all-gather.10.cloned.1.call-update) | async-done | bytes 16777232 | tf_op jit(solution)/shard_map/all_gather | solution.py:409
  428.2 11.0 select_reduce_fusion.2
  441.2 13.0 convolution_convert_fusion.5
  454.2 10.1 copy.297
  464.3 11.2 fusion.112
  475.5 11.6 fusion.111
  487.1 14.1 fusion.12
  511.2 10.4 fusion.113
  521.7 13.9 add_convert_fusion
  535.6 10.1 copy.307
  545.7 12.2 convolution_convert_fusion
  559.1 9.9 dynamic_update_slice.3
  569.0 16.1 pad_maximum_fusion.1
  585.1 379.0 %reduce-scatter.11.cloned.1.call-done = bf16[128,2176]{1,0:T(8,128)(2,1)} async-done(((bf16[4096,2176]{1,0:T(8,128)(2,1)}), bf16[128,2176]{1,0:T(8,128)(2,1)}) %reduce-scatter.11.cloned.1.call-update) | async-done | bytes 557072 | tf_op jit(solution)/shard_map/reduce_scatter | solution.py:413
  978.5 15.8 all-gather.14.cloned.1.call-done
  1048.0 13.5 reduce-scatter.13.cloned.1.call-done
  1077.6 9.9 multiply_convert_fusion
  1087.6 10.2 copy.303
  1097.8 12.3 convolution_convert_fusion.1
  1124.0 11.1 reduce-scatter.17.cloned.1.call-done
  1135.1 16.5 pad_maximum_fusion
  1151.7 12.3 fusion.115
  1164.0 12.8 fusion.114
  1183.1 310.8 %reduce-scatter.9.cloned.1.call-done = bf16[128,2048]{1,0:T(8,128)(2,1)} async-done(((bf16[4096,2048]{1,0:T(8,128)(2,1)}), bf16[128,2048]{1,0:T(8,128)(2,1)}) %reduce-scatter.9.cloned.1.call-update) | async-done | bytes 524304 | tf_op jit(solution)/shard_map/reduce_scatter | solution.py:413
  1497.7 20.4 %all-reduce.4.cloned.1.call-done = f32[128,128]{0,1:T(8,128)} async-done(((f32[128,128]{0,1:T(8,128)}), f32[128,128]{0,1:T(8,128)}) %all-reduce.4.cloned.1.call-update) | async-done | bytes 65552 | tf_op jit(solution)/shard_map/psum | solution.py:701
  1522.0 195.7 %reduce-scatter.15.cloned.1.call-done = bf16[128,4608]{1,0:T(8,128)(2,1)} async-done(((bf16[2048,4608]{1,0:T(8,128)(2,1)}), bf16[128,4608]{1,0:T(8,128)(2,1)}) %reduce-scatter.15.cloned.1.call-update) | async-done | bytes 1179664 | tf_op jit(solution)/shard_map/reduce_scatter | solution.py:417
  (366 shorter events, 225.0 us)
Async XLA Ops:
  8.0 479.1 %copy-start = (bf16[2,384,2048]{2,1,0:T(8,128)(2,1)S(1)}, bf16[2,384,2048]{2,1,0:T(8,128)(2,1)}, u32[]{:S(2)}) copy-start(bf16[2,384,2048]{2,1,0:T(8,128)(2,1)} %param.43) | copy-start | bytes 9437188
  8.0 23.9 %copy-start.67 = (bf16[128,32]{0,1:T(8,128)(2,1)S(1)}, bf16[128,32]{0,1:T(8,128)(2,1)}, u32[]{:S(2)}) copy-start(bf16[128,32]{0,1:T(8,128)(2,1)} %param.40) | copy-start | bytes 24580
  8.0 25.2 %copy-start.79 = (s32[16]{0:T(128)S(1)}, s32[16]{0:T(128)}, u32[]{:S(2)}) copy-start(s32[16]{0:T(128)} %param.50) | copy-start | bytes 196
  8.0 25.2 %copy-start.1 = (s32[16]{0:T(128)S(1)}, s32[16]{0:T(128)}, u32[]{:S(2)}) copy-start(s32[16]{0:T(128)} %param.49) | copy-start | bytes 196
  8.1 29.1 %all-gather.6.cloned.1.call-start = ((), (), s32[]{:S(2)}) async-start(), calls=%async_computation.6 | async-start | bytes 1572864 | tf_op jit(solution)/shard_map/all_gather | solution.py:482
  8.8 137.2 %all-gather.8.cloned.1.call-start = ((), (), s32[]{:S(2)}) async-start(), calls=%async_computation.7 | async-start | bytes 20611072 | tf_op jit(solution)/shard_map/all_gather | solution.py:405
  33.1 176.7 %reduce-scatter.7.cloned.1.call-start = ((), (), s32[]{:S(2)}) async-start(), calls=%async_computation.8 | async-start | bytes 1572864 | tf_op jit(solution)/shard_map/reduce_scatter | solution.py:523
  37.2 132.0 %copy-start.23 = (f32[256,64]{1,0:T(8,128)}, f32[256,64]{1,0:T(8,128)S(1)}, u32[]{:S(2)}) copy-start(f32[256,64]{1,0:T(8,128)S(1)} %get-tuple-element.290) | copy-start | bytes 196612
  38.7 114.4 %copy-start.58 = (f32[256]{0:T(256)}, f32[256]{0:T(256)S(1)}, u32[]{:S(2)}) copy-start(f32[256]{0:T(256)S(1)} %add_rsqrt_fusion.2) | copy-start | bytes 3076
  147.1 64.1 %copy-start.43 = (f32[2048,1]{0,1:T(1,128)}, f32[2048,1]{0,1:T(1,128)S(1)}, u32[]{:S(2)}) copy-start(f32[2048,1]{0,1:T(1,128)S(1)} %get-tuple-element.266) | copy-start | bytes 24580
  190.1 24.1 %copy-start.66 = (s32[256,8]{0,1:T(8,128)S(1)}, s32[256,8]{0,1:T(8,128)}, u32[]{:S(2)}) copy-start(s32[256,8]{0,1:T(8,128)} %param.48) | copy-start | bytes 24580
  190.1 51.6 %copy-start.76 = (s32[16]{0:T(128)S(1)}, s32[16]{0:T(128)}, u32[]{:S(2)}) copy-start(s32[16]{0:T(128)} %copy-done.75) | copy-start | bytes 196
  190.1 121.2 %all-gather.12.cloned.1.call-start = ((), (), s32[]{:S(2)}) async-start(), calls=%async_computation.11 | async-start | bytes 17301504 | tf_op jit(solution)/shard_map/all_gather | solution.py:409
  190.7 237.5 %all-gather.10.cloned.1.call-start = ((), (), s32[]{:S(2)}) async-start(), calls=%async_computation.9 | async-start | bytes 17301504 | tf_op jit(solution)/shard_map/all_gather | solution.py:409
  213.5 750.6 %reduce-scatter.11.cloned.1.call-start = ((), (), s32[]{:S(2)}) async-start(), calls=%async_computation.12 | async-start | bytes 18382848 | tf_op jit(solution)/shard_map/reduce_scatter | solution.py:413
  585.1 382.0 %copy-start.44 = (f32[2048,1]{0,1:T(1,128)S(1)}, f32[2048,1]{0,1:T(1,128)}, u32[]{:S(2)}) copy-start(f32[2048,1]{0,1:T(1,128)} %copy-done.43) | copy-start | bytes 24580
  585.1 382.0 %copy-start.61 = (f32[128]{0:T(128)S(1)}, f32[128]{0:T(128)}, u32[]{:S(2)}) copy-start(f32[128]{0:T(128)} %copy-done.60) | copy-start | bytes 1540
  585.1 409.2 %all-gather.14.cloned.1.call-start = ((), (), s32[]{:S(2)}) async-start(), calls=%async_computation.13 | async-start | bytes 1572864 | tf_op jit(solution)/shard_map/all_gather | solution.py:644
  971.8 89.7 %reduce-scatter.13.cloned.1.call-start = ((), (), s32[]{:S(2)}) async-start(), calls=%async_computation.14 | async-start | bytes 1572864 | tf_op jit(solution)/shard_map/reduce_scatter | solution.py:683
  978.5 22.2 %copy-start.51 = (f32[2,8,256]{2,1,0:T(8,128)S(1)}, f32[2,8,256]{2,1,0:T(8,128)}, u32[]{:S(2)}) copy-start(f32[2,8,256]{2,1,0:T(8,128)} %copy-done.50) | copy-start | bytes 49156
  1041.0 20.5 %copy-start.47 = (f32[2048,1]{0,1:T(1,128)S(1)}, f32[2048,1]{0,1:T(1,128)}, u32[]{:S(2)}) copy-start(f32[2048,1]{0,1:T(1,128)} %copy-done.46) | copy-start | bytes 24580
  1041.0 94.0 %reduce-scatter.17.cloned.1.call-start = ((), (), s32[]{:S(2)}) async-start(), calls=%async_computation.16 | async-start | bytes 1114112 | tf_op jit(solution)/shard_map/reduce_scatter | solution.py:417
  1043.0 20.9 %copy-start.56 = (f32[2048]{0:T(1024)S(1)}, f32[2048]{0:T(1024)}, u32[]{:S(2)}) copy-start(f32[2048]{0:T(1024)} %get-tuple-element.222) | copy-start | bytes 24580
  1046.8 30.8 %copy-start.49 = (f32[2,1280]{1,0:T(2,128)S(1)}, f32[2,1280]{1,0:T(2,128)}, u32[]{:S(2)}) copy-start(f32[2,1280]{1,0:T(2,128)} %copy-done.48) | copy-start | bytes 30724
  1077.6 416.3 %reduce-scatter.9.cloned.1.call-start = ((), (), s32[]{:S(2)}) async-start(), calls=%async_computation.10 | async-start | bytes 17301504 | tf_op jit(solution)/shard_map/reduce_scatter | solution.py:413
  1110.1 408.0 %all-reduce.4.cloned.1.call-start = ((), (), s32[]{:S(2)}) async-start(), calls=%async_computation.17 | async-start | bytes 131072 | tf_op jit(solution)/shard_map/psum | solution.py:701
  1135.0 582.6 %reduce-scatter.15.cloned.1.call-start = ((), (), s32[]{:S(2)}) async-start(), calls=%async_computation.15 | async-start | bytes 20054016 | tf_op jit(solution)/shard_map/reduce_scatter | solution.py:417
  1151.7 25.1 %slice-start = ((s8[10485760]{0:T(1024)(128)(4,1)}), s8[4194304]{0:T(1024)(128)(4,1)S(1)}, s32[]{:S(2)}) async-start(s8[10485760]{0:T(1024)(128)(4,1)} %bitcast.291), calls=%async_computation.18 | async-start | bytes 8388608
  1151.7 25.1 %slice-start.1 = ((s8[10485760]{0:T(1024)(128)(4,1)}), s8[4194304]{0:T(1024)(128)(4,1)S(1)}, s32[]{:S(2)}) async-start(s8[10485760]{0:T(1024)(128)(4,1)} %bitcast.291), calls=%async_computation.19 | async-start | bytes 8388608
  1176.8 317.0 %copy-start.45 = (f32[2048,1]{0,1:T(1,128)S(1)}, f32[2048,1]{0,1:T(1,128)}, u32[]{:S(2)}) copy-start(f32[2048,1]{0,1:T(1,128)} %copy-done.43) | copy-start | bytes 24580
  1176.9 317.0 %copy-start.62 = (f32[128]{0:T(128)S(1)}, f32[128]{0:T(128)}, u32[]{:S(2)}) copy-start(f32[128]{0:T(128)} %copy-done.60) | copy-start | bytes 1540
  1176.9 317.0 %copy-start.74 = (f32[128]{0:T(128)S(1)}, f32[128]{0:T(128)}, u32[]{:S(2)}) copy-start(f32[128]{0:T(128)} %copy-done.73) | copy-start | bytes 1540
  (63 other events, 286.0 us)
Sparse Core Ops, SparseCore 0:
  10.4 23.9 all-gather.5
  36.6 109.3 all-gather.7
  190.2 19.4 reduce-scatter.6
  972.0 22.2 all-gather.13
  1041.1 20.3 reduce-scatter.12
  1077.7 57.2 reduce-scatter.16
  1137.4 356.4 reduce-scatter.8
  1496.2 21.8 all-reduce.3
  1522.8 194.7 reduce-scatter.14
Sparse Core Ops, SparseCore 1:
  194.0 117.3 all-gather.11
  315.2 112.9 all-gather.9
  585.2 378.9 reduce-scatter.10

commit v2 on v1

--- a/solution.py
+++ b/solution.py
@@ -3,6 +3,8 @@
 import jax
 import jax.numpy as jnp
 from jax import lax
+from jax.experimental import pallas as pl
+from jax.experimental.pallas import tpu as pltpu
 from jax.sharding import PartitionSpec as P
 
 HEAD_SIZE = 128
@@ -401,20 +403,617 @@
 AUX = 128
 
 
-def gather_dp(value):
-    return lax.all_gather(value, "dp", axis=0, tiled=True)
-
-
-def gather_all(value):
-    return lax.all_gather(value, ("dp", "tensor"), axis=0, tiled=True)
-
-
-def scatter_all(value):
-    return lax.psum_scatter(value, ("dp", "tensor"), scatter_dimension=0, tiled=True)
-
-
-def scatter_dp(value):
-    return lax.psum_scatter(value, "dp", scatter_dimension=0, tiled=True)
+GRID_Z = 4
+VMEM_LIMIT = 56 * 1024 * 1024
+
+
+def remote(src, dst, send_sem, recv_sem, device):
+    return pltpu.make_async_remote_copy(
+        src_ref=src,
+        dst_ref=dst,
+        send_sem=send_sem,
+        recv_sem=recv_sem,
+        device_id=device,
+        device_id_type=pl.DeviceIdType.MESH,
+    )
+
+
+class Place:
+    def __init__(self):
+        self.dp = lax.axis_index("dp")
+        self.y = lax.axis_index("tensor")
+        self.z = self.dp // 4
+        self.x = (self.dp // 2) % 2
+        self.core = self.dp % 2
+        self.sibling = (self.dp + 1 - 2 * self.core, self.y)
+        self.x_mate = (self.dp + 2 - 4 * self.x, self.y)
+        self.y_mate = (self.dp, 1 - self.y)
+        self.above = (self.dp + 4, self.y)
+        self.below = (self.dp - 4, self.y)
+        self.has_above = self.z < GRID_Z - 1
+        self.has_below = self.z > 0
+
+    def farthest(self, k):
+        return (3 - 3 * (self.z // 2), (2 + 3 * self.z) % 5, 1 + self.z % 2, self.z)[k]
+
+    def dp_at(self, z, flip_x, flip_core):
+        x = self.x + flip_x * (1 - 2 * self.x)
+        core = self.core + flip_core * (1 - 2 * self.core)
+        return z * 4 + x * 2 + core
+
+    def y_at(self, flip_y):
+        return self.y + flip_y * (1 - 2 * self.y)
+
+    def greet(self):
+        barrier = pltpu.get_barrier_semaphore()
+        for mate in (self.sibling, self.x_mate, self.y_mate):
+            pl.semaphore_signal(barrier, 1, device_id=mate, device_id_type=pl.DeviceIdType.MESH)
+
+        @pl.when(self.has_above)
+        def _():
+            pl.semaphore_signal(
+                barrier, 1, device_id=self.above, device_id_type=pl.DeviceIdType.MESH
+            )
+
+        @pl.when(self.has_below)
+        def _():
+            pl.semaphore_signal(
+                barrier, 1, device_id=self.below, device_id_type=pl.DeviceIdType.MESH
+            )
+
+        pl.semaphore_wait(barrier, 4 + self.z * (GRID_Z - 1 - self.z) // 2)
+
+
+def add_rows(target, sources, rows, step=16):
+    start, count = rows
+
+    def one(i, carry):
+        at = pl.ds(pl.multiple_of(start + i * step, step), step)
+        total = target[at, :].astype(jnp.float32)
+        for source, shift in sources:
+            there = pl.ds(pl.multiple_of(start - shift + i * step, step), step)
+            total = total + source[there, :].astype(jnp.float32)
+        target[at, :] = total.astype(target.dtype)
+        return carry
+
+    lax.fori_loop(0, count // step, one, 0)
+
+
+def scatter_kernel(
+    part, out, own, core, diag_a, diag_b, from_x, from_y, from_z, result,
+    load_s, core_s, diag_s, x_s, y_s, z_s, out_s,
+):
+    me = Place()
+    rows = own.shape[3]
+    half = rows // 2
+    low, high = (0, half), (half, half)
+    loads, sends = {}, []
+
+    def chunk(k, flip_x, flip_y, flip_core):
+        return part.at[me.dp_at(me.farthest(k), flip_x, flip_core) * 2 + me.y_at(flip_y)]
+
+    order = ((1, 1), (1, 0), (0, 1), (0, 0))
+    for k in range(GRID_Z):
+        for fx, fy in order:
+            copy = pltpu.make_async_copy(
+                chunk(k, fx, fy, 0), own.at[k, fx, fy], load_s.at[k, fx, fy]
+            )
+            copy.start()
+            loads[k, fx, fy] = copy
+    me.greet()
+    cores = {}
+    for k in range(GRID_Z):
+        for fx, fy in order:
+            copy = remote(
+                chunk(k, fx, fy, 1), core.at[k, fx, fy],
+                core_s.at[0, k, fx, fy], core_s.at[1, k, fx, fy], me.sibling,
+            )
+            copy.start()
+            cores[k, fx, fy] = copy
+            sends.append(copy)
+
+    da = [remote(own.at[k, 1, 1, pl.ds(0, half)], diag_a.at[k], diag_s.at[0, k], diag_s.at[1, k], me.y_mate) for k in range(4)]
+    db = [remote(own.at[k, 1, 1, pl.ds(half, half)], diag_b.at[k], diag_s.at[2, k], diag_s.at[3, k], me.x_mate) for k in range(4)]
+    xs = [[remote(own.at[k, 1, 0, pl.ds(h * half, half)], from_x.at[k, pl.ds(h * half, half)], x_s.at[0, k, h], x_s.at[1, k, h], me.x_mate) for h in range(2)] for k in range(4)]
+    ys = [[remote(own.at[k, 0, 1, pl.ds(h * half, half)], from_y.at[k, pl.ds(h * half, half)], y_s.at[0, k, h], y_s.at[1, k, h], me.y_mate) for h in range(2)] for k in range(4)]
+
+    def arrive(k, fx, fy):
+        loads[k, fx, fy].wait()
+        cores[k, fx, fy].wait_recv()
+
+    def early(k):
+        arrive(k, 1, 1)
+        add_rows(own.at[k, 1, 1], [(core.at[k, 1, 1], 0)], low)
+        da[k].start()
+        add_rows(own.at[k, 1, 1], [(core.at[k, 1, 1], 0)], high)
+        db[k].start()
+        arrive(k, 1, 0)
+        add_rows(own.at[k, 1, 0], [(core.at[k, 1, 0], 0)], high)
+        xs[k][1].start()
+        arrive(k, 0, 1)
+        add_rows(own.at[k, 0, 1], [(core.at[k, 0, 1], 0)], low)
+        ys[k][0].start()
+
+    def late(k):
+        da[k].wait_recv()
+        add_rows(own.at[k, 1, 0], [(core.at[k, 1, 0], 0), (diag_a.at[k], 0)], low)
+        xs[k][0].start()
+        db[k].wait_recv()
+        add_rows(own.at[k, 0, 1], [(core.at[k, 0, 1], 0), (diag_b.at[k], half)], high)
+        ys[k][1].start()
+
+    whole = (0, rows)
+
+    def column(k):
+        arrive(k, 0, 0)
+        for h in range(2):
+            xs[k][h].wait_recv()
+            ys[k][h].wait_recv()
+        mine = own.at[k, 0, 0]
+        rest = [(core.at[k, 0, 0], 0), (from_x.at[k], 0), (from_y.at[k], 0)]
+        if k < GRID_Z - 1:
+            to = me.farthest(k)
+            add_rows(mine, rest, whole)
+            for side, ahead, mate, more in (
+                (0, to > me.z, me.above, me.has_below),
+                (1, to < me.z, me.below, me.has_above),
+            ):
+                copy = remote(
+                    mine, from_z.at[side, to], z_s.at[0, side, to], z_s.at[1, side, to], mate
+                )
+
+                @pl.when(ahead)
+                def _():
+                    @pl.when(more)
+                    def _():
+                        copy.wait_recv()
+                        add_rows(mine, [(from_z.at[side, to], 0)], whole)
+
+                    copy.start()
+        else:
+            add_rows(mine, rest, whole)
+            for side, more in ((0, me.has_below), (1, me.has_above)):
+                copy = remote(
+                    mine, from_z.at[side, me.z], z_s.at[0, side, me.z], z_s.at[1, side, me.z],
+                    me.y_mate,
+                )
+
+                @pl.when(more)
+                def _():
+                    copy.wait_recv()
+                    add_rows(mine, [(from_z.at[side, me.z], 0)], whole)
+
+    early(0)
+    early(1)
+    late(0)
+    early(2)
+    late(1)
+    column(0)
+    early(3)
+    late(2)
+    column(1)
+    late(3)
+    column(2)
+    column(3)
+    copy = pltpu.make_async_copy(own.at[3, 0, 0], out, out_s)
+    copy.start()
+    for k in range(GRID_Z):
+        da[k].wait_send()
+        db[k].wait_send()
+        for h in range(2):
+            xs[k][h].wait_send()
+            ys[k][h].wait_send()
+        if k < GRID_Z - 1:
+            to = me.farthest(k)
+            for side, ahead, mate in ((0, to > me.z, me.above), (1, to < me.z, me.below)):
+                @pl.when(ahead)
+                def _():
+                    remote(
+                        own.at[k, 0, 0], from_z.at[side, to],
+                        z_s.at[0, side, to], z_s.at[1, side, to], mate,
+                    ).wait_send()
+    for sent in sends:
+        sent.wait_send()
+    copy.wait()
+
+
+def scatter_all(value, collective_id):
+    devices = lax.axis_size("dp") * lax.axis_size("tensor")
+    rows, width = value.shape[0] // devices, value.shape[1]
+    half = rows // 2
+    dma = pltpu.SemaphoreType.DMA
+    low = value.dtype
+    return pl.pallas_call(
+        scatter_kernel,
+        out_shape=jax.ShapeDtypeStruct((rows, width), low),
+        in_specs=[pl.BlockSpec(memory_space=pl.ANY)],
+        out_specs=pl.BlockSpec(memory_space=pl.ANY),
+        scratch_shapes=[
+            pltpu.VMEM((4, 2, 2, rows, width), low),
+            pltpu.VMEM((4, 2, 2, rows, width), low),
+            pltpu.VMEM((4, half, width), low),
+            pltpu.VMEM((4, half, width), low),
+            pltpu.VMEM((4, rows, width), low),
+            pltpu.VMEM((4, rows, width), low),
+            pltpu.VMEM((2, 4, rows, width), low),
+            pltpu.VMEM((8, 128), low),
+            dma((4, 2, 2)),
+            dma((2, 4, 2, 2)),
+            dma((4, 4)),
+            dma((2, 4, 2)),
+            dma((2, 4, 2)),
+            dma((2, 2, 4)),
+            dma(()),
+        ],
+        compiler_params=pltpu.CompilerParams(
+            collective_id=collective_id, has_side_effects=True, vmem_limit_bytes=VMEM_LIMIT
+        ),
+    )(value.reshape(devices, rows, width))
+
+
+def gather_kernel(src, out, own_s, z_s, x_s, y_s, dx_s, dy_s, core_s):
+    me = Place()
+    rows = src.shape[0]
+    half = rows // 2
+    low, high = pl.ds(0, half), pl.ds(half, half)
+
+    def near(k):
+        return me.farthest(GRID_Z - 1 - k)
+
+    def at(k, fx, fy, fc):
+        return out.at[me.dp_at(near(k), fx, fc) * 2 + me.y_at(fy)]
+
+    mine = pltpu.make_async_copy(src, at(0, 0, 0, 0), own_s)
+    mine.start()
+    me.greet()
+
+    def over(source, k, fx, fy, send, recv, mate):
+        return remote(source, at(k, fx, fy, 0), send, recv, mate)
+
+    def z_copy(k, source, side, mate):
+        zn = near(k)
+        return remote(source, at(k, 0, 0, 0), z_s.at[0, side, zn], z_s.at[1, side, zn], mate)
+
+    xs, ys, dxs, dys, cores = {}, {}, {}, {}, {}
+    for k in range(GRID_Z):
+        source = src if k == 0 else at(k, 0, 0, 0)
+        xs[k] = over(source, k, 0, 0, x_s.at[0, k], x_s.at[1, k], me.x_mate)
+        ys[k] = over(source, k, 0, 0, y_s.at[0, k], y_s.at[1, k], me.y_mate)
+        dys[k] = remote(at(k, 1, 0, 0).at[low], at(k, 1, 0, 0).at[low], dy_s.at[0, k], dy_s.at[1, k], me.y_mate)
+        dxs[k] = remote(at(k, 0, 1, 0).at[high], at(k, 0, 1, 0).at[high], dx_s.at[0, k], dx_s.at[1, k], me.x_mate)
+        for fx in range(2):
+            for fy in range(2):
+                block = source if (fx, fy) == (0, 0) else at(k, fx, fy, 0)
+                if (fx, fy) == (1, 1):
+                    for h, part in enumerate((low, high)):
+                        cores[k, fx, fy, h] = remote(
+                            block.at[part], block.at[part],
+                            core_s.at[0, k, 3 + h], core_s.at[1, k, 3 + h], me.sibling,
+                        )
+                else:
+                    cores[k, fx, fy] = remote(
+                        block, at(k, fx, fy, 0), core_s.at[0, k, fx * 2 + fy],
+                        core_s.at[1, k, fx * 2 + fy], me.sibling,
+                    )
+
+    def own(k):
+        if k == 0:
+            for side, more, mate in ((0, me.has_above, me.above), (1, me.has_below, me.below)):
+                copy = z_copy(0, src, side, mate)
+
+                @pl.when(more)
+                def _():
+                    copy.start()
+        else:
+            zn = near(k)
+            for side, came, more, mate in (
+                (0, zn < me.z, me.has_above, me.above),
+                (1, zn > me.z, me.has_below, me.below),
+            ):
+                copy = z_copy(k, at(k, 0, 0, 0), side, mate)
+
+                @pl.when(came)
+                def _():
+                    copy.wait_recv()
+
+                    @pl.when(more)
+                    def _():
+                        copy.start()
+
+        xs[k].start()
+        ys[k].start()
+        cores[k, 0, 0].start()
+
+    def diag(k):
+        xs[k].wait_recv()
+        dys[k].start()
+        cores[k, 1, 0].start()
+        ys[k].wait_recv()
+        dxs[k].start()
+        cores[k, 0, 1].start()
+
+    def corner(k):
+        dys[k].wait_recv()
+        cores[k, 1, 1, 0].start()
+        dxs[k].wait_recv()
+        cores[k, 1, 1, 1].start()
+
+    own(0)
+    own(1)
+    diag(0)
+    own(2)
+    diag(1)
+    corner(0)
+    own(3)
+    diag(2)
+    corner(1)
+    diag(3)
+    corner(2)
+    corner(3)
+    mine.wait()
+    for k in range(GRID_Z):
+        zn = near(k)
+        for side, came, more, mate in (
+            (0, zn <= me.z, me.has_above, me.above),
+            (1, zn >= me.z, me.has_below, me.below),
+        ):
+            copy = z_copy(k, src if k == 0 else at(k, 0, 0, 0), side, mate)
+
+            @pl.when(came)
+            def _():
+                @pl.when(more)
+                def _():
+                    copy.wait_send()
+        for copy in (xs[k], ys[k], dxs[k], dys[k]):
+            copy.wait_send()
+    for copy in cores.values():
+        copy.wait()
+
+
+def gather_all(value, collective_id):
+    devices = lax.axis_size("dp") * lax.axis_size("tensor")
+    rows, width = value.shape
+    dma = pltpu.SemaphoreType.DMA
+    return pl.pallas_call(
+        gather_kernel,
+        out_shape=jax.ShapeDtypeStruct((devices, rows, width), value.dtype),
+        in_specs=[pl.BlockSpec(memory_space=pl.ANY)],
+        out_specs=pl.BlockSpec(memory_space=pl.ANY),
+        scratch_shapes=[
+            dma(()),
+            dma((2, 2, 4)),
+            dma((2, 4)),
+            dma((2, 4)),
+            dma((2, 4)),
+            dma((2, 4)),
+            dma((2, 4, 5)),
+        ],
+        compiler_params=pltpu.CompilerParams(collective_id=collective_id, has_side_effects=True),
+    )(value).reshape(devices * rows, width)
+
+
+def plane_gather_kernel(src, out, own_s, z_s, x_s, core_s):
+    me = Place()
+
+    def near(k):
+        return me.farthest(GRID_Z - 1 - k)
+
+    def at(k, fx):
+        return out.at[me.dp_at(near(k), fx, 0)]
+
+    mine = pltpu.make_async_copy(src, at(0, 0), own_s)
+    mine.start()
+    me.greet()
+
+    def z_copy(k, side, mate):
+        zn = near(k)
+        return remote(
+            src if k == 0 else at(k, 0), at(k, 0), z_s.at[0, side, zn], z_s.at[1, side, zn], mate
+        )
+
+    xs, cores = {}, {}
+    for k in range(GRID_Z):
+        source = src if k == 0 else at(k, 0)
+        xs[k] = remote(source, at(k, 0), x_s.at[0, k], x_s.at[1, k], me.x_mate)
+        cores[k, 0] = remote(source, at(k, 0), core_s.at[0, k, 0], core_s.at[1, k, 0], me.sibling)
+        cores[k, 1] = remote(at(k, 1), at(k, 1), core_s.at[0, k, 1], core_s.at[1, k, 1], me.sibling)
+
+    def own(k):
+        zn = near(k)
+        for side, came, more, mate in (
+            (0, zn < me.z, me.has_above, me.above),
+            (1, zn > me.z, me.has_below, me.below),
+        ):
+            copy = z_copy(k, side, mate)
+            if k == 0:
+
+                @pl.when(more)
+                def _():
+                    copy.start()
+            else:
+
+                @pl.when(came)
+                def _():
+                    copy.wait_recv()
+
+                    @pl.when(more)
+                    def _():
+                        copy.start()
+
+        xs[k].start()
+        cores[k, 0].start()
+
+    def diag(k):
+        xs[k].wait_recv()
+        cores[k, 1].start()
+
+    own(0)
+    own(1)
+    diag(0)
+    own(2)
+    diag(1)
+    own(3)
+    diag(2)
+    diag(3)
+    mine.wait()
+    for k in range(GRID_Z):
+        zn = near(k)
+        for side, came, more, mate in (
+            (0, zn <= me.z, me.has_above, me.above),
+            (1, zn >= me.z, me.has_below, me.below),
+        ):
+            copy = z_copy(k, side, mate)
+
+            @pl.when(came)
+            def _():
+                @pl.when(more)
+                def _():
+                    copy.wait_send()
+
+        xs[k].wait_send()
+    for copy in cores.values():
+        copy.wait()
+
+
+def gather_dp(value, collective_id):
+    devices = lax.axis_size("dp")
+    rows, width = value.shape
+    dma = pltpu.SemaphoreType.DMA
+    return pl.pallas_call(
+        plane_gather_kernel,
+        out_shape=jax.ShapeDtypeStruct((devices, rows, width), value.dtype),
+        in_specs=[pl.BlockSpec(memory_space=pl.ANY)],
+        out_specs=pl.BlockSpec(memory_space=pl.ANY),
+        scratch_shapes=[dma(()), dma((2, 2, 4)), dma((2, 4)), dma((2, 4, 2))],
+        compiler_params=pltpu.CompilerParams(collective_id=collective_id, has_side_effects=True),
+    )(value).reshape(devices * rows, width)
+
+
+def plane_scatter_kernel(
+    part, out, own, core, from_x, from_z, load_s, core_s, x_s, z_s, out_s
+):
+    me = Place()
+    rows = own.shape[2]
+    whole = (0, rows)
+    loads, cores = {}, {}
+
+    def chunk(k, flip_x, flip_core):
+        return part.at[me.dp_at(me.farthest(k), flip_x, flip_core)]
+
+    for k in range(GRID_Z):
+        for fx in (1, 0):
+            loads[k, fx] = pltpu.make_async_copy(chunk(k, fx, 0), own.at[k, fx], load_s.at[k, fx])
+            loads[k, fx].start()
+    me.greet()
+    for k in range(GRID_Z):
+        for fx in (1, 0):
+            cores[k, fx] = remote(
+                chunk(k, fx, 1), core.at[k, fx],
+                core_s.at[0, k, fx], core_s.at[1, k, fx], me.sibling,
+            )
+            cores[k, fx].start()
+    half = rows // 2
+    xs = [
+        [
+            remote(
+                own.at[k, 1, pl.ds(h * half, half)], from_x.at[k, pl.ds(h * half, half)],
+                x_s.at[0, k, h], x_s.at[1, k, h], me.x_mate,
+            )
+            for h in range(2)
+        ]
+        for k in range(GRID_Z)
+    ]
+
+    def z_copy(k, side, mate):
+        to = me.farthest(k)
+        return remote(
+            own.at[k, 0], from_z.at[side, to], z_s.at[0, side, to], z_s.at[1, side, to], mate
+        )
+
+    def across(k):
+        loads[k, 1].wait()
+        cores[k, 1].wait_recv()
+        for h in range(2):
+            add_rows(own.at[k, 1], [(core.at[k, 1], 0)], (h * half, half))
+            xs[k][h].start()
+
+    def column(k):
+        loads[k, 0].wait()
+        cores[k, 0].wait_recv()
+        for h in range(2):
+            xs[k][h].wait_recv()
+        mine = own.at[k, 0]
+        add_rows(mine, [(core.at[k, 0], 0), (from_x.at[k], 0)], whole)
+        to = me.farthest(k)
+        for side, ahead, mate, more in (
+            (0, to > me.z, me.above, me.has_below),
+            (1, to < me.z, me.below, me.has_above),
+        ):
+            copy = z_copy(k, side, mate)
+            if k < GRID_Z - 1:
+
+                @pl.when(ahead)
+                def _():
+                    @pl.when(more)
+                    def _():
+                        copy.wait_recv()
+                        add_rows(mine, [(from_z.at[side, to], 0)], whole)
+
+                    copy.start()
+            else:
+
+                @pl.when(more)
+                def _():
+                    copy.wait_recv()
+                    add_rows(mine, [(from_z.at[side, to], 0)], whole)
+
+    for k in range(GRID_Z):
+        across(k)
+        if k:
+            column(k - 1)
+    column(GRID_Z - 1)
+    copy = pltpu.make_async_copy(own.at[3, 0], out, out_s)
+    copy.start()
+    for k in range(GRID_Z):
+        for h in range(2):
+            xs[k][h].wait_send()
+        if k < GRID_Z - 1:
+            to = me.farthest(k)
+            for side, ahead, mate in ((0, to > me.z, me.above), (1, to < me.z, me.below)):
+
+                @pl.when(ahead)
+                def _():
+                    z_copy(k, side, mate).wait_send()
+    for sent in cores.values():
+        sent.wait_send()
+    copy.wait()
+
+
+def scatter_dp(value, collective_id):
+    devices = lax.axis_size("dp")
+    rows, width = value.shape[0] // devices, value.shape[1]
+    dma = pltpu.SemaphoreType.DMA
+    low = value.dtype
+    return pl.pallas_call(
+        plane_scatter_kernel,
+        out_shape=jax.ShapeDtypeStruct((rows, width), low),
+        in_specs=[pl.BlockSpec(memory_space=pl.ANY)],
+        out_specs=pl.BlockSpec(memory_space=pl.ANY),
+        scratch_shapes=[
+            pltpu.VMEM((4, 2, rows, width), low),
+            pltpu.VMEM((4, 2, rows, width), low),
+            pltpu.VMEM((4, rows, width), low),
+            pltpu.VMEM((2, 4, rows, width), low),
+            dma((4, 2)),
+            dma((2, 4, 2)),
+            dma((2, 4, 2)),
+            dma((2, 2, 4)),
+            dma(()),
+        ],
+        compiler_params=pltpu.CompilerParams(
+            collective_id=collective_id, has_side_effects=True, vmem_limit_bytes=VMEM_LIMIT
+        ),
+    )(value.reshape(devices, rows, width))
 
 
 def split_high_low(value):
@@ -464,7 +1063,7 @@
         [query_weight, key_projection, value_projection, context_weight.T, router_weight, gains],
         axis=1,
     )
-    packed = gather_dp(packed)
+    packed = gather_dp(packed, 0)
     edges = [0]
     for width in (query_width, key_width, key_width, query_width, expert_count, AUX - expert_count):
         edges.append(edges[-1] + width)
@@ -477,8 +1076,8 @@
     query_factor = head_gains[:, :, 2].reshape(-1)
     key_factor = head_gains[:, :, 3].reshape(-1)
 
-    cot_all = gather_all(output_cotangent)
-    routes_all = gather_dp(routes)
+    cot_all = lax.all_gather(output_cotangent, ("dp", "tensor"), axis=0, tiled=True)
+    routes_all = lax.all_gather(routes, "dp", axis=0, tiled=True)
     input_rows = lax.all_gather(layer_input, "tensor", axis=0, tiled=True)
     position = jnp.arange(block_rows, dtype=jnp.int32)
     block_lengths = lengths[sequence_order]
@@ -530,7 +1129,7 @@
     unit_second, scale_second = rms_normalize(residual)
     normed_second = (unit_second * gain_two).astype(bf16)
 
-    normed_all = gather_all(normed_second)
+    normed_all = gather_all(normed_second, 1)
     logits = matrix_product(normed_all, router_all)
     expert_ids = jnp.arange(expert_count, dtype=jnp.int32)
     chosen = jnp.zeros((tokens, expert_count), jnp.bool_)
@@ -598,7 +1197,7 @@
     gate_act = gate_pre * sigmoid_gate
     hidden = (gate_act * up_pre).astype(bf16)
     out_partial = jnp.einsum("enf,efd->end", hidden, expert_down, preferred_element_type=f32)
-    expert_sum = scatter_all(put(out_partial * slot_gate))
+    expert_sum = scatter_all(put(out_partial * slot_gate), 2)
     layer_output = (residual + expert_sum.astype(f32)).astype(bf16)
 
     down_cot = jnp.einsum("end,efd->enf", cot_in, expert_down, preferred_element_type=f32)
@@ -626,7 +1225,7 @@
         quad,
         (0, tensor_index * 2 * expert_count + dp_index * 2 * EXP_DEV),
     )
-    returned = scatter_all(jnp.concatenate([put(row_partial), aux], axis=1)).astype(f32)
+    returned = scatter_all(jnp.concatenate([put(row_partial), aux], axis=1), 3).astype(f32)
     gate_cot = jnp.sum(
         returned[:, features:].reshape(own_rows, tensor_count, expert_count, 2), axis=(1, 3)
     )
@@ -697,9 +1296,9 @@
     small = small.at[:, :, expert_count + 1].set(midnorm_part.reshape(dp_count, shard))
     small = small.at[:, :norm_part, expert_count + 2].set(querynorm_part.reshape(dp_count, -1))
     small = small.at[:, :norm_part, expert_count + 3].set(keynorm_part.reshape(dp_count, -1))
-    small = scatter_dp(small.reshape(features, AUX))
+    small = lax.psum_scatter(small.reshape(features, AUX), "dp", scatter_dimension=0, tiled=True)
     small = lax.psum(small, "tensor")
-    summed = scatter_dp(jnp.concatenate([qkv_part.astype(bf16), context_part.astype(bf16)], axis=1))
+    summed = scatter_dp(jnp.concatenate([qkv_part.astype(bf16), context_part.astype(bf16)], axis=1), 4)
     summed = summed.astype(f32)
     return (
         layer_output,

time: 1750 us -> 1060 us (0.61)
  waiting for transfers between devices: 1230 us -> 27.8 us
  Pallas kernels: 0 us -> 525 us
    reduce_scatter x4 -> x1, waiting for transfers between devices: 896 us -> 0.01 us  [gathered_body(): lax.psum_scatter(small.reshape(features, AUX), 'dp', scatter_dimension=0,...]
    pallas_call x0 -> x5, Pallas kernels: none -> 525 us  [the longest x2 168 us: scatter_all(): pl.pallas_call(scatter_kernel, out_shape=jax.ShapeDtypeStruct((rows, widt...]
    all_gather x3 -> x1, waiting for transfers between devices: 264 us -> 0.01 us  [gathered_body(): lax.all_gather(output_cotangent, ('dp', 'tensor'), axis=0, tiled=True)]
    reduce_scatter x1, waiting for transfers between devices: 19 us -> 0.01 us  [gathered_body(): lax.psum_scatter(transposed(context, context_all).astype(bf16), 'tensor',...]
  transfers between devices with their start and end apart: 12 -> 7, of which waited for: 11 -> 2; matrix products, arithmetic and copies ran while one was open for 11% -> 18% of each run, Pallas kernels for 0% -> 42%
where the time goes in v2:
time: 1060 us; the launch traced here: 1050 us
  Pallas kernels  525 us (50%)
  matrix products  224 us (21%)
  local copies, waits for them, and re-layouts  133 us (13%)
  other arithmetic  102 us (10%)
  waiting for transfers between devices  27.8 us (3%)
  blocking collectives  19.2 us (2%)
  between operations  17 us (2%)
    pallas_call x2, Pallas kernels, scatter_all(): pl.pallas_call(scatter_kernel, out_shape=jax.ShapeDtypeStruct((rows, widt...  168 us
    pallas_call x1, Pallas kernels, scatter_dp(): pl.pallas_call(plane_scatter_kernel, out_shape=jax.ShapeDtypeStruct((rows...  125 us
    pallas_call x1, Pallas kernels, gather_all(): pl.pallas_call(gather_kernel, out_shape=jax.ShapeDtypeStruct((devices, ro...  117 us
    pallas_call x1, Pallas kernels, gather_dp(): pl.pallas_call(plane_gather_kernel, out_shape=jax.ShapeDtypeStruct((devic...  115 us
    dot_general x2, matrix products, take(): jnp.einsum('bst,btd->bsd', place_low, rows.reshape(dp_count, block_rows,...  25.6 us
    dot_general x3, matrix products, matrix_product(): return jnp.dot(former, latter, preferred_element_type=jnp.float32)  24.5 us
    dot_general x2, matrix products, put(): jnp.einsum('bst,bsd->btd', place_low, ordered, preferred_element_type=f32)  24.2 us
    unnamed x173, local copies, waits for them, and re-layouts  23.6 us
  transfers between devices with their start and end apart: 7, of which 2 were waited for; matrix products, arithmetic and copies ran while one was open for 18% of the time, Pallas kernels for 42%

profile of v2, /device:TPU:0, one launch (start us, length us, event | category | flops | bytes accessed | tf_op | source)
XLA Modules:
  0.0 1049.5 jit_solution(8516514776194905352)
XLA Ops:
  31.0 115.2 %shard_map.272 = bf16[16,128,4736]{2,1,0:T(8,128)(2,1)} custom-call(bf16[128,4736]{1,0:T(8,128)(2,1)} %concatenate.64.src), custom_call_target="tpu_custom_call" | custom-call | tf_op jit(solution)/shard_map/pallas_call | solution.py:882
  160.4 6.5 fusion.3
  195.9 6.8 fusion.21
  204.0 19.2 %all_gather.13 = s32[4096,8]{0,1:T(8,128)S(1)} all-gather(s32[256,8]{0,1:T(8,128)S(1)} %copy-done.70), channel_id=1, replica_groups=mesh['dp'=16,'tensor'=2] {'dp'}, dimensions={0}, use_global_device_ids=true | all-gather | bytes 139264 | tf_op jit(solution)/shard_map/all_gather | solution.py:1080
  247.3 117.4 %shard_map.273 = bf16[32,128,2048]{2,1,0:T(8,128)(2,1)} custom-call(bf16[128,2048]{1,0:T(8,128)(2,1)} %multiply_convert_fusion.5.src), custom_call_target="tpu_custom_call" | custom-call | tf_op jit(solution)/shard_map/pallas_call | solution.py:777
  364.8 11.8 %select_reduce_fusion.2 = (f32[4096]{0:T(1024)S(1)}, f32[4096,32]{0,1:T(8,128)}) fusion(s32[4096]{0:T(1024)S(1)} %bitcast.357, s32[4096]{0:T(1024)S(1)} %bitcast.354, s32[4096]{0:T(1024)S(1)} %bitcast.351, s32[4096]{0:T(1024)S(1)} %bitcast.348, s32[4096]{0:T(1024)S(1)} %bitcast.345, s32[4096]{0:T(1024)S(1)} %bitcast.342, s32[4096]{0:T(1024)S(1)} %bitcast.339, ...), kind=kOutput, calls=%fused_computation.107 | convolution fusion | flops 539095040 | bytes 17973248 | tf_op jit(solution)/shard_map/dot_general | solution.py:58
  380.7 12.8 %convolution_convert_fusion.5 = bf16[16,160,2048]{2,1,0:T(8,128)(2,1)} fusion(pred[16,160,256]{2,1,0:T(32,128)(4,1)} %fusion.17, bf16[16,256,2048]{2,1,0:T(8,128)(2,1)} %bitcast.285), kind=kOutput, calls=%fused_computation.19 | convolution fusion | flops 2689597440 | bytes 27918336 | tf_op jit(solution)/shard_map/bst,btd->bsd/dot_general | solution.py:1167
  393.5 10.0 copy.325
  403.6 11.6 %fusion.111 = f32[2,1280,384]{1,2,0:T(8,128)} fusion(bf16[2,1280,2048]{2,1,0:T(8,128)(2,1)} %bitcast.306, bf16[2,2048,384]{2,1,0:T(8,128)(2,1)} %param.42), kind=kOutput, calls=%fused_computation.258 | convolution fusion | flops 4026531840 | bytes 17563648 | tf_op jit(solution)/shard_map/end,edf->enf/dot_general | solution.py:1195
  415.2 11.1 %fusion.110 = f32[2,1280,384]{1,2,0:T(8,128)} fusion(bf16[2,1280,2048]{2,1,0:T(8,128)(2,1)} %bitcast.307, bf16[2,2048,384]{2,1,0:T(8,128)(2,1)} %param.41), kind=kOutput, calls=%fused_computation.257 | convolution fusion | flops 4026531840 | bytes 17563648 | tf_op jit(solution)/shard_map/end,edf->enf/dot_general | solution.py:1194
  426.3 12.8 %convolution_convert_fusion.4 = bf16[16,160,2048]{2,1,0:T(8,128)(2,1)} fusion(pred[16,160,256]{2,1,0:T(32,128)(4,1)} %fusion.17, bf16[16,256,2048]{2,1,0:T(8,128)(2,1)} %bitcast.296), kind=kOutput, calls=%fused_computation.18 | convolution fusion | flops 2689597440 | bytes 27918336 | tf_op jit(solution)/shard_map/bst,btd->bsd/dot_general | solution.py:1167
  439.1 10.0 copy.332
  449.1 14.3 %fusion.12 = (f32[2,1280]{1,0:T(2,128)S(1)}, bf16[2,1280,384]{1,2,0:T(8,128)(2,1)}, f32[2,1280,384]{1,2,0:T(8,128)}) fusion(f32[2,1280,384]{1,2,0:T(8,128)} %fusion.111, f32[2,1280,384]{1,2,0:T(8,128)} %fusion.110, bf16[2,1280,2048]{2,1,0:T(8,128)(2,1)} %bitcast.293, bf16[2,384,2048]{2,1,0:T(8,128)(2,1)S(1)} %copy-done), kind=kOutput, calls=%fused_computation.29 | convolution fusion | flops 4035376640 | bytes 27404288 | tf_op jit(solution)/shard_map/end,efd->enf/dot_general | solution.py:1203
  465.4 11.6 %fusion.35 = f32[2,384,2048]{2,1,0:T(8,128)} fusion(bf16[2,1280,2048]{2,1,0:T(8,128)(2,1)} %bitcast.294, bf16[2,1280,384]{1,2,0:T(8,128)(2,1)} %get-tuple-element.243, f32[2,1280]{1,0:T(2,128)S(1)} %mul.670), kind=kOutput, calls=%fused_computation.71 | convolution fusion | flops 4029480960 | bytes 18753536 | tf_op jit(solution)/shard_map/enf,end->efd/dot_general | solution.py:1211
  477.0 8.2 multiply_convert_fusion
  489.8 12.4 %fusion.112 = f32[2,1280,2048]{2,1,0:T(8,128)} fusion(bf16[2,1280,384]{1,2,0:T(8,128)(2,1)S(1)} %get-tuple-element.247, bf16[2,2048,384]{2,1,0:T(8,128)(2,1)} %param.41), kind=kOutput, calls=%fused_computation.259 | convolution fusion | flops 4026531840 | bytes 26083328 | tf_op jit(solution)/shard_map/enf,edf->end/dot_general | solution.py:1214
  502.2 13.8 %add_convert_fusion = bf16[2,1280,2048]{2,1,0:T(8,128)(2,1)} fusion(f32[2,1280,2048]{2,1,0:T(8,128)} %fusion.112, bf16[2,1280,384]{1,2,0:T(8,128)(2,1)} %get-tuple-element.246, bf16[2,2048,384]{2,1,0:T(8,128)(2,1)} %param.42), kind=kOutput, calls=%fused_computation.2 | convolution fusion | flops 4037017600 | bytes 36569088 | tf_op jit(solution)/shard_map/enf,edf->end/dot_general | solution.py:1215
  516.1 10.2 copy.335
  526.3 12.1 %convolution_convert_fusion = bf16[16,256,2048]{2,1,0:T(8,128)(2,1)} fusion(pred[16,160,256]{2,1,0:T(32,128)(4,1)S(1)} %copy-done.8, bf16[16,160,2048]{2,1,0:T(8,128)(2,1)} %bitcast.292), kind=kOutput, calls=%fused_computation.6 | convolution fusion | flops 2692743168 | bytes 27918336 | tf_op jit(solution)/shard_map/bst,bsd->btd/dot_general | solution.py:1187
  538.5 9.3 dynamic_update_slice.3
  547.8 14.2 %pad_maximum_fusion.1.part = bf16[32,128,2176]{2,1,0:T(8,128)(2,1)} fusion(bf16[32,128,128]{2,1,0:T(8,128)(2,1)S(1)} %bitcast.322, bf16[32,128,2048]{2,1,0:T(8,128)(2,1)} %bitcast.287), kind=kLoop, calls=%fused_computation.5 | loop fusion | flops 35651584 | bytes 35651584 | tf_op jit(solution)/shard_map/concatenate | solution.py:1228
  562.0 86.4 %shard_map.275 = bf16[128,2176]{1,0:T(8,128)(2,1)} custom-call(bf16[32,128,2176]{2,1,0:T(8,128)(2,1)} %pad_maximum_fusion.1.part), custom_call_target="tpu_custom_call" | custom-call | tf_op jit(solution)/shard_map/pallas_call | solution.py:626
  651.3 10.0 copy.331
  661.3 12.2 %convolution_convert_fusion.1 = bf16[16,256,2048]{2,1,0:T(8,128)(2,1)} fusion(pred[16,160,256]{2,1,0:T(32,128)(4,1)S(1)} %copy-done.8, bf16[16,160,2048]{2,1,0:T(8,128)(2,1)} %bitcast.291), kind=kOutput, calls=%fused_computation.7 | convolution fusion | flops 2692743168 | bytes 27918336 | tf_op jit(solution)/shard_map/bst,bsd->btd/dot_general | solution.py:1187
  678.4 12.1 %fusion.114 = f32[2,2048,384]{2,1,0:T(8,128)} fusion(bf16[2,1280,2048]{2,1,0:T(8,128)(2,1)} %bitcast.308, bf16[2,1280,384]{1,2,0:T(8,128)(2,1)} %get-tuple-element.246), kind=kOutput, calls=%fused_computation.261 | convolution fusion | flops 4026531840 | bytes 18743296 | tf_op jit(solution)/shard_map/end,enf->edf/dot_general | solution.py:1213
  690.5 10.7 %all-gather.8.cloned.1.call-done = bf16[256,2048]{1,0:T(8,128)(2,1)} async-done(((bf16[128,2048]{1,0:T(8,128)(2,1)}), bf16[256,2048]{1,0:T(8,128)(2,1)}) %all-gather.8.cloned.1.call-update) | async-done | bytes 1048592 | tf_op jit(solution)/shard_map/all_gather | solution.py:1243
  735.2 8.3 fusion.18
  743.5 12.7 %fusion.113 = f32[2,2048,384]{2,1,0:T(8,128)} fusion(bf16[2,1280,2048]{2,1,0:T(8,128)(2,1)} %bitcast.309, bf16[2,1280,384]{1,2,0:T(8,128)(2,1)S(1)} %copy-done.19), kind=kOutput, calls=%fused_computation.260 | convolution fusion | flops 4026531840 | bytes 18743296 | tf_op jit(solution)/shard_map/end,enf->edf/dot_general | solution.py:1212
  756.3 81.5 %shard_map.274 = bf16[128,2048]{1,0:T(8,128)(2,1)} custom-call(bf16[32,128,2048]{2,1,0:T(8,128)(2,1)} %bitcast.286), custom_call_target="tpu_custom_call" | custom-call | tf_op jit(solution)/shard_map/pallas_call | solution.py:626
  868.0 16.4 %pad_maximum_fusion = bf16[2048,4608]{1,0:T(8,128)(2,1)} fusion(bf16[2048,2048]{1,0:T(8,128)(2,1)} %convolution_convert_fusion.3, bf16[2048,2560]{1,0:T(8,128)(2,1)} %convolution_convert_fusion.2), kind=kLoop, calls=%fused_computation.4 | loop fusion | flops 37748736 | bytes 37748736 | tf_op jit(solution)/shard_map/concatenate | solution.py:1301
  884.4 124.8 %shard_map.276 = bf16[128,4608]{1,0:T(8,128)(2,1)} custom-call(bf16[16,128,4608]{2,1,0:T(8,128)(2,1)} %bitcast.288), custom_call_target="tpu_custom_call" | custom-call | tf_op jit(solution)/shard_map/pallas_call | solution.py:997
  1022.1 15.8 %all-reduce.4.cloned.1.call-done = f32[128,128]{0,1:T(8,128)} async-done(((f32[128,128]{0,1:T(8,128)}), f32[128,128]{0,1:T(8,128)}) %all-reduce.4.cloned.1.call-update) | async-done | bytes 65552 | tf_op jit(solution)/shard_map/psum | solution.py:1300
  (347 shorter events, 190.1 us)
Async XLA Ops:
  8.0 441.1 %copy-start = (bf16[2,384,2048]{2,1,0:T(8,128)(2,1)S(1)}, bf16[2,384,2048]{2,1,0:T(8,128)(2,1)}, u32[]{:S(2)}) copy-start(bf16[2,384,2048]{2,1,0:T(8,128)(2,1)} %param.43) | copy-start | bytes 9437188
  8.0 150.8 %all-gather.4.cloned.1.call-start = ((), (), s32[]{:S(2)}) async-start(), calls=%async_computation.3 | async-start | bytes 1572864 | tf_op jit(solution)/shard_map/all_gather | solution.py:1081
  8.8 234.9 %reduce-scatter.4.cloned.1.call-start = ((), (), s32[]{:S(2)}) async-start(), calls=%async_computation.4 | async-start | bytes 1572864 | tf_op jit(solution)/shard_map/reduce_scatter | solution.py:1122
  158.0 23.7 %copy-start.32 = (f32[256,64]{1,0:T(8,128)}, f32[256,64]{1,0:T(8,128)S(1)}, u32[]{:S(2)}) copy-start(f32[256,64]{1,0:T(8,128)S(1)} %get-tuple-element.288) | copy-start | bytes 196612
  158.8 86.3 %copy-start.52 = (f32[2048,1]{0,1:T(1,128)}, f32[2048,1]{0,1:T(1,128)S(1)}, u32[]{:S(2)}) copy-start(f32[2048,1]{0,1:T(1,128)S(1)} %get-tuple-element.272) | copy-start | bytes 24580
  160.4 80.5 %copy-start.63 = (f32[256]{0:T(256)}, f32[256]{0:T(256)S(1)}, u32[]{:S(2)}) copy-start(f32[256]{0:T(256)S(1)} %add_rsqrt_fusion.2) | copy-start | bytes 3076
  168.6 12.6 %copy-start.34 = (f32[32,2,8,128]{3,2,1,0:T(8,128)}, f32[32,2,8,128]{3,2,1,0:T(8,128)S(1)}, u32[]{:S(2)}) copy-start(f32[32,2,8,128]{3,2,1,0:T(8,128)S(1)} %get-tuple-element.255) | copy-start | bytes 786436
  177.7 57.2 %copy-start.60 = (f32[256,2]{0,1:T(2,128)}, f32[256,2]{0,1:T(2,128)S(1)}, u32[]{:S(2)}) copy-start(f32[256,2]{0,1:T(2,128)S(1)} %add_rsqrt_fusion.1) | copy-start | bytes 6148
  195.9 28.4 %copy-start.76 = (s32[16]{0:T(128)S(1)}, s32[16]{0:T(128)}, u32[]{:S(2)}) copy-start(s32[16]{0:T(128)} %gather_fusion) | copy-start | bytes 196
  202.7 223.6 %all-gather.6.cloned.1.call-start = ((), (), s32[]{:S(2)}) async-start(), calls=%async_computation.5 | async-start | bytes 17301504 | tf_op jit(solution)/shard_map/all_gather | solution.py:1079
  203.3 497.9 %all-gather.8.cloned.1.call-start = ((), (), s32[]{:S(2)}) async-start(), calls=%async_computation.6 | async-start | bytes 1572864 | tf_op jit(solution)/shard_map/all_gather | solution.py:1243
  245.1 119.7 %copy-start.65 = (f32[128]{0:T(128)}, f32[128]{0:T(128)S(1)}, u32[]{:S(2)}) copy-start(f32[128]{0:T(128)S(1)} %add_rsqrt_fusion.3) | copy-start | bytes 1540
  465.4 11.7 %copy-start.17 = (bf16[2,1280,384]{1,2,0:T(8,128)(2,1)S(1)}, bf16[2,1280,384]{1,2,0:T(8,128)(2,1)}, u32[]{:S(2)}) copy-start(bf16[2,1280,384]{1,2,0:T(8,128)(2,1)} %get-tuple-element.243) | copy-start | bytes 5898244
  488.2 14.0 %copy-start.18 = (bf16[2,1280,384]{1,2,0:T(8,128)(2,1)}, bf16[2,1280,384]{1,2,0:T(8,128)(2,1)S(1)}, u32[]{:S(2)}) copy-start(bf16[2,1280,384]{1,2,0:T(8,128)(2,1)S(1)} %get-tuple-element.247) | copy-start | bytes 5898244
  516.1 10.2 copy-start.8
  661.3 13.1 %copy-start.6 = (bf16[128,2048]{1,0:T(8,128)(2,1)S(1)}, bf16[128,2048]{1,0:T(8,128)(2,1)}, u32[]{:S(2)}) copy-start(bf16[128,2048]{1,0:T(8,128)(2,1)} %param.35) | copy-start | bytes 1572868
  661.3 13.1 %copy-start.9 = (bf16[128,2048]{1,0:T(8,128)(2,1)S(1)}, bf16[128,2048]{1,0:T(8,128)(2,1)}, u32[]{:S(2)}) copy-start(bf16[128,2048]{1,0:T(8,128)(2,1)} %reduce-scatter.4.cloned.1.call-done) | copy-start | bytes 1572868
  661.3 13.1 %copy-start.53 = (f32[2048,1]{0,1:T(1,128)S(1)}, f32[2048,1]{0,1:T(1,128)}, u32[]{:S(2)}) copy-start(f32[2048,1]{0,1:T(1,128)} %copy-done.52) | copy-start | bytes 24580
  661.3 13.1 %copy-start.66 = (f32[128]{0:T(128)S(1)}, f32[128]{0:T(128)}, u32[]{:S(2)}) copy-start(f32[128]{0:T(128)} %copy-done.65) | copy-start | bytes 1540
  677.0 13.4 %copy-start.11 = (f32[128,2048]{1,0:T(8,128)}, f32[128,2048]{1,0:T(8,128)S(1)}, u32[]{:S(2)}) copy-start(f32[128,2048]{1,0:T(8,128)S(1)} %get-tuple-element.302) | copy-start | bytes 3145732
  677.0 13.4 %copy-start.74 = (f32[128]{0:T(128)}, f32[128]{0:T(128)S(1)}, u32[]{:S(2)}) copy-start(f32[128]{0:T(128)S(1)} %broadcast_multiply_fusion.3) | copy-start | bytes 1540
  678.3 174.1 %reduce-scatter.6.cloned.1.call-start = ((), (), s32[]{:S(2)}) async-start(), calls=%async_computation.7 | async-start | bytes 1572864 | tf_op jit(solution)/shard_map/reduce_scatter | solution.py:1282
  690.5 17.2 %copy-start.46 = (bf16[256,2,128]{2,1,0:T(2,128)(2,1)S(1)}, bf16[256,2,128]{2,1,0:T(2,128)(2,1)}, u32[]{:S(2)}) copy-start(bf16[256,2,128]{2,1,0:T(2,128)(2,1)} %reshape.728) | copy-start | bytes 393220
  690.5 17.2 %copy-start.58 = (f32[2,8,256]{2,1,0:T(8,128)S(1)}, f32[2,8,256]{2,1,0:T(8,128)}, u32[]{:S(2)}) copy-start(f32[2,8,256]{2,1,0:T(8,128)} %copy-done.57) | copy-start | bytes 49156
  735.1 8.3 copy-start.22
  735.2 8.3 copy-start.19
  743.4 274.8 %reduce-scatter.8.cloned.1.call-start = ((), (), s32[]{:S(2)}) async-start(), calls=%async_computation.8 | async-start | bytes 1114112 | tf_op jit(solution)/shard_map/reduce_scatter | solution.py:1299
  756.3 81.5 %copy-start.20 = (bf16[128,2048]{1,0:T(8,128)(2,1)S(1)}, bf16[128,2048]{1,0:T(8,128)(2,1)}, u32[]{:S(2)}) copy-start(bf16[128,2048]{1,0:T(8,128)(2,1)} %multiply_convert_fusion.5.src) | copy-start | bytes 1572868
  756.3 81.5 %copy-start.72 = (f32[128]{0:T(128)S(1)}, f32[128]{0:T(128)}, u32[]{:S(2)}) copy-start(f32[128]{0:T(128)} %copy-done.71) | copy-start | bytes 1540
  846.1 8.3 copy-start.62
  868.0 170.0 %all-reduce.4.cloned.1.call-start = ((), (), s32[]{:S(2)}) async-start(), calls=%async_computation.9 | async-start | bytes 131072 | tf_op jit(solution)/shard_map/psum | solution.py:1300
  1013.9 27.9 %copy-start.1 = (bf16[2,384,2048]{2,1,0:T(8,128)(2,1)S(1)}, bf16[2,384,2048]{2,1,0:T(8,128)(2,1)}, u32[]{:S(2)}) copy-start(bf16[2,384,2048]{2,1,0:T(8,128)(2,1)} %param.43) | copy-start | bytes 9437188
  (54 other events, 199.0 us)
Sparse Core Ops, SparseCore 0:
  10.4 23.9 all-gather.3
  202.8 18.6 reduce-scatter.3
  678.4 22.7 all-gather.7
  743.6 22.0 reduce-scatter.5
  868.1 63.7 reduce-scatter.7
  1018.3 19.5 all-reduce.3
Sparse Core Ops, SparseCore 1:
  206.6 157.2 all-gather.5

commit v3 on v2

--- a/solution.py
+++ b/solution.py
@@ -1016,6 +1016,264 @@
     )(value.reshape(devices, rows, width))
 
 
+WINDOW_ALIGN = 16
+EXPERT_VMEM = 60 * 1024 * 1024
+
+
+def dot(left, right, dims=((1,), (0,))):
+    return lax.dot_general(left, right, (dims, ((), ())), preferred_element_type=jnp.float32)
+
+
+def expert_kernel(
+    info, pos, rows_in, cots_in, gate_w, up_w, down_w,
+    out, back, gate_g, up_g, down_g,
+    x, dy, wgu, wd, slot_out, slot_row, gu, hg, rows_b, cots_b, g_stage, d_stage,
+    load_s, w_s, out_s, g_s, d_s,
+):
+    bf16, f32 = jnp.bfloat16, jnp.float32
+    blocks, block_rows, wide = rows_in.shape
+    features = cots_in.shape[2]
+    experts, padded = x.shape[0], x.shape[1]
+    part = hg.shape[2]
+    cap = hg.shape[1]
+    window = padded - cap
+    tile = 256
+    chunk = 512
+
+    def load(b):
+        slot = b % 2
+        return (
+            pltpu.make_async_copy(rows_in.at[b], rows_b.at[slot], load_s.at[slot, 0]),
+            pltpu.make_async_copy(cots_in.at[b], cots_b.at[slot], load_s.at[slot, 1]),
+        )
+
+    for copy in load(0):
+        copy.start()
+    weights = []
+    for e in range(experts):
+        weights.append(pltpu.make_async_copy(gate_w.at[e], wgu.at[e, :, pl.ds(0, part)], w_s.at[e, 0]))
+        weights.append(pltpu.make_async_copy(up_w.at[e], wgu.at[e, :, pl.ds(part, part)], w_s.at[e, 1]))
+        weights.append(pltpu.make_async_copy(down_w.at[e], wd.at[e], w_s.at[e, 2]))
+    for copy in weights:
+        copy.start()
+
+    def clear(i, carry):
+        at = pl.ds(pl.multiple_of(i * 16, 16), 16)
+        for e in range(experts):
+            x[e, at, :] = jnp.zeros((16, wide), bf16)
+            dy[e, at, :] = jnp.zeros((16, features), bf16)
+        return carry
+
+    lax.fori_loop(0, padded // 16, clear, 0)
+    for e in range(experts):
+        slot_out[e, pl.ds(cap, window), :] = jnp.zeros((window, features), bf16)
+        slot_row[e, pl.ds(cap, window), :] = jnp.zeros((window, wide), bf16)
+
+    def starts(b):
+        return [pl.multiple_of(info[1 + b * experts + e], WINDOW_ALIGN) for e in range(experts)]
+
+    def picks(b, begin):
+        slots = lax.broadcasted_iota(jnp.int32, (window, block_rows), 0)
+        return jnp.concatenate(
+            [(slots + begin[e] == pos[b, pl.ds(e, 1), :]).astype(f32) for e in range(experts)],
+            axis=0,
+        )
+
+    def take(b, carry):
+        slot = b % 2
+
+        @pl.when(b + 1 < blocks)
+        def _():
+            for copy in load(b + 1):
+                copy.start()
+
+        begin = starts(b)
+        picked = picks(b, begin).astype(bf16)
+        for copy in load(b):
+            copy.wait()
+        for source, target, width in ((rows_b, x, wide), (cots_b, dy, features)):
+            for first in range(0, width, chunk):
+                cols = pl.ds(first, min(chunk, width - first))
+                got = dot(picked, source[slot, :, cols]).astype(bf16)
+                for e in range(experts):
+                    at = pl.ds(begin[e], window)
+                    target[e, at, cols] += got[e * window : (e + 1) * window]
+        return carry
+
+    lax.fori_loop(0, blocks, take, 0)
+    for copy in weights:
+        copy.wait()
+
+    lanes = lax.broadcasted_iota(jnp.int32, (tile, AUX), 1)
+
+    def mlp(step, carry):
+        e = step // (cap // tile)
+        at = pl.ds(pl.multiple_of((step % (cap // tile)) * tile, tile), tile)
+        own = info[0] * experts + e
+        total = blocks * experts
+        aux = x[e, at, pl.ds(features, AUX)].astype(f32)
+        gate = jnp.sum(
+            jnp.where((lanes == own) | (lanes == own + total), aux, 0.0), axis=1, keepdims=True
+        )
+        pre = dot(x[e, at, pl.ds(0, features)], wgu[e])
+        gate_pre, up_pre = pre[:, :part], pre[:, part:]
+        sig = 1.0 / (1.0 + jnp.exp(-gate_pre))
+        act = gate_pre * sig
+        hidden = (act * up_pre).astype(bf16).astype(f32)
+        gated = (hidden * gate).astype(bf16)
+        hg[e, at, :] = gated
+        down_cot = dot(dy[e, at, :], wd[e], ((1,), (1,)))
+        slot_cot = jnp.sum(hidden * down_cot, axis=1, keepdims=True)
+        hidden_cot = down_cot * gate
+        gu[e, at, pl.ds(0, part)] = (
+            hidden_cot * up_pre * sig * (1.0 + gate_pre * (1.0 - sig))
+        ).astype(bf16)
+        gu[e, at, pl.ds(part, part)] = (hidden_cot * act).astype(bf16)
+        for first in range(0, features, chunk):
+            cols = pl.ds(first, chunk)
+            slot_out[e, at, cols] = dot(gated, wd[e, :, cols]).astype(bf16)
+            slot_row[e, at, cols] = dot(
+                gu[e, at, :], wgu[e, pl.ds(first, chunk), :], ((1,), (1,))
+            ).astype(bf16)
+        high = slot_cot.astype(bf16).astype(f32)
+        place = info[1 + blocks * experts] * 2 * total + own * 2
+        slot_row[e, at, pl.ds(features, AUX)] = jnp.where(
+            lanes == place, high, jnp.where(lanes == place + 1, slot_cot - high, 0.0)
+        ).astype(bf16)
+        return carry
+
+    lax.fori_loop(0, experts * (cap // tile), mlp, 0)
+
+    def stored(b):
+        slot = b % 2
+        return (
+            pltpu.make_async_copy(cots_b.at[slot], out.at[b], out_s.at[slot, 0]),
+            pltpu.make_async_copy(rows_b.at[slot], back.at[b], out_s.at[slot, 1]),
+        )
+
+    def put(b, carry):
+        slot = b % 2
+
+        @pl.when(b >= 2)
+        def _():
+            for copy in stored(b - 2):
+                copy.wait()
+
+        begin = starts(b)
+        spread = picks(b, begin).T.astype(bf16)
+        for source, target, width in ((slot_out, cots_b, features), (slot_row, rows_b, wide)):
+            for first in range(0, width, chunk):
+                cols = pl.ds(first, min(chunk, width - first))
+                held = jnp.concatenate(
+                    [source[e, pl.ds(begin[e], window), cols] for e in range(experts)], axis=0
+                )
+                target[slot, :, cols] = dot(spread, held).astype(bf16)
+        for copy in stored(b):
+            copy.start()
+        return carry
+
+    lax.fori_loop(0, blocks, put, 0)
+
+    tiles = features // tile
+
+    def g_copies(step):
+        slot = step % 2
+        e, at = step // tiles, pl.ds(pl.multiple_of((step % tiles) * tile, tile), tile)
+        return (
+            pltpu.make_async_copy(g_stage.at[slot, :, pl.ds(0, part)], gate_g.at[e, at], g_s.at[slot, 0]),
+            pltpu.make_async_copy(g_stage.at[slot, :, pl.ds(part, part)], up_g.at[e, at], g_s.at[slot, 1]),
+        )
+
+    def wide_grad(step, carry):
+        slot = step % 2
+        e, at = step // tiles, pl.ds(pl.multiple_of((step % tiles) * tile, tile), tile)
+
+        @pl.when(step >= 2)
+        def _():
+            for copy in g_copies(step - 2):
+                copy.wait()
+
+        g_stage[slot] = dot(x[e, pl.ds(0, cap), at], gu[e], ((0,), (0,)))
+        for copy in g_copies(step):
+            copy.start()
+        return carry
+
+    lax.fori_loop(0, experts * tiles, wide_grad, 0)
+    parts = features // chunk
+
+    def d_copy(step):
+        slot = step % 2
+        e, at = step // parts, pl.ds(pl.multiple_of((step % parts) * chunk, chunk), chunk)
+        return pltpu.make_async_copy(d_stage.at[slot], down_g.at[e, :, at], d_s.at[slot])
+
+    def down_grad(step, carry):
+        slot = step % 2
+        e, at = step // parts, pl.ds(pl.multiple_of((step % parts) * chunk, chunk), chunk)
+
+        @pl.when(step >= 2)
+        def _():
+            d_copy(step - 2).wait()
+
+        d_stage[slot] = dot(hg[e], dy[e, pl.ds(0, cap), at], ((0,), (0,)))
+        d_copy(step).start()
+        return carry
+
+    lax.fori_loop(0, experts * parts, down_grad, 0)
+    for last in (2, 1):
+        for copy in stored(blocks - last):
+            copy.wait()
+        for copy in g_copies(experts * tiles - last):
+            copy.wait()
+        d_copy(experts * parts - last).wait()
+
+
+def expert_layer(info, pos, rows_in, cots_in, gate_w, up_w, down_w, capacity, most):
+    bf16, f32 = jnp.bfloat16, jnp.float32
+    blocks, block_rows, wide = rows_in.shape
+    features = cots_in.shape[2]
+    experts, part = gate_w.shape[0], gate_w.shape[2]
+    padded = capacity + -(-most // WINDOW_ALIGN) * WINDOW_ALIGN + WINDOW_ALIGN
+    dma = pltpu.SemaphoreType.DMA
+    shape = jax.ShapeDtypeStruct
+    anywhere = pl.BlockSpec(memory_space=pl.ANY)
+    return pl.pallas_call(
+        expert_kernel,
+        out_shape=(
+            shape((blocks, block_rows, features), bf16),
+            shape((blocks, block_rows, wide), bf16),
+            shape(gate_w.shape, f32),
+            shape(up_w.shape, f32),
+            shape(down_w.shape, f32),
+        ),
+        in_specs=[
+            pl.BlockSpec(memory_space=pltpu.SMEM),
+            pl.BlockSpec(memory_space=pltpu.VMEM),
+        ]
+        + [anywhere] * 5,
+        out_specs=(anywhere,) * 5,
+        scratch_shapes=[
+            pltpu.VMEM((experts, padded, wide), bf16),
+            pltpu.VMEM((experts, padded, features), bf16),
+            pltpu.VMEM((experts, features, 2 * part), bf16),
+            pltpu.VMEM((experts, part, features), bf16),
+            pltpu.VMEM((experts, padded, features), bf16),
+            pltpu.VMEM((experts, padded, wide), bf16),
+            pltpu.VMEM((experts, capacity, 2 * part), bf16),
+            pltpu.VMEM((experts, capacity, part), bf16),
+            pltpu.VMEM((2, block_rows, wide), bf16),
+            pltpu.VMEM((2, block_rows, features), bf16),
+            pltpu.VMEM((2, 256, 2 * part), f32),
+            pltpu.VMEM((2, part, 512), f32),
+            dma((2, 2)),
+            dma((experts, 3)),
+            dma((2, 2)),
+            dma((2, 2)),
+            dma((2,)),
+        ],
+        compiler_params=pltpu.CompilerParams(vmem_limit_bytes=EXPERT_VMEM),
+    )(info, pos, rows_in, cots_in, gate_w, up_w, down_w)
+
+
 def split_high_low(value):
     high = value.astype(jnp.bfloat16)
     return high, (value - high.astype(jnp.float32)).astype(jnp.bfloat16)
@@ -1077,7 +1335,7 @@
     key_factor = head_gains[:, :, 3].reshape(-1)
 
     cot_all = lax.all_gather(output_cotangent, ("dp", "tensor"), axis=0, tiled=True)
-    routes_all = lax.all_gather(routes, "dp", axis=0, tiled=True)
+    routes_all = lax.all_gather(routes.T, "dp")
     input_rows = lax.all_gather(layer_input, "tensor", axis=0, tiled=True)
     position = jnp.arange(block_rows, dtype=jnp.int32)
     block_lengths = lengths[sequence_order]
@@ -1129,110 +1387,52 @@
     unit_second, scale_second = rms_normalize(residual)
     normed_second = (unit_second * gain_two).astype(bf16)
 
-    normed_all = gather_all(normed_second, 1)
-    logits = matrix_product(normed_all, router_all)
+    row_start = tensor_index * own_rows
+    routes_own = lax.dynamic_slice_in_dim(routes, row_start, own_rows, 0)
     expert_ids = jnp.arange(expert_count, dtype=jnp.int32)
-    chosen = jnp.zeros((tokens, expert_count), jnp.bool_)
-    for j in range(TOP):
-        chosen = chosen | (routes_all[:, j : j + 1] == expert_ids[None, :])
-    peak = jnp.max(jnp.where(chosen, logits, masked_score), axis=-1, keepdims=True)
-    spread = jnp.where(chosen, jnp.exp(jnp.minimum(logits - peak, 0.0)), 0.0)
+    chosen = jnp.any(routes_own[:, :, None] == expert_ids[None, None, :], axis=1)
+    logits = jnp.where(chosen, matrix_product(normed_second, router_all), masked_score)
+    spread = jnp.exp(logits - jnp.max(logits, axis=-1, keepdims=True))
     gates = spread / jnp.sum(spread, axis=-1, keepdims=True)
+    high, low = split_high_low(gates)
+    sent = jnp.concatenate(
+        [normed_second, high, low, jnp.zeros((own_rows, AUX - 2 * expert_count), bf16)], axis=1
+    )
+    normed_all = gather_all(sent, 1).reshape(dp_count, block_rows, features + AUX)
+
+    expert_own = dp_index * EXP_DEV + jnp.arange(EXP_DEV, dtype=jnp.int32)
     live = position[None, :] < block_lengths[:, None]
-    hot = chosen.reshape(dp_count, block_rows, expert_count) & live[:, :, None]
-    hot_low = hot.astype(bf16)
-    below = (position[None, :] < position[:, None]).astype(bf16)
-    rank = jnp.einsum("ts,bse->bte", below, hot_low, preferred_element_type=f32)
-    counts = jnp.sum(hot.astype(f32), axis=1)
+    hot = jnp.any(routes_all[:, None, :, :] == expert_own[None, :, None, None], axis=2)
+    hot = hot & live[:, None, :]
+    before = (position[:, None] < position[None, :]).astype(bf16)
+    rank = jnp.einsum("bes,st->bet", hot.astype(bf16), before, preferred_element_type=f32)
+    rank = rank.astype(jnp.int32)
+    counts = rank[:, :, -1] + hot[:, :, -1]
     earlier = jnp.cumsum(counts, axis=0) - counts
-    kept = hot & (earlier[:, None, :] + rank < capacity)
-
-    first_expert = dp_index * EXP_DEV
-    rank_own = lax.dynamic_slice_in_dim(rank, first_expert, EXP_DEV, 2)
-    kept_own = lax.dynamic_slice_in_dim(kept, first_expert, EXP_DEV, 2)
-    gates_own = lax.dynamic_slice_in_dim(
-        gates.reshape(dp_count, block_rows, expert_count), first_expert, EXP_DEV, 2
-    )
-    slots = jnp.arange(most_rows, dtype=f32)
-    place = kept_own.transpose(0, 2, 1)[:, :, None, :] & (
-        rank_own.transpose(0, 2, 1)[:, :, None, :] == slots[None, None, :, None]
-    )
-    place_low = place.astype(bf16).reshape(dp_count, EXP_DEV * most_rows, block_rows)
-    slot_gate = jnp.sum(
-        jnp.where(place, gates_own.transpose(0, 2, 1)[:, :, None, :], 0.0), axis=-1
-    )
-    slot_gate = slot_gate.transpose(1, 0, 2).reshape(EXP_DEV, dp_count * most_rows, 1)
-
-    def take(rows):
-        taken = jnp.einsum(
-            "bst,btd->bsd",
-            place_low,
-            rows.reshape(dp_count, block_rows, features),
-            preferred_element_type=f32,
-        ).astype(bf16)
-        return (
-            taken.reshape(dp_count, EXP_DEV, most_rows, features)
-            .transpose(1, 0, 2, 3)
-            .reshape(EXP_DEV, dp_count * most_rows, features)
-        )
-
-    def put(slot_rows):
-        ordered = (
-            slot_rows.astype(bf16)
-            .reshape(EXP_DEV, dp_count, most_rows, features)
-            .transpose(1, 0, 2, 3)
-            .reshape(dp_count, EXP_DEV * most_rows, features)
-        )
-        return (
-            jnp.einsum("bst,bsd->btd", place_low, ordered, preferred_element_type=f32)
-            .astype(bf16)
-            .reshape(tokens, features)
-        )
-
-    rows_in = take(normed_all)
-    cot_in = take(cot_all)
-    gate_pre = jnp.einsum("end,edf->enf", rows_in, expert_gate, preferred_element_type=f32)
-    up_pre = jnp.einsum("end,edf->enf", rows_in, expert_up, preferred_element_type=f32)
-    sigmoid_gate = jax.nn.sigmoid(gate_pre)
-    gate_act = gate_pre * sigmoid_gate
-    hidden = (gate_act * up_pre).astype(bf16)
-    out_partial = jnp.einsum("enf,efd->end", hidden, expert_down, preferred_element_type=f32)
-    expert_sum = scatter_all(put(out_partial * slot_gate), 2)
+    slot = earlier[:, :, None] + rank
+    slot = jnp.where(hot & (slot < capacity), slot, -capacity)
+    begin = jnp.minimum(earlier, capacity) // WINDOW_ALIGN * WINDOW_ALIGN
+    info = jnp.concatenate([dp_index[None], begin.reshape(-1), tensor_index[None]])
+    out_part, back_part, gate_gradient, up_gradient, down_gradient = expert_layer(
+        info.astype(jnp.int32),
+        slot,
+        normed_all,
+        cot_all.reshape(dp_count, block_rows, features),
+        expert_gate,
+        expert_up,
+        expert_down,
+        capacity,
+        most_rows,
+    )
+    returned = scatter_all(back_part.reshape(tokens, features + AUX), 3).astype(f32)
+    expert_sum = scatter_all(out_part.reshape(tokens, features), 2)
     layer_output = (residual + expert_sum.astype(f32)).astype(bf16)
 
-    down_cot = jnp.einsum("end,efd->enf", cot_in, expert_down, preferred_element_type=f32)
-    slot_cot = jnp.sum(hidden.astype(f32) * down_cot, axis=-1)
-    hidden_cot = down_cot * slot_gate
-    gating_cot = (
-        hidden_cot * up_pre * sigmoid_gate * (1.0 + gate_pre * (1.0 - sigmoid_gate))
-    ).astype(bf16)
-    upward_cot = (hidden_cot * gate_act).astype(bf16)
-    hidden_gated = (hidden.astype(f32) * slot_gate).astype(bf16)
-    down_gradient = jnp.einsum("enf,end->efd", hidden_gated, cot_in, preferred_element_type=f32)
-    gate_gradient = jnp.einsum("end,enf->edf", rows_in, gating_cot, preferred_element_type=f32)
-    up_gradient = jnp.einsum("end,enf->edf", rows_in, upward_cot, preferred_element_type=f32)
-    row_partial = jnp.einsum("enf,edf->end", gating_cot, expert_gate, preferred_element_type=f32)
-    row_partial = row_partial + jnp.einsum(
-        "enf,edf->end", upward_cot, expert_up, preferred_element_type=f32
-    )
-    slot_cot = slot_cot.reshape(EXP_DEV, dp_count, most_rows).transpose(1, 0, 2)
-    token_cot = jnp.sum(jnp.where(place, slot_cot[:, :, :, None], 0.0), axis=2)
-    token_cot = token_cot.transpose(0, 2, 1).reshape(tokens, EXP_DEV)
-    high, low = split_high_low(token_cot)
-    quad = jnp.stack([high, low], axis=-1).reshape(tokens, 2 * EXP_DEV)
-    aux = lax.dynamic_update_slice(
-        jnp.zeros((tokens, 2 * tensor_count * expert_count), bf16),
-        quad,
-        (0, tensor_index * 2 * expert_count + dp_index * 2 * EXP_DEV),
-    )
-    returned = scatter_all(jnp.concatenate([put(row_partial), aux], axis=1), 3).astype(f32)
     gate_cot = jnp.sum(
         returned[:, features:].reshape(own_rows, tensor_count, expert_count, 2), axis=(1, 3)
     )
-    own_start = (dp_index * tensor_count + tensor_index) * own_rows
-    gates_mine = lax.dynamic_slice_in_dim(gates, own_start, own_rows, 0)
     logit_cot = (
-        gates_mine * (gate_cot - jnp.sum(gates_mine * gate_cot, axis=-1, keepdims=True))
+        gates * (gate_cot - jnp.sum(gates * gate_cot, axis=-1, keepdims=True))
     ).astype(bf16)
     router_part = contract(normed_second, logit_cot)
     normed_cot = returned[:, :features] + transposed(logit_cot, router_all)
@@ -1282,7 +1482,6 @@
     first_cot = lax.psum_scatter(
         transposed(raw_cot, qkv_all).astype(bf16), "tensor", scatter_dimension=0, tiled=True
     ).astype(f32)
-    row_start = tensor_index * own_rows
     unit_own = lax.dynamic_slice_in_dim(unit_first, row_start, own_rows, 0)
     scale_own = lax.dynamic_slice_in_dim(scale_first, row_start, own_rows, 0)
     prenorm_part = jnp.sum(first_cot * unit_own, axis=0)

time: 1060 us -> 913 us (0.86)
  matrix products: 224 us -> 57.5 us
  Pallas kernels: 525 us -> 614 us
  local copies, waits for them, and re-layouts: 133 us -> 77.4 us
  other arithmetic: 102 us -> 76.6 us
  waiting for transfers between devices: 27.8 us -> 38.6 us
    dot_general x14 -> x1, matrix products: 158 us -> 0.15 us  [gathered_body(): jnp.einsum('bes,st->bet', hot.astype(bf16), before, preferred_element_typ...]
    pallas_call x0 -> x1, Pallas kernels: none -> 73.1 us  [expert_layer(): pl.pallas_call(expert_kernel, out_shape=(shape((blocks, block_rows, featu...]
    transpose x8 -> x0, local copies, waits for them, and re-layouts: 30.4 us -> none  [the longest x2 20.3 us: put(): ordered = slot_rows.astype(bf16).reshape(EXP_DEV, dp_count, most_rows, fe...]
    concatenate x1, other arithmetic: 14.2 us -> 0.59 us  [gathered_body(): jnp.concatenate([dp_index[None], begin.reshape(-1), tensor_index[None]])]
    reshape x4 -> x0, local copies, waits for them, and re-layouts: 11.6 us -> none  [the longest x1 10 us: take(): taken.reshape(dp_count, EXP_DEV, most_rows, features).transpose(1, 0, 2, 3)]
    dot_general x3, matrix products: 24.5 us -> 13.8 us  [matrix_product(): return jnp.dot(former, latter, preferred_element_type=jnp.float32)]
    unnamed x173 -> x151, local copies, waits for them, and re-layouts: 23.6 us -> 24.4 us
  transfers between devices with their start and end apart: 7 -> 7, of which waited for: 2 -> 3; matrix products, arithmetic and copies ran while one was open for 18% -> 10% of each run, Pallas kernels for 42% -> 51%
where the time goes in v3:
time: 913 us; the launch traced here: 901 us
  Pallas kernels  614 us (67%)
  local copies, waits for them, and re-layouts  77.4 us (8%)
  other arithmetic  76.6 us (8%)
  matrix products  57.5 us (6%)
  waiting for transfers between devices  38.6 us (4%)
  blocking collectives  19.1 us (2%)
  between operations  17.1 us (2%)
    pallas_call x2, Pallas kernels, scatter_all(): pl.pallas_call(scatter_kernel, out_shape=jax.ShapeDtypeStruct((rows, widt...  176 us
    pallas_call x1, Pallas kernels, gather_all(): pl.pallas_call(gather_kernel, out_shape=jax.ShapeDtypeStruct((devices, ro...  126 us
    pallas_call x1, Pallas kernels, scatter_dp(): pl.pallas_call(plane_scatter_kernel, out_shape=jax.ShapeDtypeStruct((rows...  123 us
    pallas_call x1, Pallas kernels, gather_dp(): pl.pallas_call(plane_gather_kernel, out_shape=jax.ShapeDtypeStruct((devic...  115 us
    pallas_call x1, Pallas kernels, expert_layer(): pl.pallas_call(expert_kernel, out_shape=(shape((blocks, block_rows, featu...  73.1 us
    unnamed x151, local copies, waits for them, and re-layouts  24.4 us
    all_gather x1, blocking collectives, gathered_body(): routes_all = lax.all_gather(routes.T, 'dp')  19.1 us
  transfers between devices with their start and end apart: 7, of which 3 were waited for; matrix products, arithmetic and copies ran while one was open for 10% of the time, Pallas kernels for 51%

profile of v3, /device:TPU:0, one launch (start us, length us, event | category | flops | bytes accessed | tf_op | source)
XLA Modules:
  0.0 901.3 jit_solution(5496973577275009677)
XLA Ops:
  25.9 2.5 concatenate.62.src
  28.4 115.2 %shard_map.272 = bf16[16,128,4736]{2,1,0:T(8,128)(2,1)} custom-call(bf16[128,4736]{1,0:T(8,128)(2,1)} %concatenate.62.src), custom_call_target="tpu_custom_call" | custom-call | tf_op jit(solution)/shard_map/pallas_call | solution.py:882
  151.6 6.0 fusion.3
  175.0 5.9 fusion.89
  180.8 2.6 fusion.77
  186.5 6.8 fusion.16
  194.7 19.1 %all-gather = s32[128,256]{1,0:T(8,128)S(1)} all-gather(s32[8,256]{1,0:T(8,128)S(1)} %bitcast.263), channel_id=2, replica_groups=mesh['dp'=16,'tensor'=2] {'dp'}, dimensions={0}, use_global_device_ids=true | all-gather | bytes 139264 | tf_op jit(solution)/shard_map/all_gather | solution.py:1338
  224.6 126.4 %shard_map.273 = bf16[32,128,2176]{2,1,0:T(8,128)(2,1)} custom-call(bf16[128,2176]{1,0:T(8,128)(2,1)} %concatenate.68.src), custom_call_target="tpu_custom_call" | custom-call | tf_op jit(solution)/shard_map/pallas_call | solution.py:777
  351.0 8.7 all-gather.7.cloned.1.call-done
  359.7 73.1 %shard_map.274 = (bf16[16,256,2048]{2,1,0:T(8,128)(2,1)}, bf16[16,256,2176]{2,1,0:T(8,128)(2,1)}, f32[2,2048,384]{2,1,0:T(8,128)}, f32[2,2048,384]{2,1,0:T(8,128)}, f32[2,384,2048]{2,1,0:T(8,128)}) custom-call(s32[34]{0:T(128)} %pad_add_fusion.2.info, s32[16,2,256]{2,1,0:T(2,128)} %and_select_fusion.pos, bf16[16,256,2176]{2,1,0:T(8,128)(2,1)} %bitcast.217, ...), custom_call_target="tpu_custom_call" | custom-call | tf_op jit(solution)/shard_map/pallas_call | solution.py:1239
  432.9 84.6 %shard_map.276 = bf16[128,2176]{1,0:T(8,128)(2,1)} custom-call(bf16[32,128,2176]{2,1,0:T(8,128)(2,1)} %bitcast.227), custom_call_target="tpu_custom_call" | custom-call | tf_op jit(solution)/shard_map/pallas_call | solution.py:626
  518.9 2.1 convert_element_type.171
  527.3 2.7 multiply_reduce_fusion.2
  539.1 4.6 copy.276
  544.9 10.9 %all-gather.9.cloned.1.call-done = bf16[256,2048]{1,0:T(8,128)(2,1)} async-done(((bf16[128,2048]{1,0:T(8,128)(2,1)}), bf16[256,2048]{1,0:T(8,128)(2,1)}) %all-gather.9.cloned.1.call-update) | async-done | bytes 1048592 | tf_op jit(solution)/shard_map/all_gather | solution.py:1443
  555.7 6.2 fusion.30
  569.4 3.7 copy.302
  573.2 3.7 copy.303
  576.9 2.7 multiply_subtract_fusion
  579.6 3.0 multiply_reduce_fusion
  585.2 2.5 fusion.37
  590.7 3.7 fusion.26
  595.4 8.0 fusion.13
  605.6 91.4 %shard_map.275 = bf16[128,2048]{1,0:T(8,128)(2,1)} custom-call(bf16[32,128,2048]{2,1,0:T(8,128)(2,1)} %bitcast.229), custom_call_target="tpu_custom_call" | custom-call | tf_op jit(solution)/shard_map/pallas_call | solution.py:626
  697.2 7.4 convolution_convert_fusion.1
  704.6 6.4 convolution_convert_fusion
  712.7 2.0 dynamic-slice_select_fusion.1
  720.9 16.4 %pad_maximum_fusion = bf16[2048,4608]{1,0:T(8,128)(2,1)} fusion(bf16[2048,2048]{1,0:T(8,128)(2,1)} %convolution_convert_fusion.1, bf16[2048,2560]{1,0:T(8,128)(2,1)} %convolution_convert_fusion), kind=kLoop, calls=%fused_computation.2 | loop fusion | flops 37748736 | bytes 37748736 | tf_op jit(solution)/shard_map/concatenate | solution.py:1500
  737.3 123.4 %shard_map.277 = bf16[128,4608]{1,0:T(8,128)(2,1)} custom-call(bf16[16,128,4608]{2,1,0:T(8,128)(2,1)} %bitcast.216), custom_call_target="tpu_custom_call" | custom-call | tf_op jit(solution)/shard_map/pallas_call | solution.py:997
  864.6 2.5 copy.279
  867.9 3.4 fusion.41
  871.2 18.3 %all-reduce.4.cloned.1.call-done = f32[128,128]{0,1:T(8,128)} async-done(((f32[128,128]{0,1:T(8,128)}), f32[128,128]{0,1:T(8,128)}) %all-reduce.4.cloned.1.call-update) | async-done | bytes 65552 | tf_op jit(solution)/shard_map/psum | solution.py:1499
  (298 shorter events, 108.5 us)
Async XLA Ops:
  8.0 137.5 %copy-start = (s32[16]{0:T(128)S(1)}, s32[16]{0:T(128)}, u32[]{:S(2)}) copy-start(s32[16]{0:T(128)} %param.49) | copy-start | bytes 196
  8.0 17.8 %copy-start.34 = (bf16[128,2048]{1,0:T(8,128)(2,1)S(1)}, bf16[128,2048]{1,0:T(8,128)(2,1)}, u32[]{:S(2)}) copy-start(bf16[128,2048]{1,0:T(8,128)(2,1)} %param.36) | copy-start | bytes 1572868
  8.0 142.0 %all-gather.5.cloned.1.call-start = ((), (), s32[]{:S(2)}) async-start(), calls=%async_computation.3 | async-start | bytes 1572864 | tf_op jit(solution)/shard_map/all_gather | solution.py:1339
  8.8 208.0 %reduce-scatter.4.cloned.1.call-start = ((), (), s32[]{:S(2)}) async-start(), calls=%async_computation.4 | async-start | bytes 1572864 | tf_op jit(solution)/shard_map/reduce_scatter | solution.py:1380
  146.2 11.5 %copy-start.64 = (s32[16]{0:T(128)}, s32[16]{0:T(128)S(1)}, u32[]{:S(2)}) copy-start(s32[16]{0:T(128)S(1)} %gather_fusion) | copy-start | bytes 196
  147.5 13.5 %copy-start.57 = (f32[128]{0:T(128)}, f32[128]{0:T(128)S(1)}, u32[]{:S(2)}) copy-start(f32[128]{0:T(128)S(1)} %mul.594) | copy-start | bytes 1540
  150.0 11.8 %copy-start.31 = (f32[256,64]{1,0:T(8,128)}, f32[256,64]{1,0:T(8,128)S(1)}, u32[]{:S(2)}) copy-start(f32[256,64]{1,0:T(8,128)S(1)} %get-tuple-element.261) | copy-start | bytes 196612
  151.6 6.0 copy-start.47
  162.9 12.0 %copy-start.19 = (bf16[256,16,64]{2,0,1:T(8,128)(2,1)}, bf16[256,16,64]{2,0,1:T(8,128)(2,1)S(1)}, u32[]{:S(2)}) copy-start(bf16[256,16,64]{2,0,1:T(8,128)(2,1)S(1)} %copy.246) | copy-start | bytes 1572868
  186.5 7.4 copy-start.46
  186.5 27.4 %copy-start.65 = (s32[16]{0:T(128)S(1)}, s32[16]{0:T(128)}, u32[]{:S(2)}) copy-start(s32[16]{0:T(128)} %copy-done.64) | copy-start | bytes 196
  193.2 23.5 %copy-start.3 = (bf16[128,2048]{1,0:T(8,128)(2,1)S(1)}, bf16[128,2048]{1,0:T(8,128)(2,1)}, u32[]{:S(2)}) copy-start(bf16[128,2048]{1,0:T(8,128)(2,1)} %param.35) | copy-start | bytes 1572868
  193.3 166.5 %all-gather.7.cloned.1.call-start = ((), (), s32[]{:S(2)}) async-start(), calls=%async_computation.5 | async-start | bytes 17301504 | tf_op jit(solution)/shard_map/all_gather | solution.py:1337
  193.8 361.9 %all-gather.9.cloned.1.call-start = ((), (), s32[]{:S(2)}) async-start(), calls=%async_computation.6 | async-start | bytes 1572864 | tf_op jit(solution)/shard_map/all_gather | solution.py:1443
  219.4 131.7 %copy-start.13 = (bf16[128,2048]{1,0:T(8,128)(2,1)}, bf16[128,2048]{1,0:T(8,128)(2,1)S(1)}, u32[]{:S(2)}) copy-start(bf16[128,2048]{1,0:T(8,128)(2,1)S(1)} %multiply_convert_fusion.1) | copy-start | bytes 1572868
  517.4 9.8 %copy-start.5 = (bf16[128,2048]{1,0:T(8,128)(2,1)S(1)}, bf16[128,2048]{1,0:T(8,128)(2,1)}, u32[]{:S(2)}) copy-start(bf16[128,2048]{1,0:T(8,128)(2,1)} %reduce-scatter.4.cloned.1.call-done) | copy-start | bytes 1572868
  525.5 5.5 copy-start.15
  525.5 5.5 copy-start.55
  532.3 178.7 %reduce-scatter.6.cloned.1.call-start = ((), (), s32[]{:S(2)}) async-start(), calls=%async_computation.7 | async-start | bytes 1572864 | tf_op jit(solution)/shard_map/reduce_scatter | solution.py:1482
  555.7 6.5 copy-start.4
  584.4 4.4 copy-start.38
  590.7 4.4 copy-start.66
  595.4 8.1 copy-start.7
  595.4 8.1 copy-start.48
  603.5 264.3 %reduce-scatter.8.cloned.1.call-start = ((), (), s32[]{:S(2)}) async-start(), calls=%async_computation.8 | async-start | bytes 1114112 | tf_op jit(solution)/shard_map/reduce_scatter | solution.py:1498
  697.2 7.4 copy-start.18
  704.6 8.1 copy-start.45
  720.9 168.6 %all-reduce.4.cloned.1.call-start = ((), (), s32[]{:S(2)}) async-start(), calls=%async_computation.9 | async-start | bytes 131072 | tf_op jit(solution)/shard_map/psum | solution.py:1499
  863.4 4.4 copy-start.56
  863.4 4.4 copy-start.63
  863.4 4.4 copy-start.67
  867.9 25.5 %copy-start.1 = (s32[16]{0:T(128)S(1)}, s32[16]{0:T(128)}, u32[]{:S(2)}) copy-start(s32[16]{0:T(128)} %param.49) | copy-start | bytes 196
  (44 other events, 91.4 us)
Sparse Core Ops, SparseCore 0:
  10.4 24.0 all-gather.4
  193.4 18.6 reduce-scatter.3
  532.4 23.2 all-gather.8
  603.6 31.4 reduce-scatter.5
  721.0 64.3 reduce-scatter.7
  868.0 21.4 all-reduce.3
Sparse Core Ops, SparseCore 1:
  197.2 162.5 all-gather.6

commit v4 on v3

--- a/solution.py
+++ b/solution.py
@@ -1,7 +1,9 @@
+import functools
 import math
 
 import jax
 import jax.numpy as jnp
+import numpy as np
 from jax import lax
 from jax.experimental import pallas as pl
 from jax.experimental.pallas import tpu as pltpu
@@ -1274,6 +1276,224 @@
     )(info, pos, rows_in, cots_in, gate_w, up_w, down_w)
 
 
+ATTENTION_VMEM = 60 * 1024 * 1024
+SCORE_SCALE = HEAD_SIZE ** (-0.5)
+def turn_tables(rows):
+    frequency = np.exp(
+        -math.log(rope_base) * np.arange(HEAD_SIZE // 2, dtype=np.float32) * (2.0 / HEAD_SIZE)
+    ).astype(np.float32)
+    angles = np.arange(rows, dtype=np.float32)[:, None] * frequency[None, :]
+    cosine, sine = np.cos(angles), np.sin(angles)
+    return (
+        np.concatenate([cosine, cosine], axis=1).astype(np.float32),
+        np.concatenate([-sine, sine], axis=1).astype(np.float32),
+    )
+
+
+def turn(value, cosine, sine):
+    return value * cosine + pltpu.roll(value, HEAD_SIZE // 2, 1) * sine
+
+
+def inverse_norm(value):
+    return lax.rsqrt(jnp.mean(value * value, axis=-1, keepdims=True) + epsilon)
+
+
+def meet_y(me):
+    barrier = pltpu.get_barrier_semaphore()
+    pl.semaphore_signal(barrier, 1, device_id=me.y_mate, device_id_type=pl.DeviceIdType.MESH)
+    pl.semaphore_wait(barrier, 1)
+
+
+def gain_rows(aux_t, experts, chunks):
+    head = [aux_t[experts + 2 + i : experts + 3 + i, :] for i in range(2)]
+    width = HEAD_SIZE
+    heads = [sum(row[:, c * width : (c + 1) * width] for c in range(chunks)) for row in head]
+    return aux_t[experts : experts + 1, :], aux_t[experts + 1 : experts + 2, :], *heads
+
+
+def probabilities(query, key, allowed):
+    scores = jnp.where(allowed, dot(query, key, ((1,), (1,))) * SCORE_SCALE, masked_score)
+    spread = jnp.exp(scores - jnp.max(scores, axis=-1, keepdims=True))
+    return spread / jnp.sum(spread, axis=-1, keepdims=True)
+
+
+def allowed_pairs(live):
+    rows = live.shape[1]
+    later = lax.broadcasted_iota(jnp.int32, (rows, rows), 0)
+    sooner = lax.broadcasted_iota(jnp.int32, (rows, rows), 1)
+    return (sooner <= later) & (live[0:1, :] > 0.0)
+
+
+def forward_kernel(
+    experts, x_pair, packed, live, chosen, cosine, sine,
+    sent_o, residual_o, normed_o, raw_o, query_o, key_o, value_o, context_o,
+    x, w, ctx, aux_w, normed, raw, query, key, value, context, att, got, residual, sent,
+    in_s, w_s, out_s, y_s,
+):
+    bf16, f32 = jnp.bfloat16, jnp.float32
+    me = Place()
+    rows, features = x.shape
+    own_rows = rows // 2
+    heads, key_heads = query.shape[0], key.shape[0]
+    qkv = w.shape[1]
+    chunk = 512
+    mine = pl.ds(pl.multiple_of(me.y * own_rows, own_rows), own_rows)
+    theirs = pl.ds(pl.multiple_of((1 - me.y) * own_rows, own_rows), own_rows)
+    loads = [
+        pltpu.make_async_copy(x_pair, x, in_s.at[0]),
+        pltpu.make_async_copy(
+            packed.at[:, pl.ds(qkv + ctx.shape[1], AUX)], aux_w, in_s.at[1]
+        ),
+        pltpu.make_async_copy(packed.at[:, pl.ds(qkv, ctx.shape[1])], ctx, in_s.at[2]),
+    ]
+    parts = [
+        pltpu.make_async_copy(
+            packed.at[:, pl.ds(c * chunk, chunk)], w.at[:, pl.ds(c * chunk, chunk)], w_s.at[c]
+        )
+        for c in range(qkv // chunk)
+    ]
+    loads[0].start()
+    loads[1].start()
+    for copy in parts:
+        copy.start()
+    loads[2].start()
+    meet_y(me)
+    loads[1].wait()
+    aux_t = aux_w[...].astype(f32).T
+    gain_one, gain_two, query_gain, key_gain = gain_rows(aux_t, experts, features // HEAD_SIZE)
+    loads[0].wait()
+
+    def first_norm(i, carry):
+        at = pl.ds(pl.multiple_of(i * 32, 32), 32)
+        stream = x[at, :].astype(f32)
+        normed[at, :] = (stream * inverse_norm(stream) * gain_one).astype(bf16)
+        return carry
+
+    lax.fori_loop(0, rows // 32, first_norm, 0)
+    for c, copy in enumerate(parts):
+        copy.wait()
+        got_raw = dot(normed[...], w[:, c * chunk : (c + 1) * chunk])
+        for h in range(chunk // HEAD_SIZE):
+            raw[c * (chunk // HEAD_SIZE) + h] = got_raw[:, h * HEAD_SIZE : (h + 1) * HEAD_SIZE]
+    turn_c, turn_s = cosine[...], sine[...]
+    for g in range(key_heads):
+        unnormed = raw[heads + g]
+        key[g] = turn(unnormed * inverse_norm(unnormed) * key_gain, turn_c, turn_s).astype(bf16)
+        value[g] = raw[heads + key_heads + g].astype(bf16)
+    allowed = allowed_pairs(live[...])
+
+    def head(h, carry):
+        g = h // (heads // key_heads)
+        unnormed = raw[h]
+        turned = turn(unnormed * inverse_norm(unnormed) * query_gain, turn_c, turn_s).astype(bf16)
+        query[h] = turned
+        probs = probabilities(turned, key[g], allowed).astype(bf16)
+        at = pl.ds(pl.multiple_of(h * HEAD_SIZE, HEAD_SIZE), HEAD_SIZE)
+        context[:, at] = dot(probs, value[g]).astype(bf16)
+        return carry
+
+    lax.fori_loop(0, heads, head, 0)
+    outs = [
+        pltpu.make_async_copy(source, target, out_s.at[i])
+        for i, (source, target) in enumerate(
+            ((normed, normed_o), (raw, raw_o), (query, query_o), (key, key_o), (value, value_o),
+             (context, context_o))
+        )
+    ]
+    for copy in outs:
+        copy.start()
+    loads[2].wait()
+    copies = []
+    for c in range(features // chunk):
+        cols = pl.ds(c * chunk, chunk)
+        att[theirs, cols] = dot(context[theirs, :], ctx[cols, :], ((1,), (1,))).astype(bf16)
+        copy = remote(
+            att.at[theirs, cols], got.at[:, cols], y_s.at[0, c], y_s.at[1, c], me.y_mate
+        )
+        copy.start()
+        copies.append(copy)
+    for c in range(features // chunk):
+        cols = pl.ds(c * chunk, chunk)
+        residual[:, cols] = dot(context[mine, :], ctx[cols, :], ((1,), (1,)))
+    for copy in copies:
+        copy.wait_recv()
+
+    def second_norm(i, carry):
+        at = pl.ds(pl.multiple_of(i * 16, 16), 16)
+        there = pl.ds(pl.multiple_of(me.y * own_rows + i * 16, 16), 16)
+        total = x[there, :].astype(f32) + (residual[at, :] + got[at, :].astype(f32))
+        residual[at, :] = total
+        sent[at, pl.ds(0, features)] = (total * inverse_norm(total) * gain_two).astype(bf16)
+        return carry
+
+    lax.fori_loop(0, own_rows // 16, second_norm, 0)
+    logits = dot(sent[:, :features], aux_w[...])
+    picked = chosen[...] > 0.0
+    logits = jnp.where(picked, logits, masked_score)
+    spread = jnp.where(picked, jnp.exp(logits - jnp.max(logits, axis=-1, keepdims=True)), 0.0)
+    gates = spread / jnp.sum(spread, axis=-1, keepdims=True)
+    high = gates.astype(bf16).astype(f32)
+    sent[:, pl.ds(features, AUX)] = (high + pltpu.roll(gates - high, experts, 1)).astype(bf16)
+    last = [
+        pltpu.make_async_copy(sent, sent_o, out_s.at[6]),
+        pltpu.make_async_copy(residual, residual_o, out_s.at[7]),
+    ]
+    for copy in last:
+        copy.start()
+    for copy in copies:
+        copy.wait_send()
+    for copy in outs + last:
+        copy.wait()
+
+
+def attention_forward(x_pair, packed, live, chosen, experts, heads, key_heads, collective_id):
+    bf16, f32 = jnp.bfloat16, jnp.float32
+    rows, features = x_pair.shape
+    qkv = (heads + 2 * key_heads) * HEAD_SIZE
+    cosine, sine = turn_tables(rows)
+    dma = pltpu.SemaphoreType.DMA
+    shapes = (
+        ((rows // 2, features + AUX), bf16),
+        ((rows // 2, features), f32),
+        ((rows, features), bf16),
+        ((heads + 2 * key_heads, rows, HEAD_SIZE), f32),
+        ((heads, rows, HEAD_SIZE), bf16),
+        ((key_heads, rows, HEAD_SIZE), bf16),
+        ((key_heads, rows, HEAD_SIZE), bf16),
+        ((rows, heads * HEAD_SIZE), bf16),
+    )
+    anywhere, vmem = pl.BlockSpec(memory_space=pl.ANY), pl.BlockSpec(memory_space=pltpu.VMEM)
+    return pl.pallas_call(
+        functools.partial(forward_kernel, experts),
+        out_shape=tuple(jax.ShapeDtypeStruct(*shape) for shape in shapes),
+        in_specs=[anywhere, anywhere, vmem, vmem, vmem, vmem],
+        out_specs=(anywhere,) * len(shapes),
+        scratch_shapes=[
+            pltpu.VMEM((rows, features), bf16),
+            pltpu.VMEM((features, qkv), bf16),
+            pltpu.VMEM((features, heads * HEAD_SIZE), bf16),
+            pltpu.VMEM((features, AUX), bf16),
+            pltpu.VMEM((rows, features), bf16),
+            pltpu.VMEM((heads + 2 * key_heads, rows, HEAD_SIZE), f32),
+            pltpu.VMEM((heads, rows, HEAD_SIZE), bf16),
+            pltpu.VMEM((key_heads, rows, HEAD_SIZE), bf16),
+            pltpu.VMEM((key_heads, rows, HEAD_SIZE), bf16),
+            pltpu.VMEM((rows, heads * HEAD_SIZE), bf16),
+            pltpu.VMEM((rows, features), bf16),
+            pltpu.VMEM((rows // 2, features), bf16),
+            pltpu.VMEM((rows // 2, features), f32),
+            pltpu.VMEM((rows // 2, features + AUX), bf16),
+            dma((3,)),
+            dma((qkv // 512,)),
+            dma((8,)),
+            dma((2, features // 512)),
+        ],
+        compiler_params=pltpu.CompilerParams(
+            collective_id=collective_id, has_side_effects=True, vmem_limit_bytes=ATTENTION_VMEM
+        ),
+    )(x_pair, packed, live, chosen, cosine, sine)
+
+
 def split_high_low(value):
     high = value.astype(jnp.bfloat16)
     return high, (value - high.astype(jnp.float32)).astype(jnp.bfloat16)
@@ -1314,9 +1534,17 @@
     key_width = key_projection.shape[1]
     norm_part = HEAD_SIZE // dp_count
 
-    gains = jnp.zeros((shard, AUX - expert_count), bf16)
-    gains = gains.at[:, 0].set(prenorm_gain).at[:, 1].set(midnorm_gain)
-    gains = gains.at[:norm_part, 2].set(querynorm_gain).at[:norm_part, 3].set(keynorm_gain)
+    place = dp_index * norm_part
+    gains = jnp.concatenate(
+        [
+            prenorm_gain[:, None],
+            midnorm_gain[:, None],
+            lax.dynamic_update_slice(jnp.zeros((shard,), bf16), querynorm_gain, (place,))[:, None],
+            lax.dynamic_update_slice(jnp.zeros((shard,), bf16), keynorm_gain, (place,))[:, None],
+            jnp.zeros((shard, AUX - expert_count - 4), bf16),
+        ],
+        axis=1,
+    )
     packed = jnp.concatenate(
         [query_weight, key_projection, value_projection, context_weight.T, router_weight, gains],
         axis=1,
@@ -1330,43 +1558,52 @@
     router_all = packed[:, edges[4] : edges[5]]
     gains_all = packed[:, edges[5] :].astype(f32)
     gain_one, gain_two = gains_all[:, 0], gains_all[:, 1]
-    head_gains = gains_all.reshape(dp_count, shard, -1)[:, :norm_part, :]
-    query_factor = head_gains[:, :, 2].reshape(-1)
-    key_factor = head_gains[:, :, 3].reshape(-1)
+    query_factor = jnp.sum(gains_all[:, 2].reshape(dp_count, shard), axis=0)
+    key_factor = jnp.sum(gains_all[:, 3].reshape(dp_count, shard), axis=0)
 
     cot_all = lax.all_gather(output_cotangent, ("dp", "tensor"), axis=0, tiled=True)
     routes_all = lax.all_gather(routes.T, "dp")
     input_rows = lax.all_gather(layer_input, "tensor", axis=0, tiled=True)
     position = jnp.arange(block_rows, dtype=jnp.int32)
     block_lengths = lengths[sequence_order]
-    seq_length = block_lengths[dp_index]
-
-    frequency = jnp.exp(
-        -math.log(rope_base) * jnp.arange(HEAD_SIZE // 2, dtype=f32) * (2.0 / HEAD_SIZE)
-    )
-    angles = position.astype(f32)[:, None] * frequency[None, :]
-    cosine_table = jnp.cos(angles)[:, None, :]
-    sine_values = jnp.sin(angles)[:, None, :]
+    live = position[None, :] < block_lengths[:, None]
+    live_own = lax.dynamic_slice_in_dim(live, dp_index, 1, 0)
+    live_own = jnp.broadcast_to(live_own.astype(f32), (8, block_rows))
     heads_query = query_width // HEAD_SIZE
     heads_key = key_width // HEAD_SIZE
     group_width = heads_query // heads_key
-    stream = input_rows.astype(f32)
-    unit_first, scale_first = rms_normalize(stream)
-    first_normed = (unit_first * gain_one).astype(bf16)
-    raw = matrix_product(first_normed, qkv_all)
-    query_unnormed = raw[:, : edges[1]].reshape(block_rows, heads_query, HEAD_SIZE)
-    key_unnormed = raw[:, edges[1] : edges[2]].reshape(block_rows, heads_key, HEAD_SIZE)
-    value_rows = raw[:, edges[2] :].astype(bf16).reshape(block_rows, heads_key, HEAD_SIZE)
-    query_unit, query_scale = rms_normalize(query_unnormed)
-    key_unit, key_scale = rms_normalize(key_unnormed)
-    query_rows = (
-        rotary_apply(query_unit * query_factor, cosine_table, sine_values)
-        .astype(bf16)
-        .reshape(block_rows, heads_key, group_width, HEAD_SIZE)
-    )
-    keys_rot = rotary_apply(key_unit * key_factor, cosine_table, sine_values).astype(bf16)
-    score_scale = HEAD_SIZE ** (-0.5)
-    allowed = (position[None, :] <= position[:, None]) & (position < seq_length)[None, :]
+    row_start = tensor_index * own_rows
+    routes_own = lax.dynamic_slice_in_dim(routes, row_start, own_rows, 0)
+    expert_ids = jnp.arange(AUX, dtype=jnp.int32)
+    chosen = jnp.any(routes_own[:, :, None] == expert_ids[None, None, :], axis=1).astype(f32)
+    (
+        sent,
+        residual,
+        first_normed,
+        raw,
+        query_heads,
+        key_heads,
+        value_heads,
+        context,
+    ) = attention_forward(
+        input_rows, packed, live_own, chosen, expert_count, heads_query, heads_key, 5
+    )
+    normed_all = gather_all(sent, 1).reshape(dp_count, block_rows, features + AUX)
+
+    cosine_table, sine_values = turn_tables(block_rows)
+    cosine_table = cosine_table[:, None, : HEAD_SIZE // 2]
+    sine_values = sine_values[:, None, HEAD_SIZE // 2 :]
+    unit_first, scale_first = rms_normalize(input_rows.astype(f32))
+    rows_first = raw.transpose(1, 0, 2)
+    query_unit, query_scale = rms_normalize(rows_first[:, :heads_query])
+    key_unit, key_scale = rms_normalize(rows_first[:, heads_query : heads_query + heads_key])
+    query_rows = query_heads.transpose(1, 0, 2).reshape(
+        block_rows, heads_key, group_width, HEAD_SIZE
+    )
+    keys_rot = key_heads.transpose(1, 0, 2)
+    value_rows = value_heads.transpose(1, 0, 2)
+    score_scale = SCORE_SCALE
+    allowed = (position[None, :] <= position[:, None]) & (live_own[0:1] > 0.0)
     scores = (
         jnp.einsum("ikrd,jkd->krij", query_rows, keys_rot, preferred_element_type=f32)
         * score_scale
@@ -1375,33 +1612,14 @@
     weights = jnp.exp(scores - jnp.max(scores, axis=-1, keepdims=True))
     soft_probs = weights / jnp.sum(weights, axis=-1, keepdims=True)
     probs_low = soft_probs.astype(bf16)
-    context = jnp.einsum("krij,jkd->ikrd", probs_low, value_rows, preferred_element_type=f32)
-    context = context.reshape(block_rows, query_width).astype(bf16)
-    attention = lax.psum_scatter(
-        transposed(context, context_all).astype(bf16),
-        "tensor",
-        scatter_dimension=0,
-        tiled=True,
-    )
-    residual = layer_input.astype(f32) + attention.astype(f32)
     unit_second, scale_second = rms_normalize(residual)
-    normed_second = (unit_second * gain_two).astype(bf16)
-
-    row_start = tensor_index * own_rows
-    routes_own = lax.dynamic_slice_in_dim(routes, row_start, own_rows, 0)
-    expert_ids = jnp.arange(expert_count, dtype=jnp.int32)
-    chosen = jnp.any(routes_own[:, :, None] == expert_ids[None, None, :], axis=1)
-    logits = jnp.where(chosen, matrix_product(normed_second, router_all), masked_score)
-    spread = jnp.exp(logits - jnp.max(logits, axis=-1, keepdims=True))
-    gates = spread / jnp.sum(spread, axis=-1, keepdims=True)
-    high, low = split_high_low(gates)
-    sent = jnp.concatenate(
-        [normed_second, high, low, jnp.zeros((own_rows, AUX - 2 * expert_count), bf16)], axis=1
-    )
-    normed_all = gather_all(sent, 1).reshape(dp_count, block_rows, features + AUX)
+    normed_second = sent[:, :features]
+    gates = (
+        sent[:, features : features + expert_count].astype(f32)
+        + sent[:, features + expert_count : features + 2 * expert_count].astype(f32)
+    )
 
     expert_own = dp_index * EXP_DEV + jnp.arange(EXP_DEV, dtype=jnp.int32)
-    live = position[None, :] < block_lengths[:, None]
     hot = jnp.any(routes_all[:, None, :, :] == expert_own[None, :, None, None], axis=2)
     hot = hot & live[:, None, :]
     before = (position[:, None] < position[None, :]).astype(bf16)

time: 913 us -> 875 us (0.958)
  Pallas kernels: 614 us -> 670 us
  local copies, waits for them, and re-layouts: 77.4 us -> 37.5 us
  other arithmetic: 76.6 us -> 48.6 us
  matrix products: 57.5 us -> 39.4 us
    pallas_call x1, Pallas kernels: 115 us -> 181 us  [gather_dp(): pl.pallas_call(plane_gather_kernel, out_shape=jax.ShapeDtypeStruct((devic...]
    pallas_call x1, Pallas kernels: 126 us -> 80.4 us  [gather_all(): pl.pallas_call(gather_kernel, out_shape=jax.ShapeDtypeStruct((devices, ro...]
    pallas_call x0 -> x1, Pallas kernels: none -> 35.9 us  [attention_forward(): pl.pallas_call(functools.partial(forward_kernel, experts), out_shape=tupl...]
    unnamed x151 -> x70, local copies, waits for them, and re-layouts: 24.4 us -> 8.36 us
    another operation x14 -> x4, other arithmetic: 16.5 us -> 4.75 us
  transfers between devices with their start and end apart: 7 -> 6, of which waited for: 3 -> 2; matrix products, arithmetic and copies ran while one was open for 10% -> 7% of each run, Pallas kernels for 51% -> 59%
where the time goes in v4:
time: 875 us; the launch traced here: 865 us
  Pallas kernels  670 us (77%)
  other arithmetic  48.6 us (6%)
  matrix products  39.4 us (5%)
  local copies, waits for them, and re-layouts  37.5 us (4%)
  waiting for transfers between devices  36.9 us (4%)
  blocking collectives  17.8 us (2%)
  between operations  15.3 us (2%)
    pallas_call x1, Pallas kernels, gather_dp(): pl.pallas_call(plane_gather_kernel, out_shape=jax.ShapeDtypeStruct((devic...  181 us
    pallas_call x2, Pallas kernels, scatter_all(): pl.pallas_call(scatter_kernel, out_shape=jax.ShapeDtypeStruct((rows, widt...  176 us
    pallas_call x1, Pallas kernels, scatter_dp(): pl.pallas_call(plane_scatter_kernel, out_shape=jax.ShapeDtypeStruct((rows...  123 us
    pallas_call x1, Pallas kernels, gather_all(): pl.pallas_call(gather_kernel, out_shape=jax.ShapeDtypeStruct((devices, ro...  80.4 us
    pallas_call x1, Pallas kernels, expert_layer(): pl.pallas_call(expert_kernel, out_shape=(shape((blocks, block_rows, featu...  73.3 us
    pallas_call x1, Pallas kernels, attention_forward(): pl.pallas_call(functools.partial(forward_kernel, experts), out_shape=tupl...  35.9 us
    psum x1, waiting for transfers between devices, gathered_body(): small = lax.psum(small, 'tensor')  18 us
    all_gather x1, blocking collectives, gathered_body(): routes_all = lax.all_gather(routes.T, 'dp')  17.8 us
  transfers between devices with their start and end apart: 6, of which 2 were waited for; matrix products, arithmetic and copies ran while one was open for 7% of the time, Pallas kernels for 59%

profile of v4, /device:TPU:0, one launch (start us, length us, event | category | flops | bytes accessed | tf_op | source)
XLA Modules:
  0.0 865.4 jit_solution(8295841356617258982)
XLA Ops:
  12.1 2.2 concatenate.34.src
  14.2 181.4 %shard_map.317 = bf16[16,128,4736]{2,1,0:T(8,128)(2,1)} custom-call(bf16[128,4736]{1,0:T(8,128)(2,1)} %concatenate.34.src), custom_call_target="tpu_custom_call" | custom-call | tf_op jit(solution)/shard_map/pallas_call | solution.py:884
  197.3 17.8 %all-gather = s32[128,256]{1,0:T(8,128)S(1)} all-gather(s32[8,256]{1,0:T(8,128)S(1)} %bitcast.180), channel_id=2, replica_groups=mesh['dp'=16,'tensor'=2] {'dp'}, dimensions={0}, use_global_device_ids=true | all-gather | bytes 139264 | tf_op jit(solution)/shard_map/all_gather | solution.py:1565
  219.3 2.0 slice_reduce_fusion
  222.7 35.9 %shard_map.318 = (bf16[128,2176]{1,0:T(8,128)(2,1)}, f32[128,2048]{1,0:T(8,128)}, bf16[256,2048]{1,0:T(8,128)(2,1)}, f32[20,256,128]{2,1,0:T(8,128)}, bf16[16,25...) custom-call(bf16[256,2048]{1,0:T(8,128)(2,1)} %all-gather.5.cloned.1, ...), custom_call_target="tpu_custom_call" | custom-call | tf_op jit(solution)/shard_map/pallas_call | solution.py:1466
  258.6 80.4 %shard_map.319 = bf16[32,128,2176]{2,1,0:T(8,128)(2,1)} custom-call(bf16[128,2176]{1,0:T(8,128)(2,1)} %get-tuple-element.88.src), custom_call_target="tpu_custom_call" | custom-call | tf_op jit(solution)/shard_map/pallas_call | solution.py:779
  339.2 73.3 %shard_map.320 = (bf16[16,256,2048]{2,1,0:T(8,128)(2,1)}, bf16[16,256,2176]{2,1,0:T(8,128)(2,1)}, f32[2,2048,384]{2,1,0:T(8,128)}, f32[2,2048,384]{2,1,0:T(8,128)}, f32[2,384,2048]{2,1,0:T(8,128)}) custom-call(s32[34]{0:T(128)} %pad_add_fusion.2.info, s32[16,2,256]{2,1,0:T(2,128)} %and_select_fusion.pos, bf16[16,256,2176]{2,1,0:T(8,128)(2,1)} %bitcast.152, ...), custom_call_target="tpu_custom_call" | custom-call | tf_op jit(solution)/shard_map/pallas_call | solution.py:1241
  412.5 84.5 %shard_map.322 = bf16[128,2176]{1,0:T(8,128)(2,1)} custom-call(bf16[32,128,2176]{2,1,0:T(8,128)(2,1)} %bitcast.160), custom_call_target="tpu_custom_call" | custom-call | tf_op jit(solution)/shard_map/pallas_call | solution.py:628
  500.2 1.7 multiply_reduce_fusion.4
  502.9 2.5 fusion.58
  506.3 4.7 fusion.65
  511.0 17.4 %all-gather.9.cloned.1.call-done = bf16[256,2048]{1,0:T(8,128)(2,1)} async-done(((bf16[128,2048]{1,0:T(8,128)(2,1)}), bf16[256,2048]{1,0:T(8,128)(2,1)}) %all-gather.9.cloned.1.call-update) | async-done | bytes 1048592 | tf_op jit(solution)/shard_map/all_gather | solution.py:1661
  528.5 6.2 fusion.18
  536.7 2.4 fusion.7
  539.1 1.9 multiply_bitcast_fusion
  541.7 3.0 copy.173
  544.8 2.9 multiply_subtract_fusion
  547.7 1.8 multiply_reduce_fusion
  549.6 2.8 multiply_convert_fusion
  552.3 2.3 copy.174
  555.5 3.4 copy.179
  560.2 8.0 fusion.9
  571.1 91.4 %shard_map.321 = bf16[128,2048]{1,0:T(8,128)(2,1)} custom-call(bf16[32,128,2048]{2,1,0:T(8,128)(2,1)} %bitcast.162), custom_call_target="tpu_custom_call" | custom-call | tf_op jit(solution)/shard_map/pallas_call | solution.py:628
  662.6 7.4 convolution_convert_fusion.1
  670.0 6.7 convolution_convert_fusion
  678.2 2.0 dynamic-slice_select_fusion.1
  681.8 2.0 dynamic-slice_select_fusion
  686.7 16.4 %pad_maximum_fusion = bf16[2048,4608]{1,0:T(8,128)(2,1)} fusion(bf16[2048,2048]{1,0:T(8,128)(2,1)} %convolution_convert_fusion.1, bf16[2048,2560]{1,0:T(8,128)(2,1)} %convolution_convert_fusion), kind=kLoop, calls=%fused_computation.2 | loop fusion | flops 37748736 | bytes 37748736 | tf_op jit(solution)/shard_map/concatenate | solution.py:1718
  703.1 123.0 %shard_map.323 = bf16[128,4608]{1,0:T(8,128)(2,1)} custom-call(bf16[16,128,4608]{2,1,0:T(8,128)(2,1)} %bitcast.151), custom_call_target="tpu_custom_call" | custom-call | tf_op jit(solution)/shard_map/pallas_call | solution.py:999
  829.8 2.5 copy.181
  833.1 3.2 fusion.29
  836.3 18.0 %all-reduce.3.cloned.1.call-done = f32[128,128]{0,1:T(8,128)} async-done(((f32[128,128]{0,1:T(8,128)}), f32[128,128]{0,1:T(8,128)}) %all-reduce.3.cloned.1.call-update) | async-done | bytes 65552 | tf_op jit(solution)/shard_map/psum | solution.py:1717
  (172 shorter events, 39.2 us)
Async XLA Ops:
  7.2 189.5 %copy-start = (s32[16]{0:T(128)S(1)}, s32[16]{0:T(128)}, u32[]{:S(2)}) copy-start(s32[16]{0:T(128)} %param.46) | copy-start | bytes 196
  7.2 4.3 copy-start.26
  7.2 4.5 copy-start.27
  7.2 4.6 copy-start.28
  7.2 4.8 copy-start.21
  7.2 4.8 copy-start.23
  7.2 4.8 copy-start.24
  7.3 214.9 %all-gather.5.cloned.1.call-start = ((), (), s32[]{:S(2)}) async-start(), calls=%async_computation.2 | async-start | bytes 1572864 | tf_op jit(solution)/shard_map/all_gather | solution.py:1566
  8.0 331.2 %all-gather.7.cloned.1.call-start = ((), (), s32[]{:S(2)}) async-start(), calls=%async_computation.3 | async-start | bytes 17301504 | tf_op jit(solution)/shard_map/all_gather | solution.py:1564
  8.7 519.7 %all-gather.9.cloned.1.call-start = ((), (), s32[]{:S(2)}) async-start(), calls=%async_computation.4 | async-start | bytes 1572864 | tf_op jit(solution)/shard_map/all_gather | solution.py:1661
  14.2 181.4 %copy-start.25 = (s32[256,8]{0,1:T(8,128)S(1)}, s32[256,8]{0,1:T(8,128)}, u32[]{:S(2)}) copy-start(s32[256,8]{0,1:T(8,128)} %param.45) | copy-start | bytes 24580
  14.2 182.4 %copy-start.31 = (s32[16]{0:T(128)S(1)}, s32[16]{0:T(128)}, u32[]{:S(2)}) copy-start(s32[16]{0:T(128)} %param.47) | copy-start | bytes 196
  258.6 80.4 %copy-start.3 = (f32[128,2048]{1,0:T(8,128)S(1)}, f32[128,2048]{1,0:T(8,128)}, u32[]{:S(2)}) copy-start(f32[128,2048]{1,0:T(8,128)} %get-tuple-element.87) | copy-start | bytes 3145732
  498.9 4.0 copy-start.10
  501.9 3.6 copy-start.2
  505.4 171.3 %reduce-scatter.3.cloned.1.call-start = ((), (), s32[]{:S(2)}) async-start(), calls=%async_computation.5 | async-start | bytes 1572864 | tf_op jit(solution)/shard_map/reduce_scatter | solution.py:1700
  528.5 6.5 copy-start.11
  534.9 1.8 copy-start.14
  539.1 1.9 copy-start.18
  541.7 3.1 copy-start.19
  541.7 3.0 copy-start.20
  555.5 3.5 copy-start.15
  560.2 8.6 copy-start.29
  560.2 9.4 %copy-start.6 = (bf16[256,2048]{1,0:T(8,128)(2,1)S(1)}, bf16[256,2048]{1,0:T(8,128)(2,1)}, u32[]{:S(2)}) copy-start(bf16[256,2048]{1,0:T(8,128)(2,1)} %all-gather.5.cloned.1.call-done.x_pair) | copy-start | bytes 3145732
  568.2 264.8 %reduce-scatter.5.cloned.1.call-start = ((), (), s32[]{:S(2)}) async-start(), calls=%async_computation.6 | async-start | bytes 1114112 | tf_op jit(solution)/shard_map/reduce_scatter | solution.py:1716
  570.6 106.1 %copy-start.9 = (f32[256,2048]{1,0:T(8,128)}, f32[256,2048]{1,0:T(8,128)S(1)}, u32[]{:S(2)}) copy-start(f32[256,2048]{1,0:T(8,128)S(1)} %convert_element_type.99) | copy-start | bytes 6291460
  662.6 7.4 copy-start.13
  662.6 7.4 copy-start.17
  686.6 167.7 %all-reduce.3.cloned.1.call-start = ((), (), s32[]{:S(2)}) async-start(), calls=%async_computation.7 | async-start | bytes 131072 | tf_op jit(solution)/shard_map/psum | solution.py:1717
  828.7 4.3 copy-start.4
  828.7 4.4 copy-start.8
  833.1 25.1 %copy-start.1 = (s32[16]{0:T(128)S(1)}, s32[16]{0:T(128)}, u32[]{:S(2)}) copy-start(s32[16]{0:T(128)} %param.46) | copy-start | bytes 196
  (6 other events, 6.7 us)
Sparse Core Ops, SparseCore 0:
  9.6 23.9 all-gather.4
  36.6 159.2 all-gather.6
  505.6 22.8 all-gather.8
  568.3 31.5 reduce-scatter.2
  686.8 64.0 reduce-scatter.4
  833.2 21.0 all-reduce.2

commit v5 on v4

--- a/solution.py
+++ b/solution.py
@@ -794,230 +794,6 @@
     )(value).reshape(devices * rows, width)
 
 
-def plane_gather_kernel(src, out, own_s, z_s, x_s, core_s):
-    me = Place()
-
-    def near(k):
-        return me.farthest(GRID_Z - 1 - k)
-
-    def at(k, fx):
-        return out.at[me.dp_at(near(k), fx, 0)]
-
-    mine = pltpu.make_async_copy(src, at(0, 0), own_s)
-    mine.start()
-    me.greet()
-
-    def z_copy(k, side, mate):
-        zn = near(k)
-        return remote(
-            src if k == 0 else at(k, 0), at(k, 0), z_s.at[0, side, zn], z_s.at[1, side, zn], mate
-        )
-
-    xs, cores = {}, {}
-    for k in range(GRID_Z):
-        source = src if k == 0 else at(k, 0)
-        xs[k] = remote(source, at(k, 0), x_s.at[0, k], x_s.at[1, k], me.x_mate)
-        cores[k, 0] = remote(source, at(k, 0), core_s.at[0, k, 0], core_s.at[1, k, 0], me.sibling)
-        cores[k, 1] = remote(at(k, 1), at(k, 1), core_s.at[0, k, 1], core_s.at[1, k, 1], me.sibling)
-
-    def own(k):
-        zn = near(k)
-        for side, came, more, mate in (
-            (0, zn < me.z, me.has_above, me.above),
-            (1, zn > me.z, me.has_below, me.below),
-        ):
-            copy = z_copy(k, side, mate)
-            if k == 0:
-
-                @pl.when(more)
-                def _():
-                    copy.start()
-            else:
-
-                @pl.when(came)
-                def _():
-                    copy.wait_recv()
-
-                    @pl.when(more)
-                    def _():
-                        copy.start()
-
-        xs[k].start()
-        cores[k, 0].start()
-
-    def diag(k):
-        xs[k].wait_recv()
-        cores[k, 1].start()
-
-    own(0)
-    own(1)
-    diag(0)
-    own(2)
-    diag(1)
-    own(3)
-    diag(2)
-    diag(3)
-    mine.wait()
-    for k in range(GRID_Z):
-        zn = near(k)
-        for side, came, more, mate in (
-            (0, zn <= me.z, me.has_above, me.above),
-            (1, zn >= me.z, me.has_below, me.below),
-        ):
-            copy = z_copy(k, side, mate)
-
-            @pl.when(came)
-            def _():
-                @pl.when(more)
-                def _():
-                    copy.wait_send()
-
-        xs[k].wait_send()
-    for copy in cores.values():
-        copy.wait()
-
-
-def gather_dp(value, collective_id):
-    devices = lax.axis_size("dp")
-    rows, width = value.shape
-    dma = pltpu.SemaphoreType.DMA
-    return pl.pallas_call(
-        plane_gather_kernel,
-        out_shape=jax.ShapeDtypeStruct((devices, rows, width), value.dtype),
-        in_specs=[pl.BlockSpec(memory_space=pl.ANY)],
-        out_specs=pl.BlockSpec(memory_space=pl.ANY),
-        scratch_shapes=[dma(()), dma((2, 2, 4)), dma((2, 4)), dma((2, 4, 2))],
-        compiler_params=pltpu.CompilerParams(collective_id=collective_id, has_side_effects=True),
-    )(value).reshape(devices * rows, width)
-
-
-def plane_scatter_kernel(
-    part, out, own, core, from_x, from_z, load_s, core_s, x_s, z_s, out_s
-):
-    me = Place()
-    rows = own.shape[2]
-    whole = (0, rows)
-    loads, cores = {}, {}
-
-    def chunk(k, flip_x, flip_core):
-        return part.at[me.dp_at(me.farthest(k), flip_x, flip_core)]
-
-    for k in range(GRID_Z):
-        for fx in (1, 0):
-            loads[k, fx] = pltpu.make_async_copy(chunk(k, fx, 0), own.at[k, fx], load_s.at[k, fx])
-            loads[k, fx].start()
-    me.greet()
-    for k in range(GRID_Z):
-        for fx in (1, 0):
-            cores[k, fx] = remote(
-                chunk(k, fx, 1), core.at[k, fx],
-                core_s.at[0, k, fx], core_s.at[1, k, fx], me.sibling,
-            )
-            cores[k, fx].start()
-    half = rows // 2
-    xs = [
-        [
-            remote(
-                own.at[k, 1, pl.ds(h * half, half)], from_x.at[k, pl.ds(h * half, half)],
-                x_s.at[0, k, h], x_s.at[1, k, h], me.x_mate,
-            )
-            for h in range(2)
-        ]
-        for k in range(GRID_Z)
-    ]
-
-    def z_copy(k, side, mate):
-        to = me.farthest(k)
-        return remote(
-            own.at[k, 0], from_z.at[side, to], z_s.at[0, side, to], z_s.at[1, side, to], mate
-        )
-
-    def across(k):
-        loads[k, 1].wait()
-        cores[k, 1].wait_recv()
-        for h in range(2):
-            add_rows(own.at[k, 1], [(core.at[k, 1], 0)], (h * half, half))
-            xs[k][h].start()
-
-    def column(k):
-        loads[k, 0].wait()
-        cores[k, 0].wait_recv()
-        for h in range(2):
-            xs[k][h].wait_recv()
-        mine = own.at[k, 0]
-        add_rows(mine, [(core.at[k, 0], 0), (from_x.at[k], 0)], whole)
-        to = me.farthest(k)
-        for side, ahead, mate, more in (
-            (0, to > me.z, me.above, me.has_below),
-            (1, to < me.z, me.below, me.has_above),
-        ):
-            copy = z_copy(k, side, mate)
-            if k < GRID_Z - 1:
-
-                @pl.when(ahead)
-                def _():
-                    @pl.when(more)
-                    def _():
-                        copy.wait_recv()
-                        add_rows(mine, [(from_z.at[side, to], 0)], whole)
-
-                    copy.start()
-            else:
-
-                @pl.when(more)
-                def _():
-                    copy.wait_recv()
-                    add_rows(mine, [(from_z.at[side, to], 0)], whole)
-
-    for k in range(GRID_Z):
-        across(k)
-        if k:
-            column(k - 1)
-    column(GRID_Z - 1)
-    copy = pltpu.make_async_copy(own.at[3, 0], out, out_s)
-    copy.start()
-    for k in range(GRID_Z):
-        for h in range(2):
-            xs[k][h].wait_send()
-        if k < GRID_Z - 1:
-            to = me.farthest(k)
-            for side, ahead, mate in ((0, to > me.z, me.above), (1, to < me.z, me.below)):
-
-                @pl.when(ahead)
-                def _():
-                    z_copy(k, side, mate).wait_send()
-    for sent in cores.values():
-        sent.wait_send()
-    copy.wait()
-
-
-def scatter_dp(value, collective_id):
-    devices = lax.axis_size("dp")
-    rows, width = value.shape[0] // devices, value.shape[1]
-    dma = pltpu.SemaphoreType.DMA
-    low = value.dtype
-    return pl.pallas_call(
-        plane_scatter_kernel,
-        out_shape=jax.ShapeDtypeStruct((rows, width), low),
-        in_specs=[pl.BlockSpec(memory_space=pl.ANY)],
-        out_specs=pl.BlockSpec(memory_space=pl.ANY),
-        scratch_shapes=[
-            pltpu.VMEM((4, 2, rows, width), low),
-            pltpu.VMEM((4, 2, rows, width), low),
-            pltpu.VMEM((4, rows, width), low),
-            pltpu.VMEM((2, 4, rows, width), low),
-            dma((4, 2)),
-            dma((2, 4, 2)),
-            dma((2, 4, 2)),
-            dma((2, 2, 4)),
-            dma(()),
-        ],
-        compiler_params=pltpu.CompilerParams(
-            collective_id=collective_id, has_side_effects=True, vmem_limit_bytes=VMEM_LIMIT
-        ),
-    )(value.reshape(devices, rows, width))
-
-
 WINDOW_ALIGN = 16
 EXPERT_VMEM = 60 * 1024 * 1024
 
@@ -1494,9 +1270,729 @@
     )(x_pair, packed, live, chosen, cosine, sine)
 
 
-def split_high_low(value):
-    high = value.astype(jnp.bfloat16)
-    return high, (value - high.astype(jnp.float32)).astype(jnp.bfloat16)
+def first_gather_kernel(
+    w_src, d_src, x_src, w_out, d_out, x_out,
+    local_s, pair_s, wz_s, wx_s, wc_s, az_s, ax_s, ay_s, bz_s, bx_s, by_s, dc_s,
+):
+    me = Place()
+    w_half, half = w_src.shape[0] // 2, d_src.shape[0] // 2
+    low, high = pl.ds(0, half), pl.ds(half, half)
+    waits, sent = [], []
+
+    def near(k):
+        return me.farthest(GRID_Z - 1 - k)
+
+    def w_at(k, fx, p):
+        return w_out.at[me.dp_at(near(k), fx, 0), pl.ds(p * w_half, w_half)]
+
+    def d_at(k, fx, fy, rows):
+        return d_out.at[me.dp_at(near(k), fx, 0) * 2 + me.y_at(fy), rows]
+
+    for i, (source, target) in enumerate(
+        (
+            (w_src, w_out.at[me.dp]),
+            (d_src, d_out.at[me.dp * 2 + me.y]),
+            (x_src, x_out.at[me.y]),
+        )
+    ):
+        copy = pltpu.make_async_copy(source, target, local_s.at[i])
+        copy.start()
+        waits.append(copy)
+    me.greet()
+
+    def line(k, source, target, sem, start_only):
+        zn = near(k)
+        for side, came, more, mate in (
+            (0, zn < me.z, me.has_above, me.above),
+            (1, zn > me.z, me.has_below, me.below),
+        ):
+            copy = remote(source, target, sem.at[0, side, zn], sem.at[1, side, zn], mate)
+            if start_only:
+
+                @pl.when(more)
+                def _():
+                    copy.start()
+            else:
+
+                @pl.when(came)
+                def _():
+                    copy.wait_recv()
+
+                    @pl.when(more)
+                    def _():
+                        copy.start()
+
+    def line_done(k, source, target, sem):
+        zn = near(k)
+        for side, came, more, mate in (
+            (0, zn <= me.z, me.has_above, me.above),
+            (1, zn >= me.z, me.has_below, me.below),
+        ):
+            copy = remote(source, target, sem.at[0, side, zn], sem.at[1, side, zn], mate)
+
+            @pl.when(came)
+            def _():
+                @pl.when(more)
+                def _():
+                    copy.wait_send()
+
+    def w_source(k, p):
+        return w_src.at[pl.ds(p * w_half, w_half)] if k == 0 else w_at(k, 0, p)
+
+    def d_source(k, rows):
+        return d_src.at[rows] if k == 0 else d_at(k, 0, 0, rows)
+
+    def go(source, target, sem, index, mate):
+        copy = remote(source, target, sem.at[(0, *index)], sem.at[(1, *index)], mate)
+        copy.start()
+        sent.append(copy)
+        return copy
+
+    def to_core(source, target, sem, index):
+        go(source, target, sem, index, me.sibling)
+
+    wx, ax, ay, by = {}, {}, {}, {}
+
+    def w_own(k, p):
+        line(k, w_source(k, p), w_at(k, 0, p), wz_s.at[p], k == 0)
+        wx[k, p] = go(w_source(k, p), w_at(k, 0, p), wx_s, (k, p), me.x_mate)
+        to_core(w_source(k, p), w_at(k, 0, p), wc_s, (k, 0, p))
+
+    def w_across(k):
+        for p in range(2):
+            wx[k, p].wait_recv()
+            to_core(w_at(k, 1, p), w_at(k, 1, p), wc_s, (k, 1, p))
+
+    def a_own(k):
+        line(k, d_source(k, low), d_at(k, 0, 0, low), az_s, k == 0)
+        ax[k] = go(d_source(k, low), d_at(k, 0, 0, low), ax_s, (k,), me.x_mate)
+        ay[k, 0] = go(d_source(k, low), d_at(k, 0, 0, low), ay_s, (k, 0), me.y_mate)
+        to_core(d_source(k, low), d_at(k, 0, 0, low), dc_s, (k, 0, 0, 0))
+
+    def a_across(k):
+        ax[k].wait_recv()
+        block = d_at(k, 1, 0, low)
+        ay[k, 1] = go(block, block, ay_s, (k, 1), me.y_mate)
+        to_core(block, block, dc_s, (k, 1, 0, 0))
+
+    def b_own(k, fx):
+        source = d_source(k, high) if fx == 0 else d_at(k, 1, 0, high)
+        block = d_at(k, fx, 0, high)
+        line(k, source, block, bz_s.at[fx], k == 0)
+        by[k, fx] = go(source, block, by_s, (k, fx), me.y_mate)
+        to_core(source, block, dc_s, (k, fx, 0, 1))
+
+    def y_done(k):
+        for fx in range(2):
+            for h, (copies, rows) in enumerate(((ay, low), (by, high))):
+                copies[k, fx].wait_recv()
+                block = d_at(k, fx, 1, rows)
+                to_core(block, block, dc_s, (k, fx, 1, h))
+
+    pair = go(x_src, x_out.at[me.y], pair_s, (0,), me.y_mate)
+    for p in range(2):
+        w_own(0, p)
+    bx = go(d_src.at[high], d_at(0, 0, 0, high), bx_s, (0,), me.x_mate)
+    a_own(0)
+    b_own(0, 0)
+    bx.wait_recv()
+    b_own(0, 1)
+    for k in range(1, GRID_Z):
+        for p in range(2):
+            w_own(k, p)
+        a_own(k)
+        for fx in range(2):
+            b_own(k, fx)
+        w_across(k - 1)
+        a_across(k - 1)
+        if k > 1:
+            y_done(k - 2)
+    y_done(GRID_Z - 2)
+    w_across(GRID_Z - 1)
+    a_across(GRID_Z - 1)
+    y_done(GRID_Z - 1)
+    for k in range(GRID_Z):
+        for p in range(2):
+            line_done(k, w_source(k, p), w_at(k, 0, p), wz_s.at[p])
+        line_done(k, d_source(k, low), d_at(k, 0, 0, low), az_s)
+        line_done(k, d_source(k, high), d_at(k, 0, 0, high), bz_s.at[0])
+        line_done(k, d_at(k, 1, 0, high), d_at(k, 1, 0, high), bz_s.at[1])
+    for copy in sent:
+        copy.wait_send()
+    pair.wait_recv()
+    for k in range(GRID_Z):
+        for fx in range(2):
+            for p in range(2):
+                block = w_at(k, fx, p)
+                remote(block, block, wc_s.at[0, k, fx, p], wc_s.at[1, k, fx, p], me.sibling).wait_recv()
+            for fy in range(2):
+                for h, rows in enumerate((low, high)):
+                    block = d_at(k, fx, fy, rows)
+                    remote(
+                        block, block, dc_s.at[0, k, fx, fy, h], dc_s.at[1, k, fx, fy, h], me.sibling
+                    ).wait_recv()
+    for copy in waits:
+        copy.wait()
+
+
+def first_gather(weights, cotangents, inputs, collective_id):
+    chips = lax.axis_size("dp")
+    pair = lax.axis_size("tensor")
+    dma = pltpu.SemaphoreType.DMA
+    low = weights.dtype
+    anywhere = pl.BlockSpec(memory_space=pl.ANY)
+    w, d, x = pl.pallas_call(
+        first_gather_kernel,
+        out_shape=(
+            jax.ShapeDtypeStruct((chips, *weights.shape), low),
+            jax.ShapeDtypeStruct((chips * pair, *cotangents.shape), low),
+            jax.ShapeDtypeStruct((pair, *inputs.shape), low),
+        ),
+        in_specs=[anywhere] * 3,
+        out_specs=(anywhere,) * 3,
+        scratch_shapes=[
+            dma((3,)),
+            dma((2, 1)),
+            dma((2, 2, 2, 4)),
+            dma((2, 4, 2)),
+            dma((2, 4, 2, 2)),
+            dma((2, 2, 4)),
+            dma((2, 4)),
+            dma((2, 4, 2)),
+            dma((2, 2, 2, 4)),
+            dma((2, 1)),
+            dma((2, 4, 2)),
+            dma((2, 4, 2, 2, 2)),
+        ],
+        compiler_params=pltpu.CompilerParams(collective_id=collective_id, has_side_effects=True),
+    )(weights, cotangents, inputs)
+    return (
+        w.reshape(-1, w.shape[2]),
+        d.reshape(chips, -1, d.shape[2]),
+        x.reshape(-1, x.shape[2]),
+    )
+
+
+def unturn(value, cosine, sine):
+    return value * cosine - pltpu.roll(value, HEAD_SIZE // 2, 1) * sine
+
+
+def backward_kernel(
+    experts, back_in, residual_in, sent_in, dy_in, x_in, packed, live, cosine, sine, normed_in,
+    raw_in, query_in, key_in, value_in, context_in,
+    grads, input_gradient,
+    back, residual, sent, dy, x, w, ctx, aux_w, normed, raw, query, key, value, context,
+    cot, context_cot, raw_cot, key_sum, value_sum, small, first, first_got, stage, result,
+    in_s, out_s, y_s, g_s,
+):
+    bf16, f32 = jnp.bfloat16, jnp.float32
+    me = Place()
+    own_rows, features = residual.shape
+    rows = 2 * own_rows
+    heads, key_heads = query.shape[0], key.shape[0]
+    group = heads // key_heads
+    qkv, wide = w.shape[1], heads * HEAD_SIZE
+    chunk = 512
+    mine = pl.ds(pl.multiple_of(me.y * own_rows, own_rows), own_rows)
+    theirs = pl.ds(pl.multiple_of((1 - me.y) * own_rows, own_rows), own_rows)
+    loads = [
+        pltpu.make_async_copy(source, target, in_s.at[i])
+        for i, (source, target) in enumerate(
+            (
+                (packed.at[:, pl.ds(qkv + wide, AUX)], aux_w),
+                (back_in, back),
+                (sent_in, sent),
+                (residual_in, residual),
+                (dy_in, dy),
+                (packed.at[:, pl.ds(qkv, wide)], ctx),
+                (context_in, context),
+                (value_in, value),
+                (key_in, key),
+                (query_in, query),
+                (raw_in, raw),
+                (packed.at[:, pl.ds(0, qkv)], w),
+                (normed_in, normed),
+                (x_in, x),
+            )
+        )
+    ]
+    for copy in loads:
+        copy.start()
+    meet_y(me)
+    for copy in loads[:5]:
+        copy.wait()
+    aux_t = aux_w[...].astype(f32).T
+    gain_one, gain_two, query_gain, key_gain = gain_rows(aux_t, experts, features // HEAD_SIZE)
+
+    lane = lax.broadcasted_iota(jnp.int32, (own_rows, AUX), 1)
+    coded = sent[:, features:].astype(f32)
+    gates = coded + pltpu.roll(coded, AUX - experts, 1)
+    gates = jnp.where(lane < experts, gates, 0.0)
+    column = lax.broadcasted_iota(jnp.int32, (AUX, AUX), 0)
+    target = lax.broadcasted_iota(jnp.int32, (AUX, AUX), 1)
+    fold = ((column % (2 * experts)) // 2 == target).astype(bf16)
+    gate_cot = dot(back[:, features:], fold)
+    logit_cot = gates * (gate_cot - jnp.sum(gates * gate_cot, axis=-1, keepdims=True))
+    logit_cot = logit_cot.astype(bf16)
+    small[...] = dot(sent[:, :features], logit_cot, ((0,), (0,)))
+    midnorm = jnp.zeros((1, features), f32)
+    step = 32
+    for i in range(own_rows // step):
+        at = slice(i * step, (i + 1) * step)
+        total = residual[at, :]
+        scale = inverse_norm(total)
+        unit = total * scale
+        normed_cot = back[at, :features].astype(f32) + dot(
+            logit_cot[at, :], aux_w[...], ((1,), (1,))
+        )
+        midnorm = midnorm + jnp.sum(normed_cot * unit, axis=0, keepdims=True)
+        gained = normed_cot * gain_two
+        total_cot = dy[at, :].astype(f32) + scale * (
+            gained - unit * jnp.mean(gained * unit, axis=-1, keepdims=True)
+        )
+        residual[at, :] = total_cot
+        cot[pl.ds(pl.multiple_of(me.y * own_rows + i * step, step), step), :] = total_cot.astype(bf16)
+    swap = remote(cot.at[mine], cot.at[mine], y_s.at[0, 0], y_s.at[1, 0], me.y_mate)
+    swap.start()
+    for copy in loads[5:10]:
+        copy.wait()
+
+    def spread_context(part):
+        for c in range(wide // chunk):
+            cols = pl.ds(c * chunk, chunk)
+            context_cot[part, cols] = dot(cot[part, :], ctx[:, cols]).astype(bf16)
+
+    spread_context(mine)
+    swap.wait_recv()
+    spread_context(theirs)
+    for copy in loads[10:]:
+        copy.wait()
+
+    turn_c, turn_s = cosine[...], sine[...]
+    allowed = allowed_pairs(live[...])
+    key_sum[...] = jnp.zeros_like(key_sum)
+    value_sum[...] = jnp.zeros_like(value_sum)
+
+    def raw_back(back_rows, unnormed, gain):
+        scale = inverse_norm(unnormed)
+        unit = unnormed * scale
+        part = jnp.sum(back_rows * unit, axis=0, keepdims=True)
+        gained = back_rows * gain
+        raw_rows = scale * (gained - unit * jnp.mean(gained * unit, axis=-1, keepdims=True))
+        return raw_rows.astype(bf16), part
+
+    def head(h, query_part):
+        g = h // group
+        at = pl.ds(pl.multiple_of(h * HEAD_SIZE, HEAD_SIZE), HEAD_SIZE)
+        probs = probabilities(query[h], key[g], allowed)
+        cots = context_cot[:, at]
+        prob_cot = dot(cots, value[g], ((1,), (1,)))
+        score_cot = probs * (prob_cot - jnp.sum(probs * prob_cot, axis=-1, keepdims=True))
+        score_cot = score_cot.astype(bf16)
+        value_sum[g] += dot(probs.astype(bf16), cots, ((0,), (0,)))
+        key_sum[g] += dot(score_cot, query[h], ((0,), (0,)))
+        turned = dot(score_cot, key[g]) * SCORE_SCALE
+        raw_cot[:, at], part = raw_back(unturn(turned, turn_c, turn_s), raw[h], query_gain)
+        return query_part + part
+
+    query_part = lax.fori_loop(0, heads, head, jnp.zeros((1, HEAD_SIZE), f32))
+    key_part = jnp.zeros((1, HEAD_SIZE), f32)
+    for g in range(key_heads):
+        turned = key_sum[g] * SCORE_SCALE
+        at = wide + g * HEAD_SIZE
+        raw_cot[:, at : at + HEAD_SIZE], part = raw_back(
+            unturn(turned, turn_c, turn_s), raw[heads + g], key_gain
+        )
+        key_part = key_part + part
+        at = at + key_heads * HEAD_SIZE
+        raw_cot[:, at : at + HEAD_SIZE] = value_sum[g].astype(bf16)
+
+    copies = []
+    for c in range(features // chunk):
+        cols = pl.ds(c * chunk, chunk)
+        first[:, cols] = dot(raw_cot[theirs, :], w[cols, :], ((1,), (1,))).astype(bf16)
+        copy = remote(
+            first.at[:, cols], first_got.at[:, cols], y_s.at[0, 1 + c], y_s.at[1, 1 + c], me.y_mate
+        )
+        copy.start()
+        copies.append(copy)
+    block = 256
+
+    def store(i):
+        slot = i % 2
+        return pltpu.make_async_copy(
+            stage.at[slot],
+            grads.at[pl.ds(pl.multiple_of(i * block, block), block), pl.ds(0, qkv + wide)],
+            g_s.at[slot],
+        )
+
+    def weight_grads(i, carry):
+        slot = i % 2
+        at = pl.ds(pl.multiple_of(i * block, block), block)
+
+        @pl.when(i >= 2)
+        def _():
+            store(i - 2).wait()
+
+        for c in range(qkv // chunk):
+            cols = pl.ds(c * chunk, chunk)
+            stage[slot, :, cols] = dot(normed[:, at], raw_cot[:, cols], ((0,), (0,))).astype(bf16)
+        for c in range(wide // chunk):
+            cols = pl.ds(c * chunk, chunk)
+            stage[slot, :, pl.ds(qkv + c * chunk, chunk)] = dot(
+                cot[:, at], context[:, cols], ((0,), (0,))
+            ).astype(bf16)
+        store(i).start()
+        return carry
+
+    lax.fori_loop(0, features // block, weight_grads, 0)
+    prenorm = jnp.zeros((1, features), f32)
+    for copy in copies:
+        copy.wait_recv()
+    for c in range(features // chunk):
+        cols = pl.ds(c * chunk, chunk)
+        back_cols = dot(raw_cot[mine, :], w[cols, :], ((1,), (1,)))
+        result_part = back_cols + first_got[:, cols].astype(f32)
+        back[:, cols] = result_part.astype(bf16)
+    step = 32
+    for i in range(own_rows // step):
+        at = slice(i * step, (i + 1) * step)
+        stream = x[pl.ds(pl.multiple_of(me.y * own_rows + i * step, step), step), :].astype(f32)
+        scale = inverse_norm(stream)
+        unit = stream * scale
+        first_cot = back[at, :features].astype(f32)
+        prenorm = prenorm + jnp.sum(first_cot * unit, axis=0, keepdims=True)
+        gained = first_cot * gain_one
+        result[at, :] = (
+            residual[at, :]
+            + scale * (gained - unit * jnp.mean(gained * unit, axis=-1, keepdims=True))
+        ).astype(bf16)
+    done = pltpu.make_async_copy(result, input_gradient, out_s.at[0])
+    done.start()
+    chunks = features // HEAD_SIZE
+    extra = jnp.concatenate(
+        [
+            jnp.zeros((experts, features), f32),
+            prenorm,
+            midnorm,
+            jnp.concatenate([query_part] * chunks, axis=1),
+            jnp.concatenate([key_part] * chunks, axis=1),
+            jnp.zeros((AUX - experts - 4, features), f32),
+        ],
+        axis=0,
+    )
+    aux_w[...] = (small[...] + extra.T).astype(bf16)
+    last = pltpu.make_async_copy(aux_w, grads.at[:, pl.ds(qkv + wide, AUX)], out_s.at[1])
+    last.start()
+    swap.wait_send()
+    for copy in copies:
+        copy.wait_send()
+    for i in (2, 1):
+        store(features // block - i).wait()
+    done.wait()
+    last.wait()
+
+
+def attention_backward(
+    back, residual, sent, dy, x_pair, packed, live, saved, experts, collective_id
+):
+    bf16, f32 = jnp.bfloat16, jnp.float32
+    normed, raw, query, key, value, context = saved
+    own_rows, features = residual.shape
+    rows = 2 * own_rows
+    heads, key_heads = query.shape[0], key.shape[0]
+    wide = heads * HEAD_SIZE
+    qkv = wide + 2 * key_heads * HEAD_SIZE
+    cosine, sine = turn_tables(rows)
+    dma = pltpu.SemaphoreType.DMA
+    anywhere, vmem = pl.BlockSpec(memory_space=pl.ANY), pl.BlockSpec(memory_space=pltpu.VMEM)
+    return pl.pallas_call(
+        functools.partial(backward_kernel, experts),
+        out_shape=(
+            jax.ShapeDtypeStruct((features, qkv + wide + AUX), bf16),
+            jax.ShapeDtypeStruct((own_rows, features), bf16),
+        ),
+        in_specs=[anywhere] * 6 + [vmem] * 3 + [anywhere] * 6,
+        out_specs=(anywhere,) * 2,
+        scratch_shapes=[
+            pltpu.VMEM((own_rows, features + AUX), bf16),
+            pltpu.VMEM((own_rows, features), f32),
+            pltpu.VMEM((own_rows, features + AUX), bf16),
+            pltpu.VMEM((own_rows, features), bf16),
+            pltpu.VMEM((rows, features), bf16),
+            pltpu.VMEM((features, qkv), bf16),
+            pltpu.VMEM((features, wide), bf16),
+            pltpu.VMEM((features, AUX), bf16),
+            pltpu.VMEM((rows, features), bf16),
+            pltpu.VMEM((heads + 2 * key_heads, rows, HEAD_SIZE), f32),
+            pltpu.VMEM((heads, rows, HEAD_SIZE), bf16),
+            pltpu.VMEM((key_heads, rows, HEAD_SIZE), bf16),
+            pltpu.VMEM((key_heads, rows, HEAD_SIZE), bf16),
+            pltpu.VMEM((rows, wide), bf16),
+            pltpu.VMEM((rows, features), bf16),
+            pltpu.VMEM((rows, wide), bf16),
+            pltpu.VMEM((rows, qkv), bf16),
+            pltpu.VMEM((key_heads, rows, HEAD_SIZE), f32),
+            pltpu.VMEM((key_heads, rows, HEAD_SIZE), f32),
+            pltpu.VMEM((features, AUX), f32),
+            pltpu.VMEM((own_rows, features), bf16),
+            pltpu.VMEM((own_rows, features), bf16),
+            pltpu.VMEM((2, 256, qkv + wide), bf16),
+            pltpu.VMEM((own_rows, features), bf16),
+            dma((14,)),
+            dma((2,)),
+            dma((2, 1 + features // 512)),
+            dma((2,)),
+        ],
+        compiler_params=pltpu.CompilerParams(
+            collective_id=collective_id, has_side_effects=True, vmem_limit_bytes=ATTENTION_VMEM
+        ),
+    )(
+        back, residual, sent, dy, x_pair, packed, live, cosine, sine,
+        normed, raw, query, key, value, context,
+    )
+
+
+def last_scatter_kernel(
+    g_part, d_part, g_out, d_out,
+    g_own, g_core, g_x, g_z, d_own, d_core, d_y, a_x, b_x, a_z, b_z, small_got,
+    gl_s, gc_s, gx_s, gz_s, dl_s, dc_s, dy_s, ax_s, bx_s, az_s, bz_s, small_s, out_s,
+):
+    me = Place()
+    g_rows, d_rows = g_own.shape[2], d_own.shape[3]
+    half, g_half = d_rows // 2, g_rows // 2
+    g_all, low, high = (0, g_rows), (0, half), (half, half)
+    low_at, high_at = pl.ds(0, half), pl.ds(half, half)
+    last = GRID_Z - 1
+    loads, cores, sends = {}, {}, []
+
+    def g_chunk(k, fx, fc):
+        return g_part.at[me.dp_at(me.farthest(k), fx, fc)]
+
+    def d_chunk(k, fx, fy, fc):
+        return d_part.at[me.dp_at(me.farthest(k), fx, fc) * 2 + me.y_at(fy)]
+
+    pairs = ((1, 1), (0, 1), (1, 0), (0, 0))
+    for k in range(GRID_Z):
+        for fx in (1, 0):
+            loads[k, fx] = pltpu.make_async_copy(g_chunk(k, fx, 0), g_own.at[k, fx], gl_s.at[k, fx])
+            loads[k, fx].start()
+        for fx, fy in pairs:
+            loads[k, fx, fy] = pltpu.make_async_copy(
+                d_chunk(k, fx, fy, 0), d_own.at[k, fx, fy], dl_s.at[k, fx, fy]
+            )
+            loads[k, fx, fy].start()
+    me.greet()
+    for k in range(GRID_Z):
+        for fx in (1, 0):
+            cores[k, fx] = remote(
+                g_chunk(k, fx, 1), g_core.at[k, fx],
+                gc_s.at[0, k, fx], gc_s.at[1, k, fx], me.sibling,
+            )
+        for fx, fy in pairs:
+            cores[k, fx, fy] = remote(
+                d_chunk(k, fx, fy, 1), d_core.at[k, fx, fy],
+                dc_s.at[0, k, fx, fy], dc_s.at[1, k, fx, fy], me.sibling,
+            )
+        for index in ((1,), (1, 1), (0, 1), (0,), (1, 0), (0, 0)):
+            cores[(k, *index)].start()
+
+    gx = [
+        [
+            remote(
+                g_own.at[k, 1, pl.ds(h * g_half, g_half)], g_x.at[k, pl.ds(h * g_half, g_half)],
+                gx_s.at[0, k, h], gx_s.at[1, k, h], me.x_mate,
+            )
+            for h in range(2)
+        ]
+        for k in range(GRID_Z)
+    ]
+    dy = {
+        (k, fx): remote(
+            d_own.at[k, fx, 1], d_y.at[k, fx], dy_s.at[0, k, fx], dy_s.at[1, k, fx], me.y_mate
+        )
+        for k in range(GRID_Z)
+        for fx in range(2)
+    }
+    ax = [
+        remote(d_own.at[k, 1, 0, low_at], a_x.at[k], ax_s.at[0, k], ax_s.at[1, k], me.x_mate)
+        for k in range(GRID_Z)
+    ]
+    bx = remote(d_own.at[last, 1, 0, high_at], b_x, bx_s.at[0], bx_s.at[1], me.x_mate)
+
+    def arrive(*index):
+        loads[index].wait()
+        cores[index].wait_recv()
+
+    def onward(source, buffer, sem, to, side, mate):
+        ends = 1 - (me.z - 1 - to + GRID_Z - 1) // GRID_Z
+        slot = to if side == 0 else to + (GRID_Z - to) * ends
+        return remote(source, buffer.at[slot], sem.at[0, to], sem.at[1, slot], mate)
+
+    def line(k, block, source, rows, buffer, sem, shift):
+        to = me.farthest(k)
+        for side, ahead, mate, more in (
+            (0, to > me.z, me.above, me.has_below),
+            (1, to < me.z, me.below, me.has_above),
+        ):
+            slot = to if k < last or side == 0 else GRID_Z
+            came = remote(source, buffer.at[slot], sem.at[0, slot], sem.at[1, slot], mate)
+
+            def gather(came=came, slot=slot):
+                came.wait_recv()
+                add_rows(block, [(buffer.at[slot], shift)], rows)
+
+            if k < last:
+
+                @pl.when(ahead)
+                def _():
+                    pl.when(more)(gather)
+                    onward(source, buffer, sem, to, side, mate).start()
+            else:
+                pl.when(more)(gather)
+
+    def line_done(k, source, buffer, sem):
+        to = me.farthest(k)
+        for side, ahead, mate in ((0, to > me.z, me.above), (1, to < me.z, me.below)):
+
+            @pl.when(ahead)
+            def _():
+                onward(source, buffer, sem, to, side, mate).wait_send()
+
+    def across(k):
+        arrive(k, 1)
+        for h in range(2):
+            add_rows(g_own.at[k, 1], [(g_core.at[k, 1], 0)], (h * g_half, g_half))
+            gx[k][h].start()
+
+    def over_y(k):
+        for fx in (1, 0):
+            arrive(k, fx, 1)
+            add_rows(d_own.at[k, fx, 1], [(d_core.at[k, fx, 1], 0)], (0, d_rows))
+            dy[k, fx].start()
+
+    def column(k):
+        arrive(k, 0)
+        for h in range(2):
+            gx[k][h].wait_recv()
+        add_rows(g_own.at[k, 0], [(g_core.at[k, 0], 0), (g_x.at[k], 0)], g_all)
+        line(k, g_own.at[k, 0], g_own.at[k, 0], g_all, g_z, gz_s, 0)
+
+    def merge(k):
+        for fx in (1, 0):
+            arrive(k, fx, 0)
+            dy[k, fx].wait_recv()
+            block = d_own.at[k, fx, 0]
+            if fx:
+                add_rows(block, [(d_core.at[k, fx, 0], 0), (d_y.at[k, fx], 0)], low)
+                ax[k].start()
+                add_rows(block, [(d_core.at[k, fx, 0], 0), (d_y.at[k, fx], 0)], high)
+            else:
+                add_rows(block, [(d_core.at[k, fx, 0], 0), (d_y.at[k, fx], 0)], (0, d_rows))
+            line(k, block, block.at[high_at], high, b_z.at[fx], bz_s.at[fx], half)
+            if fx and k == last:
+                bx.start()
+
+    def settle(k):
+        ax[k].wait_recv()
+        block = d_own.at[k, 0, 0]
+        add_rows(block, [(a_x.at[k], 0)], low)
+        line(k, block, block.at[low_at], low, a_z, az_s, 0)
+
+    for k in range(GRID_Z):
+        across(k)
+        over_y(k)
+        if k >= 1:
+            column(k - 1)
+            merge(k - 1)
+        if k >= 2:
+            settle(k - 2)
+    merge(last)
+    column(last)
+    settle(last - 1)
+    width = g_own.shape[3]
+    small = remote(
+        g_own.at[last, 0, :, pl.ds(width - AUX, AUX)], small_got,
+        small_s.at[0], small_s.at[1], me.y_mate,
+    )
+    small.start()
+    settle(last)
+    bx.wait_recv()
+    add_rows(d_own.at[last, 0, 0], [(b_x, half)], high)
+    outs = [pltpu.make_async_copy(d_own.at[last, 0, 0], d_out, out_s.at[0])]
+    outs[0].start()
+    small.wait()
+    block = g_own.at[last, 0, :, pl.ds(width - AUX, AUX)]
+    block[...] = (block[...].astype(jnp.float32) + small_got[...].astype(jnp.float32)).astype(
+        block.dtype
+    )
+    outs.append(pltpu.make_async_copy(g_own.at[last, 0], g_out, out_s.at[1]))
+    outs[1].start()
+    for k in range(GRID_Z):
+        for h in range(2):
+            gx[k][h].wait_send()
+        for fx in range(2):
+            dy[k, fx].wait_send()
+        ax[k].wait_send()
+        if k < last:
+            line_done(k, g_own.at[k, 0], g_z, gz_s)
+            for fx in range(2):
+                line_done(k, d_own.at[k, fx, 0, high_at], b_z.at[fx], bz_s.at[fx])
+            line_done(k, d_own.at[k, 0, 0, low_at], a_z, az_s)
+    bx.wait_send()
+    for sent in cores.values():
+        sent.wait_send()
+    for copy in outs:
+        copy.wait()
+
+
+def last_scatter(grads, sums, collective_id):
+    chips, pair = lax.axis_size("dp"), lax.axis_size("tensor")
+    g_rows, g_wide = grads.shape[0] // chips, grads.shape[1]
+    d_rows, d_wide = sums.shape[0] // (chips * pair), sums.shape[1]
+    half = d_rows // 2
+    dma = pltpu.SemaphoreType.DMA
+    low = grads.dtype
+    anywhere = pl.BlockSpec(memory_space=pl.ANY)
+    return pl.pallas_call(
+        last_scatter_kernel,
+        out_shape=(
+            jax.ShapeDtypeStruct((g_rows, g_wide), low),
+            jax.ShapeDtypeStruct((d_rows, d_wide), low),
+        ),
+        in_specs=[anywhere] * 2,
+        out_specs=(anywhere,) * 2,
+        scratch_shapes=[
+            pltpu.VMEM((4, 2, g_rows, g_wide), low),
+            pltpu.VMEM((4, 2, g_rows, g_wide), low),
+            pltpu.VMEM((4, g_rows, g_wide), low),
+            pltpu.VMEM((5, g_rows, g_wide), low),
+            pltpu.VMEM((4, 2, 2, d_rows, d_wide), low),
+            pltpu.VMEM((4, 2, 2, d_rows, d_wide), low),
+            pltpu.VMEM((4, 2, d_rows, d_wide), low),
+            pltpu.VMEM((4, half, d_wide), low),
+            pltpu.VMEM((half, d_wide), low),
+            pltpu.VMEM((5, half, d_wide), low),
+            pltpu.VMEM((2, 5, half, d_wide), low),
+            pltpu.VMEM((g_rows, AUX), low),
+            dma((4, 2)),
+            dma((2, 4, 2)),
+            dma((2, 4, 2)),
+            dma((2, 5)),
+            dma((4, 2, 2)),
+            dma((2, 4, 2, 2)),
+            dma((2, 4, 2)),
+            dma((2, 4)),
+            dma((2,)),
+            dma((2, 5)),
+            dma((2, 2, 5)),
+            dma((2,)),
+            dma((2,)),
+        ],
+        compiler_params=pltpu.CompilerParams(
+            collective_id=collective_id, has_side_effects=True, vmem_limit_bytes=60 * 1024 * 1024
+        ),
+    )(grads.reshape(chips, g_rows, g_wide), sums.reshape(chips * pair, d_rows, d_wide))
 
 
 def gathered_body(
@@ -1535,13 +2031,15 @@
     norm_part = HEAD_SIZE // dp_count
 
     place = dp_index * norm_part
+    route_wide = block_rows * TOP // shard
     gains = jnp.concatenate(
         [
             prenorm_gain[:, None],
             midnorm_gain[:, None],
             lax.dynamic_update_slice(jnp.zeros((shard,), bf16), querynorm_gain, (place,))[:, None],
             lax.dynamic_update_slice(jnp.zeros((shard,), bf16), keynorm_gain, (place,))[:, None],
-            jnp.zeros((shard, AUX - expert_count - 4), bf16),
+            routes.T.reshape(shard, -1).astype(bf16),
+            jnp.zeros((shard, AUX - expert_count - 4 - route_wide), bf16),
         ],
         axis=1,
     )
@@ -1549,21 +2047,10 @@
         [query_weight, key_projection, value_projection, context_weight.T, router_weight, gains],
         axis=1,
     )
-    packed = gather_dp(packed, 0)
-    edges = [0]
-    for width in (query_width, key_width, key_width, query_width, expert_count, AUX - expert_count):
-        edges.append(edges[-1] + width)
-    qkv_all = packed[:, : edges[3]]
-    context_all = packed[:, edges[3] : edges[4]]
-    router_all = packed[:, edges[4] : edges[5]]
-    gains_all = packed[:, edges[5] :].astype(f32)
-    gain_one, gain_two = gains_all[:, 0], gains_all[:, 1]
-    query_factor = jnp.sum(gains_all[:, 2].reshape(dp_count, shard), axis=0)
-    key_factor = jnp.sum(gains_all[:, 3].reshape(dp_count, shard), axis=0)
-
-    cot_all = lax.all_gather(output_cotangent, ("dp", "tensor"), axis=0, tiled=True)
-    routes_all = lax.all_gather(routes.T, "dp")
-    input_rows = lax.all_gather(layer_input, "tensor", axis=0, tiled=True)
+    packed, cot_all, input_rows = first_gather(packed, output_cotangent, layer_input, 0)
+    route_from = packed.shape[1] - AUX + expert_count + 4
+    routes_all = packed[:, route_from : route_from + route_wide].astype(jnp.int32)
+    routes_all = routes_all.reshape(dp_count, TOP, block_rows)
     position = jnp.arange(block_rows, dtype=jnp.int32)
     block_lengths = lengths[sequence_order]
     live = position[None, :] < block_lengths[:, None]
@@ -1571,53 +2058,14 @@
     live_own = jnp.broadcast_to(live_own.astype(f32), (8, block_rows))
     heads_query = query_width // HEAD_SIZE
     heads_key = key_width // HEAD_SIZE
-    group_width = heads_query // heads_key
     row_start = tensor_index * own_rows
     routes_own = lax.dynamic_slice_in_dim(routes, row_start, own_rows, 0)
     expert_ids = jnp.arange(AUX, dtype=jnp.int32)
     chosen = jnp.any(routes_own[:, :, None] == expert_ids[None, None, :], axis=1).astype(f32)
-    (
-        sent,
-        residual,
-        first_normed,
-        raw,
-        query_heads,
-        key_heads,
-        value_heads,
-        context,
-    ) = attention_forward(
+    sent, residual, *saved = attention_forward(
         input_rows, packed, live_own, chosen, expert_count, heads_query, heads_key, 5
     )
     normed_all = gather_all(sent, 1).reshape(dp_count, block_rows, features + AUX)
-
-    cosine_table, sine_values = turn_tables(block_rows)
-    cosine_table = cosine_table[:, None, : HEAD_SIZE // 2]
-    sine_values = sine_values[:, None, HEAD_SIZE // 2 :]
-    unit_first, scale_first = rms_normalize(input_rows.astype(f32))
-    rows_first = raw.transpose(1, 0, 2)
-    query_unit, query_scale = rms_normalize(rows_first[:, :heads_query])
-    key_unit, key_scale = rms_normalize(rows_first[:, heads_query : heads_query + heads_key])
-    query_rows = query_heads.transpose(1, 0, 2).reshape(
-        block_rows, heads_key, group_width, HEAD_SIZE
-    )
-    keys_rot = key_heads.transpose(1, 0, 2)
-    value_rows = value_heads.transpose(1, 0, 2)
-    score_scale = SCORE_SCALE
-    allowed = (position[None, :] <= position[:, None]) & (live_own[0:1] > 0.0)
-    scores = (
-        jnp.einsum("ikrd,jkd->krij", query_rows, keys_rot, preferred_element_type=f32)
-        * score_scale
-    )
-    scores = jnp.where(allowed, scores, masked_score)
-    weights = jnp.exp(scores - jnp.max(scores, axis=-1, keepdims=True))
-    soft_probs = weights / jnp.sum(weights, axis=-1, keepdims=True)
-    probs_low = soft_probs.astype(bf16)
-    unit_second, scale_second = rms_normalize(residual)
-    normed_second = sent[:, :features]
-    gates = (
-        sent[:, features : features + expert_count].astype(f32)
-        + sent[:, features + expert_count : features + 2 * expert_count].astype(f32)
-    )
 
     expert_own = dp_index * EXP_DEV + jnp.arange(EXP_DEV, dtype=jnp.int32)
     hot = jnp.any(routes_all[:, None, :, :] == expert_own[None, :, None, None], axis=2)
@@ -1635,103 +2083,49 @@
         info.astype(jnp.int32),
         slot,
         normed_all,
-        cot_all.reshape(dp_count, block_rows, features),
+        cot_all,
         expert_gate,
         expert_up,
         expert_down,
         capacity,
         most_rows,
     )
-    returned = scatter_all(back_part.reshape(tokens, features + AUX), 3).astype(f32)
-    expert_sum = scatter_all(out_part.reshape(tokens, features), 2)
+    returned = scatter_all(back_part.reshape(tokens, features + AUX), 3)
+    grads, input_gradient = attention_backward(
+        returned,
+        residual,
+        sent,
+        output_cotangent,
+        input_rows,
+        packed,
+        live_own,
+        saved,
+        expert_count,
+        6,
+    )
+    summed, expert_sum = last_scatter(grads, out_part.reshape(tokens, features), 4)
+    summed = summed.astype(f32)
     layer_output = (residual + expert_sum.astype(f32)).astype(bf16)
-
-    gate_cot = jnp.sum(
-        returned[:, features:].reshape(own_rows, tensor_count, expert_count, 2), axis=(1, 3)
-    )
-    logit_cot = (
-        gates * (gate_cot - jnp.sum(gates * gate_cot, axis=-1, keepdims=True))
-    ).astype(bf16)
-    router_part = contract(normed_second, logit_cot)
-    normed_cot = returned[:, :features] + transposed(logit_cot, router_all)
-    midnorm_part = jnp.sum(normed_cot * unit_second, axis=0)
-    residual_cot = output_cotangent.astype(f32) + norm_back(
-        normed_cot * gain_two, unit_second, scale_second
-    )
-    attention_cot = lax.all_gather(residual_cot.astype(bf16), "tensor", axis=0, tiled=True)
-
-    context_part = contract(attention_cot, context)
-    context_cot = (
-        matrix_product(attention_cot, context_all)
-        .astype(bf16)
-        .reshape(block_rows, heads_key, group_width, HEAD_SIZE)
-    )
-    prob_cot = jnp.einsum("ikrd,jkd->krij", context_cot, value_rows, preferred_element_type=f32)
-    score_cot = (
-        soft_probs * (prob_cot - jnp.sum(soft_probs * prob_cot, axis=-1, keepdims=True))
-    ).astype(bf16)
-    value_cot = jnp.einsum("krij,ikrd->jkd", probs_low, context_cot, preferred_element_type=f32)
-    value_cot = value_cot.astype(bf16).reshape(block_rows, key_width)
-    query_turned = (
-        jnp.einsum("krij,jkd->ikrd", score_cot, keys_rot, preferred_element_type=f32).reshape(
-            block_rows, heads_query, HEAD_SIZE
-        )
-        * score_scale
-    )
-    key_turned = (
-        jnp.einsum("krij,ikrd->jkd", score_cot, query_rows, preferred_element_type=f32)
-        * score_scale
-    )
-    query_back = rotary_apply(query_turned, cosine_table, -sine_values)
-    key_back = rotary_apply(key_turned, cosine_table, -sine_values)
-    querynorm_part = jnp.sum(query_back * query_unit, axis=(0, 1))
-    keynorm_part = jnp.sum(key_back * key_unit, axis=(0, 1))
-    query_raw_cot = norm_back(query_back * query_factor, query_unit, query_scale).astype(bf16)
-    key_raw_cot = norm_back(key_back * key_factor, key_unit, key_scale).astype(bf16)
-    raw_cot = jnp.concatenate(
-        [
-            query_raw_cot.reshape(block_rows, query_width),
-            key_raw_cot.reshape(block_rows, key_width),
-            value_cot,
-        ],
-        axis=1,
-    )
-    qkv_part = contract(first_normed, raw_cot)
-    first_cot = lax.psum_scatter(
-        transposed(raw_cot, qkv_all).astype(bf16), "tensor", scatter_dimension=0, tiled=True
-    ).astype(f32)
-    unit_own = lax.dynamic_slice_in_dim(unit_first, row_start, own_rows, 0)
-    scale_own = lax.dynamic_slice_in_dim(scale_first, row_start, own_rows, 0)
-    prenorm_part = jnp.sum(first_cot * unit_own, axis=0)
-    input_gradient = (
-        residual_cot + norm_back(first_cot * gain_one, unit_own, scale_own)
-    ).astype(bf16)
-
-    small = jnp.zeros((dp_count, shard, AUX), f32)
-    small = small.at[:, :, :expert_count].set(router_part.reshape(dp_count, shard, expert_count))
-    small = small.at[:, :, expert_count].set(prenorm_part.reshape(dp_count, shard))
-    small = small.at[:, :, expert_count + 1].set(midnorm_part.reshape(dp_count, shard))
-    small = small.at[:, :norm_part, expert_count + 2].set(querynorm_part.reshape(dp_count, -1))
-    small = small.at[:, :norm_part, expert_count + 3].set(keynorm_part.reshape(dp_count, -1))
-    small = lax.psum_scatter(small.reshape(features, AUX), "dp", scatter_dimension=0, tiled=True)
-    small = lax.psum(small, "tensor")
-    summed = scatter_dp(jnp.concatenate([qkv_part.astype(bf16), context_part.astype(bf16)], axis=1), 4)
-    summed = summed.astype(f32)
+    ends = [0]
+    for width in (query_width, key_width, key_width, query_width, AUX):
+        ends.append(ends[-1] + width)
+    small = summed[:, ends[4] :]
+    head_small = lax.dynamic_slice_in_dim(small, place, norm_part, 0)
     return (
         layer_output,
         input_gradient,
-        summed[:, : edges[1]],
-        summed[:, edges[1] : edges[2]],
-        summed[:, edges[2] : edges[3]],
-        summed[:, edges[3] :].T,
+        summed[:, : ends[1]],
+        summed[:, ends[1] : ends[2]],
+        summed[:, ends[2] : ends[3]],
+        summed[:, ends[3] : ends[4]].T,
         small[:, :expert_count],
         gate_gradient,
         up_gradient,
         down_gradient,
         small[:, expert_count],
         small[:, expert_count + 1],
-        small[:norm_part, expert_count + 2],
-        small[:norm_part, expert_count + 3],
+        head_small[:, expert_count + 2],
+        head_small[:, expert_count + 3],
     )
 
 

time: 875 us -> 678 us (0.77)
  other arithmetic: 48.6 us -> 9.11 us
  matrix products: 39.4 us -> 0.15 us
  waiting for transfers between devices: 36.9 us -> 0 us
  Pallas kernels: 670 us -> 639 us
  blocking collectives: 17.8 us -> 0 us
  local copies, waits for them, and re-layouts: 37.5 us -> 21 us
  between operations: 15.3 us -> 0.87 us
    pallas_call x2 -> x1, Pallas kernels: 176 us -> 85 us  [scatter_all(): pl.pallas_call(scatter_kernel, out_shape=jax.ShapeDtypeStruct((rows, widt...]
    pallas_call x2 -> x3, Pallas kernels: 304 us -> 364 us  [the longest x1 158 us: last_scatter(): pl.pallas_call(last_scatter_kernel, out_shape=(jax.ShapeDtypeStruct((g_ro...]
    dot_general x10 -> x0, matrix products: 34.5 us -> none  [the longest x3 14.4 us: contract(): lax.dot_general(former, latter, (((0,), (0,)), ((), ())), preferred_eleme...]
    psum x1 -> x0, waiting for transfers between devices: 18 us -> none  [gathered_body(): small = lax.psum(small, 'tensor')]
    all_gather x1 -> x0, blocking collectives: 17.8 us -> none  [gathered_body(): routes_all = lax.all_gather(routes.T, 'dp')]
    all_gather x3 -> x0, waiting for transfers between devices: 17.4 us -> none  [the longest x1 17.4 us: gathered_body(): lax.all_gather(residual_cot.astype(bf16), 'tensor', axis=0, tiled=True)]
    concatenate x1 -> x0, other arithmetic: 16.4 us -> none  [gathered_body(): jnp.concatenate([qkv_part.astype(bf16), context_part.astype(bf16)], axis=1)]
    convert_element_type x8 -> x2, other arithmetic: 13.8 us -> 2.72 us  [the longest x1 2.02 us: gathered_body(): layer_output = (residual + expert_sum.astype(f32)).astype(bf16)]
  transfers between devices with their start and end apart: 6 -> 0, of which waited for: 2 -> 0; matrix products, arithmetic and copies ran while one was open for 7% -> 0% of each run, Pallas kernels for 59% -> 0%
where the time goes in v5:
time: 678 us; the launch traced here: 670 us
  Pallas kernels  639 us (94%)
  local copies, waits for them, and re-layouts  21 us (3%)
  other arithmetic  9.11 us (1%)
    pallas_call x1, Pallas kernels, last_scatter(): pl.pallas_call(last_scatter_kernel, out_shape=(jax.ShapeDtypeStruct((g_ro...  158 us
    pallas_call x1, Pallas kernels, first_gather(): pl.pallas_call(first_gather_kernel, out_shape=(jax.ShapeDtypeStruct((chip...  157 us
    pallas_call x1, Pallas kernels, scatter_all(): pl.pallas_call(scatter_kernel, out_shape=jax.ShapeDtypeStruct((rows, widt...  85 us
    pallas_call x1, Pallas kernels, gather_all(): pl.pallas_call(gather_kernel, out_shape=jax.ShapeDtypeStruct((devices, ro...  78.4 us
    pallas_call x1, Pallas kernels, expert_layer(): pl.pallas_call(expert_kernel, out_shape=(shape((blocks, block_rows, featu...  73.3 us
    pallas_call x1, Pallas kernels, attention_backward(): pl.pallas_call(functools.partial(backward_kernel, experts), out_shape=(ja...  48.8 us
    pallas_call x1, Pallas kernels, attention_forward(): pl.pallas_call(functools.partial(forward_kernel, experts), out_shape=tupl...  38.3 us

profile of v5, /device:TPU:0, one launch (start us, length us, event | category | flops | bytes accessed | tf_op | source)
XLA Modules:
  0.0 670.0 jit_solution(9297695076320993694)
XLA Ops:
  0.7 0.7 compare_select_fusion
  1.3 0.7 copy.87
  2.1 0.7 copy.88
  2.8 0.7 gather_fusion
  3.6 0.7 constant_dynamic-slice_fusion.1
  4.3 0.7 convert_bitcast_fusion
  5.7 0.8 copy.89
  6.5 0.8 copy.90
  7.3 0.8 copy.91
  8.5 0.6 convert_element_type.38.chosen
  9.1 1.2 copy.86
  10.4 2.9 concatenate.6.w_src
  13.3 156.7 %shard_map.308 = (bf16[16,128,4736]{2,1,0:T(8,128)(2,1)}, bf16[32,128,2048]{2,1,0:T(8,128)(2,1)}, bf16[2,128,2048]{2,1,0:T(8,128)(2,1)}) custom-call(bf16[128,4736]{1,0:T(8,128)(2,1)} %concatenate.6.w_src, bf16[128,2048]{1,0:T(8,128)(2,1)} %dy_in.1, bf16[128,2048]{1,0:T(8,128)(2,1)} %x_src.1), custom_call_target="tpu_custom_call" | custom-call | tf_op jit(solution)/shard_map/pallas_call | solution.py:1444
  170.0 1.3 slice_convert_fusion
  174.0 0.7 and_select_fusion.pos
  174.7 38.3 %shard_map.309 = (bf16[128,2176]{1,0:T(8,128)(2,1)}, f32[128,2048]{1,0:T(8,128)}, bf16[256,2048]{1,0:T(8,128)(2,1)}, f32[20,256,128]{2,1,0:T(8,128)}, bf16[16,25...) custom-call(bf16[256,2048]{1,0:T(8,128)(2,1)} %bitcast.33, ...), custom_call_target="tpu_custom_call" | custom-call | tf_op jit(solution)/shard_map/pallas_call | solution.py:1242
  213.0 78.4 %shard_map.310 = bf16[32,128,2176]{2,1,0:T(8,128)(2,1)} custom-call(bf16[128,2176]{1,0:T(8,128)(2,1)} %get-tuple-element.37.src.sent_in), custom_call_target="tpu_custom_call" | custom-call | tf_op jit(solution)/shard_map/pallas_call | solution.py:779
  291.3 73.3 %shard_map.311 = (bf16[16,256,2048]{2,1,0:T(8,128)(2,1)}, bf16[16,256,2176]{2,1,0:T(8,128)(2,1)}, f32[2,2048,384]{2,1,0:T(8,128)}, f32[2,2048,384]{2,1,0:T(8,128)}, f32[2,384,2048]{2,1,0:T(8,128)}) custom-call(s32[34]{0:T(128)} %pad_add_fusion.info, s32[16,2,256]{2,1,0:T(2,128)} %and_select_fusion.pos, bf16[16,256,2176]{2,1,0:T(8,128)(2,1)} %bitcast.28, ...), custom_call_target="tpu_custom_call" | custom-call | tf_op jit(solution)/shard_map/pallas_call | solution.py:1017
  364.7 85.0 %shard_map.312.back_in = bf16[128,2176]{1,0:T(8,128)(2,1)} custom-call(bf16[32,128,2176]{2,1,0:T(8,128)(2,1)} %bitcast.30), custom_call_target="tpu_custom_call" | custom-call | tf_op jit(solution)/shard_map/pallas_call | solution.py:628
  449.7 48.8 %shard_map.313 = (bf16[2048,4736]{1,0:T(8,128)(2,1)}, bf16[128,2048]{1,0:T(8,128)(2,1)}) custom-call(bf16[128,2176]{1,0:T(8,128)(2,1)} %shard_map.312.back_in, f32[128,2048]{1,0:T(8,128)} %get-tuple-element.36.residual_in, bf16[128,2176]{1,0:T(8,128)(2,1)} %get-tuple-element.37.src.sent_in, bf16[128,2048]{1,0:T(8,128)(2,1)} %dy_in.1, ...), custom_call_target="tpu_custom_call" | custom-call | tf_op jit(solution)/shard_map/pallas_call | solution.py:1709
  498.5 158.4 %shard_map.314 = (bf16[128,4736]{1,0:T(8,128)(2,1)}, bf16[128,2048]{1,0:T(8,128)(2,1)}) custom-call(bf16[16,128,4736]{2,1,0:T(8,128)(2,1)} %bitcast.29, bf16[32,128,2048]{2,1,0:T(8,128)(2,1)} %bitcast.32), custom_call_target="tpu_custom_call" | custom-call | tf_op jit(solution)/shard_map/pallas_call | solution.py:1957
  657.0 2.0 add_convert_fusion
  659.0 0.8 slice.64
  659.7 0.7 copy.102
  660.4 0.8 slice.67
  661.2 0.7 slice_reduce_fusion.2
  661.9 1.6 fusion.9
  663.5 2.1 slice.60
  665.6 1.4 convert_element_type.43
  667.1 0.7 slice_reduce_fusion
  667.9 1.3 copy.101
  669.2 0.8 copy.113
  (40 shorter events, 3.9 us)
Async XLA Ops:
  0.6 2.2 copy-start
  498.5 158.4 %copy-start.2 = (f32[128,2048]{1,0:T(8,128)S(1)}, f32[128,2048]{1,0:T(8,128)}, u32[]{:S(2)}) copy-start(f32[128,2048]{1,0:T(8,128)} %get-tuple-element.36.residual_in) | copy-start | bytes 3145732
  656.9 12.3 %copy-start.3 = (bf16[128,2048]{1,0:T(8,128)(2,1)S(1)}, bf16[128,2048]{1,0:T(8,128)(2,1)}, u32[]{:S(2)}) copy-start(bf16[128,2048]{1,0:T(8,128)(2,1)} %get-tuple-element.133) | copy-start | bytes 1572868
  656.9 13.0 %copy-start.1 = (s32[16]{0:T(128)S(1)}, s32[16]{0:T(128)}, u32[]{:S(2)}) copy-start(s32[16]{0:T(128)} %param.35) | copy-start | bytes 196

commit v6 on v5

--- a/solution.py
+++ b/solution.py
@@ -1100,190 +1100,40 @@
     return (sooner <= later) & (live[0:1, :] > 0.0)
 
 
-def forward_kernel(
-    experts, x_pair, packed, live, chosen, cosine, sine,
+OPENING_PLAN = (
+    ("bx",), ("w", 0, 0), ("w", 1, 0), ("ay0",), ("a", 0), ("w", 2, 0), ("pair",), ("a", 1),
+    ("b", 0, 0), ("wx", 1, 0), ("a", 2), ("ax", 0), ("w", 3, 0), ("wx", 0, 0), ("b", 1, 0),
+    ("w", 0, 1), ("ax", 1), ("a", 3), ("wx", 2, 0), ("w", 1, 1), ("wx", 3, 0), ("ax", 2),
+    ("prep",), ("w", 2, 1), ("b", 0, 1), ("b", 2, 0), ("wx", 0, 1), ("qkv",), ("h", 0),
+    ("ax", 3), ("w", 3, 1), ("y", 0), ("b", 1, 1), ("h", 1), ("b", 2, 1), ("h", 2), ("b", 3, 0),
+    ("wx", 1, 1), ("wx", 2, 1), ("h", 3), ("b", 3, 1), ("wx", 3, 1), ("y", 1), ("ctx",),
+    ("ctx2",), ("y", 2), ("y", 3), ("fin",),
+)
+
+
+def opening_kernel(
+    experts, qkv,
+    w_src, d_src, x_src, live, chosen, cosine, sine,
+    w_out, d_out, x_out,
     sent_o, residual_o, normed_o, raw_o, query_o, key_o, value_o, context_o,
     x, w, ctx, aux_w, normed, raw, query, key, value, context, att, got, residual, sent,
+    local_s, pair_s, wz_s, wx_s, wc_s, az_s, ax_s, ay_s, bz_s, bx_s, by_s, dc_s,
     in_s, w_s, out_s, y_s,
 ):
     bf16, f32 = jnp.bfloat16, jnp.float32
     me = Place()
-    rows, features = x.shape
-    own_rows = rows // 2
-    heads, key_heads = query.shape[0], key.shape[0]
-    qkv = w.shape[1]
-    chunk = 512
-    mine = pl.ds(pl.multiple_of(me.y * own_rows, own_rows), own_rows)
-    theirs = pl.ds(pl.multiple_of((1 - me.y) * own_rows, own_rows), own_rows)
-    loads = [
-        pltpu.make_async_copy(x_pair, x, in_s.at[0]),
-        pltpu.make_async_copy(
-            packed.at[:, pl.ds(qkv + ctx.shape[1], AUX)], aux_w, in_s.at[1]
-        ),
-        pltpu.make_async_copy(packed.at[:, pl.ds(qkv, ctx.shape[1])], ctx, in_s.at[2]),
-    ]
-    parts = [
-        pltpu.make_async_copy(
-            packed.at[:, pl.ds(c * chunk, chunk)], w.at[:, pl.ds(c * chunk, chunk)], w_s.at[c]
-        )
-        for c in range(qkv // chunk)
-    ]
-    loads[0].start()
-    loads[1].start()
-    for copy in parts:
-        copy.start()
-    loads[2].start()
-    meet_y(me)
-    loads[1].wait()
-    aux_t = aux_w[...].astype(f32).T
-    gain_one, gain_two, query_gain, key_gain = gain_rows(aux_t, experts, features // HEAD_SIZE)
-    loads[0].wait()
-
-    def first_norm(i, carry):
-        at = pl.ds(pl.multiple_of(i * 32, 32), 32)
-        stream = x[at, :].astype(f32)
-        normed[at, :] = (stream * inverse_norm(stream) * gain_one).astype(bf16)
-        return carry
-
-    lax.fori_loop(0, rows // 32, first_norm, 0)
-    for c, copy in enumerate(parts):
-        copy.wait()
-        got_raw = dot(normed[...], w[:, c * chunk : (c + 1) * chunk])
-        for h in range(chunk // HEAD_SIZE):
-            raw[c * (chunk // HEAD_SIZE) + h] = got_raw[:, h * HEAD_SIZE : (h + 1) * HEAD_SIZE]
-    turn_c, turn_s = cosine[...], sine[...]
-    for g in range(key_heads):
-        unnormed = raw[heads + g]
-        key[g] = turn(unnormed * inverse_norm(unnormed) * key_gain, turn_c, turn_s).astype(bf16)
-        value[g] = raw[heads + key_heads + g].astype(bf16)
-    allowed = allowed_pairs(live[...])
-
-    def head(h, carry):
-        g = h // (heads // key_heads)
-        unnormed = raw[h]
-        turned = turn(unnormed * inverse_norm(unnormed) * query_gain, turn_c, turn_s).astype(bf16)
-        query[h] = turned
-        probs = probabilities(turned, key[g], allowed).astype(bf16)
-        at = pl.ds(pl.multiple_of(h * HEAD_SIZE, HEAD_SIZE), HEAD_SIZE)
-        context[:, at] = dot(probs, value[g]).astype(bf16)
-        return carry
-
-    lax.fori_loop(0, heads, head, 0)
-    outs = [
-        pltpu.make_async_copy(source, target, out_s.at[i])
-        for i, (source, target) in enumerate(
-            ((normed, normed_o), (raw, raw_o), (query, query_o), (key, key_o), (value, value_o),
-             (context, context_o))
-        )
-    ]
-    for copy in outs:
-        copy.start()
-    loads[2].wait()
-    copies = []
-    for c in range(features // chunk):
-        cols = pl.ds(c * chunk, chunk)
-        att[theirs, cols] = dot(context[theirs, :], ctx[cols, :], ((1,), (1,))).astype(bf16)
-        copy = remote(
-            att.at[theirs, cols], got.at[:, cols], y_s.at[0, c], y_s.at[1, c], me.y_mate
-        )
-        copy.start()
-        copies.append(copy)
-    for c in range(features // chunk):
-        cols = pl.ds(c * chunk, chunk)
-        residual[:, cols] = dot(context[mine, :], ctx[cols, :], ((1,), (1,)))
-    for copy in copies:
-        copy.wait_recv()
-
-    def second_norm(i, carry):
-        at = pl.ds(pl.multiple_of(i * 16, 16), 16)
-        there = pl.ds(pl.multiple_of(me.y * own_rows + i * 16, 16), 16)
-        total = x[there, :].astype(f32) + (residual[at, :] + got[at, :].astype(f32))
-        residual[at, :] = total
-        sent[at, pl.ds(0, features)] = (total * inverse_norm(total) * gain_two).astype(bf16)
-        return carry
-
-    lax.fori_loop(0, own_rows // 16, second_norm, 0)
-    logits = dot(sent[:, :features], aux_w[...])
-    picked = chosen[...] > 0.0
-    logits = jnp.where(picked, logits, masked_score)
-    spread = jnp.where(picked, jnp.exp(logits - jnp.max(logits, axis=-1, keepdims=True)), 0.0)
-    gates = spread / jnp.sum(spread, axis=-1, keepdims=True)
-    high = gates.astype(bf16).astype(f32)
-    sent[:, pl.ds(features, AUX)] = (high + pltpu.roll(gates - high, experts, 1)).astype(bf16)
-    last = [
-        pltpu.make_async_copy(sent, sent_o, out_s.at[6]),
-        pltpu.make_async_copy(residual, residual_o, out_s.at[7]),
-    ]
-    for copy in last:
-        copy.start()
-    for copy in copies:
-        copy.wait_send()
-    for copy in outs + last:
-        copy.wait()
-
-
-def attention_forward(x_pair, packed, live, chosen, experts, heads, key_heads, collective_id):
-    bf16, f32 = jnp.bfloat16, jnp.float32
-    rows, features = x_pair.shape
-    qkv = (heads + 2 * key_heads) * HEAD_SIZE
-    cosine, sine = turn_tables(rows)
-    dma = pltpu.SemaphoreType.DMA
-    shapes = (
-        ((rows // 2, features + AUX), bf16),
-        ((rows // 2, features), f32),
-        ((rows, features), bf16),
-        ((heads + 2 * key_heads, rows, HEAD_SIZE), f32),
-        ((heads, rows, HEAD_SIZE), bf16),
-        ((key_heads, rows, HEAD_SIZE), bf16),
-        ((key_heads, rows, HEAD_SIZE), bf16),
-        ((rows, heads * HEAD_SIZE), bf16),
-    )
-    anywhere, vmem = pl.BlockSpec(memory_space=pl.ANY), pl.BlockSpec(memory_space=pltpu.VMEM)
-    return pl.pallas_call(
-        functools.partial(forward_kernel, experts),
-        out_shape=tuple(jax.ShapeDtypeStruct(*shape) for shape in shapes),
-        in_specs=[anywhere, anywhere, vmem, vmem, vmem, vmem],
-        out_specs=(anywhere,) * len(shapes),
-        scratch_shapes=[
-            pltpu.VMEM((rows, features), bf16),
-            pltpu.VMEM((features, qkv), bf16),
-            pltpu.VMEM((features, heads * HEAD_SIZE), bf16),
-            pltpu.VMEM((features, AUX), bf16),
-            pltpu.VMEM((rows, features), bf16),
-            pltpu.VMEM((heads + 2 * key_heads, rows, HEAD_SIZE), f32),
-            pltpu.VMEM((heads, rows, HEAD_SIZE), bf16),
-            pltpu.VMEM((key_heads, rows, HEAD_SIZE), bf16),
-            pltpu.VMEM((key_heads, rows, HEAD_SIZE), bf16),
-            pltpu.VMEM((rows, heads * HEAD_SIZE), bf16),
-            pltpu.VMEM((rows, features), bf16),
-            pltpu.VMEM((rows // 2, features), bf16),
-            pltpu.VMEM((rows // 2, features), f32),
-            pltpu.VMEM((rows // 2, features + AUX), bf16),
-            dma((3,)),
-            dma((qkv // 512,)),
-            dma((8,)),
-            dma((2, features // 512)),
-        ],
-        compiler_params=pltpu.CompilerParams(
-            collective_id=collective_id, has_side_effects=True, vmem_limit_bytes=ATTENTION_VMEM
-        ),
-    )(x_pair, packed, live, chosen, cosine, sine)
-
-
-def first_gather_kernel(
-    w_src, d_src, x_src, w_out, d_out, x_out,
-    local_s, pair_s, wz_s, wx_s, wc_s, az_s, ax_s, ay_s, bz_s, bx_s, by_s, dc_s,
-):
-    me = Place()
-    w_half, half = w_src.shape[0] // 2, d_src.shape[0] // 2
+    half = d_src.shape[0] // 2
     low, high = pl.ds(0, half), pl.ds(half, half)
-    waits, sent = [], []
+    width = w_src.shape[1]
+    first_cols = qkv + AUX
+    columns = (pl.ds(0, first_cols), pl.ds(first_cols, width - first_cols))
+    waits, sent_on = [], []
 
     def near(k):
         return me.farthest(GRID_Z - 1 - k)
 
     def w_at(k, fx, p):
-        return w_out.at[me.dp_at(near(k), fx, 0), pl.ds(p * w_half, w_half)]
+        return w_out.at[me.dp_at(near(k), fx, 0), :, columns[p]]
 
     def d_at(k, fx, fy, rows):
         return d_out.at[me.dp_at(near(k), fx, 0) * 2 + me.y_at(fy), rows]
@@ -1337,7 +1187,7 @@
                     copy.wait_send()
 
     def w_source(k, p):
-        return w_src.at[pl.ds(p * w_half, w_half)] if k == 0 else w_at(k, 0, p)
+        return w_src.at[:, columns[p]] if k == 0 else w_at(k, 0, p)
 
     def d_source(k, rows):
         return d_src.at[rows] if k == 0 else d_at(k, 0, 0, rows)
@@ -1345,7 +1195,7 @@
     def go(source, target, sem, index, mate):
         copy = remote(source, target, sem.at[(0, *index)], sem.at[(1, *index)], mate)
         copy.start()
-        sent.append(copy)
+        sent_on.append(copy)
         return copy
 
     def to_core(source, target, sem, index):
@@ -1358,15 +1208,23 @@
         wx[k, p] = go(w_source(k, p), w_at(k, 0, p), wx_s, (k, p), me.x_mate)
         to_core(w_source(k, p), w_at(k, 0, p), wc_s, (k, 0, p))
 
-    def w_across(k):
-        for p in range(2):
-            wx[k, p].wait_recv()
-            to_core(w_at(k, 1, p), w_at(k, 1, p), wc_s, (k, 1, p))
+    def w_across(k, p):
+        wx[k, p].wait_recv()
+        to_core(w_at(k, 1, p), w_at(k, 1, p), wc_s, (k, 1, p))
+
+    def w_from_core(k, p):
+        for fx in range(2):
+            block = w_at(k, fx, p)
+            remote(block, block, wc_s.at[0, k, fx, p], wc_s.at[1, k, fx, p], me.sibling).wait_recv()
+
+    def a_over_y(k):
+        ay[k, 0] = go(d_source(k, low), d_at(k, 0, 0, low), ay_s, (k, 0), me.y_mate)
 
     def a_own(k):
         line(k, d_source(k, low), d_at(k, 0, 0, low), az_s, k == 0)
+        if k:
+            a_over_y(k)
         ax[k] = go(d_source(k, low), d_at(k, 0, 0, low), ax_s, (k,), me.x_mate)
-        ay[k, 0] = go(d_source(k, low), d_at(k, 0, 0, low), ay_s, (k, 0), me.y_mate)
         to_core(d_source(k, low), d_at(k, 0, 0, low), dc_s, (k, 0, 0, 0))
 
     def a_across(k):
@@ -1389,68 +1247,222 @@
                 block = d_at(k, fx, 1, rows)
                 to_core(block, block, dc_s, (k, fx, 1, h))
 
-    pair = go(x_src, x_out.at[me.y], pair_s, (0,), me.y_mate)
-    for p in range(2):
-        w_own(0, p)
-    bx = go(d_src.at[high], d_at(0, 0, 0, high), bx_s, (0,), me.x_mate)
-    a_own(0)
-    b_own(0, 0)
-    bx.wait_recv()
-    b_own(0, 1)
-    for k in range(1, GRID_Z):
-        for p in range(2):
-            w_own(k, p)
-        a_own(k)
-        for fx in range(2):
-            b_own(k, fx)
-        w_across(k - 1)
-        a_across(k - 1)
-        if k > 1:
-            y_done(k - 2)
-    y_done(GRID_Z - 2)
-    w_across(GRID_Z - 1)
-    a_across(GRID_Z - 1)
-    y_done(GRID_Z - 1)
+    rows, features = x.shape[0] * x.shape[1], x.shape[2]
+    own_rows = rows // 2
+    heads, key_heads = query.shape[0], key.shape[0]
+    chunk = 512
+    mine = pl.ds(pl.multiple_of(me.y * own_rows, own_rows), own_rows)
+    theirs = pl.ds(pl.multiple_of((1 - me.y) * own_rows, own_rows), own_rows)
+    turn_c, turn_s = cosine[...], sine[...]
+    held, outs, copies = {}, [], []
+
+    def pair_rows():
+        held["pair"] = go(x_src, x_out.at[me.y], pair_s, (0,), me.y_mate)
+
+    def b_over_x():
+        held["bx"] = go(d_src.at[high], d_at(0, 0, 0, high), bx_s, (0,), me.x_mate)
+
+    def b_step(k, fx):
+        if (k, fx) == (0, 1):
+            held["bx"].wait_recv()
+        b_own(k, fx)
+
+    def prepare():
+        held["pair"].wait_recv()
+        waits[2].wait()
+        for k in range(GRID_Z):
+            w_from_core(k, 0)
+        waits[0].wait()
+        loads = [
+            pltpu.make_async_copy(w_out.at[:, :, pl.ds(qkv, AUX)], aux_w, in_s.at[1]),
+            pltpu.make_async_copy(x_out, x, in_s.at[0]),
+        ]
+        held["parts"] = [
+            pltpu.make_async_copy(
+                w_out.at[:, :, pl.ds(c * chunk, chunk)],
+                w.at[:, :, pl.ds(c * chunk, chunk)],
+                w_s.at[c],
+            )
+            for c in range(qkv // chunk)
+        ]
+        for copy in loads + held["parts"]:
+            copy.start()
+        loads[0].wait()
+        aux_t = aux_w[...].reshape(features, AUX).astype(f32).T
+        held["gains"] = gain_rows(aux_t, experts, features // HEAD_SIZE)
+        gain_one = held["gains"][0]
+        loads[1].wait()
+
+        def one(i, carry):
+            at = pl.ds(pl.multiple_of(i * 32, 32), 32)
+            for part in range(2):
+                stream = x[part, at, :].astype(f32)
+                there = pl.ds(pl.multiple_of(part * own_rows + i * 32, 32), 32)
+                normed[there, :] = (stream * inverse_norm(stream) * gain_one).astype(bf16)
+            return carry
+
+        lax.fori_loop(0, own_rows // 32, one, 0)
+
+    def project():
+        for c, copy in enumerate(held["parts"]):
+            copy.wait()
+            cols = slice(c * chunk, (c + 1) * chunk)
+            got_raw = dot(normed[...], w[:, :, cols].reshape(features, chunk))
+            for h in range(chunk // HEAD_SIZE):
+                raw[c * (chunk // HEAD_SIZE) + h] = got_raw[:, h * HEAD_SIZE : (h + 1) * HEAD_SIZE]
+        for g in range(key_heads):
+            unnormed = raw[heads + g]
+            gained = unnormed * inverse_norm(unnormed) * held["gains"][3]
+            key[g] = turn(gained, turn_c, turn_s).astype(bf16)
+            value[g] = raw[heads + key_heads + g].astype(bf16)
+
+    def attend(part):
+        allowed = allowed_pairs(live[...])
+        query_gain = held["gains"][2]
+
+        def head(h, carry):
+            g = h // (heads // key_heads)
+            unnormed = raw[h]
+            gained = unnormed * inverse_norm(unnormed) * query_gain
+            turned = turn(gained, turn_c, turn_s).astype(bf16)
+            query[h] = turned
+            probs = probabilities(turned, key[g], allowed).astype(bf16)
+            at = pl.ds(pl.multiple_of(h * HEAD_SIZE, HEAD_SIZE), HEAD_SIZE)
+            context[:, at] = dot(probs, value[g]).astype(bf16)
+            return carry
+
+        share = heads // 4
+        lax.fori_loop(part * share, (part + 1) * share, head, 0)
+
+    def save(pairs):
+        for source, target in pairs:
+            copy = pltpu.make_async_copy(source, target, out_s.at[len(outs)])
+            copy.start()
+            outs.append(copy)
+
+    def ctx_part(c):
+        span = chunk // ctx.shape[1]
+        return ctx[c * span : (c + 1) * span].reshape(chunk, ctx.shape[2])
+
+    def output_over_y():
+        save(
+            (
+                (normed, normed_o), (raw, raw_o), (query, query_o), (key, key_o),
+                (value, value_o), (context, context_o),
+            )
+        )
+        for k in range(GRID_Z):
+            w_from_core(k, 1)
+        load = pltpu.make_async_copy(w_out.at[:, :, columns[1]], ctx, in_s.at[2])
+        load.start()
+        load.wait()
+        for c in range(features // chunk):
+            cols = pl.ds(c * chunk, chunk)
+            att[:, cols] = dot(context[theirs, :], ctx_part(c), ((1,), (1,))).astype(bf16)
+            copy = remote(att.at[:, cols], got.at[:, cols], y_s.at[0, c], y_s.at[1, c], me.y_mate)
+            copy.start()
+            copies.append(copy)
+
+    def output_own():
+        for c in range(features // chunk):
+            residual[:, pl.ds(c * chunk, chunk)] = dot(context[mine, :], ctx_part(c), ((1,), (1,)))
+
+    def finish():
+        for copy in copies:
+            copy.wait_recv()
+        gain_two = held["gains"][1]
+
+        def second_norm(i, carry):
+            at = pl.ds(pl.multiple_of(i * 16, 16), 16)
+            total = x[me.y, at, :].astype(f32) + (residual[at, :] + got[at, :].astype(f32))
+            residual[at, :] = total
+            sent[at, pl.ds(0, features)] = (total * inverse_norm(total) * gain_two).astype(bf16)
+            return carry
+
+        lax.fori_loop(0, own_rows // 16, second_norm, 0)
+        logits = dot(sent[:, :features], aux_w[...].reshape(features, AUX))
+        picked = chosen[...] > 0.0
+        logits = jnp.where(picked, logits, masked_score)
+        spread = jnp.where(picked, jnp.exp(logits - jnp.max(logits, axis=-1, keepdims=True)), 0.0)
+        gates = spread / jnp.sum(spread, axis=-1, keepdims=True)
+        coarse = gates.astype(bf16).astype(f32)
+        sent[:, pl.ds(features, AUX)] = (coarse + pltpu.roll(gates - coarse, experts, 1)).astype(bf16)
+        save(((sent, sent_o), (residual, residual_o)))
+
+    actions = {
+        "pair": pair_rows, "bx": b_over_x, "ay0": lambda: a_over_y(0), "w": w_own, "wx": w_across,
+        "a": a_own, "ax": a_across, "b": b_step, "y": y_done, "prep": prepare, "qkv": project,
+        "h": attend, "ctx": output_over_y, "ctx2": output_own, "fin": finish,
+    }
+    for name, *which in OPENING_PLAN:
+        actions[name](*which)
     for k in range(GRID_Z):
         for p in range(2):
             line_done(k, w_source(k, p), w_at(k, 0, p), wz_s.at[p])
         line_done(k, d_source(k, low), d_at(k, 0, 0, low), az_s)
         line_done(k, d_source(k, high), d_at(k, 0, 0, high), bz_s.at[0])
         line_done(k, d_at(k, 1, 0, high), d_at(k, 1, 0, high), bz_s.at[1])
-    for copy in sent:
+    for copy in sent_on + copies:
         copy.wait_send()
-    pair.wait_recv()
     for k in range(GRID_Z):
         for fx in range(2):
-            for p in range(2):
-                block = w_at(k, fx, p)
-                remote(block, block, wc_s.at[0, k, fx, p], wc_s.at[1, k, fx, p], me.sibling).wait_recv()
             for fy in range(2):
-                for h, rows in enumerate((low, high)):
-                    block = d_at(k, fx, fy, rows)
+                for h, at in enumerate((low, high)):
+                    block = d_at(k, fx, fy, at)
                     remote(
                         block, block, dc_s.at[0, k, fx, fy, h], dc_s.at[1, k, fx, fy, h], me.sibling
                     ).wait_recv()
-    for copy in waits:
+    waits[1].wait()
+    for copy in outs:
         copy.wait()
 
 
-def first_gather(weights, cotangents, inputs, collective_id):
-    chips = lax.axis_size("dp")
-    pair = lax.axis_size("tensor")
+def opening(
+    weights, cotangents, inputs, live, chosen, experts, heads, key_heads, collective_id
+):
+    bf16, f32 = jnp.bfloat16, jnp.float32
+    chips, pair = lax.axis_size("dp"), lax.axis_size("tensor")
+    own_rows, features = inputs.shape
+    rows = pair * own_rows
+    shard = weights.shape[0]
+    wide = heads * HEAD_SIZE
+    qkv = (heads + 2 * key_heads) * HEAD_SIZE
+    cosine, sine = turn_tables(rows)
     dma = pltpu.SemaphoreType.DMA
-    low = weights.dtype
-    anywhere = pl.BlockSpec(memory_space=pl.ANY)
-    w, d, x = pl.pallas_call(
-        first_gather_kernel,
-        out_shape=(
-            jax.ShapeDtypeStruct((chips, *weights.shape), low),
-            jax.ShapeDtypeStruct((chips * pair, *cotangents.shape), low),
-            jax.ShapeDtypeStruct((pair, *inputs.shape), low),
-        ),
-        in_specs=[anywhere] * 3,
-        out_specs=(anywhere,) * 3,
+    shapes = (
+        ((chips, *weights.shape), bf16),
+        ((chips * pair, *cotangents.shape), bf16),
+        ((pair, *inputs.shape), bf16),
+        ((own_rows, features + AUX), bf16),
+        ((own_rows, features), f32),
+        ((rows, features), bf16),
+        ((heads + 2 * key_heads, rows, HEAD_SIZE), f32),
+        ((heads, rows, HEAD_SIZE), bf16),
+        ((key_heads, rows, HEAD_SIZE), bf16),
+        ((key_heads, rows, HEAD_SIZE), bf16),
+        ((rows, wide), bf16),
+    )
+    anywhere, vmem = pl.BlockSpec(memory_space=pl.ANY), pl.BlockSpec(memory_space=pltpu.VMEM)
+    w, d, x, *rest = pl.pallas_call(
+        functools.partial(opening_kernel, experts, qkv),
+        out_shape=tuple(jax.ShapeDtypeStruct(*shape) for shape in shapes),
+        in_specs=[anywhere] * 3 + [vmem] * 4,
+        out_specs=(anywhere,) * len(shapes),
         scratch_shapes=[
+            pltpu.VMEM((pair, own_rows, features), bf16),
+            pltpu.VMEM((chips, shard, qkv), bf16),
+            pltpu.VMEM((chips, shard, wide), bf16),
+            pltpu.VMEM((chips, shard, AUX), bf16),
+            pltpu.VMEM((rows, features), bf16),
+            pltpu.VMEM((heads + 2 * key_heads, rows, HEAD_SIZE), f32),
+            pltpu.VMEM((heads, rows, HEAD_SIZE), bf16),
+            pltpu.VMEM((key_heads, rows, HEAD_SIZE), bf16),
+            pltpu.VMEM((key_heads, rows, HEAD_SIZE), bf16),
+            pltpu.VMEM((rows, wide), bf16),
+            pltpu.VMEM((own_rows, features), bf16),
+            pltpu.VMEM((own_rows, features), bf16),
+            pltpu.VMEM((own_rows, features), f32),
+            pltpu.VMEM((own_rows, features + AUX), bf16),
             dma((3,)),
             dma((2, 1)),
             dma((2, 2, 2, 4)),
@@ -1463,13 +1475,20 @@
             dma((2, 1)),
             dma((2, 4, 2)),
             dma((2, 4, 2, 2, 2)),
+            dma((3,)),
+            dma((qkv // 512,)),
+            dma((8,)),
+            dma((2, features // 512)),
         ],
-        compiler_params=pltpu.CompilerParams(collective_id=collective_id, has_side_effects=True),
-    )(weights, cotangents, inputs)
+        compiler_params=pltpu.CompilerParams(
+            collective_id=collective_id, has_side_effects=True, vmem_limit_bytes=ATTENTION_VMEM
+        ),
+    )(weights, cotangents, inputs, live, chosen, cosine, sine)
     return (
         w.reshape(-1, w.shape[2]),
         d.reshape(chips, -1, d.shape[2]),
         x.reshape(-1, x.shape[2]),
+        *rest,
     )
 
 
@@ -1499,12 +1518,12 @@
         pltpu.make_async_copy(source, target, in_s.at[i])
         for i, (source, target) in enumerate(
             (
-                (packed.at[:, pl.ds(qkv + wide, AUX)], aux_w),
+                (packed.at[:, pl.ds(qkv, AUX)], aux_w),
                 (back_in, back),
                 (sent_in, sent),
                 (residual_in, residual),
                 (dy_in, dy),
-                (packed.at[:, pl.ds(qkv, wide)], ctx),
+                (packed.at[:, pl.ds(qkv + AUX, wide)], ctx),
                 (context_in, context),
                 (value_in, value),
                 (key_in, key),
@@ -1753,6 +1772,19 @@
     )
 
 
+LAST_CUT = 5
+LAST_PLAN = (
+    ("gx", 0, 0), ("dy", 0, 1, 1), ("gx", 0, 1), ("dy", 0, 0, 1), ("dy", 1, 1, 1), ("db", 0, 1),
+    ("gx", 1, 1), ("db", 0, 0), ("dy", 2, 1, 1), ("dy", 1, 1, 0), ("gx", 1, 0), ("db", 1, 1),
+    ("dy", 2, 1, 0), ("gx", 2, 0), ("db", 2, 1), ("dy", 0, 1, 0), ("dy", 2, 0, 1),
+    ("dy", 0, 0, 0), ("dy", 3, 1, 1), ("gc", 0), ("dy", 1, 0, 0), ("dy", 1, 0, 1),
+    ("dy", 3, 1, 0), ("dy", 2, 0, 0), ("gx", 2, 1), ("dax", 2), ("dax", 0), ("dax", 1),
+    ("gc", 1), ("gc", 2), ("gx", 3, 0), ("dy", 3, 0, 1), ("gx", 3, 1), ("da", 0), ("dax", 3),
+    ("dy", 3, 0, 0), ("db", 1, 0), ("da", 1), ("db", 2, 0), ("da", 2), ("gc", 3), ("sm",),
+    ("db", 3, 1), ("db", 3, 0), ("sm2",), ("da", 3), ("bx",),
+)
+
+
 def last_scatter_kernel(
     g_part, d_part, g_out, d_out,
     g_own, g_core, g_x, g_z, d_own, d_core, d_y, a_x, b_x, a_z, b_z, small_got,
@@ -1760,9 +1792,9 @@
 ):
     me = Place()
     g_rows, d_rows = g_own.shape[2], d_own.shape[3]
-    half, g_half = d_rows // 2, g_rows // 2
-    g_all, low, high = (0, g_rows), (0, half), (half, half)
-    low_at, high_at = pl.ds(0, half), pl.ds(half, half)
+    cut, g_half = a_x.shape[1], g_rows // 2
+    g_all, low, high = (0, g_rows), (0, cut), (cut, d_rows - cut)
+    low_at, high_at = pl.ds(0, cut), pl.ds(cut, d_rows - cut)
     last = GRID_Z - 1
     loads, cores, sends = {}, {}, []
 
@@ -1808,11 +1840,13 @@
         for k in range(GRID_Z)
     ]
     dy = {
-        (k, fx): remote(
-            d_own.at[k, fx, 1], d_y.at[k, fx], dy_s.at[0, k, fx], dy_s.at[1, k, fx], me.y_mate
+        (k, fx, h): remote(
+            d_own.at[k, fx, 1, at], d_y.at[k, fx, at],
+            dy_s.at[0, k, fx, h], dy_s.at[1, k, fx, h], me.y_mate,
         )
         for k in range(GRID_Z)
         for fx in range(2)
+        for h, at in enumerate((low_at, high_at))
     }
     ax = [
         remote(d_own.at[k, 1, 0, low_at], a_x.at[k], ax_s.at[0, k], ax_s.at[1, k], me.x_mate)
@@ -1820,9 +1854,13 @@
     ]
     bx = remote(d_own.at[last, 1, 0, high_at], b_x, bx_s.at[0], bx_s.at[1], me.x_mate)
 
+    here = set()
+
     def arrive(*index):
-        loads[index].wait()
-        cores[index].wait_recv()
+        if index not in here:
+            here.add(index)
+            loads[index].wait()
+            cores[index].wait_recv()
 
     def onward(source, buffer, sem, to, side, mate):
         ends = 1 - (me.z - 1 - to + GRID_Z - 1) // GRID_Z
@@ -1859,80 +1897,77 @@
             def _():
                 onward(source, buffer, sem, to, side, mate).wait_send()
 
-    def across(k):
+    width = g_own.shape[3]
+    small_block = g_own.at[last, 0, :, pl.ds(width - AUX, AUX)]
+    small = remote(small_block, small_got, small_s.at[0], small_s.at[1], me.y_mate)
+
+    def g_across(k, h):
         arrive(k, 1)
-        for h in range(2):
-            add_rows(g_own.at[k, 1], [(g_core.at[k, 1], 0)], (h * g_half, g_half))
-            gx[k][h].start()
-
-    def over_y(k):
-        for fx in (1, 0):
-            arrive(k, fx, 1)
-            add_rows(d_own.at[k, fx, 1], [(d_core.at[k, fx, 1], 0)], (0, d_rows))
-            dy[k, fx].start()
-
-    def column(k):
+        add_rows(g_own.at[k, 1], [(g_core.at[k, 1], 0)], (h * g_half, g_half))
+        gx[k][h].start()
+
+    def g_column(k):
         arrive(k, 0)
         for h in range(2):
             gx[k][h].wait_recv()
         add_rows(g_own.at[k, 0], [(g_core.at[k, 0], 0), (g_x.at[k], 0)], g_all)
         line(k, g_own.at[k, 0], g_own.at[k, 0], g_all, g_z, gz_s, 0)
 
-    def merge(k):
-        for fx in (1, 0):
-            arrive(k, fx, 0)
-            dy[k, fx].wait_recv()
-            block = d_own.at[k, fx, 0]
-            if fx:
-                add_rows(block, [(d_core.at[k, fx, 0], 0), (d_y.at[k, fx], 0)], low)
-                ax[k].start()
-                add_rows(block, [(d_core.at[k, fx, 0], 0), (d_y.at[k, fx], 0)], high)
-            else:
-                add_rows(block, [(d_core.at[k, fx, 0], 0), (d_y.at[k, fx], 0)], (0, d_rows))
-            line(k, block, block.at[high_at], high, b_z.at[fx], bz_s.at[fx], half)
-            if fx and k == last:
-                bx.start()
-
-    def settle(k):
+    def over_y(k, fx, h):
+        arrive(k, fx, 1)
+        add_rows(d_own.at[k, fx, 1], [(d_core.at[k, fx, 1], 0)], (low, high)[h])
+        dy[k, fx, h].start()
+
+    def from_y(k, fx, h, *more):
+        arrive(k, fx, 0)
+        dy[k, fx, h].wait_recv()
+        rest = [(d_core.at[k, fx, 0], 0), (d_y.at[k, fx], 0), *more]
+        add_rows(d_own.at[k, fx, 0], rest, (low, high)[h])
+
+    def b_line(k, fx):
+        from_y(k, fx, 1)
+        block = d_own.at[k, fx, 0]
+        line(k, block, block.at[high_at], high, b_z.at[fx], bz_s.at[fx], cut)
+        if fx and k == last:
+            bx.start()
+
+    def a_over_x(k):
+        from_y(k, 1, 0)
+        ax[k].start()
+
+    def a_line(k):
         ax[k].wait_recv()
+        from_y(k, 0, 0, (a_x.at[k], 0))
         block = d_own.at[k, 0, 0]
-        add_rows(block, [(a_x.at[k], 0)], low)
         line(k, block, block.at[low_at], low, a_z, az_s, 0)
 
-    for k in range(GRID_Z):
-        across(k)
-        over_y(k)
-        if k >= 1:
-            column(k - 1)
-            merge(k - 1)
-        if k >= 2:
-            settle(k - 2)
-    merge(last)
-    column(last)
-    settle(last - 1)
-    width = g_own.shape[3]
-    small = remote(
-        g_own.at[last, 0, :, pl.ds(width - AUX, AUX)], small_got,
-        small_s.at[0], small_s.at[1], me.y_mate,
-    )
-    small.start()
-    settle(last)
-    bx.wait_recv()
-    add_rows(d_own.at[last, 0, 0], [(b_x, half)], high)
-    outs = [pltpu.make_async_copy(d_own.at[last, 0, 0], d_out, out_s.at[0])]
-    outs[0].start()
-    small.wait()
-    block = g_own.at[last, 0, :, pl.ds(width - AUX, AUX)]
-    block[...] = (block[...].astype(jnp.float32) + small_got[...].astype(jnp.float32)).astype(
-        block.dtype
-    )
-    outs.append(pltpu.make_async_copy(g_own.at[last, 0], g_out, out_s.at[1]))
-    outs[1].start()
+    def b_from_x():
+        bx.wait_recv()
+        add_rows(d_own.at[last, 0, 0], [(b_x, cut)], high)
+
+    def small_sum():
+        small.wait()
+        total = small_block[...].astype(jnp.float32) + small_got[...].astype(jnp.float32)
+        small_block[...] = total.astype(small_got.dtype)
+
+    actions = {
+        "gx": g_across, "gc": g_column, "dy": over_y, "db": b_line, "dax": a_over_x, "da": a_line,
+        "bx": b_from_x, "sm": small.start, "sm2": small_sum,
+    }
+    for name, *which in LAST_PLAN:
+        actions[name](*which)
+    outs = [
+        pltpu.make_async_copy(d_own.at[last, 0, 0], d_out, out_s.at[0]),
+        pltpu.make_async_copy(g_own.at[last, 0], g_out, out_s.at[1]),
+    ]
+    for copy in outs:
+        copy.start()
     for k in range(GRID_Z):
         for h in range(2):
             gx[k][h].wait_send()
         for fx in range(2):
-            dy[k, fx].wait_send()
+            for h in range(2):
+                dy[k, fx, h].wait_send()
         ax[k].wait_send()
         if k < last:
             line_done(k, g_own.at[k, 0], g_z, gz_s)
@@ -1950,7 +1985,7 @@
     chips, pair = lax.axis_size("dp"), lax.axis_size("tensor")
     g_rows, g_wide = grads.shape[0] // chips, grads.shape[1]
     d_rows, d_wide = sums.shape[0] // (chips * pair), sums.shape[1]
-    half = d_rows // 2
+    cut = d_rows * LAST_CUT // 8
     dma = pltpu.SemaphoreType.DMA
     low = grads.dtype
     anywhere = pl.BlockSpec(memory_space=pl.ANY)
@@ -1970,10 +2005,10 @@
             pltpu.VMEM((4, 2, 2, d_rows, d_wide), low),
             pltpu.VMEM((4, 2, 2, d_rows, d_wide), low),
             pltpu.VMEM((4, 2, d_rows, d_wide), low),
-            pltpu.VMEM((4, half, d_wide), low),
-            pltpu.VMEM((half, d_wide), low),
-            pltpu.VMEM((5, half, d_wide), low),
-            pltpu.VMEM((2, 5, half, d_wide), low),
+            pltpu.VMEM((4, cut, d_wide), low),
+            pltpu.VMEM((d_rows - cut, d_wide), low),
+            pltpu.VMEM((5, cut, d_wide), low),
+            pltpu.VMEM((2, 5, d_rows - cut, d_wide), low),
             pltpu.VMEM((g_rows, AUX), low),
             dma((4, 2)),
             dma((2, 4, 2)),
@@ -1981,7 +2016,7 @@
             dma((2, 5)),
             dma((4, 2, 2)),
             dma((2, 4, 2, 2)),
-            dma((2, 4, 2)),
+            dma((2, 4, 2, 2)),
             dma((2, 4)),
             dma((2,)),
             dma((2, 5)),
@@ -2044,13 +2079,9 @@
         axis=1,
     )
     packed = jnp.concatenate(
-        [query_weight, key_projection, value_projection, context_weight.T, router_weight, gains],
+        [query_weight, key_projection, value_projection, router_weight, gains, context_weight.T],
         axis=1,
     )
-    packed, cot_all, input_rows = first_gather(packed, output_cotangent, layer_input, 0)
-    route_from = packed.shape[1] - AUX + expert_count + 4
-    routes_all = packed[:, route_from : route_from + route_wide].astype(jnp.int32)
-    routes_all = routes_all.reshape(dp_count, TOP, block_rows)
     position = jnp.arange(block_rows, dtype=jnp.int32)
     block_lengths = lengths[sequence_order]
     live = position[None, :] < block_lengths[:, None]
@@ -2062,9 +2093,20 @@
     routes_own = lax.dynamic_slice_in_dim(routes, row_start, own_rows, 0)
     expert_ids = jnp.arange(AUX, dtype=jnp.int32)
     chosen = jnp.any(routes_own[:, :, None] == expert_ids[None, None, :], axis=1).astype(f32)
-    sent, residual, *saved = attention_forward(
-        input_rows, packed, live_own, chosen, expert_count, heads_query, heads_key, 5
-    )
+    packed, cot_all, input_rows, sent, residual, *saved = opening(
+        packed,
+        output_cotangent,
+        layer_input,
+        live_own,
+        chosen,
+        expert_count,
+        heads_query,
+        heads_key,
+        0,
+    )
+    route_from = query_width + 2 * key_width + expert_count + 4
+    routes_all = packed[:, route_from : route_from + route_wide].astype(jnp.int32)
+    routes_all = routes_all.reshape(dp_count, TOP, block_rows)
     normed_all = gather_all(sent, 1).reshape(dp_count, block_rows, features + AUX)
 
     expert_own = dp_index * EXP_DEV + jnp.arange(EXP_DEV, dtype=jnp.int32)

time: 678 us -> 627 us (0.925)
  Pallas kernels: 639 us -> 594 us
    pallas_call x2 -> x1, Pallas kernels: 195 us -> 164 us  [opening(): pl.pallas_call(functools.partial(opening_kernel, experts, qkv), out_shape...]
    pallas_call x1, Pallas kernels: 158 us -> 145 us  [last_scatter(): pl.pallas_call(last_scatter_kernel, out_shape=(jax.ShapeDtypeStruct((g_ro...]
where the time goes in v6:
time: 627 us; the launch traced here: 625 us
  Pallas kernels  594 us (95%)
  local copies, waits for them, and re-layouts  21 us (3%)
  other arithmetic  9.11 us (1%)
    pallas_call x1, Pallas kernels, opening(): pl.pallas_call(functools.partial(opening_kernel, experts, qkv), out_shape...  164 us
    pallas_call x1, Pallas kernels, last_scatter(): pl.pallas_call(last_scatter_kernel, out_shape=(jax.ShapeDtypeStruct((g_ro...  145 us
    pallas_call x1, Pallas kernels, scatter_all(): pl.pallas_call(scatter_kernel, out_shape=jax.ShapeDtypeStruct((rows, widt...  85.4 us
    pallas_call x1, Pallas kernels, gather_all(): pl.pallas_call(gather_kernel, out_shape=jax.ShapeDtypeStruct((devices, ro...  78 us
    pallas_call x1, Pallas kernels, expert_layer(): pl.pallas_call(expert_kernel, out_shape=(shape((blocks, block_rows, featu...  73.3 us
    pallas_call x1, Pallas kernels, attention_backward(): pl.pallas_call(functools.partial(backward_kernel, experts), out_shape=(ja...  48.3 us

profile of v6, /device:TPU:0, one launch (start us, length us, event | category | flops | bytes accessed | tf_op | source)
XLA Modules:
  0.0 624.8 jit_solution(11470751979087268644)
XLA Ops:
  0.7 0.7 compare_select_fusion
  1.3 0.7 copy.86
  2.1 0.7 copy.87
  2.8 0.7 gather_fusion
  3.6 0.7 constant_dynamic-slice_fusion.1
  4.3 0.7 convert_bitcast_fusion
  5.0 0.6 broadcast_in_dim.58.live
  5.7 0.8 copy.89
  6.5 0.8 copy.90
  7.3 0.8 copy.91
  8.5 0.6 convert_element_type.38.chosen
  9.1 1.2 copy.88
  10.4 2.9 concatenate.6.w_src
  13.3 164.0 %shard_map.308 = (bf16[16,128,4736]{2,1,0:T(8,128)(2,1)}, bf16[32,128,2048]{2,1,0:T(8,128)(2,1)}, bf16[2,128,2048]{2,1,0:T(8,128)(2,1)}, bf16[128,2176]{1,0:T(8,...) custom-call(bf16[128,4736]{1,0:T(8,128)(2,1)} %concatenate.6.w_src, ...), custom_call_target="tpu_custom_call" | custom-call | tf_op jit(solution)/shard_map/pallas_call | solution.py:1446
  177.4 1.3 slice_convert_fusion
  181.3 0.7 and_select_fusion.pos
  182.0 78.0 %shard_map.309 = bf16[32,128,2176]{2,1,0:T(8,128)(2,1)} custom-call(bf16[128,2176]{1,0:T(8,128)(2,1)} %get-tuple-element.36.src.sent_in), custom_call_target="tpu_custom_call" | custom-call | tf_op jit(solution)/shard_map/pallas_call | solution.py:779
  260.0 73.3 %shard_map.310 = (bf16[16,256,2048]{2,1,0:T(8,128)(2,1)}, bf16[16,256,2176]{2,1,0:T(8,128)(2,1)}, f32[2,2048,384]{2,1,0:T(8,128)}, f32[2,2048,384]{2,1,0:T(8,128)}, f32[2,384,2048]{2,1,0:T(8,128)}) custom-call(s32[34]{0:T(128)} %pad_add_fusion.info, s32[16,2,256]{2,1,0:T(2,128)} %and_select_fusion.pos, bf16[16,256,2176]{2,1,0:T(8,128)(2,1)} %bitcast.25, ...), custom_call_target="tpu_custom_call" | custom-call | tf_op jit(solution)/shard_map/pallas_call | solution.py:1017
  333.3 85.4 %shard_map.311.back_in = bf16[128,2176]{1,0:T(8,128)(2,1)} custom-call(bf16[32,128,2176]{2,1,0:T(8,128)(2,1)} %bitcast.29), custom_call_target="tpu_custom_call" | custom-call | tf_op jit(solution)/shard_map/pallas_call | solution.py:628
  418.7 48.3 %shard_map.312 = (bf16[2048,4736]{1,0:T(8,128)(2,1)}, bf16[128,2048]{1,0:T(8,128)(2,1)}) custom-call(bf16[128,2176]{1,0:T(8,128)(2,1)} %shard_map.311.back_in, f32[128,2048]{1,0:T(8,128)} %get-tuple-element.34.residual_in, bf16[128,2176]{1,0:T(8,128)(2,1)} %get-tuple-element.36.src.sent_in, bf16[128,2048]{1,0:T(8,128)(2,1)} %dy_in.1, ...), custom_call_target="tpu_custom_call" | custom-call | tf_op jit(solution)/shard_map/pallas_call | solution.py:1728
  467.1 144.6 %shard_map.313 = (bf16[128,4736]{1,0:T(8,128)(2,1)}, bf16[128,2048]{1,0:T(8,128)(2,1)}) custom-call(bf16[16,128,4736]{2,1,0:T(8,128)(2,1)} %bitcast.28, bf16[32,128,2048]{2,1,0:T(8,128)(2,1)} %bitcast.31), custom_call_target="tpu_custom_call" | custom-call | tf_op jit(solution)/shard_map/pallas_call | solution.py:1992
  611.7 2.0 add_convert_fusion
  613.7 0.8 slice.64
  614.5 0.7 copy.102
  615.2 0.8 slice.67
  616.0 0.7 slice_reduce_fusion.2
  616.7 1.6 fusion.9
  618.3 2.1 slice.60
  620.4 1.4 convert_element_type.43
  621.8 0.7 slice_reduce_fusion
  622.6 1.3 copy.101
  624.0 0.8 copy.113
  (39 shorter events, 3.3 us)
Async XLA Ops:
  0.6 2.2 copy-start
  467.1 144.6 %copy-start.2 = (f32[128,2048]{1,0:T(8,128)S(1)}, f32[128,2048]{1,0:T(8,128)}, u32[]{:S(2)}) copy-start(f32[128,2048]{1,0:T(8,128)} %get-tuple-element.34.residual_in) | copy-start | bytes 3145732
  611.7 12.3 %copy-start.3 = (bf16[128,2048]{1,0:T(8,128)(2,1)S(1)}, bf16[128,2048]{1,0:T(8,128)(2,1)}, u32[]{:S(2)}) copy-start(bf16[128,2048]{1,0:T(8,128)(2,1)} %get-tuple-element.133) | copy-start | bytes 1572868
  611.7 13.0 %copy-start.1 = (s32[16]{0:T(128)S(1)}, s32[16]{0:T(128)}, u32[]{:S(2)}) copy-start(s32[16]{0:T(128)} %param.35) | copy-start | bytes 196

commit v7 on v6

--- a/solution.py
+++ b/solution.py
@@ -653,147 +653,6 @@
     )(value.reshape(devices, rows, width))
 
 
-def gather_kernel(src, out, own_s, z_s, x_s, y_s, dx_s, dy_s, core_s):
-    me = Place()
-    rows = src.shape[0]
-    half = rows // 2
-    low, high = pl.ds(0, half), pl.ds(half, half)
-
-    def near(k):
-        return me.farthest(GRID_Z - 1 - k)
-
-    def at(k, fx, fy, fc):
-        return out.at[me.dp_at(near(k), fx, fc) * 2 + me.y_at(fy)]
-
-    mine = pltpu.make_async_copy(src, at(0, 0, 0, 0), own_s)
-    mine.start()
-    me.greet()
-
-    def over(source, k, fx, fy, send, recv, mate):
-        return remote(source, at(k, fx, fy, 0), send, recv, mate)
-
-    def z_copy(k, source, side, mate):
-        zn = near(k)
-        return remote(source, at(k, 0, 0, 0), z_s.at[0, side, zn], z_s.at[1, side, zn], mate)
-
-    xs, ys, dxs, dys, cores = {}, {}, {}, {}, {}
-    for k in range(GRID_Z):
-        source = src if k == 0 else at(k, 0, 0, 0)
-        xs[k] = over(source, k, 0, 0, x_s.at[0, k], x_s.at[1, k], me.x_mate)
-        ys[k] = over(source, k, 0, 0, y_s.at[0, k], y_s.at[1, k], me.y_mate)
-        dys[k] = remote(at(k, 1, 0, 0).at[low], at(k, 1, 0, 0).at[low], dy_s.at[0, k], dy_s.at[1, k], me.y_mate)
-        dxs[k] = remote(at(k, 0, 1, 0).at[high], at(k, 0, 1, 0).at[high], dx_s.at[0, k], dx_s.at[1, k], me.x_mate)
-        for fx in range(2):
-            for fy in range(2):
-                block = source if (fx, fy) == (0, 0) else at(k, fx, fy, 0)
-                if (fx, fy) == (1, 1):
-                    for h, part in enumerate((low, high)):
-                        cores[k, fx, fy, h] = remote(
-                            block.at[part], block.at[part],
-                            core_s.at[0, k, 3 + h], core_s.at[1, k, 3 + h], me.sibling,
-                        )
-                else:
-                    cores[k, fx, fy] = remote(
-                        block, at(k, fx, fy, 0), core_s.at[0, k, fx * 2 + fy],
-                        core_s.at[1, k, fx * 2 + fy], me.sibling,
-                    )
-
-    def own(k):
-        if k == 0:
-            for side, more, mate in ((0, me.has_above, me.above), (1, me.has_below, me.below)):
-                copy = z_copy(0, src, side, mate)
-
-                @pl.when(more)
-                def _():
-                    copy.start()
-        else:
-            zn = near(k)
-            for side, came, more, mate in (
-                (0, zn < me.z, me.has_above, me.above),
-                (1, zn > me.z, me.has_below, me.below),
-            ):
-                copy = z_copy(k, at(k, 0, 0, 0), side, mate)
-
-                @pl.when(came)
-                def _():
-                    copy.wait_recv()
-
-                    @pl.when(more)
-                    def _():
-                        copy.start()
-
-        xs[k].start()
-        ys[k].start()
-        cores[k, 0, 0].start()
-
-    def diag(k):
-        xs[k].wait_recv()
-        dys[k].start()
-        cores[k, 1, 0].start()
-        ys[k].wait_recv()
-        dxs[k].start()
-        cores[k, 0, 1].start()
-
-    def corner(k):
-        dys[k].wait_recv()
-        cores[k, 1, 1, 0].start()
-        dxs[k].wait_recv()
-        cores[k, 1, 1, 1].start()
-
-    own(0)
-    own(1)
-    diag(0)
-    own(2)
-    diag(1)
-    corner(0)
-    own(3)
-    diag(2)
-    corner(1)
-    diag(3)
-    corner(2)
-    corner(3)
-    mine.wait()
-    for k in range(GRID_Z):
-        zn = near(k)
-        for side, came, more, mate in (
-            (0, zn <= me.z, me.has_above, me.above),
-            (1, zn >= me.z, me.has_below, me.below),
-        ):
-            copy = z_copy(k, src if k == 0 else at(k, 0, 0, 0), side, mate)
-
-            @pl.when(came)
-            def _():
-                @pl.when(more)
-                def _():
-                    copy.wait_send()
-        for copy in (xs[k], ys[k], dxs[k], dys[k]):
-            copy.wait_send()
-    for copy in cores.values():
-        copy.wait()
-
-
-def gather_all(value, collective_id):
-    devices = lax.axis_size("dp") * lax.axis_size("tensor")
-    rows, width = value.shape
-    dma = pltpu.SemaphoreType.DMA
-    return pl.pallas_call(
-        gather_kernel,
-        out_shape=jax.ShapeDtypeStruct((devices, rows, width), value.dtype),
-        in_specs=[pl.BlockSpec(memory_space=pl.ANY)],
-        out_specs=pl.BlockSpec(memory_space=pl.ANY),
-        scratch_shapes=[
-            dma(()),
-            dma((2, 2, 4)),
-            dma((2, 4)),
-            dma((2, 4)),
-            dma((2, 4)),
-            dma((2, 4)),
-            dma((2, 4, 5)),
-        ],
-        compiler_params=pltpu.CompilerParams(collective_id=collective_id, has_side_effects=True),
-    )(value).reshape(devices * rows, width)
-
-
 WINDOW_ALIGN = 16
 EXPERT_VMEM = 60 * 1024 * 1024
 
@@ -1093,32 +952,47 @@
     return spread / jnp.sum(spread, axis=-1, keepdims=True)
 
 
-def allowed_pairs(live):
-    rows = live.shape[1]
+def allowed_pairs(length, rows):
     later = lax.broadcasted_iota(jnp.int32, (rows, rows), 0)
     sooner = lax.broadcasted_iota(jnp.int32, (rows, rows), 1)
-    return (sooner <= later) & (live[0:1, :] > 0.0)
+    return (sooner <= later) & (sooner < length)
+
+
+def placed(count, offset):
+    row = lax.broadcasted_iota(jnp.int32, (count, AUX), 0)
+    return (row + offset == lax.broadcasted_iota(jnp.int32, (count, AUX), 1)).astype(jnp.bfloat16)
 
 
 OPENING_PLAN = (
-    ("bx",), ("w", 0, 0), ("w", 1, 0), ("ay0",), ("a", 0), ("w", 2, 0), ("pair",), ("a", 1),
-    ("b", 0, 0), ("wx", 1, 0), ("a", 2), ("ax", 0), ("w", 3, 0), ("wx", 0, 0), ("b", 1, 0),
-    ("w", 0, 1), ("ax", 1), ("a", 3), ("wx", 2, 0), ("w", 1, 1), ("wx", 3, 0), ("ax", 2),
-    ("prep",), ("w", 2, 1), ("b", 0, 1), ("b", 2, 0), ("wx", 0, 1), ("qkv",), ("h", 0),
-    ("ax", 3), ("w", 3, 1), ("y", 0), ("b", 1, 1), ("h", 1), ("b", 2, 1), ("h", 2), ("b", 3, 0),
-    ("wx", 1, 1), ("wx", 2, 1), ("h", 3), ("b", 3, 1), ("wx", 3, 1), ("y", 1), ("ctx",),
-    ("ctx2",), ("y", 2), ("y", 3), ("fin",),
+    ("w", 0, 0), ("a", 0), ("w", 1, 0), ("pair",), ("a", 1), ("b", 0, 0), ("w", 2, 0), ("a", 2),
+    ("ax", 0), ("bx",), ("w", 3, 0), ("w", 0, 1), ("y1", 1, 0, 0), ("ax", 2), ("b", 0, 1),
+    ("ax", 1), ("wx", 1, 0), ("b", 1, 1), ("ay0",), ("w", 1, 1), ("wx", 0, 0), ("b", 1, 0),
+    ("wx", 2, 0), ("b", 2, 1), ("w", 2, 1), ("wx", 3, 0), ("y1", 1, 1, 0), ("prep",), ("qkv",),
+    ("h", 0), ("y1", 1, 0, 1), ("b", 2, 0), ("w", 3, 1), ("y1", 0, 0, 1), ("h", 1), ("b", 3, 0),
+    ("wx", 1, 1), ("h", 2), ("wx", 2, 1), ("a", 3), ("h", 3), ("wx", 0, 1), ("b", 3, 1),
+    ("wx", 3, 1), ("ctx",), ("ax", 3), ("ctx2",), ("fin",), ("n", 0), ("y1", 0, 1, 0),
+    ("y1", 1, 1, 1), ("c0",), ("n", 1), ("n", 2), ("c1",), ("n", 3), ("nx", 1), ("c2", 0),
+    ("cz", 1, 1, 0), ("nx", 0), ("c2", 1), ("cz", 1, 1, 1), ("ny", 1), ("ny", 2),
+    ("cz", 2, 1, 0), ("cz", 1, 0, 0), ("y1", 2, 0, 1), ("ny", 3), ("y1", 0, 1, 1),
+    ("y1", 3, 1, 0), ("y1", 2, 1, 0), ("ny", 0), ("nx", 3), ("cz", 2, 1, 1), ("y1", 3, 0, 1),
+    ("nx", 2), ("y1", 0, 0, 0), ("cz", 3, 1, 0), ("y1", 2, 0, 0), ("cz", 3, 1, 1),
+    ("y1", 3, 0, 0), ("y1", 3, 1, 1), ("y1", 2, 1, 1), ("cz", 2, 0, 0), ("cz", 1, 0, 1),
+    ("nca", 1), ("cz", 2, 0, 1), ("cz", 3, 0, 1), ("nca", 0), ("ncb", 2), ("ncb", 0),
+    ("nca", 3), ("ncb", 1), ("ncb", 3), ("cz", 3, 0, 0), ("nca", 2),
 )
 
 
 def opening_kernel(
     experts, qkv,
-    w_src, d_src, x_src, live, chosen, cosine, sine,
+    lengths, sequence_order, query_w, key_w, value_w, context_w, router_t, prenorm, midnorm,
+    querynorm, keynorm, routes_t, d_src, x_src, cosine_in, sine_in,
     w_out, d_out, x_out,
-    sent_o, residual_o, normed_o, raw_o, query_o, key_o, value_o, context_o,
+    rows_o, sent_o, residual_o, normed_o, raw_o, query_o, key_o, value_o, context_o,
     x, w, ctx, aux_w, normed, raw, query, key, value, context, att, got, residual, sent,
     local_s, pair_s, wz_s, wx_s, wc_s, az_s, ax_s, ay_s, bz_s, bx_s, by_s, dc_s,
     in_s, w_s, out_s, y_s,
+    w_src, flat_ctx, flat_router, flat_gains, head_gains, flat_routes, cosine, sine, load_s,
+    nl_s, nz_s, nx_s, ny_s, ndx_s, ndy_s, nc_s, cx_s, cy_s, cz_s, cc_s,
 ):
     bf16, f32 = jnp.bfloat16, jnp.float32
     me = Place()
@@ -1138,6 +1012,51 @@
     def d_at(k, fx, fy, rows):
         return d_out.at[me.dp_at(near(k), fx, 0) * 2 + me.y_at(fy), rows]
 
+    wide, narrow = query_w.shape[1], key_w.shape[1]
+    loads = [
+        pltpu.make_async_copy(source, target, load_s.at[i])
+        for i, (source, target) in enumerate(
+            (
+                (context_w, flat_ctx),
+                (router_t, flat_router),
+                (prenorm, flat_gains.at[0]),
+                (midnorm, flat_gains.at[1]),
+                (querynorm, head_gains.at[0]),
+                (keynorm, head_gains.at[1]),
+                (routes_t, flat_routes),
+                (query_w, w_src.at[:, pl.ds(0, wide)]),
+                (key_w, w_src.at[:, pl.ds(wide, narrow)]),
+                (value_w, w_src.at[:, pl.ds(wide + narrow, narrow)]),
+                (cosine_in, cosine),
+                (sine_in, sine),
+            )
+        )
+    ]
+    for copy in loads:
+        copy.start()
+    for copy in loads[:7]:
+        copy.wait()
+    count = head_gains.shape[2]
+    top, block_rows = flat_routes.shape
+    w_src[:, pl.ds(first_cols, width - first_cols)] = flat_ctx[...].astype(f32).T.astype(bf16)
+    gains = jnp.concatenate(
+        [
+            flat_gains[0].astype(f32),
+            flat_gains[1].astype(f32),
+            dot(head_gains[0], placed(count, me.dp * count)),
+            dot(head_gains[1], placed(count, me.dp * count)),
+            jnp.zeros((4, AUX), f32),
+        ],
+        axis=0,
+    ).T.astype(bf16)
+    aux = dot(flat_router[...].astype(f32).T.astype(bf16), placed(experts, 0))
+    aux = aux + dot(gains, placed(8, experts))
+    for part in range(block_rows // AUX):
+        some = flat_routes[:, part * AUX : (part + 1) * AUX].astype(f32).T.astype(bf16)
+        aux = aux + dot(some, placed(top, experts + 4 + part * top))
+    w_src[:, pl.ds(qkv, AUX)] = aux.astype(bf16)
+    for copy in loads[7:]:
+        copy.wait()
     for i, (source, target) in enumerate(
         (
             (w_src, w_out.at[me.dp]),
@@ -1240,12 +1159,10 @@
         by[k, fx] = go(source, block, by_s, (k, fx), me.y_mate)
         to_core(source, block, dc_s, (k, fx, 0, 1))
 
-    def y_done(k):
-        for fx in range(2):
-            for h, (copies, rows) in enumerate(((ay, low), (by, high))):
-                copies[k, fx].wait_recv()
-                block = d_at(k, fx, 1, rows)
-                to_core(block, block, dc_s, (k, fx, 1, h))
+    def y_done(k, fx, h):
+        (ay, by)[h][k, fx].wait_recv()
+        block = d_at(k, fx, 1, (low, high)[h])
+        to_core(block, block, dc_s, (k, fx, 1, h))
 
     rows, features = x.shape[0] * x.shape[1], x.shape[2]
     own_rows = rows // 2
@@ -1317,7 +1234,7 @@
             value[g] = raw[heads + key_heads + g].astype(bf16)
 
     def attend(part):
-        allowed = allowed_pairs(live[...])
+        allowed = allowed_pairs(lengths[sequence_order[me.dp]], rows)
         query_gain = held["gains"][2]
 
         def head(h, carry):
@@ -1381,7 +1298,11 @@
 
         lax.fori_loop(0, own_rows // 16, second_norm, 0)
         logits = dot(sent[:, :features], aux_w[...].reshape(features, AUX))
-        picked = chosen[...] > 0.0
+        own = flat_routes[:, pl.ds(pl.multiple_of(me.y * own_rows, own_rows), own_rows)]
+        own = own.astype(f32).T
+        lane = lax.broadcasted_iota(jnp.int32, (own_rows, AUX), 1).astype(f32)
+        hits = [lane == own[:, j : j + 1] for j in range(top)]
+        picked = functools.reduce(jnp.logical_or, hits)
         logits = jnp.where(picked, logits, masked_score)
         spread = jnp.where(picked, jnp.exp(logits - jnp.max(logits, axis=-1, keepdims=True)), 0.0)
         gates = spread / jnp.sum(spread, axis=-1, keepdims=True)
@@ -1389,9 +1310,75 @@
         sent[:, pl.ds(features, AUX)] = (coarse + pltpu.roll(gates - coarse, experts, 1)).astype(bf16)
         save(((sent, sent_o), (residual, residual_o)))
 
+    third = 3 * own_rows // 8
+    n_low, n_high = pl.ds(0, third), pl.ds(third, third)
+    n_most, n_rest = pl.ds(0, 2 * third), pl.ds(2 * third, own_rows - 2 * third)
+    nx, ny, ndx, ndy, cy = {}, {}, {}, {}, {}
+
+    def n_at(k, fx, fy, rows):
+        return rows_o.at[me.dp_at(near(k), fx, 0) * 2 + me.y_at(fy), rows]
+
+    def n_source(k, rows):
+        return sent.at[rows] if k == 0 else n_at(k, 0, 0, rows)
+
+    def n_own(k):
+        source, block = n_source(k, n_most), n_at(k, 0, 0, n_most)
+        line(k, source, block, nz_s, k == 0)
+        nx[k] = go(source, block, nx_s, (k,), me.x_mate)
+        ny[k] = go(source, block, ny_s, (k,), me.y_mate)
+        to_core(source, block, nc_s, (k, 0))
+        if k == 0:
+            copy = pltpu.make_async_copy(sent, rows_o.at[me.dp * 2 + me.y], nl_s.at[0])
+            copy.start()
+            outs.append(copy)
+
+    def n_over_y(k):
+        nx[k].wait_recv()
+        block = n_at(k, 1, 0, n_low)
+        ndy[k] = go(block, block, ndy_s, (k,), me.y_mate)
+        block = n_at(k, 1, 0, n_most)
+        to_core(block, block, nc_s, (k, 1))
+
+    def n_over_x(k):
+        ny[k].wait_recv()
+        block = n_at(k, 0, 1, n_high)
+        ndx[k] = go(block, block, ndx_s, (k,), me.x_mate)
+        block = n_at(k, 0, 1, n_most)
+        to_core(block, block, nc_s, (k, 2))
+
+    def n_corner(k, copies, rows, index):
+        copies[k].wait_recv()
+        block = n_at(k, 1, 1, rows)
+        to_core(block, block, nc_s, (k, index))
+
+    def c_line(k, fx, fy, source=None):
+        block = n_at(k, fx, fy, n_rest)
+        source = block if source is None else source
+        line(k, source, block, cz_s.at[fx, fy], k == 0)
+        to_core(source, block, cc_s, (k, fx, fy))
+
+    def c_own():
+        source, block = sent.at[n_rest], n_at(0, 0, 0, n_rest)
+        held["cx"] = go(source, block, cx_s, (0,), me.x_mate)
+        cy[0] = go(source, block, cy_s, (0,), me.y_mate)
+        c_line(0, 0, 0, source)
+
+    def c_from_x():
+        held["cx"].wait_recv()
+        block = n_at(0, 1, 0, n_rest)
+        cy[1] = go(block, block, cy_s, (1,), me.y_mate)
+        c_line(0, 1, 0)
+
+    def c_from_y(fx):
+        cy[fx].wait_recv()
+        c_line(0, fx, 1)
+
     actions = {
+        "n": n_own, "nx": n_over_y, "ny": n_over_x,
+        "nca": lambda k: n_corner(k, ndy, n_low, 3), "ncb": lambda k: n_corner(k, ndx, n_high, 4),
+        "c0": c_own, "c1": c_from_x, "c2": c_from_y, "cz": c_line,
         "pair": pair_rows, "bx": b_over_x, "ay0": lambda: a_over_y(0), "w": w_own, "wx": w_across,
-        "a": a_own, "ax": a_across, "b": b_step, "y": y_done, "prep": prepare, "qkv": project,
+        "a": a_own, "ax": a_across, "b": b_step, "y1": y_done, "prep": prepare, "qkv": project,
         "h": attend, "ctx": output_over_y, "ctx2": output_own, "fin": finish,
     }
     for name, *which in OPENING_PLAN:
@@ -1402,6 +1389,11 @@
         line_done(k, d_source(k, low), d_at(k, 0, 0, low), az_s)
         line_done(k, d_source(k, high), d_at(k, 0, 0, high), bz_s.at[0])
         line_done(k, d_at(k, 1, 0, high), d_at(k, 1, 0, high), bz_s.at[1])
+        line_done(k, n_source(k, n_most), n_at(k, 0, 0, n_most), nz_s)
+        for fx in range(2):
+            for fy in range(2):
+                source = n_source(k, n_rest) if (fx, fy) == (0, 0) else n_at(k, fx, fy, n_rest)
+                line_done(k, source, n_at(k, fx, fy, n_rest), cz_s.at[fx, fy])
     for copy in sent_on + copies:
         copy.wait_send()
     for k in range(GRID_Z):
@@ -1412,27 +1404,41 @@
                     remote(
                         block, block, dc_s.at[0, k, fx, fy, h], dc_s.at[1, k, fx, fy, h], me.sibling
                     ).wait_recv()
+            for fy in range(2):
+                block = n_at(k, fx, fy, n_rest)
+                remote(
+                    block, block, cc_s.at[0, k, fx, fy], cc_s.at[1, k, fx, fy], me.sibling
+                ).wait_recv()
+        for i, (fx, fy, at) in enumerate(
+            ((0, 0, n_most), (1, 0, n_most), (0, 1, n_most), (1, 1, n_low), (1, 1, n_high))
+        ):
+            block = n_at(k, fx, fy, at)
+            remote(block, block, nc_s.at[0, k, i], nc_s.at[1, k, i], me.sibling).wait_recv()
     waits[1].wait()
     for copy in outs:
         copy.wait()
 
 
 def opening(
-    weights, cotangents, inputs, live, chosen, experts, heads, key_heads, collective_id
+    lengths, sequence_order, weights, gains, routes, cotangents, inputs, experts, collective_id
 ):
     bf16, f32 = jnp.bfloat16, jnp.float32
     chips, pair = lax.axis_size("dp"), lax.axis_size("tensor")
     own_rows, features = inputs.shape
     rows = pair * own_rows
-    shard = weights.shape[0]
-    wide = heads * HEAD_SIZE
+    query, key, value, context, router = weights
+    shard, wide = query.shape
+    heads, key_heads = wide // HEAD_SIZE, key.shape[1] // HEAD_SIZE
+    width = 2 * wide + 2 * key.shape[1] + AUX
+    count, top = gains[2].shape[0], routes.shape[1]
     qkv = (heads + 2 * key_heads) * HEAD_SIZE
     cosine, sine = turn_tables(rows)
     dma = pltpu.SemaphoreType.DMA
     shapes = (
-        ((chips, *weights.shape), bf16),
+        ((chips, shard, width), bf16),
         ((chips * pair, *cotangents.shape), bf16),
         ((pair, *inputs.shape), bf16),
+        ((chips * pair, own_rows, features + AUX), bf16),
         ((own_rows, features + AUX), bf16),
         ((own_rows, features), f32),
         ((rows, features), bf16),
@@ -1442,11 +1448,11 @@
         ((key_heads, rows, HEAD_SIZE), bf16),
         ((rows, wide), bf16),
     )
-    anywhere, vmem = pl.BlockSpec(memory_space=pl.ANY), pl.BlockSpec(memory_space=pltpu.VMEM)
-    w, d, x, *rest = pl.pallas_call(
+    anywhere, smem = pl.BlockSpec(memory_space=pl.ANY), pl.BlockSpec(memory_space=pltpu.SMEM)
+    w, d, x, gathered, *rest = pl.pallas_call(
         functools.partial(opening_kernel, experts, qkv),
         out_shape=tuple(jax.ShapeDtypeStruct(*shape) for shape in shapes),
-        in_specs=[anywhere] * 3 + [vmem] * 4,
+        in_specs=[smem] * 2 + [anywhere] * 14,
         out_specs=(anywhere,) * len(shapes),
         scratch_shapes=[
             pltpu.VMEM((pair, own_rows, features), bf16),
@@ -1479,15 +1485,39 @@
             dma((qkv // 512,)),
             dma((8,)),
             dma((2, features // 512)),
+            pltpu.VMEM((shard, width), bf16),
+            pltpu.VMEM(context.shape, bf16),
+            pltpu.VMEM((experts, shard), bf16),
+            pltpu.VMEM((2, 1, shard), bf16),
+            pltpu.VMEM((2, 1, count), bf16),
+            pltpu.VMEM((top, rows), jnp.int32),
+            pltpu.VMEM((rows, HEAD_SIZE), f32),
+            pltpu.VMEM((rows, HEAD_SIZE), f32),
+            dma((12,)),
+            dma((1,)),
+            dma((2, 2, 4)),
+            dma((2, 4)),
+            dma((2, 4)),
+            dma((2, 4)),
+            dma((2, 4)),
+            dma((2, 4, 5)),
+            dma((2, 1)),
+            dma((2, 2)),
+            dma((2, 2, 2, 2, 4)),
+            dma((2, 4, 2, 2)),
         ],
         compiler_params=pltpu.CompilerParams(
             collective_id=collective_id, has_side_effects=True, vmem_limit_bytes=ATTENTION_VMEM
         ),
-    )(weights, cotangents, inputs, live, chosen, cosine, sine)
+    )(
+        lengths, sequence_order, query, key, value, context, router.T,
+        *(gain[None] for gain in gains), routes.T, cotangents, inputs, cosine, sine,
+    )
     return (
         w.reshape(-1, w.shape[2]),
         d.reshape(chips, -1, d.shape[2]),
         x.reshape(-1, x.shape[2]),
+        gathered.reshape(chips, -1, gathered.shape[2]),
         *rest,
     )
 
@@ -1497,12 +1527,13 @@
 
 
 def backward_kernel(
-    experts, back_in, residual_in, sent_in, dy_in, x_in, packed, live, cosine, sine, normed_in,
+    experts, lengths, sequence_order, back_in, residual_in, sent_in, dy_in, x_in, packed,
+    cosine_in, sine_in, normed_in,
     raw_in, query_in, key_in, value_in, context_in,
     grads, input_gradient,
     back, residual, sent, dy, x, w, ctx, aux_w, normed, raw, query, key, value, context,
     cot, context_cot, raw_cot, key_sum, value_sum, small, first, first_got, stage, result,
-    in_s, out_s, y_s, g_s,
+    cosine, sine, in_s, out_s, y_s, g_s,
 ):
     bf16, f32 = jnp.bfloat16, jnp.float32
     me = Place()
@@ -1532,6 +1563,8 @@
                 (packed.at[:, pl.ds(0, qkv)], w),
                 (normed_in, normed),
                 (x_in, x),
+                (cosine_in, cosine),
+                (sine_in, sine),
             )
         )
     ]
@@ -1588,7 +1621,7 @@
         copy.wait()
 
     turn_c, turn_s = cosine[...], sine[...]
-    allowed = allowed_pairs(live[...])
+    allowed = allowed_pairs(lengths[sequence_order[me.dp]], rows)
     key_sum[...] = jnp.zeros_like(key_sum)
     value_sum[...] = jnp.zeros_like(value_sum)
 
@@ -1713,7 +1746,7 @@
 
 
 def attention_backward(
-    back, residual, sent, dy, x_pair, packed, live, saved, experts, collective_id
+    lengths, sequence_order, back, residual, sent, dy, x_pair, packed, saved, experts, collective_id
 ):
     bf16, f32 = jnp.bfloat16, jnp.float32
     normed, raw, query, key, value, context = saved
@@ -1724,14 +1757,14 @@
     qkv = wide + 2 * key_heads * HEAD_SIZE
     cosine, sine = turn_tables(rows)
     dma = pltpu.SemaphoreType.DMA
-    anywhere, vmem = pl.BlockSpec(memory_space=pl.ANY), pl.BlockSpec(memory_space=pltpu.VMEM)
+    anywhere, smem = pl.BlockSpec(memory_space=pl.ANY), pl.BlockSpec(memory_space=pltpu.SMEM)
     return pl.pallas_call(
         functools.partial(backward_kernel, experts),
         out_shape=(
             jax.ShapeDtypeStruct((features, qkv + wide + AUX), bf16),
             jax.ShapeDtypeStruct((own_rows, features), bf16),
         ),
-        in_specs=[anywhere] * 6 + [vmem] * 3 + [anywhere] * 6,
+        in_specs=[smem] * 2 + [anywhere] * 14,
         out_specs=(anywhere,) * 2,
         scratch_shapes=[
             pltpu.VMEM((own_rows, features + AUX), bf16),
@@ -1758,7 +1791,9 @@
             pltpu.VMEM((own_rows, features), bf16),
             pltpu.VMEM((2, 256, qkv + wide), bf16),
             pltpu.VMEM((own_rows, features), bf16),
-            dma((14,)),
+            pltpu.VMEM((rows, HEAD_SIZE), f32),
+            pltpu.VMEM((rows, HEAD_SIZE), f32),
+            dma((16,)),
             dma((2,)),
             dma((2, 1 + features // 512)),
             dma((2,)),
@@ -1767,7 +1802,7 @@
             collective_id=collective_id, has_side_effects=True, vmem_limit_bytes=ATTENTION_VMEM
         ),
     )(
-        back, residual, sent, dy, x_pair, packed, live, cosine, sine,
+        lengths, sequence_order, back, residual, sent, dy, x_pair, packed, cosine, sine,
         normed, raw, query, key, value, context,
     )
 
@@ -2030,6 +2065,59 @@
     )(grads.reshape(chips, g_rows, g_wide), sums.reshape(chips * pair, d_rows, d_wide))
 
 
+def unpack_kernel(
+    experts, summed, added, residual,
+    layer_output, query, key, value, context, router, prenorm, midnorm, querynorm, keynorm,
+):
+    f32 = jnp.float32
+    wide, narrow = query.shape[1], key.shape[1]
+    layer_output[...] = (residual[...] + added[...].astype(f32)).astype(layer_output.dtype)
+    query[...] = summed[:, pl.ds(0, wide)].astype(f32)
+    key[...] = summed[:, pl.ds(wide, narrow)].astype(f32)
+    value[...] = summed[:, pl.ds(wide + narrow, narrow)].astype(f32)
+    start = wide + 2 * narrow
+    context[...] = summed[:, pl.ds(start, wide)].astype(f32).T
+    small = summed[:, pl.ds(start + wide, AUX)].astype(f32)
+    router[...] = small[:, :experts]
+    rows = small.T
+    prenorm[...] = rows[experts : experts + 1, :]
+    midnorm[...] = rows[experts + 1 : experts + 2, :]
+    count = querynorm.shape[1]
+    lane = lax.broadcasted_iota(jnp.int32, (count, AUX), 1)
+    row = lax.broadcasted_iota(jnp.int32, (count, AUX), 0)
+    pick = row + lax.axis_index("dp") * count == lane
+    for target, at in ((querynorm, experts + 2), (keynorm, experts + 3)):
+        part = jnp.where(pick, rows[at : at + 1, :], 0.0)
+        target[...] = jnp.sum(part, axis=1, keepdims=True).T
+
+
+def unpack(summed, added, residual, query_width, key_width, experts, norm_part):
+    bf16, f32 = jnp.bfloat16, jnp.float32
+    shard = summed.shape[0]
+    own_rows, features = residual.shape
+    shapes = (
+        ((own_rows, features), bf16),
+        ((shard, query_width), f32),
+        ((shard, key_width), f32),
+        ((shard, key_width), f32),
+        ((query_width, shard), f32),
+        ((shard, experts), f32),
+        ((1, shard), f32),
+        ((1, shard), f32),
+        ((1, norm_part), f32),
+        ((1, norm_part), f32),
+    )
+    vmem = pl.BlockSpec(memory_space=pltpu.VMEM)
+    *large, first, second, third, fourth = pl.pallas_call(
+        functools.partial(unpack_kernel, experts),
+        out_shape=tuple(jax.ShapeDtypeStruct(*shape) for shape in shapes),
+        in_specs=[vmem] * 3,
+        out_specs=(vmem,) * len(shapes),
+        compiler_params=pltpu.CompilerParams(vmem_limit_bytes=32 * 1024 * 1024),
+    )(summed, added, residual)
+    return (*large, first[0], second[0], third[0], fourth[0])
+
+
 def gathered_body(
     layer_input,
     query_weight,
@@ -2065,49 +2153,23 @@
     key_width = key_projection.shape[1]
     norm_part = HEAD_SIZE // dp_count
 
-    place = dp_index * norm_part
-    route_wide = block_rows * TOP // shard
-    gains = jnp.concatenate(
-        [
-            prenorm_gain[:, None],
-            midnorm_gain[:, None],
-            lax.dynamic_update_slice(jnp.zeros((shard,), bf16), querynorm_gain, (place,))[:, None],
-            lax.dynamic_update_slice(jnp.zeros((shard,), bf16), keynorm_gain, (place,))[:, None],
-            routes.T.reshape(shard, -1).astype(bf16),
-            jnp.zeros((shard, AUX - expert_count - 4 - route_wide), bf16),
-        ],
-        axis=1,
-    )
-    packed = jnp.concatenate(
-        [query_weight, key_projection, value_projection, router_weight, gains, context_weight.T],
-        axis=1,
-    )
-    position = jnp.arange(block_rows, dtype=jnp.int32)
-    block_lengths = lengths[sequence_order]
-    live = position[None, :] < block_lengths[:, None]
-    live_own = lax.dynamic_slice_in_dim(live, dp_index, 1, 0)
-    live_own = jnp.broadcast_to(live_own.astype(f32), (8, block_rows))
-    heads_query = query_width // HEAD_SIZE
-    heads_key = key_width // HEAD_SIZE
-    row_start = tensor_index * own_rows
-    routes_own = lax.dynamic_slice_in_dim(routes, row_start, own_rows, 0)
-    expert_ids = jnp.arange(AUX, dtype=jnp.int32)
-    chosen = jnp.any(routes_own[:, :, None] == expert_ids[None, None, :], axis=1).astype(f32)
-    packed, cot_all, input_rows, sent, residual, *saved = opening(
-        packed,
+    packed, cot_all, input_rows, normed_all, sent, residual, *saved = opening(
+        lengths,
+        sequence_order,
+        (query_weight, key_projection, value_projection, context_weight, router_weight),
+        (prenorm_gain, midnorm_gain, querynorm_gain, keynorm_gain),
+        routes,
         output_cotangent,
         layer_input,
-        live_own,
-        chosen,
         expert_count,
-        heads_query,
-        heads_key,
         0,
     )
     route_from = query_width + 2 * key_width + expert_count + 4
-    routes_all = packed[:, route_from : route_from + route_wide].astype(jnp.int32)
+    routes_all = packed[:, route_from : route_from + 2 * TOP].astype(jnp.int32)
+    routes_all = routes_all.reshape(dp_count, shard, 2, TOP).transpose(0, 3, 2, 1)
     routes_all = routes_all.reshape(dp_count, TOP, block_rows)
-    normed_all = gather_all(sent, 1).reshape(dp_count, block_rows, features + AUX)
+    position = jnp.arange(block_rows, dtype=jnp.int32)
+    live = position[None, :] < lengths[sequence_order][:, None]
 
     expert_own = dp_index * EXP_DEV + jnp.arange(EXP_DEV, dtype=jnp.int32)
     hot = jnp.any(routes_all[:, None, :, :] == expert_own[None, :, None, None], axis=2)
@@ -2134,40 +2196,46 @@
     )
     returned = scatter_all(back_part.reshape(tokens, features + AUX), 3)
     grads, input_gradient = attention_backward(
+        lengths,
+        sequence_order,
         returned,
         residual,
         sent,
         output_cotangent,
         input_rows,
         packed,
-        live_own,
         saved,
         expert_count,
         6,
     )
     summed, expert_sum = last_scatter(grads, out_part.reshape(tokens, features), 4)
-    summed = summed.astype(f32)
-    layer_output = (residual + expert_sum.astype(f32)).astype(bf16)
-    ends = [0]
-    for width in (query_width, key_width, key_width, query_width, AUX):
-        ends.append(ends[-1] + width)
-    small = summed[:, ends[4] :]
-    head_small = lax.dynamic_slice_in_dim(small, place, norm_part, 0)
+    (
+        layer_output,
+        query_gradient,
+        key_gradient,
+        value_gradient,
+        context_gradient,
+        router_gradient,
+        prenorm_gradient,
+        midnorm_gradient,
+        querynorm_gradient,
+        keynorm_gradient,
+    ) = unpack(summed, expert_sum, residual, query_width, key_width, expert_count, norm_part)
     return (
         layer_output,
         input_gradient,
-        summed[:, : ends[1]],
-        summed[:, ends[1] : ends[2]],
-        summed[:, ends[2] : ends[3]],
-        summed[:, ends[3] : ends[4]].T,
-        small[:, :expert_count],
+        query_gradient,
+        key_gradient,
+        value_gradient,
+        context_gradient,
+        router_gradient,
         gate_gradient,
         up_gradient,
         down_gradient,
-        small[:, expert_count],
-        small[:, expert_count + 1],
-        head_small[:, expert_count + 2],
-        head_small[:, expert_count + 3],
+        prenorm_gradient,
+        midnorm_gradient,
+        querynorm_gradient,
+        keynorm_gradient,
     )
 
 

time: 627 us -> 594 us (0.947)
  local copies, waits for them, and re-layouts: 21 us -> 6.23 us
  Pallas kernels: 594 us -> 581 us
    pallas_call x1, Pallas kernels: 78 us -> 1.89 us  [unpack(): pl.pallas_call(functools.partial(unpack_kernel, experts), out_shape=tuple...]
    pallas_call x1, Pallas kernels: 164 us -> 228 us  [opening(): pl.pallas_call(functools.partial(opening_kernel, experts, qkv), out_shape...]
    slice x6 -> x0, local copies, waits for them, and re-layouts: 6.66 us -> none  [the longest x1 2.12 us: gathered_body(): summed[:, :ends[1]]]
where the time goes in v7:
time: 594 us; the launch traced here: 592 us
  Pallas kernels  581 us (98%)
  local copies, waits for them, and re-layouts  6.23 us (1%)
    pallas_call x1, Pallas kernels, opening(): pl.pallas_call(functools.partial(opening_kernel, experts, qkv), out_shape...  228 us
    pallas_call x1, Pallas kernels, last_scatter(): pl.pallas_call(last_scatter_kernel, out_shape=(jax.ShapeDtypeStruct((g_ro...  144 us
    pallas_call x1, Pallas kernels, scatter_all(): pl.pallas_call(scatter_kernel, out_shape=jax.ShapeDtypeStruct((rows, widt...  84.6 us
    pallas_call x1, Pallas kernels, expert_layer(): pl.pallas_call(expert_kernel, out_shape=(shape((blocks, block_rows, featu...  73.4 us
    pallas_call x1, Pallas kernels, attention_backward(): pl.pallas_call(functools.partial(backward_kernel, experts), out_shape=(ja...  48.5 us

profile of v7, /device:TPU:0, one launch (start us, length us, event | category | flops | bytes accessed | tf_op | source)
XLA Modules:
  0.0 591.9 jit_solution(3212749462070532585)
XLA Ops:
  0.7 0.7 compare_select_fusion
  1.3 1.3 gather_fusion
  2.6 0.1 iota_compare_fusion.1
  2.7 227.8 %shard_map.308 = (bf16[16,128,4736]{2,1,0:T(8,128)(2,1)}, bf16[32,128,2048]{2,1,0:T(8,128)(2,1)}, bf16[2,128,2048]{2,1,0:T(8,128)(2,1)}, bf16[32,128,2176]{2,1,0...) custom-call(s32[16]{0:T(128)} %lengths.3, ...), custom_call_target="tpu_custom_call" | custom-call | tf_op jit(solution)/shard_map/pallas_call | solution.py:1452
  230.6 1.3 slice_convert_fusion
  231.9 0.3 copy.66
  232.3 0.2 compare_reduce_fusion
  232.5 0.1 fusion.1
  232.7 0.4 fusion.6
  233.1 0.1 add.41
  233.2 0.1 copy.70
  233.3 0.1 copy.71
  233.4 0.1 reduce_window_sum.16
  233.5 0.6 pad_add_fusion.info
  234.1 0.2 copy.73
  234.3 0.1 copy.74
  234.4 0.1 copy.75
  234.5 0.7 and_select_fusion.pos
  235.2 73.4 %shard_map.309 = (bf16[16,256,2048]{2,1,0:T(8,128)(2,1)}, bf16[16,256,2176]{2,1,0:T(8,128)(2,1)}, f32[2,2048,384]{2,1,0:T(8,128)}, f32[2,2048,384]{2,1,0:T(8,128)}, f32[2,384,2048]{2,1,0:T(8,128)}) custom-call(s32[34]{0:T(128)} %pad_add_fusion.info, s32[16,2,256]{2,1,0:T(2,128)} %and_select_fusion.pos, bf16[16,256,2176]{2,1,0:T(8,128)(2,1)} %bitcast.41, ...), custom_call_target="tpu_custom_call" | custom-call | tf_op jit(solution)/shard_map/pallas_call | solution.py:876
  308.6 84.6 %shard_map.310.back_in = bf16[128,2176]{1,0:T(8,128)(2,1)} custom-call(bf16[32,128,2176]{2,1,0:T(8,128)(2,1)} %bitcast.42), custom_call_target="tpu_custom_call" | custom-call | tf_op jit(solution)/shard_map/pallas_call | solution.py:628
  393.2 48.5 %shard_map.311 = (bf16[2048,4736]{1,0:T(8,128)(2,1)}, bf16[128,2048]{1,0:T(8,128)(2,1)}) custom-call(s32[16]{0:T(128)} %lengths.3, s32[16]{0:T(128)} %sequence_order.3, bf16[128,2176]{1,0:T(8,128)(2,1)} %shard_map.310.back_in, f32[128,2048]{1,0:T(8,128)} %get-tuple-element.49.residual_in.residual, bf16[128,2176]{1,0:T(8,128)(2,1)} %get-tuple-element.50.sent_in, ...), custom_call_target="tpu_custom_call" | custom-call | tf_op jit(solution)/shard_map/pallas_call | solution.py:1761
  441.8 0.0 copy-start
  441.8 0.0 copy-start.3
  441.8 144.4 %shard_map.312 = (bf16[128,4736]{1,0:T(8,128)(2,1)}, bf16[128,2048]{1,0:T(8,128)(2,1)}) custom-call(bf16[16,128,4736]{2,1,0:T(8,128)(2,1)} %bitcast.40, bf16[32,128,2048]{2,1,0:T(8,128)(2,1)} %bitcast.44), custom_call_target="tpu_custom_call" | custom-call | tf_op jit(solution)/shard_map/pallas_call | solution.py:2027
  586.2 0.0 copy-done
  586.2 0.0 copy-start.1
  586.2 1.3 copy-done.1
  587.5 1.0 copy-done.2
  588.5 1.9 shard_map.313
  590.4 0.7 copy.76
  591.1 0.0 copy-done.3
  591.1 0.8 copy.90
  (10 shorter events, 0.2 us)
Async XLA Ops:
  441.8 144.4 %copy-start = (f32[128,2048]{1,0:T(8,128)S(1)}, f32[128,2048]{1,0:T(8,128)}, u32[]{:S(2)}) copy-start(f32[128,2048]{1,0:T(8,128)} %get-tuple-element.49.residual_in.residual) | copy-start | bytes 3145732
  441.8 149.3 %copy-start.3 = (bf16[128,2048]{1,0:T(8,128)(2,1)S(1)}, bf16[128,2048]{1,0:T(8,128)(2,1)}, u32[]{:S(2)}) copy-start(bf16[128,2048]{1,0:T(8,128)(2,1)} %get-tuple-element.149) | copy-start | bytes 1572868
  586.2 1.3 copy-start.1
  587.5 1.0 copy-start.2

commit v8 on v7

--- a/solution.py
+++ b/solution.py
@@ -481,15 +481,67 @@
     lax.fori_loop(0, count // step, one, 0)
 
 
-def scatter_kernel(
-    part, out, own, core, diag_a, diag_b, from_x, from_y, from_z, result,
-    load_s, core_s, diag_s, x_s, y_s, z_s, out_s,
+def line_onward(me, source, buffer, sem, to, side, mate):
+    ends = 1 - (me.z - 1 - to + GRID_Z - 1) // GRID_Z
+    slot = to if side == 0 else to + (GRID_Z - to) * ends
+    return remote(source, buffer.at[slot], sem.at[0, to], sem.at[1, slot], mate)
+
+
+def line_sum(me, k, block, source, rows, buffer, sem, shift):
+    to = me.farthest(k)
+    for side, ahead, mate, more in (
+        (0, to > me.z, me.above, me.has_below),
+        (1, to < me.z, me.below, me.has_above),
+    ):
+        slot = to if k < GRID_Z - 1 or side == 0 else GRID_Z
+        came = remote(source, buffer.at[slot], sem.at[0, slot], sem.at[1, slot], mate)
+
+        def gather(came=came, slot=slot):
+            came.wait_recv()
+            add_rows(block, [(buffer.at[slot], shift)], rows)
+
+        if k < GRID_Z - 1:
+
+            @pl.when(ahead)
+            def _():
+                pl.when(more)(gather)
+                line_onward(me, source, buffer, sem, to, side, mate).start()
+        else:
+            pl.when(more)(gather)
+
+
+def line_sent(me, k, source, buffer, sem):
+    to = me.farthest(k)
+    for side, ahead, mate in ((0, to > me.z, me.above), (1, to < me.z, me.below)):
+
+        @pl.when(ahead)
+        def _():
+            line_onward(me, source, buffer, sem, to, side, mate).wait_send()
+
+
+ROW_PLAN = (
+    ("eda", 0), ("cz", 0, 1, 1), ("edb", 0), ("ey", 0), ("cz", 0, 0, 1), ("ex", 0), ("eda", 1),
+    ("cz", 0, 0, 0), ("cz", 1, 0, 1), ("edb", 1), ("lx", 0), ("cz", 1, 1, 1), ("eda", 2),
+    ("cz", 2, 1, 1), ("ly", 0), ("ly", 1), ("cz", 2, 0, 1), ("lx", 2), ("ex", 1), ("eda", 3),
+    ("cz", 0, 1, 0), ("cz", 1, 1, 0), ("edb", 2), ("lx", 1), ("ey", 1), ("ey", 2), ("col", 0),
+    ("edb", 3), ("cz", 2, 1, 0), ("cz", 1, 0, 0), ("cz", 3, 0, 1), ("cy", 0), ("cz", 3, 1, 1),
+    ("ly", 2), ("ex", 2), ("col", 1), ("ly", 3), ("cz", 2, 0, 0), ("lx", 3), ("ex", 3),
+    ("col", 2), ("cy", 1), ("ey", 3), ("cz", 3, 0, 0), ("cz", 3, 1, 0), ("cx",), ("cend",),
+    ("col", 3),
+)
+
+
+def row_scatter_kernel(
+    part, out, own, core, diag_a, diag_b, from_x, from_y, from_z, c_z, c_y, c_x,
+    load_s, core_s, diag_s, x_s, y_s, z_s, cz_s, cy_s, cx_s, out_s,
 ):
     me = Place()
-    rows = own.shape[3]
-    half = rows // 2
-    low, high = (0, half), (half, half)
-    loads, sends = {}, []
+    rows, third = own.shape[3], diag_a.shape[1]
+    last = GRID_Z - 1
+    spans = ((0, third), (third, third), (2 * third, rows - 2 * third))
+    a_at, b_at, c_at = (pl.ds(*span) for span in spans)
+    most, most_at = (0, 2 * third), pl.ds(0, 2 * third)
+    loads, cores, here = {}, {}, set()
 
     def chunk(k, flip_x, flip_y, flip_core):
         return part.at[me.dp_at(me.farthest(k), flip_x, flip_core) * 2 + me.y_at(flip_y)]
@@ -503,7 +555,6 @@
             copy.start()
             loads[k, fx, fy] = copy
     me.greet()
-    cores = {}
     for k in range(GRID_Z):
         for fx, fy in order:
             copy = remote(
@@ -512,92 +563,97 @@
             )
             copy.start()
             cores[k, fx, fy] = copy
-            sends.append(copy)
-
-    da = [remote(own.at[k, 1, 1, pl.ds(0, half)], diag_a.at[k], diag_s.at[0, k], diag_s.at[1, k], me.y_mate) for k in range(4)]
-    db = [remote(own.at[k, 1, 1, pl.ds(half, half)], diag_b.at[k], diag_s.at[2, k], diag_s.at[3, k], me.x_mate) for k in range(4)]
-    xs = [[remote(own.at[k, 1, 0, pl.ds(h * half, half)], from_x.at[k, pl.ds(h * half, half)], x_s.at[0, k, h], x_s.at[1, k, h], me.x_mate) for h in range(2)] for k in range(4)]
-    ys = [[remote(own.at[k, 0, 1, pl.ds(h * half, half)], from_y.at[k, pl.ds(h * half, half)], y_s.at[0, k, h], y_s.at[1, k, h], me.y_mate) for h in range(2)] for k in range(4)]
-
-    def arrive(k, fx, fy):
-        loads[k, fx, fy].wait()
-        cores[k, fx, fy].wait_recv()
-
-    def early(k):
-        arrive(k, 1, 1)
-        add_rows(own.at[k, 1, 1], [(core.at[k, 1, 1], 0)], low)
+
+    def pieces(make):
+        return [make(k) for k in range(GRID_Z)]
+
+    da = pieces(lambda k: remote(own.at[k, 1, 1, a_at], diag_a.at[k], diag_s.at[0, k], diag_s.at[1, k], me.y_mate))
+    db = pieces(lambda k: remote(own.at[k, 1, 1, b_at], diag_b.at[k], diag_s.at[2, k], diag_s.at[3, k], me.x_mate))
+    xs = pieces(
+        lambda k: [
+            remote(own.at[k, 1, 0, at], from_x.at[k, at], x_s.at[0, k, h], x_s.at[1, k, h], me.x_mate)
+            for h, at in enumerate((a_at, b_at))
+        ]
+    )
+    ys = pieces(
+        lambda k: [
+            remote(own.at[k, 0, 1, at], from_y.at[k, at], y_s.at[0, k, h], y_s.at[1, k, h], me.y_mate)
+            for h, at in enumerate((a_at, b_at))
+        ]
+    )
+    cy = [
+        remote(own.at[last, fx, 1, c_at], c_y.at[fx], cy_s.at[0, fx], cy_s.at[1, fx], me.y_mate)
+        for fx in range(2)
+    ]
+    cx = remote(own.at[last, 1, 0, c_at], c_x, cx_s.at[0], cx_s.at[1], me.x_mate)
+
+    def add(k, fx, fy, h, *more):
+        if (k, fx, fy) not in here:
+            here.add((k, fx, fy))
+            loads[k, fx, fy].wait()
+            cores[k, fx, fy].wait_recv()
+        span = most if h is None else spans[h]
+        add_rows(own.at[k, fx, fy], [(core.at[k, fx, fy], 0), *more], span)
+
+    def diagonal_a(k):
+        add(k, 1, 1, 0)
         da[k].start()
-        add_rows(own.at[k, 1, 1], [(core.at[k, 1, 1], 0)], high)
+
+    def diagonal_b(k):
+        add(k, 1, 1, 1)
         db[k].start()
-        arrive(k, 1, 0)
-        add_rows(own.at[k, 1, 0], [(core.at[k, 1, 0], 0)], high)
+
+    def early_x(k):
+        add(k, 1, 0, 1)
         xs[k][1].start()
-        arrive(k, 0, 1)
-        add_rows(own.at[k, 0, 1], [(core.at[k, 0, 1], 0)], low)
+
+    def early_y(k):
+        add(k, 0, 1, 0)
         ys[k][0].start()
 
-    def late(k):
+    def late_x(k):
         da[k].wait_recv()
-        add_rows(own.at[k, 1, 0], [(core.at[k, 1, 0], 0), (diag_a.at[k], 0)], low)
+        add(k, 1, 0, 0, (diag_a.at[k], 0))
         xs[k][0].start()
+
+    def late_y(k):
         db[k].wait_recv()
-        add_rows(own.at[k, 0, 1], [(core.at[k, 0, 1], 0), (diag_b.at[k], half)], high)
+        add(k, 0, 1, 1, (diag_b.at[k], third))
         ys[k][1].start()
 
-    whole = (0, rows)
-
     def column(k):
-        arrive(k, 0, 0)
         for h in range(2):
             xs[k][h].wait_recv()
             ys[k][h].wait_recv()
-        mine = own.at[k, 0, 0]
-        rest = [(core.at[k, 0, 0], 0), (from_x.at[k], 0), (from_y.at[k], 0)]
-        if k < GRID_Z - 1:
-            to = me.farthest(k)
-            add_rows(mine, rest, whole)
-            for side, ahead, mate, more in (
-                (0, to > me.z, me.above, me.has_below),
-                (1, to < me.z, me.below, me.has_above),
-            ):
-                copy = remote(
-                    mine, from_z.at[side, to], z_s.at[0, side, to], z_s.at[1, side, to], mate
-                )
-
-                @pl.when(ahead)
-                def _():
-                    @pl.when(more)
-                    def _():
-                        copy.wait_recv()
-                        add_rows(mine, [(from_z.at[side, to], 0)], whole)
-
-                    copy.start()
-        else:
-            add_rows(mine, rest, whole)
-            for side, more in ((0, me.has_below), (1, me.has_above)):
-                copy = remote(
-                    mine, from_z.at[side, me.z], z_s.at[0, side, me.z], z_s.at[1, side, me.z],
-                    me.y_mate,
-                )
-
-                @pl.when(more)
-                def _():
-                    copy.wait_recv()
-                    add_rows(mine, [(from_z.at[side, me.z], 0)], whole)
-
-    early(0)
-    early(1)
-    late(0)
-    early(2)
-    late(1)
-    column(0)
-    early(3)
-    late(2)
-    column(1)
-    late(3)
-    column(2)
-    column(3)
-    copy = pltpu.make_async_copy(own.at[3, 0, 0], out, out_s)
+        add(k, 0, 0, None, (from_x.at[k], 0), (from_y.at[k], 0))
+        block = own.at[k, 0, 0]
+        line_sum(me, k, block, block.at[most_at], most, from_z, z_s, 0)
+
+    def c_line(k, fx, fy):
+        add(k, fx, fy, 2)
+        block = own.at[k, fx, fy]
+        line_sum(
+            me, k, block, block.at[c_at], spans[2], c_z.at[fx, fy], cz_s.at[fx, fy], 2 * third
+        )
+
+    def c_over_x():
+        cy[1].wait_recv()
+        add_rows(own.at[last, 1, 0], [(c_y.at[1], 2 * third)], spans[2])
+        cx.start()
+
+    def c_end():
+        cy[0].wait_recv()
+        cx.wait_recv()
+        add_rows(own.at[last, 0, 0], [(c_y.at[0], 2 * third), (c_x, 2 * third)], spans[2])
+
+    actions = {
+        "eda": diagonal_a, "edb": diagonal_b, "ex": early_x, "ey": early_y, "lx": late_x,
+        "ly": late_y, "col": column, "cz": c_line, "cy": lambda fx: cy[fx].start(),
+        "cx": c_over_x, "cend": c_end,
+    }
+    for name, *which in ROW_PLAN:
+        actions[name](*which)
+    copy = pltpu.make_async_copy(own.at[last, 0, 0], out, out_s)
     copy.start()
     for k in range(GRID_Z):
         da[k].wait_send()
@@ -605,16 +661,11 @@
         for h in range(2):
             xs[k][h].wait_send()
             ys[k][h].wait_send()
-        if k < GRID_Z - 1:
-            to = me.farthest(k)
-            for side, ahead, mate in ((0, to > me.z, me.above), (1, to < me.z, me.below)):
-                @pl.when(ahead)
-                def _():
-                    remote(
-                        own.at[k, 0, 0], from_z.at[side, to],
-                        z_s.at[0, side, to], z_s.at[1, side, to], mate,
-                    ).wait_send()
-    for sent in sends:
+        if k < last:
+            line_sent(me, k, own.at[k, 0, 0, most_at], from_z, z_s)
+            for fx, fy in order:
+                line_sent(me, k, own.at[k, fx, fy, c_at], c_z.at[fx, fy], cz_s.at[fx, fy])
+    for sent in (*cores.values(), *cy, cx):
         sent.wait_send()
     copy.wait()
 
@@ -622,29 +673,29 @@
 def scatter_all(value, collective_id):
     devices = lax.axis_size("dp") * lax.axis_size("tensor")
     rows, width = value.shape[0] // devices, value.shape[1]
-    half = rows // 2
+    third = 3 * rows // 8
     dma = pltpu.SemaphoreType.DMA
     low = value.dtype
+    shapes = (
+        (4, 2, 2, rows), (4, 2, 2, rows), (4, third), (4, third), (4, 2 * third), (4, 2 * third),
+        (5, 2 * third), (2, 2, 5, rows - 2 * third), (2, rows - 2 * third), (rows - 2 * third,),
+    )
     return pl.pallas_call(
-        scatter_kernel,
+        row_scatter_kernel,
         out_shape=jax.ShapeDtypeStruct((rows, width), low),
         in_specs=[pl.BlockSpec(memory_space=pl.ANY)],
         out_specs=pl.BlockSpec(memory_space=pl.ANY),
         scratch_shapes=[
-            pltpu.VMEM((4, 2, 2, rows, width), low),
-            pltpu.VMEM((4, 2, 2, rows, width), low),
-            pltpu.VMEM((4, half, width), low),
-            pltpu.VMEM((4, half, width), low),
-            pltpu.VMEM((4, rows, width), low),
-            pltpu.VMEM((4, rows, width), low),
-            pltpu.VMEM((2, 4, rows, width), low),
-            pltpu.VMEM((8, 128), low),
+            *(pltpu.VMEM((*shape, width), low) for shape in shapes),
             dma((4, 2, 2)),
             dma((2, 4, 2, 2)),
             dma((4, 4)),
             dma((2, 4, 2)),
             dma((2, 4, 2)),
-            dma((2, 2, 4)),
+            dma((2, 5)),
+            dma((2, 2, 2, 5)),
+            dma((2, 2)),
+            dma((2,)),
             dma(()),
         ],
         compiler_params=pltpu.CompilerParams(
@@ -733,8 +784,11 @@
                 cols = pl.ds(first, min(chunk, width - first))
                 got = dot(picked, source[slot, :, cols]).astype(bf16)
                 for e in range(experts):
-                    at = pl.ds(begin[e], window)
-                    target[e, at, cols] += got[e * window : (e + 1) * window]
+                    first_at = pl.ds(begin[e], WINDOW_ALIGN)
+                    rest_at = pl.ds(begin[e] + WINDOW_ALIGN, window - WINDOW_ALIGN)
+                    split = e * window + WINDOW_ALIGN
+                    target[e, first_at, cols] += got[e * window : split]
+                    target[e, rest_at, cols] = got[split : (e + 1) * window]
         return carry
 
     lax.fori_loop(0, blocks, take, 0)
@@ -1533,7 +1587,7 @@
     grads, input_gradient,
     back, residual, sent, dy, x, w, ctx, aux_w, normed, raw, query, key, value, context,
     cot, context_cot, raw_cot, key_sum, value_sum, small, first, first_got, stage, result,
-    cosine, sine, in_s, out_s, y_s, g_s,
+    cosine, sine, probs, in_s, out_s, y_s, g_s,
 ):
     bf16, f32 = jnp.bfloat16, jnp.float32
     me = Place()
@@ -1588,7 +1642,7 @@
     logit_cot = logit_cot.astype(bf16)
     small[...] = dot(sent[:, :features], logit_cot, ((0,), (0,)))
     midnorm = jnp.zeros((1, features), f32)
-    step = 32
+    step, swaps = 32, []
     for i in range(own_rows // step):
         at = slice(i * step, (i + 1) * step)
         total = residual[at, :]
@@ -1603,9 +1657,11 @@
             gained - unit * jnp.mean(gained * unit, axis=-1, keepdims=True)
         )
         residual[at, :] = total_cot
-        cot[pl.ds(pl.multiple_of(me.y * own_rows + i * step, step), step), :] = total_cot.astype(bf16)
-    swap = remote(cot.at[mine], cot.at[mine], y_s.at[0, 0], y_s.at[1, 0], me.y_mate)
-    swap.start()
+        there = pl.ds(pl.multiple_of(me.y * own_rows + i * step, step), step)
+        cot[there, :] = total_cot.astype(bf16)
+        swap = remote(cot.at[there], cot.at[there], y_s.at[0, i], y_s.at[1, i], me.y_mate)
+        swap.start()
+        swaps.append(swap)
     for copy in loads[5:10]:
         copy.wait()
 
@@ -1614,14 +1670,21 @@
             cols = pl.ds(c * chunk, chunk)
             context_cot[part, cols] = dot(cot[part, :], ctx[:, cols]).astype(bf16)
 
+    allowed = allowed_pairs(lengths[sequence_order[me.dp]], rows)
+
+    def recall(h, carry):
+        probs[h] = probabilities(query[h], key[h // group], allowed)
+        return carry
+
     spread_context(mine)
-    swap.wait_recv()
+    lax.fori_loop(0, heads, recall, 0)
+    for swap in swaps:
+        swap.wait_recv()
     spread_context(theirs)
     for copy in loads[10:]:
         copy.wait()
 
     turn_c, turn_s = cosine[...], sine[...]
-    allowed = allowed_pairs(lengths[sequence_order[me.dp]], rows)
     key_sum[...] = jnp.zeros_like(key_sum)
     value_sum[...] = jnp.zeros_like(value_sum)
 
@@ -1636,12 +1699,12 @@
     def head(h, query_part):
         g = h // group
         at = pl.ds(pl.multiple_of(h * HEAD_SIZE, HEAD_SIZE), HEAD_SIZE)
-        probs = probabilities(query[h], key[g], allowed)
+        soft = probs[h]
         cots = context_cot[:, at]
         prob_cot = dot(cots, value[g], ((1,), (1,)))
-        score_cot = probs * (prob_cot - jnp.sum(probs * prob_cot, axis=-1, keepdims=True))
+        score_cot = soft * (prob_cot - jnp.sum(soft * prob_cot, axis=-1, keepdims=True))
         score_cot = score_cot.astype(bf16)
-        value_sum[g] += dot(probs.astype(bf16), cots, ((0,), (0,)))
+        value_sum[g] += dot(soft.astype(bf16), cots, ((0,), (0,)))
         key_sum[g] += dot(score_cot, query[h], ((0,), (0,)))
         turned = dot(score_cot, key[g]) * SCORE_SCALE
         raw_cot[:, at], part = raw_back(unturn(turned, turn_c, turn_s), raw[h], query_gain)
@@ -1664,7 +1727,7 @@
         cols = pl.ds(c * chunk, chunk)
         first[:, cols] = dot(raw_cot[theirs, :], w[cols, :], ((1,), (1,))).astype(bf16)
         copy = remote(
-            first.at[:, cols], first_got.at[:, cols], y_s.at[0, 1 + c], y_s.at[1, 1 + c], me.y_mate
+            first.at[:, cols], first_got.at[:, cols], y_s.at[0, len(swaps) + c], y_s.at[1, len(swaps) + c], me.y_mate
         )
         copy.start()
         copies.append(copy)
@@ -1736,7 +1799,8 @@
     aux_w[...] = (small[...] + extra.T).astype(bf16)
     last = pltpu.make_async_copy(aux_w, grads.at[:, pl.ds(qkv + wide, AUX)], out_s.at[1])
     last.start()
-    swap.wait_send()
+    for swap in swaps:
+        swap.wait_send()
     for copy in copies:
         copy.wait_send()
     for i in (2, 1):
@@ -1793,9 +1857,10 @@
             pltpu.VMEM((own_rows, features), bf16),
             pltpu.VMEM((rows, HEAD_SIZE), f32),
             pltpu.VMEM((rows, HEAD_SIZE), f32),
+            pltpu.VMEM((heads, rows, rows), f32),
             dma((16,)),
             dma((2,)),
-            dma((2, 1 + features // 512)),
+            dma((2, own_rows // 32 + features // 512)),
             dma((2,)),
         ],
         compiler_params=pltpu.CompilerParams(

time: 594 us -> 576 us (0.970)
  Pallas kernels: 581 us -> 564 us
    pallas_call x1, Pallas kernels: 84.6 us -> 68.4 us  [scatter_all(): pl.pallas_call(row_scatter_kernel, out_shape=jax.ShapeDtypeStruct((rows,...]
where the time goes in v8:
time: 576 us; the launch traced here: 575 us
  Pallas kernels  564 us (98%)
  local copies, waits for them, and re-layouts  6.23 us (1%)
    pallas_call x1, Pallas kernels, opening(): pl.pallas_call(functools.partial(opening_kernel, experts, qkv), out_shape...  228 us
    pallas_call x1, Pallas kernels, last_scatter(): pl.pallas_call(last_scatter_kernel, out_shape=(jax.ShapeDtypeStruct((g_ro...  145 us
    pallas_call x1, Pallas kernels, expert_layer(): pl.pallas_call(expert_kernel, out_shape=(shape((blocks, block_rows, featu...  73.4 us
    pallas_call x1, Pallas kernels, scatter_all(): pl.pallas_call(row_scatter_kernel, out_shape=jax.ShapeDtypeStruct((rows,...  68.4 us
    pallas_call x1, Pallas kernels, attention_backward(): pl.pallas_call(functools.partial(backward_kernel, experts), out_shape=(ja...  47.2 us

profile of v8, /device:TPU:0, one launch (start us, length us, event | category | flops | bytes accessed | tf_op | source)
XLA Modules:
  0.0 575.1 jit_solution(4427737981476055951)
XLA Ops:
  0.7 0.7 compare_select_fusion
  1.3 1.3 gather_fusion
  2.6 0.1 iota_compare_fusion.1
  2.7 227.8 %shard_map.308 = (bf16[16,128,4736]{2,1,0:T(8,128)(2,1)}, bf16[32,128,2048]{2,1,0:T(8,128)(2,1)}, bf16[2,128,2048]{2,1,0:T(8,128)(2,1)}, bf16[32,128,2176]{2,1,0...) custom-call(s32[16]{0:T(128)} %lengths.3, ...), custom_call_target="tpu_custom_call" | custom-call | tf_op jit(solution)/shard_map/pallas_call | solution.py:1506
  230.6 1.3 slice_convert_fusion
  231.9 0.3 copy.66
  232.3 0.2 compare_reduce_fusion
  232.5 0.1 fusion.1
  232.7 0.4 fusion.6
  233.1 0.1 add.41
  233.2 0.1 copy.70
  233.3 0.1 copy.71
  233.4 0.1 reduce_window_sum.16
  233.5 0.6 pad_add_fusion.info
  234.1 0.2 copy.73
  234.3 0.1 copy.74
  234.4 0.1 copy.75
  234.5 0.7 and_select_fusion.pos
  235.2 73.4 %shard_map.309 = (bf16[16,256,2048]{2,1,0:T(8,128)(2,1)}, bf16[16,256,2176]{2,1,0:T(8,128)(2,1)}, f32[2,2048,384]{2,1,0:T(8,128)}, f32[2,2048,384]{2,1,0:T(8,128)}, f32[2,384,2048]{2,1,0:T(8,128)}) custom-call(s32[34]{0:T(128)} %pad_add_fusion.info, s32[16,2,256]{2,1,0:T(2,128)} %and_select_fusion.pos, bf16[16,256,2176]{2,1,0:T(8,128)(2,1)} %bitcast.41, ...), custom_call_target="tpu_custom_call" | custom-call | tf_op jit(solution)/shard_map/pallas_call | solution.py:930
  308.6 68.4 %shard_map.310.back_in = bf16[128,2176]{1,0:T(8,128)(2,1)} custom-call(bf16[32,128,2176]{2,1,0:T(8,128)(2,1)} %bitcast.42), custom_call_target="tpu_custom_call" | custom-call | tf_op jit(solution)/shard_map/pallas_call | solution.py:683
  376.9 47.2 %shard_map.311 = (bf16[2048,4736]{1,0:T(8,128)(2,1)}, bf16[128,2048]{1,0:T(8,128)(2,1)}) custom-call(s32[16]{0:T(128)} %lengths.3, s32[16]{0:T(128)} %sequence_order.3, bf16[128,2176]{1,0:T(8,128)(2,1)} %shard_map.310.back_in, f32[128,2048]{1,0:T(8,128)} %get-tuple-element.49.residual_in.residual, bf16[128,2176]{1,0:T(8,128)(2,1)} %get-tuple-element.50.sent_in, ...), custom_call_target="tpu_custom_call" | custom-call | tf_op jit(solution)/shard_map/pallas_call | solution.py:1825
  424.1 0.0 copy-start
  424.1 0.0 copy-start.3
  424.2 145.3 %shard_map.312 = (bf16[128,4736]{1,0:T(8,128)(2,1)}, bf16[128,2048]{1,0:T(8,128)(2,1)}) custom-call(bf16[16,128,4736]{2,1,0:T(8,128)(2,1)} %bitcast.40, bf16[32,128,2048]{2,1,0:T(8,128)(2,1)} %bitcast.44), custom_call_target="tpu_custom_call" | custom-call | tf_op jit(solution)/shard_map/pallas_call | solution.py:2092
  569.4 0.0 copy-done
  569.4 0.0 copy-start.1
  569.5 1.3 copy-done.1
  570.7 1.0 copy-done.2
  571.8 1.9 shard_map.313
  573.7 0.7 copy.76
  574.3 0.0 copy-done.3
  574.3 0.8 copy.90
  (10 shorter events, 0.2 us)
Async XLA Ops:
  424.1 145.3 %copy-start = (f32[128,2048]{1,0:T(8,128)S(1)}, f32[128,2048]{1,0:T(8,128)}, u32[]{:S(2)}) copy-start(f32[128,2048]{1,0:T(8,128)} %get-tuple-element.49.residual_in.residual) | copy-start | bytes 3145732
  424.1 150.2 %copy-start.3 = (bf16[128,2048]{1,0:T(8,128)(2,1)S(1)}, bf16[128,2048]{1,0:T(8,128)(2,1)}, u32[]{:S(2)}) copy-start(bf16[128,2048]{1,0:T(8,128)(2,1)} %get-tuple-element.149) | copy-start | bytes 1572868
  569.4 1.3 copy-start.1
  570.7 1.0 copy-start.2

commit v9 on v8

--- a/solution.py
+++ b/solution.py
@@ -725,8 +725,8 @@
     part = hg.shape[2]
     cap = hg.shape[1]
     window = padded - cap
-    tile = 256
-    chunk = 512
+    tile = cap // 2
+    chunk = d_stage.shape[2]
 
     def load(b):
         slot = b % 2
@@ -865,6 +865,7 @@
 
     lax.fori_loop(0, blocks, put, 0)
 
+    tile = g_stage.shape[1]
     tiles = features // tile
 
     def g_copies(step):
@@ -953,8 +954,8 @@
             pltpu.VMEM((experts, capacity, part), bf16),
             pltpu.VMEM((2, block_rows, wide), bf16),
             pltpu.VMEM((2, block_rows, features), bf16),
-            pltpu.VMEM((2, 256, 2 * part), f32),
-            pltpu.VMEM((2, part, 512), f32),
+            pltpu.VMEM((2, features // 2, 2 * part), f32),
+            pltpu.VMEM((2, part, features // 2), f32),
             dma((2, 2)),
             dma((experts, 3)),
             dma((2, 2)),
@@ -987,6 +988,13 @@
     return lax.rsqrt(jnp.mean(value * value, axis=-1, keepdims=True) + epsilon)
 
 
+def split_pair(me, both):
+    half = both.shape[0] // 2
+    first = me.y == 0
+    lower, upper = both[:half], both[half:]
+    return jnp.where(first, upper, lower), jnp.where(first, lower, upper)
+
+
 def meet_y(me):
     barrier = pltpu.get_barrier_semaphore()
     pl.semaphore_signal(barrier, 1, device_id=me.y_mate, device_id_type=pl.DeviceIdType.MESH)
@@ -1024,7 +1032,7 @@
     ("wx", 2, 0), ("b", 2, 1), ("w", 2, 1), ("wx", 3, 0), ("y1", 1, 1, 0), ("prep",), ("qkv",),
     ("h", 0), ("y1", 1, 0, 1), ("b", 2, 0), ("w", 3, 1), ("y1", 0, 0, 1), ("h", 1), ("b", 3, 0),
     ("wx", 1, 1), ("h", 2), ("wx", 2, 1), ("a", 3), ("h", 3), ("wx", 0, 1), ("b", 3, 1),
-    ("wx", 3, 1), ("ctx",), ("ax", 3), ("ctx2",), ("fin",), ("n", 0), ("y1", 0, 1, 0),
+    ("wx", 3, 1), ("ctx",), ("ax", 3), ("fin",), ("n", 0), ("y1", 0, 1, 0),
     ("y1", 1, 1, 1), ("c0",), ("n", 1), ("n", 2), ("c1",), ("n", 3), ("nx", 1), ("c2", 0),
     ("cz", 1, 1, 0), ("nx", 0), ("c2", 1), ("cz", 1, 1, 1), ("ny", 1), ("ny", 2),
     ("cz", 2, 1, 0), ("cz", 1, 0, 0), ("y1", 2, 0, 1), ("ny", 3), ("y1", 0, 1, 1),
@@ -1222,8 +1230,6 @@
     own_rows = rows // 2
     heads, key_heads = query.shape[0], key.shape[0]
     chunk = 512
-    mine = pl.ds(pl.multiple_of(me.y * own_rows, own_rows), own_rows)
-    theirs = pl.ds(pl.multiple_of((1 - me.y) * own_rows, own_rows), own_rows)
     turn_c, turn_s = cosine[...], sine[...]
     held, outs, copies = {}, [], []
 
@@ -1329,14 +1335,13 @@
         load.wait()
         for c in range(features // chunk):
             cols = pl.ds(c * chunk, chunk)
-            att[:, cols] = dot(context[theirs, :], ctx_part(c), ((1,), (1,))).astype(bf16)
+            their_part, residual[:, cols] = split_pair(
+                me, dot(context[...], ctx_part(c), ((1,), (1,)))
+            )
+            att[:, cols] = their_part.astype(bf16)
             copy = remote(att.at[:, cols], got.at[:, cols], y_s.at[0, c], y_s.at[1, c], me.y_mate)
             copy.start()
             copies.append(copy)
-
-    def output_own():
-        for c in range(features // chunk):
-            residual[:, pl.ds(c * chunk, chunk)] = dot(context[mine, :], ctx_part(c), ((1,), (1,)))
 
     def finish():
         for copy in copies:
@@ -1433,7 +1438,7 @@
         "c0": c_own, "c1": c_from_x, "c2": c_from_y, "cz": c_line,
         "pair": pair_rows, "bx": b_over_x, "ay0": lambda: a_over_y(0), "w": w_own, "wx": w_across,
         "a": a_own, "ax": a_across, "b": b_step, "y1": y_done, "prep": prepare, "qkv": project,
-        "h": attend, "ctx": output_over_y, "ctx2": output_own, "fin": finish,
+        "h": attend, "ctx": output_over_y, "fin": finish,
     }
     for name, *which in OPENING_PLAN:
         actions[name](*which)
@@ -1587,7 +1592,7 @@
     grads, input_gradient,
     back, residual, sent, dy, x, w, ctx, aux_w, normed, raw, query, key, value, context,
     cot, context_cot, raw_cot, key_sum, value_sum, small, first, first_got, stage, result,
-    cosine, sine, probs, in_s, out_s, y_s, g_s,
+    cosine, sine, probs, own_first, in_s, out_s, y_s, g_s,
 ):
     bf16, f32 = jnp.bfloat16, jnp.float32
     me = Place()
@@ -1597,8 +1602,6 @@
     group = heads // key_heads
     qkv, wide = w.shape[1], heads * HEAD_SIZE
     chunk = 512
-    mine = pl.ds(pl.multiple_of(me.y * own_rows, own_rows), own_rows)
-    theirs = pl.ds(pl.multiple_of((1 - me.y) * own_rows, own_rows), own_rows)
     loads = [
         pltpu.make_async_copy(source, target, in_s.at[i])
         for i, (source, target) in enumerate(
@@ -1665,22 +1668,18 @@
     for copy in loads[5:10]:
         copy.wait()
 
-    def spread_context(part):
-        for c in range(wide // chunk):
-            cols = pl.ds(c * chunk, chunk)
-            context_cot[part, cols] = dot(cot[part, :], ctx[:, cols]).astype(bf16)
-
     allowed = allowed_pairs(lengths[sequence_order[me.dp]], rows)
 
     def recall(h, carry):
         probs[h] = probabilities(query[h], key[h // group], allowed)
         return carry
 
-    spread_context(mine)
-    lax.fori_loop(0, heads, recall, 0)
+    lax.fori_loop(0, heads, recall, 0, unroll=2)
     for swap in swaps:
         swap.wait_recv()
-    spread_context(theirs)
+    for c in range(wide // chunk):
+        cols = pl.ds(c * chunk, chunk)
+        context_cot[:, cols] = dot(cot[...], ctx[:, cols]).astype(bf16)
     for copy in loads[10:]:
         copy.wait()
 
@@ -1710,7 +1709,7 @@
         raw_cot[:, at], part = raw_back(unturn(turned, turn_c, turn_s), raw[h], query_gain)
         return query_part + part
 
-    query_part = lax.fori_loop(0, heads, head, jnp.zeros((1, HEAD_SIZE), f32))
+    query_part = lax.fori_loop(0, heads, head, jnp.zeros((1, HEAD_SIZE), f32), unroll=2)
     key_part = jnp.zeros((1, HEAD_SIZE), f32)
     for g in range(key_heads):
         turned = key_sum[g] * SCORE_SCALE
@@ -1725,13 +1724,16 @@
     copies = []
     for c in range(features // chunk):
         cols = pl.ds(c * chunk, chunk)
-        first[:, cols] = dot(raw_cot[theirs, :], w[cols, :], ((1,), (1,))).astype(bf16)
+        their_part, own_first[:, cols] = split_pair(
+            me, dot(raw_cot[...], w[cols, :], ((1,), (1,)))
+        )
+        first[:, cols] = their_part.astype(bf16)
         copy = remote(
             first.at[:, cols], first_got.at[:, cols], y_s.at[0, len(swaps) + c], y_s.at[1, len(swaps) + c], me.y_mate
         )
         copy.start()
         copies.append(copy)
-    block = 256
+    block = stage.shape[1]
 
     def store(i):
         slot = i % 2
@@ -1749,14 +1751,14 @@
         def _():
             store(i - 2).wait()
 
+        normed_t = normed[:, at].astype(f32).T.astype(bf16)
+        cot_t = cot[:, at].astype(f32).T.astype(bf16)
         for c in range(qkv // chunk):
             cols = pl.ds(c * chunk, chunk)
-            stage[slot, :, cols] = dot(normed[:, at], raw_cot[:, cols], ((0,), (0,))).astype(bf16)
+            stage[slot, :, cols] = dot(normed_t, raw_cot[:, cols]).astype(bf16)
         for c in range(wide // chunk):
             cols = pl.ds(c * chunk, chunk)
-            stage[slot, :, pl.ds(qkv + c * chunk, chunk)] = dot(
-                cot[:, at], context[:, cols], ((0,), (0,))
-            ).astype(bf16)
+            stage[slot, :, pl.ds(qkv + c * chunk, chunk)] = dot(cot_t, context[:, cols]).astype(bf16)
         store(i).start()
         return carry
 
@@ -1766,8 +1768,7 @@
         copy.wait_recv()
     for c in range(features // chunk):
         cols = pl.ds(c * chunk, chunk)
-        back_cols = dot(raw_cot[mine, :], w[cols, :], ((1,), (1,)))
-        result_part = back_cols + first_got[:, cols].astype(f32)
+        result_part = own_first[:, cols] + first_got[:, cols].astype(f32)
         back[:, cols] = result_part.astype(bf16)
     step = 32
     for i in range(own_rows // step):
@@ -1853,11 +1854,12 @@
             pltpu.VMEM((features, AUX), f32),
             pltpu.VMEM((own_rows, features), bf16),
             pltpu.VMEM((own_rows, features), bf16),
-            pltpu.VMEM((2, 256, qkv + wide), bf16),
+            pltpu.VMEM((2, 512, qkv + wide), bf16),
             pltpu.VMEM((own_rows, features), bf16),
             pltpu.VMEM((rows, HEAD_SIZE), f32),
             pltpu.VMEM((rows, HEAD_SIZE), f32),
             pltpu.VMEM((heads, rows, rows), f32),
+            pltpu.VMEM((own_rows, features), f32),
             dma((16,)),
             dma((2,)),
             dma((2, own_rows // 32 + features // 512)),

time: 576 us -> 565 us (0.981)
  Pallas kernels: 564 us -> 551 us
    pallas_call x1, Pallas kernels: 73.4 us -> 66.6 us  [expert_layer(): pl.pallas_call(expert_kernel, out_shape=(shape((blocks, block_rows, featu...]
where the time goes in v9:
time: 565 us; the launch traced here: 562 us
  Pallas kernels  551 us (98%)
  local copies, waits for them, and re-layouts  6.23 us (1%)
    pallas_call x1, Pallas kernels, opening(): pl.pallas_call(functools.partial(opening_kernel, experts, qkv), out_shape...  228 us
    pallas_call x1, Pallas kernels, last_scatter(): pl.pallas_call(last_scatter_kernel, out_shape=(jax.ShapeDtypeStruct((g_ro...  143 us
    pallas_call x1, Pallas kernels, scatter_all(): pl.pallas_call(row_scatter_kernel, out_shape=jax.ShapeDtypeStruct((rows,...  68.3 us
    pallas_call x1, Pallas kernels, expert_layer(): pl.pallas_call(expert_kernel, out_shape=(shape((blocks, block_rows, featu...  66.6 us
    pallas_call x1, Pallas kernels, attention_backward(): pl.pallas_call(functools.partial(backward_kernel, experts), out_shape=(ja...  43.4 us

profile of v9, /device:TPU:0, one launch (start us, length us, event | category | flops | bytes accessed | tf_op | source)
XLA Modules:
  0.0 562.4 jit_solution(16194277287036717796)
XLA Ops:
  0.7 0.7 compare_select_fusion
  1.3 1.3 gather_fusion
  2.6 0.1 iota_compare_fusion.1
  2.7 227.8 %shard_map.308 = (bf16[16,128,4736]{2,1,0:T(8,128)(2,1)}, bf16[32,128,2048]{2,1,0:T(8,128)(2,1)}, bf16[2,128,2048]{2,1,0:T(8,128)(2,1)}, bf16[32,128,2176]{2,1,0...) custom-call(s32[16]{0:T(128)} %lengths.3, ...), custom_call_target="tpu_custom_call" | custom-call | tf_op jit(solution)/shard_map/pallas_call | solution.py:1511
  230.5 1.3 slice_convert_fusion
  231.8 0.3 copy.66
  232.2 0.2 compare_reduce_fusion
  232.4 0.1 fusion.1
  232.6 0.4 fusion.6
  233.0 0.1 add.41
  233.1 0.1 copy.70
  233.2 0.1 copy.71
  233.3 0.1 reduce_window_sum.16
  233.4 0.6 pad_add_fusion.info
  234.0 0.2 copy.73
  234.2 0.1 copy.74
  234.3 0.1 copy.75
  234.4 0.7 and_select_fusion.pos
  235.1 66.6 %shard_map.309 = (bf16[16,256,2048]{2,1,0:T(8,128)(2,1)}, bf16[16,256,2176]{2,1,0:T(8,128)(2,1)}, f32[2,2048,384]{2,1,0:T(8,128)}, f32[2,2048,384]{2,1,0:T(8,128)}, f32[2,384,2048]{2,1,0:T(8,128)}) custom-call(s32[34]{0:T(128)} %pad_add_fusion.info, s32[16,2,256]{2,1,0:T(2,128)} %and_select_fusion.pos, bf16[16,256,2176]{2,1,0:T(8,128)(2,1)} %bitcast.41, ...), custom_call_target="tpu_custom_call" | custom-call | tf_op jit(solution)/shard_map/pallas_call | solution.py:931
  301.7 68.3 %shard_map.310.back_in = bf16[128,2176]{1,0:T(8,128)(2,1)} custom-call(bf16[32,128,2176]{2,1,0:T(8,128)(2,1)} %bitcast.42), custom_call_target="tpu_custom_call" | custom-call | tf_op jit(solution)/shard_map/pallas_call | solution.py:683
  370.0 43.4 %shard_map.311 = (bf16[2048,4736]{1,0:T(8,128)(2,1)}, bf16[128,2048]{1,0:T(8,128)(2,1)}) custom-call(s32[16]{0:T(128)} %lengths.3, s32[16]{0:T(128)} %sequence_order.3, bf16[128,2176]{1,0:T(8,128)(2,1)} %shard_map.310.back_in, f32[128,2048]{1,0:T(8,128)} %get-tuple-element.49.residual_in.residual, bf16[128,2176]{1,0:T(8,128)(2,1)} %get-tuple-element.50.sent_in, ...), custom_call_target="tpu_custom_call" | custom-call | tf_op jit(solution)/shard_map/pallas_call | solution.py:1826
  413.5 0.0 copy-start
  413.5 0.0 copy-start.3
  413.5 143.2 %shard_map.312 = (bf16[128,4736]{1,0:T(8,128)(2,1)}, bf16[128,2048]{1,0:T(8,128)(2,1)}) custom-call(bf16[16,128,4736]{2,1,0:T(8,128)(2,1)} %bitcast.40, bf16[32,128,2048]{2,1,0:T(8,128)(2,1)} %bitcast.44), custom_call_target="tpu_custom_call" | custom-call | tf_op jit(solution)/shard_map/pallas_call | solution.py:2094
  556.7 0.0 copy-done
  556.7 0.0 copy-start.1
  556.8 1.3 copy-done.1
  558.0 1.0 copy-done.2
  559.1 1.9 shard_map.313
  561.0 0.7 copy.76
  561.6 0.0 copy-done.3
  561.6 0.8 copy.90
  (10 shorter events, 0.2 us)
Async XLA Ops:
  413.5 143.3 %copy-start = (f32[128,2048]{1,0:T(8,128)S(1)}, f32[128,2048]{1,0:T(8,128)}, u32[]{:S(2)}) copy-start(f32[128,2048]{1,0:T(8,128)} %get-tuple-element.49.residual_in.residual) | copy-start | bytes 3145732
  413.5 148.2 %copy-start.3 = (bf16[128,2048]{1,0:T(8,128)(2,1)S(1)}, bf16[128,2048]{1,0:T(8,128)(2,1)}, u32[]{:S(2)}) copy-start(bf16[128,2048]{1,0:T(8,128)(2,1)} %get-tuple-element.149) | copy-start | bytes 1572868
  556.7 1.3 copy-start.1
  558.0 1.0 copy-start.2

commit v10 on v9

--- a/solution.py
+++ b/solution.py
@@ -1874,28 +1874,34 @@
     )
 
 
-LAST_CUT = 5
+LAST_CUT = 6
 LAST_PLAN = (
-    ("gx", 0, 0), ("dy", 0, 1, 1), ("gx", 0, 1), ("dy", 0, 0, 1), ("dy", 1, 1, 1), ("db", 0, 1),
-    ("gx", 1, 1), ("db", 0, 0), ("dy", 2, 1, 1), ("dy", 1, 1, 0), ("gx", 1, 0), ("db", 1, 1),
-    ("dy", 2, 1, 0), ("gx", 2, 0), ("db", 2, 1), ("dy", 0, 1, 0), ("dy", 2, 0, 1),
-    ("dy", 0, 0, 0), ("dy", 3, 1, 1), ("gc", 0), ("dy", 1, 0, 0), ("dy", 1, 0, 1),
-    ("dy", 3, 1, 0), ("dy", 2, 0, 0), ("gx", 2, 1), ("dax", 2), ("dax", 0), ("dax", 1),
-    ("gc", 1), ("gc", 2), ("gx", 3, 0), ("dy", 3, 0, 1), ("gx", 3, 1), ("da", 0), ("dax", 3),
-    ("dy", 3, 0, 0), ("db", 1, 0), ("da", 1), ("db", 2, 0), ("da", 2), ("gc", 3), ("sm",),
-    ("db", 3, 1), ("db", 3, 0), ("sm2",), ("da", 3), ("bx",),
+    ("gx", 0, 1), ("dy", 0, 1, 1), ("hz", 0, 1), ("dy", 0, 0, 1), ("hz", 0, 0), ("gx", 0, 0),
+    ("dy", 0, 1, 0), ("hz", 1, 1), ("db", 0, 0), ("db", 0, 1), ("hz", 2, 1), ("hz", 1, 0),
+    ("gx", 1, 0), ("dy", 1, 1, 1), ("dy", 1, 1, 0), ("dy", 0, 0, 0), ("db", 1, 1),
+    ("dy", 2, 1, 0), ("dax", 0), ("gx", 1, 1), ("gx", 2, 1), ("dy", 1, 0, 1), ("hz", 2, 0),
+    ("gc", 0), ("dax", 1), ("dy", 2, 0, 1), ("dy", 2, 0, 0), ("da", 0), ("gx", 2, 0),
+    ("dy", 3, 1, 0), ("dy", 3, 0, 0), ("db", 1, 0), ("dy", 2, 1, 1), ("gc", 1), ("dy", 1, 0, 0),
+    ("gx", 3, 1), ("dy", 3, 1, 1), ("gx", 3, 0), ("hz", 3, 1), ("hz", 3, 0), ("db", 2, 1),
+    ("hx",), ("dax", 2), ("dy", 3, 0, 1), ("gc", 2), ("da", 1), ("gc", 3), ("db", 2, 0),
+    ("dax", 3), ("da", 2), ("hend",), ("sm",), ("db", 3, 1), ("db", 3, 0), ("sm2",), ("da", 3),
+    ("bx",),
 )
 
 
 def last_scatter_kernel(
     g_part, d_part, g_out, d_out,
-    g_own, g_core, g_x, g_z, d_own, d_core, d_y, a_x, b_x, a_z, b_z, small_got,
-    gl_s, gc_s, gx_s, gz_s, dl_s, dc_s, dy_s, ax_s, bx_s, az_s, bz_s, small_s, out_s,
+    g_own, g_core, g_x, g_z, d_own, d_core, d_y, a_x, b_x, a_z, b_z, small_got, h_z, h_x,
+    gl_s, gc_s, gx_s, gz_s, dl_s, dc_s, dy_s, ax_s, bx_s, az_s, bz_s, small_s, hz_s, hx_s, out_s,
 ):
     me = Place()
     g_rows, d_rows = g_own.shape[2], d_own.shape[3]
-    cut, g_half = a_x.shape[1], g_rows // 2
-    g_all, low, high = (0, g_rows), (0, cut), (cut, d_rows - cut)
+    cut, g_most = a_x.shape[1], g_x.shape[1]
+    g_half = g_rows // 2
+    g_spans = ((0, g_half), (g_half, g_most - g_half))
+    g_all, g_rest = (0, g_most), (g_most, g_rows - g_most)
+    g_all_at, g_rest_at = pl.ds(*g_all), pl.ds(*g_rest)
+    low, high = (0, cut), (cut, d_rows - cut)
     low_at, high_at = pl.ds(0, cut), pl.ds(cut, d_rows - cut)
     last = GRID_Z - 1
     loads, cores, sends = {}, {}, []
@@ -1934,7 +1940,7 @@
     gx = [
         [
             remote(
-                g_own.at[k, 1, pl.ds(h * g_half, g_half)], g_x.at[k, pl.ds(h * g_half, g_half)],
+                g_own.at[k, 1, pl.ds(*g_spans[h])], g_x.at[k, pl.ds(*g_spans[h])],
                 gx_s.at[0, k, h], gx_s.at[1, k, h], me.x_mate,
             )
             for h in range(2)
@@ -2005,7 +2011,7 @@
 
     def g_across(k, h):
         arrive(k, 1)
-        add_rows(g_own.at[k, 1], [(g_core.at[k, 1], 0)], (h * g_half, g_half))
+        add_rows(g_own.at[k, 1], [(g_core.at[k, 1], 0)], g_spans[h])
         gx[k][h].start()
 
     def g_column(k):
@@ -2013,7 +2019,20 @@
         for h in range(2):
             gx[k][h].wait_recv()
         add_rows(g_own.at[k, 0], [(g_core.at[k, 0], 0), (g_x.at[k], 0)], g_all)
-        line(k, g_own.at[k, 0], g_own.at[k, 0], g_all, g_z, gz_s, 0)
+        block = g_own.at[k, 0]
+        line(k, block, block.at[g_all_at], g_all, g_z, gz_s, 0)
+
+    def rest_line(k, fx):
+        arrive(k, fx)
+        block = g_own.at[k, fx]
+        add_rows(block, [(g_core.at[k, fx], 0)], g_rest)
+        line(k, block, block.at[g_rest_at], g_rest, h_z.at[fx], hz_s.at[fx], g_most)
+
+    rest_x = remote(g_own.at[last, 1, g_rest_at], h_x, hx_s.at[0], hx_s.at[1], me.x_mate)
+
+    def rest_end():
+        rest_x.wait_recv()
+        add_rows(g_own.at[last, 0], [(h_x, g_most)], g_rest)
 
     def over_y(k, fx, h):
         arrive(k, fx, 1)
@@ -2054,7 +2073,7 @@
 
     actions = {
         "gx": g_across, "gc": g_column, "dy": over_y, "db": b_line, "dax": a_over_x, "da": a_line,
-        "bx": b_from_x, "sm": small.start, "sm2": small_sum,
+        "bx": b_from_x, "hz": rest_line, "hx": rest_x.start, "hend": rest_end, "sm": small.start, "sm2": small_sum,
     }
     for name, *which in LAST_PLAN:
         actions[name](*which)
@@ -2072,11 +2091,13 @@
                 dy[k, fx, h].wait_send()
         ax[k].wait_send()
         if k < last:
-            line_done(k, g_own.at[k, 0], g_z, gz_s)
+            line_done(k, g_own.at[k, 0, g_all_at], g_z, gz_s)
             for fx in range(2):
+                line_done(k, g_own.at[k, fx, g_rest_at], h_z.at[fx], hz_s.at[fx])
                 line_done(k, d_own.at[k, fx, 0, high_at], b_z.at[fx], bz_s.at[fx])
             line_done(k, d_own.at[k, 0, 0, low_at], a_z, az_s)
     bx.wait_send()
+    rest_x.wait_send()
     for sent in cores.values():
         sent.wait_send()
     for copy in outs:
@@ -2087,7 +2108,7 @@
     chips, pair = lax.axis_size("dp"), lax.axis_size("tensor")
     g_rows, g_wide = grads.shape[0] // chips, grads.shape[1]
     d_rows, d_wide = sums.shape[0] // (chips * pair), sums.shape[1]
-    cut = d_rows * LAST_CUT // 8
+    cut, most = d_rows * LAST_CUT // 8, 7 * g_rows // 8
     dma = pltpu.SemaphoreType.DMA
     low = grads.dtype
     anywhere = pl.BlockSpec(memory_space=pl.ANY)
@@ -2102,8 +2123,8 @@
         scratch_shapes=[
             pltpu.VMEM((4, 2, g_rows, g_wide), low),
             pltpu.VMEM((4, 2, g_rows, g_wide), low),
-            pltpu.VMEM((4, g_rows, g_wide), low),
-            pltpu.VMEM((5, g_rows, g_wide), low),
+            pltpu.VMEM((4, most, g_wide), low),
+            pltpu.VMEM((5, most, g_wide), low),
             pltpu.VMEM((4, 2, 2, d_rows, d_wide), low),
             pltpu.VMEM((4, 2, 2, d_rows, d_wide), low),
             pltpu.VMEM((4, 2, d_rows, d_wide), low),
@@ -2112,6 +2133,8 @@
             pltpu.VMEM((5, cut, d_wide), low),
             pltpu.VMEM((2, 5, d_rows - cut, d_wide), low),
             pltpu.VMEM((g_rows, AUX), low),
+            pltpu.VMEM((2, 5, g_rows - most, g_wide), low),
+            pltpu.VMEM((g_rows - most, g_wide), low),
             dma((4, 2)),
             dma((2, 4, 2)),
             dma((2, 4, 2)),
@@ -2122,6 +2145,8 @@
             dma((2, 4)),
             dma((2,)),
             dma((2, 5)),
+            dma((2, 2, 5)),
+            dma((2,)),
             dma((2, 2, 5)),
             dma((2,)),
             dma((2,)),

time: 565 us -> 564 us (level)
  no operation moved by 1% of the time
where the time goes in v10:
time: 564 us; the launch traced here: 557 us
  Pallas kernels  546 us (97%)
  local copies, waits for them, and re-layouts  6.23 us (1%)
    pallas_call x1, Pallas kernels, opening(): pl.pallas_call(functools.partial(opening_kernel, experts, qkv), out_shape...  228 us
    pallas_call x1, Pallas kernels, last_scatter(): pl.pallas_call(last_scatter_kernel, out_shape=(jax.ShapeDtypeStruct((g_ro...  138 us
    pallas_call x1, Pallas kernels, scatter_all(): pl.pallas_call(row_scatter_kernel, out_shape=jax.ShapeDtypeStruct((rows,...  68.4 us
    pallas_call x1, Pallas kernels, expert_layer(): pl.pallas_call(expert_kernel, out_shape=(shape((blocks, block_rows, featu...  66.6 us
    pallas_call x1, Pallas kernels, attention_backward(): pl.pallas_call(functools.partial(backward_kernel, experts), out_shape=(ja...  43.5 us

profile of v10, /device:TPU:0, one launch (start us, length us, event | category | flops | bytes accessed | tf_op | source)
XLA Modules:
  0.0 557.3 jit_solution(8692147824396489064)
XLA Ops:
  0.7 0.7 compare_select_fusion
  1.3 1.3 gather_fusion
  2.6 0.1 iota_compare_fusion.1
  2.7 227.8 %shard_map.308 = (bf16[16,128,4736]{2,1,0:T(8,128)(2,1)}, bf16[32,128,2048]{2,1,0:T(8,128)(2,1)}, bf16[2,128,2048]{2,1,0:T(8,128)(2,1)}, bf16[32,128,2176]{2,1,0...) custom-call(s32[16]{0:T(128)} %lengths.3, ...), custom_call_target="tpu_custom_call" | custom-call | tf_op jit(solution)/shard_map/pallas_call | solution.py:1511
  230.5 1.3 slice_convert_fusion
  231.8 0.3 copy.66
  232.2 0.2 compare_reduce_fusion
  232.4 0.1 fusion.1
  232.6 0.4 fusion.6
  233.0 0.1 add.41
  233.1 0.1 copy.70
  233.2 0.1 copy.71
  233.3 0.1 reduce_window_sum.16
  233.4 0.6 pad_add_fusion.info
  234.0 0.2 copy.73
  234.2 0.1 copy.74
  234.3 0.1 copy.75
  234.4 0.7 and_select_fusion.pos
  235.1 66.6 %shard_map.309 = (bf16[16,256,2048]{2,1,0:T(8,128)(2,1)}, bf16[16,256,2176]{2,1,0:T(8,128)(2,1)}, f32[2,2048,384]{2,1,0:T(8,128)}, f32[2,2048,384]{2,1,0:T(8,128)}, f32[2,384,2048]{2,1,0:T(8,128)}) custom-call(s32[34]{0:T(128)} %pad_add_fusion.info, s32[16,2,256]{2,1,0:T(2,128)} %and_select_fusion.pos, bf16[16,256,2176]{2,1,0:T(8,128)(2,1)} %bitcast.41, ...), custom_call_target="tpu_custom_call" | custom-call | tf_op jit(solution)/shard_map/pallas_call | solution.py:931
  301.7 68.4 %shard_map.310.back_in = bf16[128,2176]{1,0:T(8,128)(2,1)} custom-call(bf16[32,128,2176]{2,1,0:T(8,128)(2,1)} %bitcast.42), custom_call_target="tpu_custom_call" | custom-call | tf_op jit(solution)/shard_map/pallas_call | solution.py:683
  370.1 43.5 %shard_map.311 = (bf16[2048,4736]{1,0:T(8,128)(2,1)}, bf16[128,2048]{1,0:T(8,128)(2,1)}) custom-call(s32[16]{0:T(128)} %lengths.3, s32[16]{0:T(128)} %sequence_order.3, bf16[128,2176]{1,0:T(8,128)(2,1)} %shard_map.310.back_in, f32[128,2048]{1,0:T(8,128)} %get-tuple-element.49.residual_in.residual, bf16[128,2176]{1,0:T(8,128)(2,1)} %get-tuple-element.50.sent_in, ...), custom_call_target="tpu_custom_call" | custom-call | tf_op jit(solution)/shard_map/pallas_call | solution.py:1826
  413.5 0.0 copy-start
  413.6 0.0 copy-start.3
  413.6 137.6 %shard_map.312 = (bf16[128,4736]{1,0:T(8,128)(2,1)}, bf16[128,2048]{1,0:T(8,128)(2,1)}) custom-call(bf16[16,128,4736]{2,1,0:T(8,128)(2,1)} %bitcast.40, bf16[32,128,2048]{2,1,0:T(8,128)(2,1)} %bitcast.44), custom_call_target="tpu_custom_call" | custom-call | tf_op jit(solution)/shard_map/pallas_call | solution.py:2115
  551.2 0.0 copy-done
  551.2 0.0 copy-start.1
  551.2 1.3 copy-done.1
  552.5 1.0 copy-done.2
  553.5 1.9 shard_map.313
  555.4 0.7 copy.76
  556.1 0.0 copy-done.3
  556.1 0.8 copy.90
  (10 shorter events, 0.2 us)
Async XLA Ops:
  413.5 137.7 %copy-start = (f32[128,2048]{1,0:T(8,128)S(1)}, f32[128,2048]{1,0:T(8,128)}, u32[]{:S(2)}) copy-start(f32[128,2048]{1,0:T(8,128)} %get-tuple-element.49.residual_in.residual) | copy-start | bytes 3145732
  413.6 142.6 %copy-start.3 = (bf16[128,2048]{1,0:T(8,128)(2,1)S(1)}, bf16[128,2048]{1,0:T(8,128)(2,1)}, u32[]{:S(2)}) copy-start(bf16[128,2048]{1,0:T(8,128)(2,1)} %get-tuple-element.149) | copy-start | bytes 1572868
  551.2 1.3 copy-start.1
  552.5 1.0 copy-start.2
